TPU v7x, 256 devices: a whole 4x4x8 slice. The times are simulated.
256 devices in a mesh: cols: 8 (over x, core), rows: 32 (over z, y).
Axes of the slice: x: 4, y: 4, z: 8, core: 2. Of those that a mesh axis runs over, the one named last changes fastest.
Arguments:
- rhs_leaf: bfloat16 [32768, 2048], P('rows', 'cols'), parts along dimension 1, may hold values from -6 to 6
- rhs_sep: bfloat16 [16384, 2048], P('rows', 'cols'), parts along dimension 1, may hold values from -6 to 6
- leaf_inv: bfloat16 [32768, 1024], P('rows'), may hold values from -1.5 to 1.5, as said below
- leaf_cpl: bfloat16 [32, 5, 128, 1024], P('rows'), may hold values from -0.09375 to 0.09375
- leaf_idx: int32 [32, 5, 128], P('rows'), may hold values from 0 to 511, as said below
- sep_inv: bfloat16 [16384, 512], P('rows'), may hold values from -1.5 to 1.5, as said below
- sep_cpl: bfloat16 [32, 4, 128, 512], P('rows'), may hold values from -0.125 to 0.125
- sep_idx: int32 [32, 4, 128], P('rows'), may hold values from 0 to 511, as said below
- stay_dofs: int32 [6, 2048], replicated, may hold values from 0 to 32767, as said below
- stay_coef: float32 [6, 2048], replicated, may hold values from -1 to 1
Outputs:
- disp_leaf: bfloat16 [32768, 2048], P('rows', 'cols'), parts along dimension 1
- disp_sep: bfloat16 [16384, 2048], P('rows', 'cols'), parts along dimension 1
- stretch: float32 [2048, 2048], P('rows', 'cols'), parts along dimension 1
There are 8 independent parts, one for each index of `cols`. A program takes and returns all parts, laid end to end along the dimension named above; an argument that names none is the same for every part. Nothing has to cross between parts.
Inputs may be any that keep to these rules, and one draw needn't show every extreme that they name: `leaf_inv`: each block of 1024 rows is lower triangular with a diagonal between 0.5 and 1.5. `sep_inv`: each block of 512 rows is lower triangular with a diagonal between 0.5 and 1.5. `leaf_idx`: the 128 rows of one subtree and level are distinct. `sep_idx`: the 128 rows of one separator and slot are distinct; slots beyond a separator's ancestors are not read. `stay_dofs`: stay e is collected by device e // 64. Of the 6 * 64 (component, stay) pairs of one device's stays, at most 12 name unknowns of any one subtree, and subtree 0 is named by exactly 12 of them.
All inputs are finite; a program needn't handle non-finite values.
Results may differ from a plain program's by a relative error of at most 0.014.
Values may be sent and summed in bfloat16 or wider, within the bound.
No kernel may reach another device: no remote copies, remote signals or barrier semaphores. Data moves between devices by JAX's collectives and lax.ppermute only.
A program may use at most 128 MiB of HBM per device.

v0:
```python
import jax
import jax.numpy as jnp
from jax import lax
from jax.sharding import PartitionSpec as P


def partner(value, axis, stride):
    mask = 2**stride
    pairs = [(source, source ^ mask) for source in range(lax.axis_size(axis))]
    return lax.ppermute(value, axis, pairs)


def spread(row_index, values, row_count):
    return jnp.zeros((row_count, values.shape[1]), jnp.float32).at[row_index].add(values)


def lead_dot(left, right):
    return lax.dot_general(
        left, right, (((0,), (0,)), ((), ())), preferred_element_type=jnp.float32
    )


def bit_order(height):
    return list(range(height))


def group_sum(partial_value, height):
    for bit_pos in bit_order(height):
        partial_value = partial_value + partner(partial_value, "rows", bit_pos)
    return partial_value


def on_device(
    rhs_leaf, rhs_sep, leaf_inv, leaf_cpl, leaf_idx, sep_inv, sep_cpl, sep_idx, stay_dofs, stay_coef
):
    devices = lax.axis_size("rows")
    depth_count = devices.bit_length() - 1
    device = lax.axis_index("rows")
    panel_rows = sep_inv.shape[0]
    columns = rhs_leaf.shape[1]
    leaf_rows = leaf_inv.shape[0]
    couple = leaf_cpl[0]
    couple_rows = leaf_idx[0]
    sep_couple = sep_cpl[0]
    sep_rows = sep_idx[0]
    slot_count = sep_couple.shape[0]
    my_height = jnp.int32(depth_count + 1)
    for height in range(depth_count, 0, -1):
        owns_here = (device + 1) % (1 << height) == 1 << height - 1
        my_height = jnp.where(owns_here, jnp.int32(height), my_height)
    panel_zero = jnp.zeros((panel_rows, columns), jnp.bfloat16)
    y_leaf = jnp.dot(leaf_inv, rhs_leaf, preferred_element_type=jnp.float32).astype(jnp.bfloat16)
    leaf_terms = jnp.einsum("hue,ec->huc", couple, y_leaf, preferred_element_type=jnp.float32)
    y_mine = panel_zero
    for height in range(1, depth_count + 1):
        slot_pos = jnp.clip(height - 1 - my_height, 0, slot_count - 1)
        own_rows = lax.dynamic_index_in_dim(sep_rows, slot_pos, 0, keepdims=False)
        own_couple = lax.dynamic_index_in_dim(sep_couple, slot_pos, 0, keepdims=False)
        own_term = spread(
            own_rows, jnp.dot(own_couple, y_mine, preferred_element_type=jnp.float32), panel_rows
        )
        partial_value = spread(couple_rows[height - 1], leaf_terms[height - 1], panel_rows)
        partial_value = partial_value + jnp.where(my_height < height, own_term, 0.0)
        summed = group_sum(partial_value, height)
        residual = (rhs_sep.astype(jnp.float32) - summed).astype(jnp.bfloat16)
        y_here = lax.cond(
            my_height == height,
            lambda: jnp.dot(sep_inv, residual, preferred_element_type=jnp.float32).astype(
                jnp.bfloat16
            ),
            lambda: panel_zero,
        )
        y_mine = jnp.where(my_height == height, y_here, y_mine)
    leaf_sub = jnp.zeros((leaf_rows, columns), jnp.float32)
    x_mine = panel_zero
    sub_mine = jnp.zeros((panel_rows, columns), jnp.float32)
    for height in range(depth_count, 0, -1):
        residual = (y_mine.astype(jnp.float32) - sub_mine).astype(jnp.bfloat16)
        x_here = lax.cond(
            my_height == height,
            lambda: lead_dot(sep_inv, residual).astype(jnp.bfloat16),
            lambda: panel_zero,
        )
        x_mine = jnp.where(my_height == height, x_here, x_mine)
        shared = x_here
        for bit_pos in bit_order(height):
            shared = shared + partner(shared, "rows", bit_pos)
        leaf_sub = leaf_sub + lead_dot(couple[height - 1], shared[couple_rows[height - 1]])
        slot_pos = jnp.clip(height - 1 - my_height, 0, slot_count - 1)
        own_rows = lax.dynamic_index_in_dim(sep_rows, slot_pos, 0, keepdims=False)
        own_couple = lax.dynamic_index_in_dim(sep_couple, slot_pos, 0, keepdims=False)
        own_term = lead_dot(own_couple, shared[own_rows])
        sub_mine = sub_mine + jnp.where(my_height < height, own_term, 0.0)
    residual = (y_leaf.astype(jnp.float32) - leaf_sub).astype(jnp.bfloat16)
    x_leaf = lead_dot(leaf_inv, residual).astype(jnp.bfloat16)
    first_row = device * leaf_rows
    local_row = stay_dofs - first_row
    inside = (local_row >= 0) & (local_row < leaf_rows)
    weight = jnp.where(inside, stay_coef, 0.0)
    picked = x_leaf[jnp.clip(local_row, 0, leaf_rows - 1)]
    partial_stretch = jnp.zeros((stay_dofs.shape[1], columns), jnp.float32)
    for component in range(stay_dofs.shape[0]):
        partial_stretch = partial_stretch + weight[component][:, None] * picked[component].astype(
            jnp.float32
        )
    stretch = lax.psum_scatter(partial_stretch, "rows", scatter_dimension=0, tiled=True)
    return (x_leaf, x_mine, stretch)


def solution(mesh):
    return jax.shard_map(
        on_device,
        mesh=mesh,
        in_specs=(
            P("rows", "cols"),
            P("rows", "cols"),
            P("rows", None),
            P("rows", None, None, None),
            P("rows", None, None),
            P("rows", None),
            P("rows", None, None, None),
            P("rows", None, None),
            P(),
            P(),
        ),
        out_specs=(P("rows", "cols"), P("rows", "cols"), P("rows", "cols")),
        check_vma=False,
    )
```

profile of v0, /device:TPU:2, one launch (start us, length us, event | category | flops | bytes accessed | tf_op | source)
XLA Modules:
  0.0 701.5 jit_solution(10895821896643235770)
XLA Ops:
  21.2 10.5 %collective-permute-done = f32[512,256]{1,0:T(8,128)} collective-permute-done((f32[512,256]{1,0:T(8,128)S(1)}, f32[512,256]{1,0:T(8,128)}, u32[]{:S(2)}, u32[]{:S(2)}) %collective-permute-start) | collective-permute-done | bytes 524320 | tf_op jit(solution)/shard_map/ppermute | solution.py:10
  41.3 12.8 %collective-permute-done.1 = f32[512,256]{1,0:T(8,128)S(1)} collective-permute-done((f32[512,256]{1,0:T(8,128)S(1)}, f32[512,256]{1,0:T(8,128)S(1)}, u32[]{:S(2)}, u32[]{:S(2)}) %collective-permute-start.1) | collective-permute-done | bytes 524320 | tf_op jit(solution)/shard_map/ppermute | solution.py:10
  59.8 8.8 %collective-permute-done.2 = f32[512,256]{1,0:T(8,128)} collective-permute-done((f32[512,256]{1,0:T(8,128)}, f32[512,256]{1,0:T(8,128)}, u32[]{:S(2)}, u32[]{:S(2)}) %collective-permute-start.2) | collective-permute-done | bytes 524320 | tf_op jit(solution)/shard_map/ppermute | solution.py:10
  79.8 9.6 %collective-permute-done.3 = f32[512,256]{1,0:T(8,128)S(1)} collective-permute-done((f32[512,256]{1,0:T(8,128)S(1)}, f32[512,256]{1,0:T(8,128)S(1)}, u32[]{:S(2)}, u32[]{:S(2)}) %collective-permute-start.3) | collective-permute-done | bytes 524320 | tf_op jit(solution)/shard_map/ppermute | solution.py:10
  92.3 9.3 %collective-permute-done.4 = f32[512,256]{1,0:T(8,128)S(1)} collective-permute-done((f32[512,256]{1,0:T(8,128)S(1)}, f32[512,256]{1,0:T(8,128)S(1)}, u32[]{:S(2)}, u32[]{:S(2)}) %collective-permute-start.4) | collective-permute-done | bytes 524320 | tf_op jit(solution)/shard_map/ppermute | solution.py:10
  105.4 6.4 collective-permute-done.5
  122.8 11.4 %collective-permute-done.6 = f32[512,256]{1,0:T(8,128)S(1)} collective-permute-done((f32[512,256]{1,0:T(8,128)S(1)}, f32[512,256]{1,0:T(8,128)S(1)}, u32[]{:S(2)}, u32[]{:S(2)}) %collective-permute-start.6) | collective-permute-done | bytes 524320 | tf_op jit(solution)/shard_map/ppermute | solution.py:10
  134.7 10.3 %collective-permute-done.7 = f32[512,256]{1,0:T(8,128)S(1)} collective-permute-done((f32[512,256]{1,0:T(8,128)S(1)}, f32[512,256]{1,0:T(8,128)S(1)}, u32[]{:S(2)}, u32[]{:S(2)}) %collective-permute-start.7) | collective-permute-done | bytes 524320 | tf_op jit(solution)/shard_map/ppermute | solution.py:10
  148.0 11.6 %collective-permute-done.8 = f32[512,256]{1,0:T(8,128)S(1)} collective-permute-done((f32[512,256]{1,0:T(8,128)S(1)}, f32[512,256]{1,0:T(8,128)S(1)}, u32[]{:S(2)}, u32[]{:S(2)}) %collective-permute-start.8) | collective-permute-done | bytes 524320 | tf_op jit(solution)/shard_map/ppermute | solution.py:10
  164.4 12.3 %collective-permute-done.9 = f32[512,256]{1,0:T(8,128)} collective-permute-done((f32[512,256]{1,0:T(8,128)}, f32[512,256]{1,0:T(8,128)}, u32[]{:S(2)}, u32[]{:S(2)}) %collective-permute-start.9) | collective-permute-done | bytes 524320 | tf_op jit(solution)/shard_map/ppermute | solution.py:10
  187.1 7.8 %collective-permute-done.10 = f32[512,256]{1,0:T(8,128)S(1)} collective-permute-done((f32[512,256]{1,0:T(8,128)S(1)}, f32[512,256]{1,0:T(8,128)S(1)}, u32[]{:S(2)}, u32[]{:S(2)}) %collective-permute-start.10) | collective-permute-done | bytes 524320 | tf_op jit(solution)/shard_map/ppermute | solution.py:10
  195.4 10.3 %collective-permute-done.11 = f32[512,256]{1,0:T(8,128)S(1)} collective-permute-done((f32[512,256]{1,0:T(8,128)S(1)}, f32[512,256]{1,0:T(8,128)S(1)}, u32[]{:S(2)}, u32[]{:S(2)}) %collective-permute-start.11) | collective-permute-done | bytes 524320 | tf_op jit(solution)/shard_map/ppermute | solution.py:10
  206.9 12.3 %collective-permute-done.12 = f32[512,256]{1,0:T(8,128)S(1)} collective-permute-done((f32[512,256]{1,0:T(8,128)S(1)}, f32[512,256]{1,0:T(8,128)S(1)}, u32[]{:S(2)}, u32[]{:S(2)}) %collective-permute-start.12) | collective-permute-done | bytes 524320 | tf_op jit(solution)/shard_map/ppermute | solution.py:10
  220.6 23.5 %collective-permute-done.13 = f32[512,256]{1,0:T(8,128)S(1)} collective-permute-done((f32[512,256]{1,0:T(8,128)S(1)}, f32[512,256]{1,0:T(8,128)S(1)}, u32[]{:S(2)}, u32[]{:S(2)}) %collective-permute-start.13) | collective-permute-done | bytes 524320 | tf_op jit(solution)/shard_map/ppermute | solution.py:10
  248.5 18.4 %collective-permute-done.14 = f32[512,256]{1,0:T(8,128)} collective-permute-done((f32[512,256]{1,0:T(8,128)}, f32[512,256]{1,0:T(8,128)}, u32[]{:S(2)}, u32[]{:S(2)}) %collective-permute-start.14) | collective-permute-done | bytes 524320 | tf_op jit(solution)/shard_map/ppermute | solution.py:10
  269.2 5.6 collective-permute-done.15
  275.5 7.3 %collective-permute-done.16 = bf16[512,256]{1,0:T(8,128)(2,1)S(1)} collective-permute-done((bf16[512,256]{1,0:T(8,128)(2,1)S(1)}, bf16[512,256]{1,0:T(8,128)(2,1)S(1)}, u32[]{:S(2)}, u32[]{:S(2)}) %collective-permute-start.16) | collective-permute-done | bytes 262176 | tf_op jit(solution)/shard_map/ppermute | solution.py:10
  283.0 6.4 collective-permute-done.17
  289.5 9.5 %collective-permute-done.18 = bf16[512,256]{1,0:T(8,128)(2,1)S(1)} collective-permute-done((bf16[512,256]{1,0:T(8,128)(2,1)S(1)}, bf16[512,256]{1,0:T(8,128)(2,1)S(1)}, u32[]{:S(2)}, u32[]{:S(2)}) %collective-permute-start.18) | collective-permute-done | bytes 262176 | tf_op jit(solution)/shard_map/ppermute | solution.py:10
  299.1 5.5 collective-permute-start.19
  304.6 7.4 %collective-permute-done.19 = bf16[512,256]{1,0:T(8,128)(2,1)S(1)} collective-permute-done((bf16[512,256]{1,0:T(8,128)(2,1)S(1)}, bf16[512,256]{1,0:T(8,128)(2,1)S(1)}, u32[]{:S(2)}, u32[]{:S(2)}) %collective-permute-start.19) | collective-permute-done | bytes 262176 | tf_op jit(solution)/shard_map/ppermute | solution.py:10
  316.0 5.6 collective-permute-done.20
  322.6 9.2 %collective-permute-done.21 = bf16[512,256]{1,0:T(8,128)(2,1)} collective-permute-done((bf16[512,256]{1,0:T(8,128)(2,1)}, bf16[512,256]{1,0:T(8,128)(2,1)}, u32[]{:S(2)}, u32[]{:S(2)}) %collective-permute-start.21) | collective-permute-done | bytes 262176 | tf_op jit(solution)/shard_map/ppermute | solution.py:10
  333.7 5.6 collective-permute-done.22
  340.1 4.2 collective-permute-start.23
  345.0 5.8 collective-permute-done.23
  357.6 6.5 collective-permute-done.24
  368.3 5.1 collective-permute-done.25
  373.7 6.3 collective-permute-done.26
  427.3 49.2 %gather_fusion.9 = bf16[12288,256]{1,0:T(8,128)(2,1)} fusion(bf16[1024,256]{1,0:T(8,128)(2,1)S(1)} %copy.23, s32[12288]{0:T(1024)S(1)} %broadcast_clamp_fusion), kind=kCustom, calls=%fused_computation.9 | custom fusion | bytes 12632064 | tf_op jit(solution)/shard_map/gather | solution.py:100
  476.5 5.6 fusion
  482.1 212.2 %reduce-scatter.2.cloned.1.call-done = f32[64,256]{1,0:T(8,128)} async-done(((f32[2048,256]{1,0:T(8,128)}), f32[64,256]{1,0:T(8,128)}) %reduce-scatter.2.cloned.1.call-update) | async-done | bytes 65552 | tf_op jit(solution)/shard_map/reduce_scatter | solution.py:106
  (229 shorter events, 157.0 us)
Async XLA Ops:
  7.2 687.1 %reduce-scatter.2.cloned.1.call-start = ((), (), s32[]{:S(2)}) async-start(), calls=%async_computation.1 | async-start | bytes 2162688 | tf_op jit(solution)/shard_map/reduce_scatter | solution.py:106
  14.5 105.0 %copy-start.28 = (s32[128]{0:T(128)}, s32[128]{0:T(128)S(1)}, u32[]{:S(2)}) copy-start(s32[128]{0:T(128)S(1)} %get-tuple-element.116) | copy-start | bytes 1540
  17.9 13.9 %collective-permute-start = (f32[512,256]{1,0:T(8,128)S(1)}, f32[512,256]{1,0:T(8,128)}, u32[]{:S(2)}, u32[]{:S(2)}) collective-permute-start(f32[512,256]{1,0:T(8,128)S(1)} %scatter_fusion), channel_id=1, source_target_pairs={{0,1},{1,0},{2,3},{3,2},{4,5},{5,4},{6,7},{7,6},{8,9},{9,8},{10,11... | collective-permute-start | bytes 1572872 | tf_op jit(solution)/shard_map/ppermute | solution.py:10
  41.2 12.9 %collective-permute-start.1 = (f32[512,256]{1,0:T(8,128)S(1)}, f32[512,256]{1,0:T(8,128)S(1)}, u32[]{:S(2)}, u32[]{:S(2)}) collective-permute-start(f32[512,256]{1,0:T(8,128)S(1)} %scatter_fusion.1), channel_id=1, source_target_pairs={{0,1},{1,0},{2,3},{3,2},{4,5},{5,4},{6,7},{7,6},{8,9},{9,8},{10,11... | collective-permute-start | bytes 1572872 | tf_op jit(solution)/shard_map/ppermute | solution.py:10
  55.0 13.7 %collective-permute-start.2 = (f32[512,256]{1,0:T(8,128)}, f32[512,256]{1,0:T(8,128)}, u32[]{:S(2)}, u32[]{:S(2)}) collective-permute-start(f32[512,256]{1,0:T(8,128)} %add.333), channel_id=1, source_target_pairs={{0,2},{1,3},{2,0},{3,1},{4,6},{5,7},{6,4},{7,5},{8,10},{9,11},{10,... | collective-permute-start | bytes 1572872 | tf_op jit(solution)/shard_map/ppermute | solution.py:10
  77.9 11.5 %collective-permute-start.3 = (f32[512,256]{1,0:T(8,128)S(1)}, f32[512,256]{1,0:T(8,128)S(1)}, u32[]{:S(2)}, u32[]{:S(2)}) collective-permute-start(f32[512,256]{1,0:T(8,128)S(1)} %scatter_fusion.2), channel_id=1, source_target_pairs={{0,1},{1,0},{2,3},{3,2},{4,5},{5,4},{6,7},{7,6},{8,9},{9,8},{10,11... | collective-permute-start | bytes 1572872 | tf_op jit(solution)/shard_map/ppermute | solution.py:10
  89.5 12.2 %collective-permute-start.4 = (f32[512,256]{1,0:T(8,128)S(1)}, f32[512,256]{1,0:T(8,128)S(1)}, u32[]{:S(2)}, u32[]{:S(2)}) collective-permute-start(f32[512,256]{1,0:T(8,128)S(1)} %add.336), channel_id=1, source_target_pairs={{0,2},{1,3},{2,0},{3,1},{4,6},{5,7},{6,4},{7,5},{8,10},{9,11},{10,... | collective-permute-start | bytes 1572872 | tf_op jit(solution)/shard_map/ppermute | solution.py:10
  101.7 10.0 %collective-permute-start.5 = (f32[512,256]{1,0:T(8,128)S(1)}, f32[512,256]{1,0:T(8,128)}, u32[]{:S(2)}, u32[]{:S(2)}) collective-permute-start(f32[512,256]{1,0:T(8,128)S(1)} %add.337), channel_id=1, source_target_pairs={{0,4},{1,5},{2,6},{3,7},{4,0},{5,1},{6,2},{7,3},{8,12},{9,13},{10,... | collective-permute-start | bytes 1572872 | tf_op jit(solution)/shard_map/ppermute | solution.py:10
  121.6 12.6 %collective-permute-start.6 = (f32[512,256]{1,0:T(8,128)S(1)}, f32[512,256]{1,0:T(8,128)S(1)}, u32[]{:S(2)}, u32[]{:S(2)}) collective-permute-start(f32[512,256]{1,0:T(8,128)S(1)} %scatter_fusion.3), channel_id=1, source_target_pairs={{0,1},{1,0},{2,3},{3,2},{4,5},{5,4},{6,7},{7,6},{8,9},{9,8},{10,11... | collective-permute-start | bytes 1572872 | tf_op jit(solution)/shard_map/ppermute | solution.py:10
  134.3 10.8 %collective-permute-start.7 = (f32[512,256]{1,0:T(8,128)S(1)}, f32[512,256]{1,0:T(8,128)S(1)}, u32[]{:S(2)}, u32[]{:S(2)}) collective-permute-start(f32[512,256]{1,0:T(8,128)S(1)} %add.340), channel_id=1, source_target_pairs={{0,2},{1,3},{2,0},{3,1},{4,6},{5,7},{6,4},{7,5},{8,10},{9,11},{10,... | collective-permute-start | bytes 1572872 | tf_op jit(solution)/shard_map/ppermute | solution.py:10
  145.1 14.5 %collective-permute-start.8 = (f32[512,256]{1,0:T(8,128)S(1)}, f32[512,256]{1,0:T(8,128)S(1)}, u32[]{:S(2)}, u32[]{:S(2)}) collective-permute-start(f32[512,256]{1,0:T(8,128)S(1)} %add.341), channel_id=1, source_target_pairs={{0,4},{1,5},{2,6},{3,7},{4,0},{5,1},{6,2},{7,3},{8,12},{9,13},{10,... | collective-permute-start | bytes 1572872 | tf_op jit(solution)/shard_map/ppermute | solution.py:10
  160.5 16.2 %collective-permute-start.9 = (f32[512,256]{1,0:T(8,128)}, f32[512,256]{1,0:T(8,128)}, u32[]{:S(2)}, u32[]{:S(2)}) collective-permute-start(f32[512,256]{1,0:T(8,128)} %add.342), channel_id=1, source_target_pairs={{0,8},{1,9},{2,10},{3,11},{4,12},{5,13},{6,14},{7,15},{8,0},{9,1},... | collective-permute-start | bytes 1572872 | tf_op jit(solution)/shard_map/ppermute | solution.py:10
  185.6 9.3 %collective-permute-start.10 = (f32[512,256]{1,0:T(8,128)S(1)}, f32[512,256]{1,0:T(8,128)S(1)}, u32[]{:S(2)}, u32[]{:S(2)}) collective-permute-start(f32[512,256]{1,0:T(8,128)S(1)} %scatter_fusion.4), channel_id=1, source_target_pairs={{0,1},{1,0},{2,3},{3,2},{4,5},{5,4},{6,7},{7,6},{8,9},{9,8},{10,11... | collective-permute-start | bytes 1572872 | tf_op jit(solution)/shard_map/ppermute | solution.py:10
  194.9 10.8 %collective-permute-start.11 = (f32[512,256]{1,0:T(8,128)S(1)}, f32[512,256]{1,0:T(8,128)S(1)}, u32[]{:S(2)}, u32[]{:S(2)}) collective-permute-start(f32[512,256]{1,0:T(8,128)S(1)} %add.345), channel_id=1, source_target_pairs={{0,2},{1,3},{2,0},{3,1},{4,6},{5,7},{6,4},{7,5},{8,10},{9,11},{10,... | collective-permute-start | bytes 1572872 | tf_op jit(solution)/shard_map/ppermute | solution.py:10
  205.8 13.4 %collective-permute-start.12 = (f32[512,256]{1,0:T(8,128)S(1)}, f32[512,256]{1,0:T(8,128)S(1)}, u32[]{:S(2)}, u32[]{:S(2)}) collective-permute-start(f32[512,256]{1,0:T(8,128)S(1)} %add.346), channel_id=1, source_target_pairs={{0,4},{1,5},{2,6},{3,7},{4,0},{5,1},{6,2},{7,3},{8,12},{9,13},{10,... | collective-permute-start | bytes 1572872 | tf_op jit(solution)/shard_map/ppermute | solution.py:10
  219.3 24.8 %collective-permute-start.13 = (f32[512,256]{1,0:T(8,128)S(1)}, f32[512,256]{1,0:T(8,128)S(1)}, u32[]{:S(2)}, u32[]{:S(2)}) collective-permute-start(f32[512,256]{1,0:T(8,128)S(1)} %add.347), channel_id=1, source_target_pairs={{0,8},{1,9},{2,10},{3,11},{4,12},{5,13},{6,14},{7,15},{8,0},{9,1},... | collective-permute-start | bytes 1572872 | tf_op jit(solution)/shard_map/ppermute | solution.py:10
  244.9 21.9 %collective-permute-start.14 = (f32[512,256]{1,0:T(8,128)}, f32[512,256]{1,0:T(8,128)}, u32[]{:S(2)}, u32[]{:S(2)}) collective-permute-start(f32[512,256]{1,0:T(8,128)} %add.348), channel_id=1, source_target_pairs={{0,16},{1,17},{2,18},{3,19},{4,20},{5,21},{6,22},{7,23},{8,24},{9,... | collective-permute-start | bytes 1572872 | tf_op jit(solution)/shard_map/ppermute | solution.py:10
  268.3 6.5 collective-permute-start.15
  274.9 8.0 %collective-permute-start.16 = (bf16[512,256]{1,0:T(8,128)(2,1)S(1)}, bf16[512,256]{1,0:T(8,128)(2,1)S(1)}, u32[]{:S(2)}, u32[]{:S(2)}) collective-permute-start(bf16[512,256]{1,0:T(8,128)(2,1)S(1)} %add.350), channel_id=1, source_target_pairs={{0,2},{1,3},{2,0},{3,1},{4,6},{5,7},{6,4},{7,5},{8,10},{9,11},{10,... | collective-permute-start | bytes 786440 | tf_op jit(solution)/shard_map/ppermute | solution.py:10
  282.9 6.5 collective-permute-start.17
  289.4 9.6 %collective-permute-start.18 = (bf16[512,256]{1,0:T(8,128)(2,1)S(1)}, bf16[512,256]{1,0:T(8,128)(2,1)S(1)}, u32[]{:S(2)}, u32[]{:S(2)}) collective-permute-start(bf16[512,256]{1,0:T(8,128)(2,1)S(1)} %add.352), channel_id=1, source_target_pairs={{0,8},{1,9},{2,10},{3,11},{4,12},{5,13},{6,14},{7,15},{8,0},{9,1},... | collective-permute-start | bytes 786440 | tf_op jit(solution)/shard_map/ppermute | solution.py:10
  299.1 12.9 %collective-permute-start.19 = (bf16[512,256]{1,0:T(8,128)(2,1)S(1)}, bf16[512,256]{1,0:T(8,128)(2,1)S(1)}, u32[]{:S(2)}, u32[]{:S(2)}) collective-permute-start(bf16[512,256]{1,0:T(8,128)(2,1)S(1)} %add.353), channel_id=1, source_target_pairs={{0,16},{1,17},{2,18},{3,19},{4,20},{5,21},{6,22},{7,23},{8,24},{9,... | collective-permute-start | bytes 786440 | tf_op jit(solution)/shard_map/ppermute | solution.py:10
  315.1 6.5 collective-permute-start.20
  322.3 9.4 %collective-permute-start.21 = (bf16[512,256]{1,0:T(8,128)(2,1)}, bf16[512,256]{1,0:T(8,128)(2,1)}, u32[]{:S(2)}, u32[]{:S(2)}) collective-permute-start(bf16[512,256]{1,0:T(8,128)(2,1)} %add.355), channel_id=1, source_target_pairs={{0,2},{1,3},{2,0},{3,1},{4,6},{5,7},{6,4},{7,5},{8,10},{9,11},{10,... | collective-permute-start | bytes 786440 | tf_op jit(solution)/shard_map/ppermute | solution.py:10
  332.9 6.5 collective-permute-start.22
  340.1 10.7 %collective-permute-start.23 = (bf16[512,256]{1,0:T(8,128)(2,1)}, bf16[512,256]{1,0:T(8,128)(2,1)}, u32[]{:S(2)}, u32[]{:S(2)}) collective-permute-start(bf16[512,256]{1,0:T(8,128)(2,1)} %add.357), channel_id=1, source_target_pairs={{0,8},{1,9},{2,10},{3,11},{4,12},{5,13},{6,14},{7,15},{8,0},{9,1},... | collective-permute-start | bytes 786440 | tf_op jit(solution)/shard_map/ppermute | solution.py:10
  355.1 9.0 %collective-permute-start.24 = (bf16[512,256]{1,0:T(8,128)(2,1)S(1)}, bf16[512,256]{1,0:T(8,128)(2,1)S(1)}, u32[]{:S(2)}, u32[]{:S(2)}) collective-permute-start(bf16[512,256]{1,0:T(8,128)(2,1)S(1)} %get-tuple-element.140), channel_id=1, source_target_pairs={{0,1},{1,0},{2,3},{3,2},{4,5},{5,4},{6,7},{7,6},{8,9},{9,8},{10,11... | collective-permute-start | bytes 786440 | tf_op jit(solution)/shard_map/ppermute | solution.py:10
  364.2 9.3 %collective-permute-start.25 = (bf16[512,256]{1,0:T(8,128)(2,1)S(1)}, bf16[512,256]{1,0:T(8,128)(2,1)S(1)}, u32[]{:S(2)}, u32[]{:S(2)}) collective-permute-start(bf16[512,256]{1,0:T(8,128)(2,1)S(1)} %add.361), channel_id=1, source_target_pairs={{0,2},{1,3},{2,0},{3,1},{4,6},{5,7},{6,4},{7,5},{8,10},{9,11},{10,... | collective-permute-start | bytes 786440 | tf_op jit(solution)/shard_map/ppermute | solution.py:10
  373.5 6.5 collective-permute-start.26
  384.0 7.9 %collective-permute-start.27 = (bf16[512,256]{1,0:T(8,128)(2,1)}, bf16[512,256]{1,0:T(8,128)(2,1)S(1)}, u32[]{:S(2)}, u32[]{:S(2)}) collective-permute-start(bf16[512,256]{1,0:T(8,128)(2,1)} %get-tuple-element.141), channel_id=1, source_target_pairs={{0,1},{1,0},{2,3},{3,2},{4,5},{5,4},{6,7},{7,6},{8,9},{9,8},{10,11... | collective-permute-start | bytes 786440 | tf_op jit(solution)/shard_map/ppermute | solution.py:10
  393.6 10.2 %collective-permute-start.28 = (bf16[512,256]{1,0:T(8,128)(2,1)}, bf16[512,256]{1,0:T(8,128)(2,1)}, u32[]{:S(2)}, u32[]{:S(2)}) collective-permute-start(bf16[512,256]{1,0:T(8,128)(2,1)} %add.366), channel_id=1, source_target_pairs={{0,2},{1,3},{2,0},{3,1},{4,6},{5,7},{6,4},{7,5},{8,10},{9,11},{10,... | collective-permute-start | bytes 786440 | tf_op jit(solution)/shard_map/ppermute | solution.py:10
  409.0 6.9 collective-permute-start.29
  (40 other events, 851.7 us)
Sparse Core Ops, SparseCore 0:
  482.2 212.0 reduce-scatter.1
where the time goes:
time: 711 us; the launch traced here: 702 us
  waiting for transfers between devices  471 us (66%)
  local copies, waits for them, and re-layouts  72.2 us (10%)
  other arithmetic  56.8 us (8%)
  starting transfers between devices  53.1 us (7%)
  matrix products  33.2 us (5%)
  between operations  15.3 us (2%)
    ppermute x30, waiting for transfers between devices, partner(): return lax.ppermute(value, axis, pairs)  259 us
    reduce_scatter x1, waiting for transfers between devices, on_device(): lax.psum_scatter(partial_stretch, 'rows', scatter_dimension=0, tiled=True)  212 us
    ppermute x30, starting transfers between devices, partner(): return lax.ppermute(value, axis, pairs)  53.1 us
    gather x1, local copies, waits for them, and re-layouts, on_device(): picked = x_leaf[jnp.clip(local_row, 0, leaf_rows - 1)]  49.2 us
    dot_general x10, matrix products, lead_dot(): lax.dot_general(left, right, (((0,), (0,)), ((), ())), preferred_element_...  22.5 us
    scatter-add x10, other arithmetic, spread(): jnp.zeros((row_count, values.shape[1]), jnp.float32).at[row_index]  19.6 us
  transfers between devices with their start and end apart: 31, of which 30 were waited for; matrix products, arithmetic and copies ran while one was open for 3% of the time, Pallas kernels for 0%

commit v1 on v0

v1 whole, which is shorter than its diff:
```python
import functools

import jax
import jax.numpy as jnp
from jax import lax
from jax.experimental import pallas as pl
from jax.experimental.pallas import tpu as pltpu
from jax.sharding import PartitionSpec as P

BF = jnp.bfloat16
F32 = jnp.float32
LEAF, PANEL, U, NC, LEVELS = 1024, 512, 128, 256, 5
RING = 4
CW = NC // RING
TERM = LEVELS * U
PACK = (TERM + PANEL) // 2
HALF = PANEL // 2
IDX0 = HALF
CPL0 = HALF + 16
WROWS = CPL0 + 4 * (U // 2)
SLOTS = 16
VMEM_LIMIT = 48 * 1024 * 1024


def dot(left, right):
    return jnp.dot(left, right, preferred_element_type=F32)


def lead_dot(left, right):
    return lax.dot_general(left, right, (((0,), (0,)), ((), ())), preferred_element_type=F32)


def call(body, outs, args, scratch=(), specs=None, flops=10**8):
    vmem = pl.BlockSpec(memory_space=pltpu.VMEM)
    return pl.pallas_call(
        body,
        out_shape=outs,
        in_specs=specs or [vmem] * len(args),
        out_specs=[vmem] * len(outs),
        scratch_shapes=list(scratch),
        compiler_params=pltpu.CompilerParams(vmem_limit_bytes=VMEM_LIMIT),
        cost_estimate=pl.CostEstimate(flops=flops, bytes_accessed=4 * 10**6, transcendentals=0),
    )(*args)


def shape(*dims, dtype=BF):
    return jax.ShapeDtypeStruct(dims, dtype)


def hot(row):
    place = lax.broadcasted_iota(jnp.int32, (PANEL, U), 0).astype(F32)
    return jnp.where(place == row, 1.0, 0.0).astype(BF)


def index_rows(block):
    block = block.astype(F32)
    leaf = [block[l : l + 1, 0:U] * 16.0 + block[l : l + 1, U : 2 * U] for l in range(LEVELS)]
    sep = [
        block[s : s + 1, 2 * U : 3 * U] * 16.0 + block[s : s + 1, 3 * U : 4 * U]
        for s in range(LEVELS - 1)
    ]
    return leaf, sep


class Factor:
    def __init__(self, mine, other, first, slots):
        self.mine, self.other, self.first = mine, other, first
        self.rows = index_rows(mine[IDX0 : IDX0 + 16])[1] if slots else []
        self.slots = slots

    def order(self, a, b):
        return jnp.where(self.first, a, b), jnp.where(self.first, b, a)

    def forward(self, resid):
        low, high = self.order(dot(self.mine[0:HALF], resid), dot(self.other[0:HALF], resid))
        return jnp.concatenate([low, high], axis=0).astype(BF)

    def backward(self, back):
        a, b = self.order(back[0:HALF], back[HALF:PANEL])
        return (lead_dot(self.mine[0:HALF], a) + lead_dot(self.other[0:HALF], b)).astype(BF)

    def couple(self, slot):
        start = CPL0 + slot * (U // 2)
        return self.mine[start : start + U // 2], self.other[start : start + U // 2]

    def push(self, slot, y):
        a, b = self.couple(slot)
        low, high = self.order(dot(a, y), dot(b, y))
        value = jnp.concatenate([low, high], axis=0).astype(BF)
        return dot(hot(self.rows[slot]), value)

    def pull(self, slot, x):
        rows = lead_dot(hot(self.rows[slot]), x).astype(BF)
        a, b = self.couple(slot)
        low, high = self.order(rows[0 : U // 2], rows[U // 2 : U])
        return lead_dot(a, low) + lead_dot(b, high)


def pack_rows(ref, start, value):
    ref[start : start + HALF, 0:CW] = value[0:HALF]
    ref[start : start + HALF, CW : 2 * CW] = value[HALF:PANEL]


def unpack_rows(value):
    return jnp.concatenate([value[:, 0:CW], value[:, CW : 2 * CW]], axis=0)


def leaf_forward(inv, rhs, cpl, rsep, y_out, send, stack):
    for i in range(4):
        span = (i + 1) * 256
        y_out[i * 256 : span] = dot(inv[i * 256 : span, 0:span], rhs[0:span]).astype(BF)
    stack[0:TERM] = dot(cpl[...], y_out[...]).astype(BF)
    stack[TERM:] = rsep[...]
    for d in range(RING):
        cols = slice(d * CW, (d + 1) * CW)
        send[d, :, 0:CW] = stack[0:PACK, cols]
        send[d, :, CW : 2 * CW] = stack[PACK : 2 * PACK, cols]


def low_forward(place, recv, gmine, gother, y_out, panels):
    first = place[0] == 0
    z = place[1]
    hold_level = place[2]
    del z
    terms, rhs, rows = [], [], []
    for j in range(RING):
        left, right = recv[j, :, 0:CW], recv[j, :, CW : 2 * CW]
        terms.append(
            [left[l * U : (l + 1) * U] for l in range(4)]
            + [jnp.concatenate([left[4 * U : PACK], right[0 : TERM - PACK]], axis=0)]
        )
        rhs.append(right[TERM - PACK :])
        rows.append(index_rows(gmine[j, IDX0 : IDX0 + 16])[0])

    def gathered(level, leaves):
        total = dot(hot(rows[leaves[0]][level - 1]), terms[leaves[0]][level - 1])
        for j in leaves[1:]:
            total = total + dot(hot(rows[j][level - 1]), terms[j][level - 1])
        return total

    factors = [Factor(gmine.at[j], gother.at[j], first, 4) for j in range(3)]
    ys = {}
    for j, leaves in ((0, (0, 1)), (2, (2, 3))):
        resid = (rhs[j].astype(F32) - gathered(1, leaves)).astype(BF)
        ys[j] = factors[j].forward(resid)
    total = {l: gathered(l, (0, 1, 2, 3)) for l in range(2, LEVELS + 1)}
    for l in range(2, LEVELS + 1):
        total[l] = total[l] + factors[0].push(l - 2, ys[0]) + factors[2].push(l - 2, ys[2])
    ys[1] = factors[1].forward((rhs[1].astype(F32) - total[2]).astype(BF))
    for l in range(3, LEVELS + 1):
        held = jnp.where(hold_level == l, rhs[3].astype(F32), 0.0)
        value = total[l] + factors[1].push(l - 3, ys[1]) - held
        pack_rows(panels, (l - 3) * HALF, value.astype(BF))
    for j in range(3):
        y_out[j] = ys[j]


def top_forward(level, place, mine, recv, wa, wb, wa_other, wb_other, y_out, panels, w, w_other):
    first = place[0] == 0
    pick = place[3 + level - 3] == 1
    count = LEVELS - level
    rows = CPL0 + count * (U // 2)
    w[0:rows] = jnp.where(pick, wa[0:rows], wb[0:rows])
    w_other[0:rows] = jnp.where(pick, wa_other[0:rows], wb_other[0:rows])
    factor = Factor(w, w_other, first, count)
    value = mine[...].astype(F32) + recv[...].astype(F32)
    y = factor.forward((-unpack_rows(value[0:HALF])).astype(BF))
    y_out[...] = y
    for k in range(count):
        total = unpack_rows(value[(k + 1) * HALF : (k + 2) * HALF]) + factor.push(k, y)
        pack_rows(panels, k * HALF, total.astype(BF))


def backward(
    place, mine, recv, y_low, y3_ref, y4_ref, gmine, gother, w3, w3o, w4, w4o, w5a, w5b, w5ao, w5bo,
    send, stack, w5, w5o,
):
    first = place[0] == 0
    hold_level = place[2]
    pick = place[5] == 1
    w5[...] = jnp.where(pick, w5a[0:HALF], w5b[0:HALF])
    w5o[...] = jnp.where(pick, w5ao[0:HALF], w5bo[0:HALF])
    top = Factor(w5, w5o, first, 0)
    total = mine[...].astype(F32) + recv[...].astype(F32)
    x5 = top.backward(top.forward((-unpack_rows(total)).astype(BF)))

    def solve(factor, y, above):
        sub = factor.pull(0, above[0])
        for k in range(1, len(above)):
            sub = sub + factor.pull(k, above[k])
        return factor.backward((y.astype(F32) - sub).astype(BF))

    x4 = solve(Factor(w4, w4o, first, 1), y4_ref[...], [x5])
    x3 = solve(Factor(w3, w3o, first, 2), y3_ref[...], [x4, x5])
    low = [Factor(gmine.at[j], gother.at[j], first, 4) for j in range(3)]
    x2 = solve(low[1], y_low[1], [x3, x4, x5])
    x1 = {j: solve(low[j], y_low[j], [x2, x3, x4, x5]) for j in (0, 2)}
    held = jnp.where(hold_level == 3, x3, jnp.where(hold_level == 4, x4, x5))
    held = jnp.where(hold_level == 0, jnp.zeros_like(held), held)
    own = [x1[0], x2, x1[2], held]
    for j in range(RING):
        rows = index_rows(gmine[j, IDX0 : IDX0 + 16])[0]
        above = [x1[0] if j < 2 else x1[2], x2, x3, x4, x5]
        for l in range(LEVELS):
            stack[l * U : (l + 1) * U] = lead_dot(hot(rows[l]), above[l]).astype(BF)
        stack[TERM:] = own[j]
        send[j, :, 0:CW] = stack[0:PACK]
        send[j, :, CW : 2 * CW] = stack[PACK : 2 * PACK]


def leaf_backward(recv, inv, cpl, y, sel, x_leaf, x_sep, picks, rows, sub):
    for d in range(RING):
        cols = slice(d * CW, (d + 1) * CW)
        rows[0:PACK, cols] = recv[d, :, 0:CW]
        rows[PACK:TERM, cols] = recv[d, 0 : TERM - PACK, CW : 2 * CW]
        x_sep[:, cols] = recv[d, TERM - PACK :, CW : 2 * CW]
    sub[...] = (y[...].astype(F32) - lead_dot(cpl[...], rows[...])).astype(BF)
    for i in range(4):
        start = i * 256
        x_leaf[start : start + 256] = lead_dot(inv[start:, start : start + 256], sub[start:]).astype(BF)
    place = lax.broadcasted_iota(jnp.int32, (32 * SLOTS, LEAF), 1)
    chosen = jnp.where(place == sel[...] - 1, 1.0, 0.0).astype(BF)
    picks[...] = dot(chosen, x_leaf[...]).astype(BF)


def stretch_sum(weight, recv, out):
    value = weight[...]
    high = value.astype(BF)
    low = (value - high.astype(F32)).astype(BF)
    out[...] = dot(high, recv[...]) + dot(low, recv[...])


def stay_plan(me, stay_dofs, stay_coef):
    k, stays = stay_dofs.shape
    per = stays // 32
    pairs = k * per
    dofs = stay_dofs.reshape(k, 32, per).transpose(1, 0, 2).reshape(32, pairs)
    before = jnp.arange(pairs)[:, None] < jnp.arange(pairs)[None, :]
    match = (dofs // LEAF) == me
    rank = dot(match.astype(BF), before.astype(BF))
    at = match[:, None, :] & (rank[:, None, :] == jnp.arange(SLOTS, dtype=F32)[None, :, None])
    sel = jnp.sum(jnp.where(at, (dofs % LEAF + 1)[:, None, :], 0), axis=2).reshape(32 * SLOTS, 1)
    mine = lax.dynamic_index_in_dim(dofs, me, 0, keepdims=False) // LEAF
    earlier = jnp.sum(jnp.where(before & (mine[:, None] == mine[None, :]), 1, 0), axis=0)
    slot = (mine * SLOTS + earlier).reshape(k, per)
    coef = lax.dynamic_slice_in_dim(stay_coef, me * per, per, 1)
    hit = slot[:, :, None] == jnp.arange(32 * SLOTS)[None, None, :]
    weight = jnp.sum(jnp.where(hit, coef[:, :, None], 0.0), axis=0)
    return sel.astype(jnp.int32), weight


def on_device(
    rhs_leaf, rhs_sep, leaf_inv, leaf_cpl, leaf_idx, sep_inv, sep_cpl, sep_idx, stay_dofs, stay_coef
):
    rows_axis, cols_axis = "rows", "cols"
    me = lax.axis_index(rows_axis)
    core = lax.axis_index(cols_axis) % 2
    y, z = me % RING, me // RING
    ring = [[zz * RING + yy for yy in range(RING)] for zz in range(8)]

    def swap_core(value):
        return lax.ppermute(value, cols_axis, [(i, i ^ 1) for i in range(lax.axis_size(cols_axis))])

    def swap_z(value, bit):
        return lax.ppermute(value, rows_axis, [(i, i ^ (bit * RING)) for i in range(32)])

    top_level = jnp.where(
        z % 2 == 0, 3, jnp.where(z % 4 == 1, 4, jnp.where(z % 8 == 3, 5, 0))
    )
    place = jnp.stack(
        [
            core,
            z,
            top_level,
            (z % 2 == 0).astype(jnp.int32),
            (z % 4 < 2).astype(jnp.int32),
            (z < 4).astype(jnp.int32),
        ]
    ).astype(jnp.int32)
    vmem = pl.BlockSpec(memory_space=pltpu.VMEM)
    smem = pl.BlockSpec(memory_space=pltpu.SMEM)

    def split(idx):
        return jnp.concatenate([idx // 16, idx % 16], axis=-1).astype(BF)

    codes = jnp.concatenate(
        [
            jnp.pad(split(leaf_idx[0]), ((0, 16 - LEVELS), (0, 0))),
            jnp.pad(split(sep_idx[0]), ((0, 16 - LEVELS + 1), (0, 0))),
        ],
        axis=1,
    )
    half_inv = lax.dynamic_slice_in_dim(sep_inv, core * HALF, HALF, 0)
    half_cpl = lax.dynamic_slice_in_dim(sep_cpl[0], core * (U // 2), U // 2, 1)
    packed = jnp.concatenate([half_inv, codes, half_cpl.reshape(4 * (U // 2), PANEL)], axis=0)
    gmine = lax.all_gather(packed, rows_axis, axis=0, axis_index_groups=ring, tiled=False)

    cpl = leaf_cpl[0].reshape(TERM, LEAF)
    y_leaf, send = call(
        leaf_forward,
        [shape(LEAF, NC), shape(RING, PACK, 2 * CW)],
        [leaf_inv, rhs_leaf, cpl, rhs_sep],
        [pltpu.VMEM((TERM + PANEL, NC), BF)],
    )
    sel, weight = stay_plan(me, stay_dofs, stay_coef)
    send, sel, weight = lax.optimization_barrier((send, sel, weight))
    recv = lax.all_to_all(send, rows_axis, 0, 0, axis_index_groups=ring, tiled=True)

    gother = swap_core(gmine)
    top_mine, top_other = gmine[3], gother[3]
    far_a = swap_z(top_mine[0 : CPL0 + U], 1)
    y_low, panels = call(
        low_forward,
        [shape(3, PANEL, CW), shape(3 * HALF, 2 * CW)],
        [place, recv, gmine, gother],
        specs=[smem, vmem, vmem, vmem],
    )
    far_ao = swap_core(far_a)
    rows_b = CPL0 + U // 2
    next_mine = jnp.where(z % 2 == 1, top_mine[0:rows_b], far_a[0:rows_b])
    far_b = swap_z(next_mine, 2)
    next_other = swap_core(next_mine)
    far_bo = swap_core(far_b)
    last_mine = jnp.where(z % 4 >= 2, next_mine[0:HALF], far_b[0:HALF])
    last_other = swap_core(last_mine)
    far_c = swap_z(last_mine, 4)
    far_co = swap_core(far_c)

    def rise(level, panels, wa, wb, wao, wbo):
        count = LEVELS - level
        rows = CPL0 + count * (U // 2)
        far = swap_z(panels, 1 << (level - 3))
        return call(
            functools.partial(top_forward, level),
            [shape(PANEL, CW), shape(count * HALF, 2 * CW), shape(rows, PANEL), shape(rows, PANEL)],
            [place, panels, far, wa, wb, wao, wbo],
            specs=[smem] + [vmem] * 6,
        )

    y3, panels, w3, w3o = rise(3, panels, top_mine, far_a, top_other, far_ao)
    y4, panels, w4, w4o = rise(4, panels, next_mine, far_b, next_other, far_bo)
    far = swap_z(panels, 4)
    (send,) = call(
        backward,
        [shape(RING, PACK, 2 * CW)],
        [
            place, panels, far, y_low, y3, y4, gmine, gother, w3, w3o, w4, w4o,
            last_mine, far_c, last_other, far_co,
        ],
        [
            pltpu.VMEM((TERM + PANEL, CW), BF),
            pltpu.VMEM((HALF, PANEL), BF),
            pltpu.VMEM((HALF, PANEL), BF),
        ],
        specs=[smem] + [vmem] * 15,
    )
    recv = lax.all_to_all(send, rows_axis, 0, 0, axis_index_groups=ring, tiled=True)
    x_leaf, x_sep, picks = call(
        leaf_backward,
        [shape(LEAF, NC), shape(PANEL, NC), shape(32 * SLOTS, NC)],
        [recv, leaf_inv, cpl, y_leaf, sel],
        [pltpu.VMEM((TERM, NC), BF), pltpu.VMEM((LEAF, NC), BF)],
    )
    got = lax.all_to_all(
        picks.reshape(32, SLOTS, NC), rows_axis, 0, 0, tiled=True
    ).reshape(32 * SLOTS, NC)
    (stretch,) = call(stretch_sum, [shape(64, NC, dtype=F32)], [weight, got])
    return (x_leaf, x_sep, stretch)


def solution(mesh):
    return jax.shard_map(
        on_device,
        mesh=mesh,
        in_specs=(
            P("rows", "cols"),
            P("rows", "cols"),
            P("rows", None),
            P("rows", None, None, None),
            P("rows", None, None),
            P("rows", None),
            P("rows", None, None, None),
            P("rows", None, None),
            P(),
            P(),
        ),
        out_specs=(P("rows", "cols"), P("rows", "cols"), P("rows", "cols")),
        check_vma=False,
    )
```

time: 711 us -> 189 us (0.27); the launches traced: 702 us -> 188 us
  waiting for transfers between devices: 471 us -> 89.9 us
  local copies, waits for them, and re-layouts: 72.2 us -> 13.6 us
  other arithmetic: 56.8 us -> 5.73 us
  matrix products: 33.2 us -> 0.16 us
  starting transfers between devices: 53.1 us -> 23.1 us
  Pallas kernels: 0 us -> 24 us
  blocking collectives: 0 us -> 17.5 us
    ppermute x30 -> x12, waiting for transfers between devices: 259 us -> 43.1 us  [the longest x6 43.1 us: swap_z(): lax.ppermute(value, rows_axis, [(i, i ^ bit * RING) for i in range(32)])]
    reduce_scatter x1 -> x0, waiting for transfers between devices: 212 us -> none  [on_device(): lax.psum_scatter(partial_stretch, 'rows', scatter_dimension=0, tiled=True)]
    gather x10 -> x0, local copies, waits for them, and re-layouts: 59.2 us -> none  [the longest x1 49.2 us: on_device(): picked = x_leaf[jnp.clip(local_row, 0, leaf_rows - 1)]]
    ppermute x30 -> x12, starting transfers between devices: 53.1 us -> 15.3 us  [the longest x6 14.2 us: swap_z(): lax.ppermute(value, rows_axis, [(i, i ^ bit * RING) for i in range(32)])]
    all_gather x0 -> x1, waiting for transfers between devices: none -> 36.6 us  [on_device(): lax.all_gather(packed, rows_axis, axis=0, axis_index_groups=ring, tiled=F...]
    dot_general x18 -> x1, matrix products: 33.2 us -> 0.16 us  [dot(): return jnp.dot(left, right, preferred_element_type=F32)]
    pallas_call x0 -> x7, Pallas kernels: none -> 24 us  [call(): pl.pallas_call(body, out_shape=outs, in_specs=specs or [vmem] * len(args)...]
    scatter-add x10 -> x0, other arithmetic: 19.6 us -> none  [spread(): jnp.zeros((row_count, values.shape[1]), jnp.float32).at[row_index]]
  transfers between devices with their start and end apart: 31 -> 15, of which waited for: 30 -> 8; matrix products, arithmetic and copies ran while one was open for 3% -> 5% of each run, Pallas kernels for 0% -> 6%
where the time goes in v1:
time: 189 us; the launch traced here: 188 us
  waiting for transfers between devices  89.9 us (48%)
  Pallas kernels  24 us (13%)
  starting transfers between devices  23.1 us (12%)
  blocking collectives  17.5 us (9%)
  between operations  14.3 us (8%)
  local copies, waits for them, and re-layouts  13.6 us (7%)
  other arithmetic  5.73 us (3%)
    ppermute x6, waiting for transfers between devices, swap_z(): lax.ppermute(value, rows_axis, [(i, i ^ bit * RING) for i in range(32)])  43.1 us
    all_gather x1, waiting for transfers between devices, on_device(): lax.all_gather(packed, rows_axis, axis=0, axis_index_groups=ring, tiled=F...  36.6 us
    pallas_call x7, Pallas kernels, call(): pl.pallas_call(body, out_shape=outs, in_specs=specs or [vmem] * len(args)...  24 us
    all_to_all x1, blocking collectives, on_device(): lax.all_to_all(picks.reshape(32, SLOTS, NC), rows_axis, 0, 0, tiled=True)  17.5 us
    ppermute x6, starting transfers between devices, swap_z(): lax.ppermute(value, rows_axis, [(i, i ^ bit * RING) for i in range(32)])  14.2 us
    all_to_all x2, waiting for transfers between devices, on_device(): lax.all_to_all(send, rows_axis, 0, 0, axis_index_groups=ring, tiled=True)  10.1 us
    all_to_all x2, starting transfers between devices, on_device(): lax.all_to_all(send, rows_axis, 0, 0, axis_index_groups=ring, tiled=True)  7.77 us
    unnamed x28, local copies, waits for them, and re-layouts  7.4 us
  transfers between devices with their start and end apart: 15, of which 8 were waited for; matrix products, arithmetic and copies ran while one was open for 5% of the time, Pallas kernels for 6%

profile of v1, /device:TPU:2, one launch (start us, length us, event | category | flops | bytes accessed | tf_op | source)
XLA Modules:
  0.0 188.3 jit_solution(914333048895446297)
XLA Ops:
  8.7 1.0 constant_dynamic-slice_fusion.1
  9.7 0.8 pad_maximum_fusion
  11.0 36.6 %all-gather.3.cloned.1.call-done = bf16[2112,512]{1,0:T(8,128)(2,1)} async-done(((bf16[528,512]{1,0:T(8,128)(2,1)}), bf16[2112,512]{1,0:T(8,128)(2,1)}) %all-gather.3.cloned.1.call-update) | async-done | bytes 2162704 | tf_op jit(solution)/shard_map/all_gather | solution.py:296
  47.9 1.8 slice_bitcast_fusion.1
  49.7 1.6 collective-permute-start.2
  52.2 1.6 copy-done.2
  53.8 1.3 copy-done.4
  55.1 1.0 copy-done.11
  56.1 1.1 shard_map.121
  58.8 3.0 %collective-permute-done.2.wb = bf16[400,512]{1,0:T(8,128)(2,1)S(1)} collective-permute-done((bf16[400,512]{1,0:T(8,128)(2,1)}, bf16[400,512]{1,0:T(8,128)(2,1)S(1)}, u32[]{:S(2)}, u32[]{:S(2)}) %collective-permute-start.2) | collective-permute-done | bytes 409632 | tf_op jit(solution)/shard_map/ppermute | solution.py:265
  61.9 2.6 %collective-permute-start.5 = (bf16[336,512]{1,0:T(8,128)(2,1)S(1)}, bf16[336,512]{1,0:T(8,128)(2,1)}, u32[]{:S(2)}, u32[]{:S(2)}) collective-permute-start(bf16[336,512]{1,0:T(8,128)(2,1)S(1)} %slice_select_fusion.wa), channel_id=1, source_target_pairs={{0,8},{1,9},{2,10},{3,11},{4,12},{5,13},{6,14},{7,15},{8,0},{9,1},... | collective-permute-start | bytes 1032200 | tf_op jit(solution)/shard_map/ppermute | solution.py:265
  65.3 4.2 %all-to-all-start = ((bf16[4,576,128]{2,1,0:T(8,128)(2,1)}), bf16[4,576,128]{2,1,0:T(8,128)(2,1)}, u32[]{:S(2)}, u32[]{:S(2)}) async-start(bf16[4,576,128]{2,1,0:T(8,128)(2,1)} %copy-done.7), calls=%async_computation | async-start | bytes 1179648 | tf_op jit(solution)/shard_map/all_to_all | solution.py:307
  69.6 10.4 %collective-permute-done.5.wb = bf16[336,512]{1,0:T(8,128)(2,1)} collective-permute-done((bf16[336,512]{1,0:T(8,128)(2,1)S(1)}, bf16[336,512]{1,0:T(8,128)(2,1)}, u32[]{:S(2)}, u32[]{:S(2)}) %collective-permute-start.5) | collective-permute-done | bytes 344096 | tf_op jit(solution)/shard_map/ppermute | solution.py:265
  80.0 1.7 slice_select_fusion.1.w5a
  81.7 5.7 %collective-permute-start.9 = (bf16[256,512]{1,0:T(8,128)(2,1)}, bf16[256,512]{1,0:T(8,128)(2,1)}, u32[]{:S(2)}, u32[]{:S(2)}) collective-permute-start(bf16[256,512]{1,0:T(8,128)(2,1)} %slice_select_fusion.1.w5a), channel_id=1, source_target_pairs={{0,16},{1,17},{2,18},{3,19},{4,20},{5,21},{6,22},{7,23},{8,24},{9,... | collective-permute-start | bytes 786440 | tf_op jit(solution)/shard_map/ppermute | solution.py:265
  88.9 10.9 %collective-permute-done.9.w5b = bf16[256,512]{1,0:T(8,128)(2,1)} collective-permute-done((bf16[256,512]{1,0:T(8,128)(2,1)}, bf16[256,512]{1,0:T(8,128)(2,1)}, u32[]{:S(2)}, u32[]{:S(2)}) %collective-permute-start.9) | collective-permute-done | bytes 262176 | tf_op jit(solution)/shard_map/ppermute | solution.py:265
  100.3 5.5 %shard_map.122 = (bf16[3,512,64]{2,1,0:T(8,128)(2,1)S(1)}, bf16[768,128]{1,0:T(8,128)(2,1)S(1)}) custom-call(s32[6]{0:T(128)S(1)} %stack.39.place, bf16[4,576,128]{2,1,0:T(8,128)(2,1)} %all-to-all-done.recv, bf16[4,528,512]{2,1,0:T(8,128)(2,1)S(1)} %bitcast.74, bf16[4,528,512]{2,1,0:T(8,128)(2,1)} %collective-permute-done.gother), custom_call_target="tpu_custom_call" | custom-call | flops 100000000 | bytes 4000000 | tf_op jit(solution)/shard_map/pallas_call | solution.py:35
  106.1 1.1 slice_bitcast_fusion.wa_other
  107.2 5.7 %collective-permute-done.1.recv = bf16[768,128]{1,0:T(8,128)(2,1)S(1)} collective-permute-done((bf16[768,128]{1,0:T(8,128)(2,1)S(1)}, bf16[768,128]{1,0:T(8,128)(2,1)S(1)}, u32[]{:S(2)}, u32[]{:S(2)}) %collective-permute-start.1) | collective-permute-done | bytes 196640 | tf_op jit(solution)/shard_map/ppermute | solution.py:265
  112.9 1.9 %shard_map.123 = (bf16[512,64]{1,0:T(8,128)(2,1)S(1)}, bf16[512,128]{1,0:T(8,128)(2,1)S(1)}, bf16[400,512]{1,0:T(8,128)(2,1)S(1)}, bf16[400,512]{1,0:T(8,128)(2,1)S(1)}) custom-call(s32[6]{0:T(128)S(1)} %stack.39.place, bf16[768,128]{1,0:T(8,128)(2,1)S(1)} %get-tuple-element.23.mine, bf16[768,128]{1,0:T(8,128)(2,1)S(1)} %collective-permute-done.1.recv, ...), custom_call_target="tpu_custom_call" | custom-call | flops 100000000 | bytes 4000000 | tf_op jit(solution)/shard_map/pallas_call | solution.py:35
  114.9 1.1 collective-permute-start.4
  116.0 7.2 %collective-permute-done.4.recv = bf16[512,128]{1,0:T(8,128)(2,1)S(1)} collective-permute-done((bf16[512,128]{1,0:T(8,128)(2,1)S(1)}, bf16[512,128]{1,0:T(8,128)(2,1)S(1)}, u32[]{:S(2)}, u32[]{:S(2)}) %collective-permute-start.4) | collective-permute-done | bytes 131104 | tf_op jit(solution)/shard_map/ppermute | solution.py:265
  123.2 2.0 %shard_map.124 = (bf16[512,64]{1,0:T(8,128)(2,1)S(1)}, bf16[256,128]{1,0:T(8,128)(2,1)S(1)}, bf16[336,512]{1,0:T(8,128)(2,1)S(1)}, bf16[336,512]{1,0:T(8,128)(2,1)S(1)}) custom-call(s32[6]{0:T(128)S(1)} %stack.39.place, bf16[512,128]{1,0:T(8,128)(2,1)S(1)} %get-tuple-element.24.mine, bf16[512,128]{1,0:T(8,128)(2,1)S(1)} %collective-permute-done.4.recv, ...), custom_call_target="tpu_custom_call" | custom-call | flops 100000000 | bytes 4000000 | tf_op jit(solution)/shard_map/pallas_call | solution.py:35
  125.2 2.8 %collective-permute-start.8 = (bf16[256,128]{1,0:T(8,128)(2,1)S(1)}, bf16[256,128]{1,0:T(8,128)(2,1)S(1)}, u32[]{:S(2)}, u32[]{:S(2)}) collective-permute-start(bf16[256,128]{1,0:T(8,128)(2,1)S(1)} %get-tuple-element.25.mine), channel_id=1, source_target_pairs={{0,16},{1,17},{2,18},{3,19},{4,20},{5,21},{6,22},{7,23},{8,24},{9,... | collective-permute-start | bytes 196616 | tf_op jit(solution)/shard_map/ppermute | solution.py:265
  128.1 5.8 %collective-permute-done.8.recv = bf16[256,128]{1,0:T(8,128)(2,1)S(1)} collective-permute-done((bf16[256,128]{1,0:T(8,128)(2,1)S(1)}, bf16[256,128]{1,0:T(8,128)(2,1)S(1)}, u32[]{:S(2)}, u32[]{:S(2)}) %collective-permute-start.8) | collective-permute-done | bytes 65568 | tf_op jit(solution)/shard_map/ppermute | solution.py:265
  133.9 9.9 %shard_map.125 = bf16[4,576,128]{2,1,0:T(8,128)(2,1)} custom-call(s32[6]{0:T(128)S(1)} %stack.39.place, bf16[256,128]{1,0:T(8,128)(2,1)S(1)} %get-tuple-element.25.mine, bf16[256,128]{1,0:T(8,128)(2,1)S(1)} %collective-permute-done.8.recv, bf16[3,512,64]{2,1,0:T(8,128)(2,1)S(1)} %get-tuple-element.26.y_low, bf16[512,64]{1,0:T(8,128)(2,1)S(1)} %get-tuple-element.27.y3_ref, ...), custom_call_target="tpu_custom_call" | custom-call | flops 100000000 | bytes 4000000 | tf_op jit(solution)/shard_map/pallas_call | solution.py:35
  143.8 3.6 %all-to-all-start.1 = ((bf16[4,576,128]{2,1,0:T(8,128)(2,1)}), bf16[4,576,128]{2,1,0:T(8,128)(2,1)S(1)}, u32[]{:S(2)}, u32[]{:S(2)}) async-start(bf16[4,576,128]{2,1,0:T(8,128)(2,1)} %shard_map.125), calls=%async_computation.1 | async-start | bytes 1179648 | tf_op jit(solution)/shard_map/all_to_all | solution.py:357
  147.6 10.1 %all-to-all-done.1.recv = bf16[4,576,128]{2,1,0:T(8,128)(2,1)S(1)} async-done(((bf16[4,576,128]{2,1,0:T(8,128)(2,1)}), bf16[4,576,128]{2,1,0:T(8,128)(2,1)S(1)}, u32[]{:S(2)}, u32[]{:S(2)}) %all-to-all-start.1) | async-done | bytes 589856 | tf_op jit(solution)/shard_map/all_to_all | solution.py:357
  157.6 1.6 copy-done.3
  159.2 1.0 copy-done.9
  160.3 2.8 %shard_map.126 = (bf16[1024,256]{1,0:T(8,128)(2,1)}, bf16[512,256]{1,0:T(8,128)(2,1)}, bf16[512,256]{1,0:T(8,128)(2,1)S(1)}) custom-call(bf16[4,576,128]{2,1,0:T(8,128)(2,1)S(1)} %all-to-all-done.1.recv, bf16[1024,1024]{1,0:T(8,128)(2,1)S(1)} %copy-done.3, bf16[640,1024]{1,0:T(8,128)(2,1)S(1)} %bitcast.77, bf16[1024,256]{1,0:T(8,128)(2,1)S(1)} %copy-done.9, ...), custom_call_target="tpu_custom_call" | custom-call | flops 100000000 | bytes 4000000 | tf_op jit(solution)/shard_map/pallas_call | solution.py:35
  163.1 17.5 %all_to_all.15 = bf16[32,16,256]{2,1,0:T(8,128)(2,1)S(1)} all-to-all(bf16[32,16,256]{2,1,0:T(8,128)(2,1)S(1)} %bitcast.79), channel_id=1, replica_groups=mesh['cols'=8,'rows'=32] {'rows'}, dimensions={0} | all-to-all | bytes 524288 | tf_op jit(solution)/shard_map/all_to_all | solution.py:364
  (64 shorter events, 8.8 us)
Async XLA Ops:
  7.2 1.5 copy-start
  7.2 40.5 %all-gather.3.cloned.1.call-start = ((), (), s32[]{:S(2)}) async-start(), calls=%async_computation.3 | async-start | bytes 2703360 | tf_op jit(solution)/shard_map/all_gather | solution.py:296
  8.7 2.0 %copy-start.13 = (s32[6,2048]{1,0:T(8,128)S(1)}, s32[6,2048]{1,0:T(8,128)}, u32[]{:S(2)}) copy-start(s32[6,2048]{1,0:T(8,128)} %param.18) | copy-start | bytes 147460
  10.6 41.6 %copy-start.12 = (bf16[512,256]{1,0:T(8,128)(2,1)S(1)}, bf16[512,256]{1,0:T(8,128)(2,1)}, u32[]{:S(2)}) copy-start(bf16[512,256]{1,0:T(8,128)(2,1)} %rsep.1) | copy-start | bytes 786436
  47.7 52.1 %collective-permute-start = (bf16[4,528,512]{2,1,0:T(8,128)(2,1)}, bf16[4,528,512]{2,1,0:T(8,128)(2,1)}, u32[]{:S(2)}, u32[]{:S(2)}) collective-permute-start(bf16[4,528,512]{2,1,0:T(8,128)(2,1)} %bitcast.71), channel_id=1, source_target_pairs={{0,32},{32,0},{64,96},{96,64},{128,160},{160,128},{192,224},{224,1... | collective-permute-start | bytes 6488072 | tf_op jit(solution)/shard_map/ppermute | solution.py:262
  49.7 12.1 %collective-permute-start.2 = (bf16[400,512]{1,0:T(8,128)(2,1)}, bf16[400,512]{1,0:T(8,128)(2,1)S(1)}, u32[]{:S(2)}, u32[]{:S(2)}) collective-permute-start(bf16[400,512]{1,0:T(8,128)(2,1)} %slice_bitcast_fusion.1), channel_id=1, source_target_pairs={{0,4},{1,5},{2,6},{3,7},{4,0},{5,1},{6,2},{7,3},{8,12},{9,13},{10,... | collective-permute-start | bytes 1228808 | tf_op jit(solution)/shard_map/ppermute | solution.py:265
  52.2 1.6 copy-start.2
  53.8 1.3 copy-start.4
  55.1 1.0 copy-start.11
  56.1 5.7 %copy-start.1 = (bf16[2112,512]{1,0:T(8,128)(2,1)S(1)}, bf16[2112,512]{1,0:T(8,128)(2,1)}, u32[]{:S(2)}) copy-start(bf16[2112,512]{1,0:T(8,128)(2,1)} %all-gather.3.cloned.1.call-done) | copy-start | bytes 6488068
  57.2 0.8 copy-start.8
  58.0 7.3 %copy-start.7 = (bf16[4,576,128]{2,1,0:T(8,128)(2,1)}, bf16[4,576,128]{2,1,0:T(8,128)(2,1)S(1)}, u32[]{:S(2)}) copy-start(bf16[4,576,128]{2,1,0:T(8,128)(2,1)S(1)} %get-tuple-element.22) | copy-start | bytes 1769476
  61.9 18.2 %collective-permute-start.5 = (bf16[336,512]{1,0:T(8,128)(2,1)S(1)}, bf16[336,512]{1,0:T(8,128)(2,1)}, u32[]{:S(2)}, u32[]{:S(2)}) collective-permute-start(bf16[336,512]{1,0:T(8,128)(2,1)S(1)} %slice_select_fusion.wa), channel_id=1, source_target_pairs={{0,8},{1,9},{2,10},{3,11},{4,12},{5,13},{6,14},{7,15},{8,0},{9,1},... | collective-permute-start | bytes 1032200 | tf_op jit(solution)/shard_map/ppermute | solution.py:265
  65.3 35.0 %all-to-all-start = ((bf16[4,576,128]{2,1,0:T(8,128)(2,1)}), bf16[4,576,128]{2,1,0:T(8,128)(2,1)}, u32[]{:S(2)}, u32[]{:S(2)}) async-start(bf16[4,576,128]{2,1,0:T(8,128)(2,1)} %copy-done.7), calls=%async_computation | async-start | bytes 1179648 | tf_op jit(solution)/shard_map/all_to_all | solution.py:307
  69.5 36.3 %collective-permute-start.3 = (bf16[400,512]{1,0:T(8,128)(2,1)S(1)}, bf16[400,512]{1,0:T(8,128)(2,1)}, u32[]{:S(2)}, u32[]{:S(2)}) collective-permute-start(bf16[400,512]{1,0:T(8,128)(2,1)S(1)} %collective-permute-done.2.wb), channel_id=1, source_target_pairs={{0,32},{32,0},{64,96},{96,64},{128,160},{160,128},{192,224},{224,1... | collective-permute-start | bytes 1228808 | tf_op jit(solution)/shard_map/ppermute | solution.py:262
  81.7 18.1 %collective-permute-start.9 = (bf16[256,512]{1,0:T(8,128)(2,1)}, bf16[256,512]{1,0:T(8,128)(2,1)}, u32[]{:S(2)}, u32[]{:S(2)}) collective-permute-start(bf16[256,512]{1,0:T(8,128)(2,1)} %slice_select_fusion.1.w5a), channel_id=1, source_target_pairs={{0,16},{1,17},{2,18},{3,19},{4,20},{5,21},{6,22},{7,23},{8,24},{9,... | collective-permute-start | bytes 786440 | tf_op jit(solution)/shard_map/ppermute | solution.py:265
  88.4 27.6 %collective-permute-start.6 = (bf16[336,512]{1,0:T(8,128)(2,1)S(1)}, bf16[336,512]{1,0:T(8,128)(2,1)}, u32[]{:S(2)}, u32[]{:S(2)}) collective-permute-start(bf16[336,512]{1,0:T(8,128)(2,1)S(1)} %slice_select_fusion.wa), channel_id=1, source_target_pairs={{0,32},{32,0},{64,96},{96,64},{128,160},{160,128},{192,224},{224,1... | collective-permute-start | bytes 1032200 | tf_op jit(solution)/shard_map/ppermute | solution.py:262
  88.4 39.7 %collective-permute-start.10 = (bf16[256,512]{1,0:T(8,128)(2,1)}, bf16[256,512]{1,0:T(8,128)(2,1)}, u32[]{:S(2)}, u32[]{:S(2)}) collective-permute-start(bf16[256,512]{1,0:T(8,128)(2,1)} %slice_select_fusion.1.w5a), channel_id=1, source_target_pairs={{0,32},{32,0},{64,96},{96,64},{128,160},{160,128},{192,224},{224,1... | collective-permute-start | bytes 786440 | tf_op jit(solution)/shard_map/ppermute | solution.py:262
  99.8 16.2 %collective-permute-start.7 = (bf16[336,512]{1,0:T(8,128)(2,1)}, bf16[336,512]{1,0:T(8,128)(2,1)}, u32[]{:S(2)}, u32[]{:S(2)}) collective-permute-start(bf16[336,512]{1,0:T(8,128)(2,1)} %collective-permute-done.5.wb), channel_id=1, source_target_pairs={{0,32},{32,0},{64,96},{96,64},{128,160},{160,128},{192,224},{224,1... | collective-permute-start | bytes 1032200 | tf_op jit(solution)/shard_map/ppermute | solution.py:262
  99.8 28.3 %collective-permute-start.11 = (bf16[256,512]{1,0:T(8,128)(2,1)}, bf16[256,512]{1,0:T(8,128)(2,1)}, u32[]{:S(2)}, u32[]{:S(2)}) collective-permute-start(bf16[256,512]{1,0:T(8,128)(2,1)} %collective-permute-done.9.w5b), channel_id=1, source_target_pairs={{0,32},{32,0},{64,96},{96,64},{128,160},{160,128},{192,224},{224,1... | collective-permute-start | bytes 786440 | tf_op jit(solution)/shard_map/ppermute | solution.py:262
  105.8 7.1 %copy-start.6 = (bf16[528,512]{1,0:T(8,128)(2,1)S(1)}, bf16[528,512]{1,0:T(8,128)(2,1)}, u32[]{:S(2)}) copy-start(bf16[528,512]{1,0:T(8,128)(2,1)} %slice.39.wa) | copy-start | bytes 1622020
  105.9 7.1 %collective-permute-start.1 = (bf16[768,128]{1,0:T(8,128)(2,1)S(1)}, bf16[768,128]{1,0:T(8,128)(2,1)S(1)}, u32[]{:S(2)}, u32[]{:S(2)}) collective-permute-start(bf16[768,128]{1,0:T(8,128)(2,1)S(1)} %get-tuple-element.23.mine), channel_id=1, source_target_pairs={{0,4},{1,5},{2,6},{3,7},{4,0},{5,1},{6,2},{7,3},{8,12},{9,13},{10,... | collective-permute-start | bytes 589832 | tf_op jit(solution)/shard_map/ppermute | solution.py:265
  114.9 8.4 %collective-permute-start.4 = (bf16[512,128]{1,0:T(8,128)(2,1)S(1)}, bf16[512,128]{1,0:T(8,128)(2,1)S(1)}, u32[]{:S(2)}, u32[]{:S(2)}) collective-permute-start(bf16[512,128]{1,0:T(8,128)(2,1)S(1)} %get-tuple-element.24.mine), channel_id=1, source_target_pairs={{0,8},{1,9},{2,10},{3,11},{4,12},{5,13},{6,14},{7,15},{8,0},{9,1},... | collective-permute-start | bytes 393224 | tf_op jit(solution)/shard_map/ppermute | solution.py:265
  125.2 8.7 %collective-permute-start.8 = (bf16[256,128]{1,0:T(8,128)(2,1)S(1)}, bf16[256,128]{1,0:T(8,128)(2,1)S(1)}, u32[]{:S(2)}, u32[]{:S(2)}) collective-permute-start(bf16[256,128]{1,0:T(8,128)(2,1)S(1)} %get-tuple-element.25.mine), channel_id=1, source_target_pairs={{0,16},{1,17},{2,18},{3,19},{4,20},{5,21},{6,22},{7,23},{8,24},{9,... | collective-permute-start | bytes 196616 | tf_op jit(solution)/shard_map/ppermute | solution.py:265
  143.8 13.8 %copy-start.5 = (bf16[1,5,128,1024]{3,2,1,0:T(8,128)(2,1)S(1)}, bf16[1,5,128,1024]{3,2,1,0:T(8,128)(2,1)}, u32[]{:S(2)}) copy-start(bf16[1,5,128,1024]{3,2,1,0:T(8,128)(2,1)} %param.13) | copy-start | bytes 3932164
  143.8 13.8 %all-to-all-start.1 = ((bf16[4,576,128]{2,1,0:T(8,128)(2,1)}), bf16[4,576,128]{2,1,0:T(8,128)(2,1)S(1)}, u32[]{:S(2)}, u32[]{:S(2)}) async-start(bf16[4,576,128]{2,1,0:T(8,128)(2,1)} %shard_map.125), calls=%async_computation.1 | async-start | bytes 1179648 | tf_op jit(solution)/shard_map/all_to_all | solution.py:357
  157.6 1.6 copy-start.3
  159.2 1.0 copy-start.9
  160.3 20.3 %copy-start.10 = (f32[64,512]{1,0:T(8,128)S(1)}, f32[64,512]{1,0:T(8,128)}, u32[]{:S(2)}) copy-start(f32[64,512]{1,0:T(8,128)} %select_reduce_fusion.weight) | copy-start | bytes 393220
Sparse Core Ops, SparseCore 0:
  10.7 36.8 all-gather.2

commit v2 on v0

v2 whole, which is shorter than its diff:
```python
import functools

import jax
import jax.numpy as jnp
from jax import lax
from jax.experimental import pallas as pl
from jax.experimental.pallas import tpu as pltpu
from jax.sharding import PartitionSpec as P

BF = jnp.bfloat16
F32 = jnp.float32
LEAF, PANEL, U, NC, LEVELS = 1024, 512, 128, 256, 5
RING, DEPTH = 4, 8
TERM = LEVELS * U
SLOTS = 16
VMEM_LIMIT = 16 * 1024 * 1024

CPL0 = PANEL + 16


def factor_rows(slots):
    return CPL0 + slots * U


def dot(left, right):
    return jnp.dot(left, right, preferred_element_type=F32)


def dot_t(left, right):
    return lax.dot_general(left, right, (((1,), (1,)), ((), ())), preferred_element_type=F32)


VMEM = pl.BlockSpec(memory_space=pltpu.VMEM)
VMEM_FREE = pl.BlockSpec(memory_space=pltpu.VMEM)
SMEM = pl.BlockSpec(memory_space=pltpu.SMEM)
HBM = pl.BlockSpec(memory_space=pltpu.HBM)
ANY = pl.BlockSpec(memory_space=pl.ANY)


def call(body, outs, args, specs, scratch=(), out_specs=None, flops=10**8, moved=10**6):
    args = [in_vmem(arg) if spec is VMEM else arg for arg, spec in zip(args, specs)]
    return pl.pallas_call(
        body,
        out_shape=outs,
        in_specs=specs,
        out_specs=out_specs or [VMEM] * len(outs),
        scratch_shapes=list(scratch),
        compiler_params=pltpu.CompilerParams(vmem_limit_bytes=VMEM_LIMIT),
        cost_estimate=pl.CostEstimate(flops=flops, bytes_accessed=moved, transcendentals=0),
    )(*args)


def dma(n):
    return pltpu.SemaphoreType.DMA((n,))


def pinned(*dims, dtype=BF):
    return pltpu.VMEM(dims, dtype)


def plain(*dims, dtype=BF):
    return jax.ShapeDtypeStruct(dims, dtype)


def in_vmem(value):
    return pltpu.with_memory_space_constraint(value, pltpu.VMEM)


def in_hbm(value):
    return pltpu.with_memory_space_constraint(value, pltpu.HBM)


def hot(rows):
    place = lax.broadcasted_iota(jnp.int32, (PANEL, rows.shape[1]), 0).astype(F32)
    return jnp.where(place == rows, 1.0, 0.0).astype(BF)


def leaf_rows(block):
    block = block.astype(F32)
    return [block[l : l + 1, 0:U] * 16.0 + block[l : l + 1, U : 2 * U] for l in range(LEVELS)]


def sep_rows(block):
    block = block.astype(F32)
    return [
        block[s : s + 1, 2 * U : 3 * U] * 16.0 + block[s : s + 1, 3 * U : 4 * U]
        for s in range(LEVELS - 1)
    ]


def push_values(factor, y, slots):
    return dot_t(y, factor[CPL0 : CPL0 + slots * U]).astype(BF)


def solve_back(factor, hots, y, above):
    back = y
    slots = len(above)
    if slots:
        taken = [dot(above[k], hots[k]).astype(BF) for k in range(slots)]
        taken = taken[0] if slots == 1 else jnp.concatenate(taken, axis=1)
        sub = dot(taken, factor[CPL0 : CPL0 + slots * U])
        back = (y.astype(F32) - sub).astype(BF)
    return dot(back, factor[0:PANEL]).astype(BF)


def pack_factor(inv, cpl, leaf_idx, sep_idx, out, codes, sems):
    copies = [
        pltpu.make_async_copy(inv, out.at[0:PANEL], sems.at[0]),
        pltpu.make_async_copy(cpl, out.at[CPL0:], sems.at[1]),
    ]
    for copy in copies:
        copy.start()
    codes[...] = jnp.zeros_like(codes)
    for ref, count, at in ((leaf_idx, LEVELS, 0), (sep_idx, LEVELS - 1, 2 * U)):
        value = ref[0]
        codes[0:count, at : at + U] = (value >> 4).astype(F32)
        codes[0:count, at + U : at + 2 * U] = (value & 15).astype(F32)
    out[PANEL:CPL0] = codes[...].astype(BF)
    for copy in copies:
        copy.wait()


def leaf_forward(
    place, inv, rhs, cpl, rsep, yt_out, keep, send, inv_v, cpl_v, rhs_v, rsep_v, y, stack, sems
):
    loads = [pltpu.make_async_copy(rhs, rhs_v, sems.at[0])]
    for i in range(4):
        rows = pl.ds(i * 256, 256)
        loads.append(pltpu.make_async_copy(inv.at[rows], inv_v.at[rows], sems.at[1 + i]))
    loads.append(pltpu.make_async_copy(cpl.at[0], cpl_v, sems.at[5]))
    loads.append(pltpu.make_async_copy(rsep, rsep_v, sems.at[6]))
    for load in loads:
        load.start()
    loads[0].wait()
    for i in range(4):
        loads[1 + i].wait()
        span = (i + 1) * 256
        y[i * 256 : span] = dot(inv_v[i * 256 : span, 0:span], rhs_v[0:span])
    yt_out[...] = y[...].T.astype(BF)
    loads[5].wait()
    for l in range(LEVELS):
        stack[:, l * U : (l + 1) * U] = dot_t(yt_out[...], cpl_v[l]).astype(BF)
    loads[6].wait()
    stack[:, TERM:] = rsep_v[...].astype(F32).T.astype(BF)
    side = place[3]
    keep[...] = stack[pl.ds(pl.multiple_of(side * 128, 128), 128)]
    send[...] = stack[pl.ds(pl.multiple_of((1 - side) * 128, 128), 128)]


ONE = 2 * U
ONE_HOTS = ONE + 4 * 3 * U


def start_chosen(cases, sources, copy_of):
    for i, source in enumerate(sources):

        @pl.when(cases[i] == 1)
        def _(source=source):
            copy_of(source).start()

    return copy_of(sources[0])


def stage(slots, count, cases, *refs):
    sources = refs[:count]
    factor, hots, sems = refs[count:]
    rows = factor_rows(slots)
    copy = start_chosen(
        cases, sources, lambda source: pltpu.make_async_copy(source.at[0:rows], factor, sems.at[0])
    )
    copy.wait()
    if slots:
        taken = sep_rows(factor[PANEL:CPL0])
        for k in range(slots):
            hots[:, k * U : (k + 1) * U] = hot(taken[k])


def stage_last(count, cases, *refs):
    factor, done, sems = refs[count:]
    copy = start_chosen(
        cases,
        refs[:count],
        lambda source: pltpu.make_async_copy(source.at[0:PANEL], factor, sems.at[0]),
    )
    done[...] = jnp.zeros_like(done)
    copy.wait()


def stage_one(cases, own, a, b, factor, hots, theirs_v, sems):
    copies = [
        start_chosen(cases, [own, a, b], lambda source: pltpu.make_async_copy(source, factor, sems.at[0]))
    ]
    rows = pl.ds(PANEL, 16)
    far = [
        pltpu.make_async_copy(a.at[rows], theirs_v.at[0], sems.at[1]),
        pltpu.make_async_copy(b.at[rows], theirs_v.at[1], sems.at[2]),
    ]
    for copy in far:
        copy.start()
    mine = leaf_rows(own[PANEL:CPL0])
    for copy in far:
        copy.wait()
    other = jnp.where(cases[3] == 0, theirs_v[0], theirs_v[1])
    theirs = leaf_rows(other)
    ours, others = sep_rows(own[PANEL:CPL0]), sep_rows(other)
    hots[:, 0:ONE] = hot(jnp.concatenate([mine[0], theirs[0]], axis=1))
    for k in range(4):
        up = jnp.where(cases[0] == 1, ours[k], others[k])
        at = ONE + k * 3 * U
        hots[:, at : at + 3 * U] = hot(jnp.concatenate([mine[k + 1], theirs[k + 1], up], axis=1))
    for copy in copies:
        copy.wait()


def level_one(place, keep, recv, factor, hots, y_out, panel_keep, panel_send, panels):
    ring, even = place[1], place[2] == 0
    total = dot_t(jnp.concatenate([keep[:, 0:U], recv[:, 0:U]], axis=1), hots[:, 0:ONE])
    rhs_keep, rhs_recv = keep[:, TERM:].astype(F32), recv[:, TERM:].astype(F32)
    resid = (jnp.where(even, rhs_keep, rhs_recv) - total).astype(BF)
    y = dot_t(resid, factor[0:PANEL]).astype(BF)
    y_out[...] = y
    values = push_values(factor, y, 4)
    held = jnp.where(even, rhs_recv, rhs_keep)
    level = jnp.where(ring < 2, 2, place[4])
    for l in range(2, LEVELS + 1):
        at = slice((l - 1) * U, l * U)
        start = ONE + (l - 2) * 3 * U
        parts = [keep[:, at], recv[:, at], values[:, (l - 2) * U : (l - 1) * U]]
        total = dot_t(jnp.concatenate(parts, axis=1), hots[:, start : start + 3 * U])
        total = total - jnp.where(level == l, held, 0.0)
        panels[:, (l - 2) * PANEL : (l - 1) * PANEL] = total.astype(BF)
    side = place[5]
    panel_keep[...] = panels[pl.ds(pl.multiple_of(side * 64, 64), 64)]
    panel_send[...] = panels[pl.ds(pl.multiple_of((1 - side) * 64, 64), 64)]


def level_up(level, mine, recv, factor, hots, y_out, panels):
    slots = LEVELS - level
    total = mine[...].astype(F32) + recv[...].astype(F32)
    y = dot_t((-total[:, 0:PANEL]).astype(BF), factor[0:PANEL]).astype(BF)
    y_out[...] = y
    values = push_values(factor, y, slots)
    for k in range(slots):
        at = slice((k + 1) * PANEL, (k + 2) * PANEL)
        term = dot_t(values[:, k * U : (k + 1) * U], hots[:, k * U : (k + 1) * U])
        panels[:, k * PANEL : (k + 1) * PANEL] = (total[:, at] + term).astype(BF)


def turn(mine, recv, f3, f4, f5, h3, h4, y3, y4, x_out):
    total = mine[...].astype(F32) + recv[...].astype(F32)
    y5 = dot_t((-total).astype(BF), f5[0:PANEL]).astype(BF)
    x5 = solve_back(f5, [], y5, [])
    x4 = solve_back(f4, [h4[...]], y4[...], [x5])
    x3 = solve_back(f3, [h3[:, 0:U], h3[:, U : 2 * U]], y3[...], [x4, x5])
    for k, x in enumerate((x3, x4, x5)):
        x_out[:, k * PANEL : (k + 1) * PANEL] = x


def level_two_back(place, mine, recv, f2, h2, y2, x_out):
    x = jnp.where(place[6] == 0, mine[...], recv[...])
    above = [x[:, k * PANEL : (k + 1) * PANEL] for k in range(3)]
    x_out[:, 0:PANEL] = solve_back(f2, [h2[:, k * U : (k + 1) * U] for k in range(3)], y2[...], above)
    x_out[:, PANEL:] = x


def level_one_back(place, mine, recv, y1, factor, hots, rows_keep, rows_send, sep_keep, sep_send, x):
    side = place[5]
    even = place[2] == 0
    x[pl.ds(pl.multiple_of(side * 64, 64), 64)] = mine[...]
    x[pl.ds(pl.multiple_of((1 - side) * 64, 64), 64)] = recv[...]
    above = [x[:, k * PANEL : (k + 1) * PANEL] for k in range(4)]
    ups = [hots[:, ONE + k * 3 * U + 2 * U : ONE + (k + 1) * 3 * U] for k in range(4)]
    x1 = solve_back(factor, ups, y1[...], above)
    for l, value in enumerate([x1] + above):
        start = 0 if l == 0 else ONE + (l - 1) * 3 * U
        both = dot(value, hots[:, start : start + 2 * U]).astype(BF)
        rows_keep[:, l * U : (l + 1) * U] = both[:, 0:U]
        rows_send[:, l * U : (l + 1) * U] = both[:, U : 2 * U]
    level = jnp.where(place[1] < 2, 2, place[4])
    held = jnp.where(level == 0, jnp.zeros_like(x1), above[0])
    for k in (1, 2, 3):
        held = jnp.where(level == k + 2, above[k], held)
    sep_keep[...] = jnp.where(even, x1, held)
    sep_send[...] = jnp.where(even, held, x1)


def stage_leaf(sel, chosen):
    place = lax.broadcasted_iota(jnp.int32, (32 * SLOTS, LEAF), 1)
    chosen[...] = jnp.where(place == sel[...] - 1, 1.0, 0.0).astype(BF)


def leaf_backward(place, keep, recv, inv, cpl, yt, chosen, x_leaf, picks, rows, sub):
    side = place[3]
    rows[pl.ds(pl.multiple_of(side * 128, 128), 128)] = keep[...]
    rows[pl.ds(pl.multiple_of((1 - side) * 128, 128), 128)] = recv[...]
    total = yt[...].astype(F32)
    for l in range(LEVELS):
        total = total - dot(rows[:, l * U : (l + 1) * U], cpl[l])
    sub[...] = total.astype(BF)
    for i in range(4):
        start = i * 256
        part = dot(sub[:, start:], inv[start:, start : start + 256])
        x_leaf[start : start + 256] = part.T.astype(BF)
    picks[...] = dot(chosen[...], x_leaf[...]).astype(BF)


def finish(place, weight, got, keep, recv, out, x_sep, xt):
    side = place[3]
    xt[pl.ds(pl.multiple_of(side * 128, 128), 128)] = keep[...].astype(F32)
    xt[pl.ds(pl.multiple_of((1 - side) * 128, 128), 128)] = recv[...].astype(F32)
    x_sep[...] = xt[...].T.astype(BF)
    value = weight[...]
    high = value.astype(BF)
    low = (value - high.astype(F32)).astype(BF)
    out[...] = dot(high, got[...]) + dot(low, got[...])


def stay_plan(me, stay_dofs, stay_coef):
    k, stays = stay_dofs.shape
    per = stays // 32
    pairs = k * per
    dofs = stay_dofs.reshape(k, 32, per).transpose(1, 0, 2).reshape(32, pairs)
    before = jnp.arange(pairs)[:, None] < jnp.arange(pairs)[None, :]
    match = (dofs // LEAF) == me
    rank = dot(match.astype(BF), before.astype(BF))
    at = match[:, None, :] & (rank[:, None, :] == jnp.arange(SLOTS, dtype=F32)[None, :, None])
    sel = jnp.sum(jnp.where(at, (dofs % LEAF + 1)[:, None, :], 0), axis=2).reshape(32 * SLOTS, 1)
    mine = lax.dynamic_index_in_dim(dofs, me, 0, keepdims=False) // LEAF
    earlier = jnp.sum(jnp.where(before & (mine[:, None] == mine[None, :]), 1, 0), axis=0)
    slot = (mine * SLOTS + earlier).reshape(k, per)
    coef = lax.dynamic_slice_in_dim(stay_coef, me * per, per, 1)
    hit = slot[:, :, None] == jnp.arange(32 * SLOTS)[None, None, :]
    weight = jnp.sum(jnp.where(hit, coef[:, :, None], 0.0), axis=0)
    return sel.astype(jnp.int32), weight


def after(value, *others):
    return lax.optimization_barrier((value, *others))[0]


def on_device(
    rhs_leaf, rhs_sep, leaf_inv, leaf_cpl, leaf_idx, sep_inv, sep_cpl, sep_idx, stay_dofs, stay_coef
):
    rows_axis, cols_axis = "rows", "cols"
    columns, rows = lax.axis_size(cols_axis), lax.axis_size(rows_axis)
    me = lax.axis_index(rows_axis)
    core = lax.axis_index(cols_axis) % 2
    y, z = me % RING, me // RING

    def swap_core(value):
        return lax.ppermute(value, cols_axis, [(i, i ^ 1) for i in range(columns)])

    def swap(value, flip):
        return lax.ppermute(value, rows_axis, [(i, i ^ flip) for i in range(rows)])

    def route(value, target):
        pairs = []
        for c in range(columns):
            for r in range(rows):
                to = target(c % 2, r % RING, r // RING)
                if to is not None:
                    pairs.append((c * rows + r, c * rows + to[1] * RING + to[0]))
        return lax.ppermute(value, (cols_axis, rows_axis), pairs)

    def cases(*values):
        return jnp.stack(values).astype(jnp.int32)

    top_level = jnp.where(z % 2 == 0, 3, jnp.where(z % 4 == 1, 4, jnp.where(z == 3, 5, 0)))
    place = cases(core, y, y % 2, (y % 2) ^ (y // 2), top_level, y // 2, z % 2)

    (own,) = call(
        pack_factor,
        [pinned(factor_rows(4), PANEL)],
        [in_hbm(sep_inv), in_hbm(sep_cpl.reshape(4 * U, PANEL)), leaf_idx, sep_idx],
        [HBM, HBM, VMEM, VMEM],
        [pltpu.VMEM((16, PANEL), F32), dma(2)],
    )
    with jax.named_scope("factors_to_neighbours"):
        near = route(own, lambda c, y, z: (y ^ (3 if c else 1), z))

    yt, keep, send, inv_v, cpl_v = call(
        leaf_forward,
        [
            pinned(NC, LEAF),
            pinned(128, TERM + PANEL),
            pinned(128, TERM + PANEL),
            pinned(LEAF, LEAF),
            pinned(LEVELS, U, LEAF),
        ],
        [after(place, own), in_hbm(leaf_inv), in_hbm(rhs_leaf), in_hbm(leaf_cpl), in_hbm(rhs_sep)],
        [SMEM, HBM, HBM, HBM, HBM],
        [
            pltpu.VMEM((LEAF, NC), BF),
            pltpu.VMEM((PANEL, NC), BF),
            pltpu.VMEM((LEAF, NC), F32),
            pltpu.VMEM((NC, TERM + PANEL), BF),
            dma(7),
        ],
    )
    with jax.named_scope("leaf_terms"):
        recv = swap(send, 1)
    sel, weight = stay_plan(me, *after((stay_dofs, stay_coef), send))
    recv, sel, weight = lax.optimization_barrier((recv, sel, weight))
    near = after(near, recv)
    with jax.named_scope("near_to_core"):
        near_o = swap_core(near)
    with jax.named_scope("factors_across"):
        far = route(
            near, lambda c, y, z: (y ^ (1 if c else 3), z) if y % 2 == 0 else None
        )
    first = core == 0
    one = (y % 2 == 1) & first, (y % 2 == 1) & ~first
    f1, h1 = call(
        stage_one,
        [pinned(factor_rows(4), PANEL), pinned(PANEL, ONE_HOTS)],
        [cases(y % 2 == 0, *one, core), own, near, near_o],
        [SMEM, VMEM, ANY, ANY],
        [pltpu.VMEM((2, 16, PANEL), BF), dma(3)],
    )
    y1, panel, send = call(
        level_one,
        [pinned(128, PANEL), pinned(64, 4 * PANEL), pinned(64, 4 * PANEL)],
        [place, keep, recv, f1, h1],
        [SMEM] + [VMEM] * 4,
        [pltpu.VMEM((128, 4 * PANEL), BF)],
    )
    with jax.named_scope("panels_ring"):
        recv = swap(send, 3)

    def ready(slots, which, sources):
        return call(
            functools.partial(stage, slots, len(sources)),
            [pinned(factor_rows(slots), PANEL), pinned(PANEL, max(slots, 1) * U)],
            [which, *sources],
            [SMEM] + [ANY] * len(sources),
            [dma(1)],
        )

    def rise(level, panel, recv, factor, hots):
        slots = LEVELS - level
        return call(
            functools.partial(level_up, level),
            [pinned(64, PANEL), pinned(64, slots * PANEL)],
            [panel, recv, factor, hots],
            [VMEM] * 4,
        )

    far = after(far, recv)
    at = [own, near, near_o, far]
    f2, h2 = ready(
        3,
        cases(
            y == 1,
            ((y == 0) & first) | ((y == 2) & ~first),
            ((y == 0) & ~first) | ((y == 2) & first),
            y == 3,
        ),
        at,
    )
    f3, h3 = ready(
        2,
        cases(
            y == 3,
            ((y == 2) & first) | ((y == 0) & ~first),
            ((y == 2) & ~first) | ((y == 0) & first),
            y == 1,
        ),
        at,
    )
    with jax.named_scope("factors_up"):
        up = route(
            f3[0 : factor_rows(1)],
            lambda c, y, z: (y, (z + (1 if c else -1)) % DEPTH) if z % 2 else None,
        )
    recv = after(recv, f2, h2)
    y2, panel = rise(2, panel, recv, f2, h2)
    with jax.named_scope("panels_z1"):
        recv = lax.ppermute(
            panel, rows_axis, [(r, r - RING) for r in range(rows) if r // RING % 2]
        )
    up = after(up, recv)
    with jax.named_scope("up_to_core"):
        up_o = swap_core(up)
    with jax.named_scope("factor_top"):
        last = route(
            up,
            lambda c, y, z: (y, 0) if (c, z) == (0, 2) else (y, 6) if (c, z) == (1, 4) else None,
        )
    y3, panel = rise(3, panel, recv, f3, h3)
    with jax.named_scope("panels_z2"):
        recv = lax.ppermute(
            panel, rows_axis, [(r, r ^ (2 * RING)) for r in range(rows) if r // RING % 2 == 0]
        )
    f4, h4 = ready(
        1, cases((z % 4 == 0) == first, (z % 4 == 0) != first), after((up, up_o), panel)
    )
    recv = after(recv, f4, h4)
    y4, panel = rise(4, panel, recv, f4, h4)
    with jax.named_scope("panels_z3"):
        recv = lax.ppermute(
            panel,
            rows_axis,
            [(r, (6 - r // RING) * RING + r % RING) for r in range(rows) if r // RING % 2 == 0],
        )
    last = after(last, panel)
    with jax.named_scope("last_to_core"):
        last_o = swap_core(last)
    inner = (z == 2) | (z == 4)
    same = (z == 2) == first
    f5, _ = call(
        functools.partial(stage_last, 4),
        [pinned(PANEL, PANEL), pinned(16, 128)],
        [cases(
            inner & same,
            inner & ~same,
            ~inner & ((z == 0) == first),
            ~inner & ((z == 0) != first),
        ), up, up_o, last, last_o],
        [SMEM] + [ANY] * 4,
        [dma(1)],
    )
    recv = after(recv, f5)
    (x,) = call(
        turn,
        [pinned(64, 3 * PANEL)],
        [panel, recv, f3, f4, f5, h3, h4, y3, y4],
        [VMEM] * 9,
    )
    with jax.named_scope("down_z1"):
        recv = lax.ppermute(
            x, rows_axis, [(r, r + RING) for r in range(rows) if r // RING % 2 == 0]
        )
    (x,) = call(
        level_two_back,
        [pinned(64, 4 * PANEL)],
        [place, x, recv, f2, h2, y2],
        [SMEM] + [VMEM] * 5,
    )
    with jax.named_scope("down_ring"):
        recv = swap(x, 3)
    rows_keep, rows_send, sep_keep, sep_send = call(
        level_one_back,
        [pinned(128, TERM), pinned(128, TERM), pinned(128, PANEL), pinned(128, PANEL)],
        [place, x, recv, y1, f1, h1],
        [SMEM] + [VMEM] * 5,
        [pltpu.VMEM((128, 4 * PANEL), BF)],
    )
    with jax.named_scope("rows_back"):
        recv = swap(rows_send, 1)
    (picked,) = call(stage_leaf, [pinned(32 * SLOTS, LEAF)], [after(sel, rows_send)], [VMEM_FREE])
    recv = after(recv, picked)
    x_leaf, picks = call(
        leaf_backward,
        [plain(LEAF, NC), pinned(32 * SLOTS, NC)],
        [place, rows_keep, recv, inv_v, cpl_v, yt, picked],
        [SMEM] + [VMEM] * 6,
        [pltpu.VMEM((NC, TERM), BF), pltpu.VMEM((NC, LEAF), BF)],
    )
    with jax.named_scope("sep_back"):
        sep_recv = swap(after(sep_send, recv), 1)
    got = lax.all_to_all(
        picks.reshape(32, SLOTS, NC), rows_axis, 0, 0, tiled=True
    ).reshape(32 * SLOTS, NC)
    stretch, x_sep = call(
        finish,
        [plain(64, NC, dtype=F32), plain(PANEL, NC)],
        [place, weight, got, sep_keep, sep_recv],
        [SMEM] + [VMEM] * 4,
        [pltpu.VMEM((NC, PANEL), F32)],
    )
    return (x_leaf, x_sep, stretch)


def solution(mesh):
    return jax.shard_map(
        on_device,
        mesh=mesh,
        in_specs=(
            P("rows", "cols"),
            P("rows", "cols"),
            P("rows", None),
            P("rows", None, None, None),
            P("rows", None, None),
            P("rows", None),
            P("rows", None, None, None),
            P("rows", None, None),
            P(),
            P(),
        ),
        out_specs=(P("rows", "cols"), P("rows", "cols"), P("rows", "cols")),
        check_vma=False,
    )
```

time: 711 us -> 147 us (0.21); the launches traced: 702 us -> 146 us
  waiting for transfers between devices: 471 us -> 64 us
  local copies, waits for them, and re-layouts: 72.2 us -> 17.2 us
  other arithmetic: 56.8 us -> 2.03 us
  matrix products: 33.2 us -> 0.16 us
  Pallas kernels: 0 us -> 24.8 us
  starting transfers between devices: 53.1 us -> 37 us
  between operations: 15.3 us -> 1.11 us
    reduce_scatter x1 -> x0, waiting for transfers between devices: 212 us -> none  [on_device(): lax.psum_scatter(partial_stretch, 'rows', scatter_dimension=0, tiled=True)]
    ppermute x30 -> x16, waiting for transfers between devices: 259 us -> 58.1 us  [the longest x5 24.4 us: swap(): return lax.ppermute(value, rows_axis, [(i, i ^ flip) for i in range(rows)])]
    gather x10 -> x0, local copies, waits for them, and re-layouts: 59.2 us -> none  [the longest x1 49.2 us: on_device(): picked = x_leaf[jnp.clip(local_row, 0, leaf_rows - 1)]]
    dot_general x18 -> x1, matrix products: 33.2 us -> 0.16 us  [dot(): return jnp.dot(left, right, preferred_element_type=F32)]
    pallas_call x0 -> x17, Pallas kernels: none -> 24.8 us  [call(): pl.pallas_call(body, out_shape=outs, in_specs=specs, out_specs=out_specs...]
    ppermute x30 -> x16, starting transfers between devices: 53.1 us -> 30.1 us  [the longest x4 10.2 us: route(): return lax.ppermute(value, (cols_axis, rows_axis), pairs)]
    scatter-add x10 -> x0, other arithmetic: 19.6 us -> none  [spread(): jnp.zeros((row_count, values.shape[1]), jnp.float32).at[row_index]]
    add x25 -> x2, other arithmetic: 15.7 us -> 0.04 us  [the longest x1 0.02 us: stay_plan(): dofs % LEAF + 1]
  transfers between devices with their start and end apart: 31 -> 17, of which waited for: 30 -> 11; matrix products, arithmetic and copies ran while one was open for 3% -> 3% of each run, Pallas kernels for 0% -> 9%
where the time goes in v2:
time: 147 us; the launch traced here: 146 us
  waiting for transfers between devices  64 us (44%)
  starting transfers between devices  37 us (25%)
  Pallas kernels  24.8 us (17%)
  local copies, waits for them, and re-layouts  17.2 us (12%)
  other arithmetic  2.03 us (1%)
    pallas_call x17, Pallas kernels, call(): pl.pallas_call(body, out_shape=outs, in_specs=specs, out_specs=out_specs...  24.8 us
    ppermute x5, waiting for transfers between devices, swap(): return lax.ppermute(value, rows_axis, [(i, i ^ flip) for i in range(rows)])  24.4 us
    unnamed x79, local copies, waits for them, and re-layouts  15.1 us
    ppermute x1, waiting for transfers between devices, on_device(): lax.ppermute(panel, rows_axis, [(r, r - RING) for r in range(rows) if r /...  11.4 us
    ppermute x4, starting transfers between devices, route(): return lax.ppermute(value, (cols_axis, rows_axis), pairs)  10.2 us
    ppermute x4, waiting for transfers between devices, route(): return lax.ppermute(value, (cols_axis, rows_axis), pairs)  9.17 us
    ppermute x1, waiting for transfers between devices, on_device(): lax.ppermute(panel, rows_axis, [(r, r ^ 2 * RING) for r in range(rows) if...  7.29 us
    all_to_all x1, starting transfers between devices, on_device(): lax.all_to_all(picks.reshape(32, SLOTS, NC), rows_axis, 0, 0, tiled=True)  6.87 us
  transfers between devices with their start and end apart: 17, of which 11 were waited for; matrix products, arithmetic and copies ran while one was open for 3% of the time, Pallas kernels for 9%

profile of v2, /device:TPU:2, one launch (start us, length us, event | category | flops | bytes accessed | tf_op | source)
XLA Modules:
  0.0 146.2 jit_solution(2041750242329890122)
XLA Ops:
  2.0 1.2 shard_map.121.own.refs_0_
  3.3 1.7 %collective-permute-start.1 = (bf16[1040,512]{1,0:T(8,128)(2,1)S(1)}, bf16[1040,512]{1,0:T(8,128)(2,1)S(1)}, u32[]{:S(2)}, u32[]{:S(2)}) collective-permute-start(bf16[1040,512]{1,0:T(8,128)(2,1)S(1)} %shard_map.121.own.refs_0_), channel_id=1, source_target_pairs={{0,1},{1,0},{2,3},{3,2},{4,5},{5,4},{6,7},{7,6},{8,9},{9,8},{10,11... | collective-permute-start | bytes 3194888 | tf_op jit(solution)/shard_map/factors_to_neighbours/ppermute | solution.py:363
  5.0 4.3 %shard_map.122 = (bf16[256,1024]{1,0:T(8,128)(2,1)S(1)}, bf16[128,1152]{1,0:T(8,128)(2,1)S(1)}, bf16[128,1152]{1,0:T(8,128)(2,1)S(1)}, bf16[1024,1024]{1,0:T(8,128)(2,1)S(1)}, bf16[5,128,1024]{2,1,0:T(8,128)(2,1)S(1)}) custom-call(s32[7]{0:T(128)S(1)} %stack.99.place, bf16[1024,1024]{1,0:T(8,128)(2,1)} %inv.3, bf16[1024,256]{1,0:T(8,128)(2,1)} %rhs.4, ...), custom_call_target="tpu_custom_call" | custom-call | flops 100000000 | bytes 1000000 | tf_op jit(solution)/shard_map/pallas_call | solution.py:42
  9.4 1.3 copy-done.9
  16.1 8.6 %collective-permute-done.recv = bf16[128,1152]{1,0:T(8,128)(2,1)S(1)} collective-permute-done((bf16[128,1152]{1,0:T(8,128)(2,1)S(1)}, bf16[128,1152]{1,0:T(8,128)(2,1)S(1)}, u32[]{:S(2)}, u32[]{:S(2)}) %collective-permute-start) | collective-permute-done | bytes 294944 | tf_op jit(solution)/shard_map/leaf_terms/ppermute | solution.py:354
  25.4 5.9 %collective-permute-start.4 = (bf16[1040,512]{1,0:T(8,128)(2,1)S(1)}, bf16[1040,512]{1,0:T(8,128)(2,1)}, u32[]{:S(2)}, u32[]{:S(2)}) collective-permute-start(bf16[1040,512]{1,0:T(8,128)(2,1)S(1)} %collective-permute-done.1.a.refs_1_), channel_id=1, source_target_pairs={{0,3},{2,1},{4,7},{6,5},{8,11},{10,9},{12,15},{14,13},{16,19},{18,... | collective-permute-start | bytes 3194888 | tf_op jit(solution)/shard_map/factors_across/ppermute | solution.py:363
  32.5 2.4 %shard_map.124 = (bf16[128,512]{1,0:T(8,128)(2,1)S(1)}, bf16[64,2048]{1,0:T(8,128)(2,1)S(1)}, bf16[64,2048]{1,0:T(8,128)(2,1)}) custom-call(s32[7]{0:T(128)S(1)} %copy-done.33, bf16[128,1152]{1,0:T(8,128)(2,1)S(1)} %get-tuple-element.53.keep, bf16[128,1152]{1,0:T(8,128)(2,1)S(1)} %copy-done.20, bf16[1040,512]{1,0:T(8,128)(2,1)S(1)} %get-tuple-element.59.factor, ...), custom_call_target="tpu_custom_call" | custom-call | flops 100000000 | bytes 1000000 | tf_op jit(solution)/shard_map/pallas_call | solution.py:42
  36.4 9.2 %collective-permute-done.4.refs_3_ = bf16[1040,512]{1,0:T(8,128)(2,1)} collective-permute-done((bf16[1040,512]{1,0:T(8,128)(2,1)S(1)}, bf16[1040,512]{1,0:T(8,128)(2,1)}, u32[]{:S(2)}, u32[]{:S(2)}) %collective-permute-start.4) | collective-permute-done | bytes 1064992 | tf_op jit(solution)/shard_map/factors_across/ppermute | solution.py:363
  45.6 2.9 %collective-permute-done.3.recv = bf16[64,2048]{1,0:T(8,128)(2,1)S(1)} collective-permute-done((bf16[64,2048]{1,0:T(8,128)(2,1)}, bf16[64,2048]{1,0:T(8,128)(2,1)S(1)}, u32[]{:S(2)}, u32[]{:S(2)}) %collective-permute-start.3) | collective-permute-done | bytes 262176 | tf_op jit(solution)/shard_map/panels_ring/ppermute | solution.py:354
  50.0 1.3 collective-permute-start.7
  54.1 1.3 collective-permute-start.5
  55.4 11.4 %collective-permute-done.5.recv = bf16[64,1536]{1,0:T(8,128)(2,1)S(1)} collective-permute-done((bf16[64,1536]{1,0:T(8,128)(2,1)S(1)}, bf16[64,1536]{1,0:T(8,128)(2,1)S(1)}, u32[]{:S(2)}, u32[]{:S(2)}) %collective-permute-start.5) | collective-permute-done | bytes 196640 | tf_op jit(solution)/shard_map/panels_z1/ppermute | solution.py:478
  66.8 1.3 collective-permute-start.10
  68.8 5.5 %collective-permute-start.6 = (bf16[64,1024]{1,0:T(8,128)(2,1)S(1)}, bf16[64,1024]{1,0:T(8,128)(2,1)S(1)}, u32[]{:S(2)}, u32[]{:S(2)}) collective-permute-start(bf16[64,1024]{1,0:T(8,128)(2,1)S(1)} %get-tuple-element.70.mine), channel_id=1, source_target_pairs={{0,8},{1,9},{2,10},{3,11},{8,0},{9,1},{10,2},{11,3},{16,24},{17,25... | collective-permute-start | bytes 393224 | tf_op jit(solution)/shard_map/panels_z2/ppermute | solution.py:491
  74.4 1.7 %shard_map.129 = (bf16[656,512]{1,0:T(8,128)(2,1)S(1)}, bf16[512,128]{1,0:T(8,128)(2,1)S(1)}) custom-call(s32[2]{0:T(128)S(1)} %add_convert_fusion.2.cases, bf16[656,512]{1,0:T(8,128)(2,1)} %collective-permute-done.7.refs_0_, bf16[656,512]{1,0:T(8,128)(2,1)S(1)} %collective-permute-done.8.refs_1_), custom_call_target="tpu_custom_call" | custom-call | flops 100000000 | bytes 1000000 | tf_op jit(solution)/shard_map/pallas_call | solution.py:42
  76.1 7.3 %collective-permute-done.6.recv = bf16[64,1024]{1,0:T(8,128)(2,1)S(1)} collective-permute-done((bf16[64,1024]{1,0:T(8,128)(2,1)S(1)}, bf16[64,1024]{1,0:T(8,128)(2,1)S(1)}, u32[]{:S(2)}, u32[]{:S(2)}) %collective-permute-start.6) | collective-permute-done | bytes 131104 | tf_op jit(solution)/shard_map/panels_z2/ppermute | solution.py:491
  84.1 5.5 %collective-permute-start.9 = (bf16[64,512]{1,0:T(8,128)(2,1)S(1)}, bf16[64,512]{1,0:T(8,128)(2,1)S(1)}, u32[]{:S(2)}, u32[]{:S(2)}) collective-permute-start(bf16[64,512]{1,0:T(8,128)(2,1)S(1)} %get-tuple-element.77.mine), channel_id=1, source_target_pairs={{0,24},{1,25},{2,26},{3,27},{8,16},{9,17},{10,18},{11,19},{16,8},{... | collective-permute-start | bytes 196616 | tf_op jit(solution)/shard_map/panels_z3/ppermute | solution.py:500
  89.7 1.2 shard_map.131
  90.9 1.7 %collective-permute-done.9.recv = bf16[64,512]{1,0:T(8,128)(2,1)S(1)} collective-permute-done((bf16[64,512]{1,0:T(8,128)(2,1)S(1)}, bf16[64,512]{1,0:T(8,128)(2,1)S(1)}, u32[]{:S(2)}, u32[]{:S(2)}) %collective-permute-start.9) | collective-permute-done | bytes 65568 | tf_op jit(solution)/shard_map/panels_z3/ppermute | solution.py:500
  92.6 1.3 shard_map.132.mine
  93.9 1.4 collective-permute-start.12
  95.3 4.2 %collective-permute-done.12.recv = bf16[64,1536]{1,0:T(8,128)(2,1)S(1)} collective-permute-done((bf16[64,1536]{1,0:T(8,128)(2,1)S(1)}, bf16[64,1536]{1,0:T(8,128)(2,1)S(1)}, u32[]{:S(2)}, u32[]{:S(2)}) %collective-permute-start.12) | collective-permute-done | bytes 196640 | tf_op jit(solution)/shard_map/down_z1/ppermute | solution.py:530
  100.6 3.8 %collective-permute-start.13 = (bf16[64,2048]{1,0:T(8,128)(2,1)S(1)}, bf16[64,2048]{1,0:T(8,128)(2,1)S(1)}, u32[]{:S(2)}, u32[]{:S(2)}) collective-permute-start(bf16[64,2048]{1,0:T(8,128)(2,1)S(1)} %shard_map.133.mine), channel_id=1, source_target_pairs={{0,3},{1,2},{2,1},{3,0},{4,7},{5,6},{6,5},{7,4},{8,11},{9,10},{10,... | collective-permute-start | bytes 786440 | tf_op jit(solution)/shard_map/down_ring/ppermute | solution.py:354
  104.4 5.6 %collective-permute-done.13.recv = bf16[64,2048]{1,0:T(8,128)(2,1)S(1)} collective-permute-done((bf16[64,2048]{1,0:T(8,128)(2,1)S(1)}, bf16[64,2048]{1,0:T(8,128)(2,1)S(1)}, u32[]{:S(2)}, u32[]{:S(2)}) %collective-permute-start.13) | collective-permute-done | bytes 262176 | tf_op jit(solution)/shard_map/down_ring/ppermute | solution.py:354
  110.0 2.2 %shard_map.134 = (bf16[128,640]{1,0:T(8,128)(2,1)S(1)}, bf16[128,640]{1,0:T(8,128)(2,1)}, bf16[128,512]{1,0:T(8,128)(2,1)S(1)}, bf16[128,512]{1,0:T(8,128)(2,1)S(1)}) custom-call(s32[7]{0:T(128)S(1)} %copy-done.34, bf16[64,2048]{1,0:T(8,128)(2,1)S(1)} %shard_map.133.mine, bf16[64,2048]{1,0:T(8,128)(2,1)S(1)} %collective-permute-done.13.recv, ...), custom_call_target="tpu_custom_call" | custom-call | flops 100000000 | bytes 1000000 | tf_op jit(solution)/shard_map/pallas_call | solution.py:42
  116.2 3.6 %collective-permute-done.14.recv = bf16[128,640]{1,0:T(8,128)(2,1)} collective-permute-done((bf16[128,640]{1,0:T(8,128)(2,1)}, bf16[128,640]{1,0:T(8,128)(2,1)}, u32[]{:S(2)}, u32[]{:S(2)}) %collective-permute-start.14) | collective-permute-done | bytes 163872 | tf_op jit(solution)/shard_map/rows_back/ppermute | solution.py:354
  120.8 3.1 %shard_map.136 = (bf16[1024,256]{1,0:T(8,128)(2,1)}, bf16[512,256]{1,0:T(8,128)(2,1)S(1)}) custom-call(s32[7]{0:T(128)S(1)} %copy-done.34, bf16[128,640]{1,0:T(8,128)(2,1)S(1)} %copy-done.27, bf16[128,640]{1,0:T(8,128)(2,1)} %collective-permute-done.14.recv, bf16[1024,1024]{1,0:T(8,128)(2,1)S(1)} %copy-done.10, bf16[5,128,1024]{2,1,0:T(8,128)(2,1)S(1)} %copy-done.14, ...), custom_call_target="tpu_custom_call" | custom-call | flops 100000000 | bytes 1000000 | tf_op jit(solution)/shard_map/pallas_call | solution.py:42
  124.6 6.9 %all-to-all-start = ((bf16[32,16,256]{2,1,0:T(8,128)(2,1)}), bf16[32,16,256]{2,1,0:T(8,128)(2,1)S(1)}, u32[]{:S(2)}, u32[]{:S(2)}) async-start(bf16[32,16,256]{2,1,0:T(8,128)(2,1)} %bitcast.28), calls=%async_computation | async-start | bytes 524288 | tf_op jit(solution)/shard_map/all_to_all | solution.py:561
  131.5 1.9 %collective-permute-start.15 = (bf16[128,512]{1,0:T(8,128)(2,1)}, bf16[128,512]{1,0:T(8,128)(2,1)S(1)}, u32[]{:S(2)}, u32[]{:S(2)}) collective-permute-start(bf16[128,512]{1,0:T(8,128)(2,1)} %copy-done.36), channel_id=1, source_target_pairs={{0,1},{1,0},{2,3},{3,2},{4,5},{5,4},{6,7},{7,6},{8,9},{9,8},{10,11... | collective-permute-start | bytes 393224 | tf_op jit(solution)/shard_map/sep_back/ppermute | solution.py:354
  133.4 3.7 %collective-permute-done.15.recv = bf16[128,512]{1,0:T(8,128)(2,1)S(1)} collective-permute-done((bf16[128,512]{1,0:T(8,128)(2,1)}, bf16[128,512]{1,0:T(8,128)(2,1)S(1)}, u32[]{:S(2)}, u32[]{:S(2)}) %collective-permute-start.15) | collective-permute-done | bytes 131104 | tf_op jit(solution)/shard_map/sep_back/ppermute | solution.py:354
  137.1 5.8 %all-to-all-done = bf16[32,16,256]{2,1,0:T(8,128)(2,1)S(1)} async-done(((bf16[32,16,256]{2,1,0:T(8,128)(2,1)}), bf16[32,16,256]{2,1,0:T(8,128)(2,1)S(1)}, u32[]{:S(2)}, u32[]{:S(2)}) %all-to-all-start) | async-done | bytes 262176 | tf_op jit(solution)/shard_map/all_to_all | solution.py:561
  144.8 1.4 shard_map.137
  (121 shorter events, 24.6 us)
Async XLA Ops:
  0.6 14.5 %copy-start = (f32[6,2048]{1,0:T(8,128)S(1)}, f32[6,2048]{1,0:T(8,128)}, u32[]{:S(2)}) copy-start(f32[6,2048]{1,0:T(8,128)} %param.19) | copy-start | bytes 147460
  3.3 22.1 %collective-permute-start.1 = (bf16[1040,512]{1,0:T(8,128)(2,1)S(1)}, bf16[1040,512]{1,0:T(8,128)(2,1)S(1)}, u32[]{:S(2)}, u32[]{:S(2)}) collective-permute-start(bf16[1040,512]{1,0:T(8,128)(2,1)S(1)} %shard_map.121.own.refs_0_), channel_id=1, source_target_pairs={{0,1},{1,0},{2,3},{3,2},{4,5},{5,4},{6,7},{7,6},{8,9},{9,8},{10,11... | collective-permute-start | bytes 3194888 | tf_op jit(solution)/shard_map/factors_to_neighbours/ppermute | solution.py:363
  5.0 4.3 %copy-start.32 = (s32[7]{0:T(128)}, s32[7]{0:T(128)S(1)}, u32[]{:S(2)}) copy-start(s32[7]{0:T(128)S(1)} %stack.99.place) | copy-start | bytes 88
  5.0 8.0 %copy-start.37 = (s32[6,2048]{1,0:T(8,128)S(1)}, s32[6,2048]{1,0:T(8,128)}, u32[]{:S(2)}) copy-start(s32[6,2048]{1,0:T(8,128)} %param.18) | copy-start | bytes 147460
  12.6 12.1 %collective-permute-start = (bf16[128,1152]{1,0:T(8,128)(2,1)S(1)}, bf16[128,1152]{1,0:T(8,128)(2,1)S(1)}, u32[]{:S(2)}, u32[]{:S(2)}) collective-permute-start(bf16[128,1152]{1,0:T(8,128)(2,1)S(1)} %get-tuple-element.54), channel_id=1, source_target_pairs={{0,1},{1,0},{2,3},{3,2},{4,5},{5,4},{6,7},{7,6},{8,9},{9,8},{10,11... | collective-permute-start | bytes 884744 | tf_op jit(solution)/shard_map/leaf_terms/ppermute | solution.py:354
  25.4 6.0 %collective-permute-start.2 = (bf16[1040,512]{1,0:T(8,128)(2,1)S(1)}, bf16[1040,512]{1,0:T(8,128)(2,1)S(1)}, u32[]{:S(2)}, u32[]{:S(2)}) collective-permute-start(bf16[1040,512]{1,0:T(8,128)(2,1)S(1)} %collective-permute-done.1.a.refs_1_), channel_id=1, source_target_pairs={{0,32},{32,0},{64,96},{96,64},{128,160},{160,128},{192,224},{224,1... | collective-permute-start | bytes 3194888 | tf_op jit(solution)/shard_map/near_to_core/ppermute | solution.py:351
  25.4 20.2 %collective-permute-start.4 = (bf16[1040,512]{1,0:T(8,128)(2,1)S(1)}, bf16[1040,512]{1,0:T(8,128)(2,1)}, u32[]{:S(2)}, u32[]{:S(2)}) collective-permute-start(bf16[1040,512]{1,0:T(8,128)(2,1)S(1)} %collective-permute-done.1.a.refs_1_), channel_id=1, source_target_pairs={{0,3},{2,1},{4,7},{6,5},{8,11},{10,9},{12,15},{14,13},{16,19},{18,... | collective-permute-start | bytes 3194888 | tf_op jit(solution)/shard_map/factors_across/ppermute | solution.py:363
  36.3 12.2 %collective-permute-start.3 = (bf16[64,2048]{1,0:T(8,128)(2,1)}, bf16[64,2048]{1,0:T(8,128)(2,1)S(1)}, u32[]{:S(2)}, u32[]{:S(2)}) collective-permute-start(bf16[64,2048]{1,0:T(8,128)(2,1)} %get-tuple-element.62), channel_id=1, source_target_pairs={{0,3},{1,2},{2,1},{3,0},{4,7},{5,6},{6,5},{7,4},{8,11},{9,10},{10,... | collective-permute-start | bytes 786440 | tf_op jit(solution)/shard_map/panels_ring/ppermute | solution.py:354
  49.9 18.1 %copy-start.3 = (bf16[784,512]{1,0:T(8,128)(2,1)}, bf16[784,512]{1,0:T(8,128)(2,1)S(1)}, u32[]{:S(2)}) copy-start(bf16[784,512]{1,0:T(8,128)(2,1)S(1)} %get-tuple-element.68.factor.f3) | copy-start | bytes 2408452
  50.0 16.8 %collective-permute-start.7 = (bf16[656,512]{1,0:T(8,128)(2,1)S(1)}, bf16[656,512]{1,0:T(8,128)(2,1)}, u32[]{:S(2)}, u32[]{:S(2)}) collective-permute-start(bf16[656,512]{1,0:T(8,128)(2,1)S(1)} %slice.3), channel_id=1, source_target_pairs={{4,0},{5,1},{6,2},{7,3},{12,8},{13,9},{14,10},{15,11},{20,16},{21,... | collective-permute-start | bytes 2015240 | tf_op jit(solution)/shard_map/factors_up/ppermute | solution.py:363
  52.2 14.5 %copy-start.11 = (bf16[512,384]{1,0:T(8,128)(2,1)}, bf16[512,384]{1,0:T(8,128)(2,1)S(1)}, u32[]{:S(2)}) copy-start(bf16[512,384]{1,0:T(8,128)(2,1)S(1)} %get-tuple-element.65.hots.h2) | copy-start | bytes 1179652
  54.1 12.7 %collective-permute-start.5 = (bf16[64,1536]{1,0:T(8,128)(2,1)S(1)}, bf16[64,1536]{1,0:T(8,128)(2,1)S(1)}, u32[]{:S(2)}, u32[]{:S(2)}) collective-permute-start(bf16[64,1536]{1,0:T(8,128)(2,1)S(1)} %get-tuple-element.67.mine), channel_id=1, source_target_pairs={{4,0},{5,1},{6,2},{7,3},{12,8},{13,9},{14,10},{15,11},{20,16},{21,... | collective-permute-start | bytes 589832 | tf_op jit(solution)/shard_map/panels_z1/ppermute | solution.py:478
  66.8 7.6 %collective-permute-start.8 = (bf16[656,512]{1,0:T(8,128)(2,1)}, bf16[656,512]{1,0:T(8,128)(2,1)S(1)}, u32[]{:S(2)}, u32[]{:S(2)}) collective-permute-start(bf16[656,512]{1,0:T(8,128)(2,1)} %collective-permute-done.7.refs_0_), channel_id=1, source_target_pairs={{0,32},{32,0},{64,96},{96,64},{128,160},{160,128},{192,224},{224,1... | collective-permute-start | bytes 2015240 | tf_op jit(solution)/shard_map/up_to_core/ppermute | solution.py:351
  66.8 17.2 %collective-permute-start.10 = (bf16[656,512]{1,0:T(8,128)(2,1)}, bf16[656,512]{1,0:T(8,128)(2,1)S(1)}, u32[]{:S(2)}, u32[]{:S(2)}) collective-permute-start(bf16[656,512]{1,0:T(8,128)(2,1)} %collective-permute-done.7.refs_0_), channel_id=1, source_target_pairs={{8,0},{9,1},{10,2},{11,3},{48,56},{49,57},{50,58},{51,59},{72,64},... | collective-permute-start | bytes 2015240 | tf_op jit(solution)/shard_map/factor_top/ppermute | solution.py:363
  68.8 14.6 %collective-permute-start.6 = (bf16[64,1024]{1,0:T(8,128)(2,1)S(1)}, bf16[64,1024]{1,0:T(8,128)(2,1)S(1)}, u32[]{:S(2)}, u32[]{:S(2)}) collective-permute-start(bf16[64,1024]{1,0:T(8,128)(2,1)S(1)} %get-tuple-element.70.mine), channel_id=1, source_target_pairs={{0,8},{1,9},{2,10},{3,11},{8,0},{9,1},{10,2},{11,3},{16,24},{17,25... | collective-permute-start | bytes 393224 | tf_op jit(solution)/shard_map/panels_z2/ppermute | solution.py:491
  83.9 5.7 %collective-permute-start.11 = (bf16[656,512]{1,0:T(8,128)(2,1)S(1)}, bf16[656,512]{1,0:T(8,128)(2,1)S(1)}, u32[]{:S(2)}, u32[]{:S(2)}) collective-permute-start(bf16[656,512]{1,0:T(8,128)(2,1)S(1)} %collective-permute-done.10.refs_2_), channel_id=1, source_target_pairs={{0,32},{32,0},{64,96},{96,64},{128,160},{160,128},{192,224},{224,1... | collective-permute-start | bytes 2015240 | tf_op jit(solution)/shard_map/last_to_core/ppermute | solution.py:351
  84.1 8.5 %collective-permute-start.9 = (bf16[64,512]{1,0:T(8,128)(2,1)S(1)}, bf16[64,512]{1,0:T(8,128)(2,1)S(1)}, u32[]{:S(2)}, u32[]{:S(2)}) collective-permute-start(bf16[64,512]{1,0:T(8,128)(2,1)S(1)} %get-tuple-element.77.mine), channel_id=1, source_target_pairs={{0,24},{1,25},{2,26},{3,27},{8,16},{9,17},{10,18},{11,19},{16,8},{... | collective-permute-start | bytes 196616 | tf_op jit(solution)/shard_map/panels_z3/ppermute | solution.py:500
  92.5 7.0 %copy-start.8 = (bf16[912,512]{1,0:T(8,128)(2,1)S(1)}, bf16[912,512]{1,0:T(8,128)(2,1)}, u32[]{:S(2)}) copy-start(bf16[912,512]{1,0:T(8,128)(2,1)} %copy-done.7) | copy-start | bytes 2801668
  92.5 7.0 %copy-start.12 = (bf16[512,384]{1,0:T(8,128)(2,1)S(1)}, bf16[512,384]{1,0:T(8,128)(2,1)}, u32[]{:S(2)}) copy-start(bf16[512,384]{1,0:T(8,128)(2,1)} %copy-done.11) | copy-start | bytes 1179652
  92.5 7.0 %copy-start.34 = (s32[7]{0:T(128)S(1)}, s32[7]{0:T(128)}, u32[]{:S(2)}) copy-start(s32[7]{0:T(128)} %copy-done.32) | copy-start | bytes 88
  92.5 17.4 %copy-start.6 = (bf16[1040,512]{1,0:T(8,128)(2,1)S(1)}, bf16[1040,512]{1,0:T(8,128)(2,1)}, u32[]{:S(2)}) copy-start(bf16[1040,512]{1,0:T(8,128)(2,1)} %copy-done.5) | copy-start | bytes 3194884
  93.8 16.1 %copy-start.2 = (bf16[512,1792]{1,0:T(8,128)(2,1)S(1)}, bf16[512,1792]{1,0:T(8,128)(2,1)}, u32[]{:S(2)}) copy-start(bf16[512,1792]{1,0:T(8,128)(2,1)} %copy-done.1) | copy-start | bytes 5505028
  93.8 16.1 %copy-start.31 = (bf16[128,512]{1,0:T(8,128)(2,1)S(1)}, bf16[128,512]{1,0:T(8,128)(2,1)}, u32[]{:S(2)}) copy-start(bf16[128,512]{1,0:T(8,128)(2,1)} %copy-done.30) | copy-start | bytes 393220
  93.9 5.7 %collective-permute-start.12 = (bf16[64,1536]{1,0:T(8,128)(2,1)S(1)}, bf16[64,1536]{1,0:T(8,128)(2,1)S(1)}, u32[]{:S(2)}, u32[]{:S(2)}) collective-permute-start(bf16[64,1536]{1,0:T(8,128)(2,1)S(1)} %shard_map.132.mine), channel_id=1, source_target_pairs={{0,4},{1,5},{2,6},{3,7},{8,12},{9,13},{10,14},{11,15},{16,20},{17,... | collective-permute-start | bytes 589832 | tf_op jit(solution)/shard_map/down_z1/ppermute | solution.py:530
  100.6 9.3 %collective-permute-start.13 = (bf16[64,2048]{1,0:T(8,128)(2,1)S(1)}, bf16[64,2048]{1,0:T(8,128)(2,1)S(1)}, u32[]{:S(2)}, u32[]{:S(2)}) collective-permute-start(bf16[64,2048]{1,0:T(8,128)(2,1)S(1)} %shard_map.133.mine), channel_id=1, source_target_pairs={{0,3},{1,2},{2,1},{3,0},{4,7},{5,6},{6,5},{7,4},{8,11},{9,10},{10,... | collective-permute-start | bytes 786440 | tf_op jit(solution)/shard_map/down_ring/ppermute | solution.py:354
  110.0 4.2 %copy-start.38 = (s32[512,1]{0,1:T(1,128)S(1)}, s32[512,1]{0,1:T(1,128)}, u32[]{:S(2)}) copy-start(s32[512,1]{0,1:T(1,128)} %reshape.142) | copy-start | bytes 6148
  110.0 9.8 %copy-start.10 = (bf16[1024,1024]{1,0:T(8,128)(2,1)S(1)}, bf16[1024,1024]{1,0:T(8,128)(2,1)}, u32[]{:S(2)}) copy-start(bf16[1024,1024]{1,0:T(8,128)(2,1)} %copy-done.9) | copy-start | bytes 6291460
  114.2 5.6 %copy-start.14 = (bf16[5,128,1024]{2,1,0:T(8,128)(2,1)S(1)}, bf16[5,128,1024]{2,1,0:T(8,128)(2,1)}, u32[]{:S(2)}) copy-start(bf16[5,128,1024]{2,1,0:T(8,128)(2,1)} %copy-done.13) | copy-start | bytes 3932164
  114.2 5.6 %collective-permute-start.14 = (bf16[128,640]{1,0:T(8,128)(2,1)}, bf16[128,640]{1,0:T(8,128)(2,1)}, u32[]{:S(2)}, u32[]{:S(2)}) collective-permute-start(bf16[128,640]{1,0:T(8,128)(2,1)} %get-tuple-element.86), channel_id=1, source_target_pairs={{0,1},{1,0},{2,3},{3,2},{4,5},{5,4},{6,7},{7,6},{8,9},{9,8},{10,11... | collective-permute-start | bytes 491528 | tf_op jit(solution)/shard_map/rows_back/ppermute | solution.py:354
  116.0 3.8 %copy-start.27 = (bf16[128,640]{1,0:T(8,128)(2,1)S(1)}, bf16[128,640]{1,0:T(8,128)(2,1)}, u32[]{:S(2)}) copy-start(bf16[128,640]{1,0:T(8,128)(2,1)} %copy-done.26) | copy-start | bytes 491524
  124.6 18.3 %all-to-all-start = ((bf16[32,16,256]{2,1,0:T(8,128)(2,1)}), bf16[32,16,256]{2,1,0:T(8,128)(2,1)S(1)}, u32[]{:S(2)}, u32[]{:S(2)}) async-start(bf16[32,16,256]{2,1,0:T(8,128)(2,1)} %bitcast.28), calls=%async_computation | async-start | bytes 524288 | tf_op jit(solution)/shard_map/all_to_all | solution.py:561
  131.5 5.6 %collective-permute-start.15 = (bf16[128,512]{1,0:T(8,128)(2,1)}, bf16[128,512]{1,0:T(8,128)(2,1)S(1)}, u32[]{:S(2)}, u32[]{:S(2)}) collective-permute-start(bf16[128,512]{1,0:T(8,128)(2,1)} %copy-done.36), channel_id=1, source_target_pairs={{0,1},{1,0},{2,3},{3,2},{4,5},{5,4},{6,7},{7,6},{8,9},{9,8},{10,11... | collective-permute-start | bytes 393224 | tf_op jit(solution)/shard_map/sep_back/ppermute | solution.py:354
  (24 other events, 26.3 us)

commit v3 on v2

v3 whole, which is shorter than its diff:
```python
import functools

import jax
import jax.numpy as jnp
from jax import lax
from jax.experimental import pallas as pl
from jax.experimental.pallas import tpu as pltpu
from jax.sharding import PartitionSpec as P

BF = jnp.bfloat16
F32 = jnp.float32
LEAF, PANEL, U, NC, LEVELS = 1024, 512, 128, 256, 5
RING, DEPTH = 4, 8
TERM = LEVELS * U
SLOTS = 16
VMEM_LIMIT = 16 * 1024 * 1024

TRI = 320
IDX = slice(TRI, TRI + 16)
CPL0 = TRI + 16


def packed_rows(slots):
    return CPL0 + slots * U


def factor_rows(slots):
    return PANEL + slots * U


def triangle_blocks():
    return [
        (slice(384, 512), slice(0, 512), slice(0, 128), slice(0, 512)),
        (slice(256, 384), slice(0, 384), slice(128, 256), slice(0, 384)),
        (slice(0, 128), slice(0, 128), slice(128, 256), slice(384, 512)),
        (slice(128, 192), slice(0, 256), slice(256, 320), slice(0, 256)),
        (slice(192, 256), slice(0, 256), slice(256, 320), slice(256, 512)),
    ]


def dot(left, right):
    return jnp.dot(left, right, preferred_element_type=F32)


def dot_t(left, right):
    return lax.dot_general(left, right, (((1,), (1,)), ((), ())), preferred_element_type=F32)


VMEM = pl.BlockSpec(memory_space=pltpu.VMEM)
SMEM = pl.BlockSpec(memory_space=pltpu.SMEM)
HBM = pl.BlockSpec(memory_space=pltpu.HBM)
ANY = pl.BlockSpec(memory_space=pl.ANY)


def call(body, outs, args, specs, scratch=(), out_specs=None, flops=10**8, moved=10**6):
    args = [
        in_vmem(arg) if spec is VMEM else in_hbm(arg) if spec is HBM else arg
        for arg, spec in zip(args, specs)
    ]
    return pl.pallas_call(
        body,
        out_shape=outs,
        in_specs=specs,
        out_specs=out_specs or [VMEM] * len(outs),
        scratch_shapes=list(scratch),
        compiler_params=pltpu.CompilerParams(vmem_limit_bytes=VMEM_LIMIT),
        cost_estimate=pl.CostEstimate(flops=flops, bytes_accessed=moved, transcendentals=0),
    )(*args)


def dma(n):
    return pltpu.SemaphoreType.DMA((n,))


def pinned(*dims, dtype=BF):
    return pltpu.VMEM(dims, dtype)


def plain(*dims, dtype=BF):
    return jax.ShapeDtypeStruct(dims, dtype)


def stored(*dims, dtype=BF):
    return pltpu.HBM(dims, dtype)


def in_vmem(value):
    return pltpu.with_memory_space_constraint(value, pltpu.VMEM)


def in_hbm(value):
    return pltpu.with_memory_space_constraint(value, pltpu.HBM)


def hot(rows):
    place = lax.broadcasted_iota(jnp.int32, (PANEL, rows.shape[1]), 0).astype(F32)
    return jnp.where(place == rows, 1.0, 0.0).astype(BF)


def leaf_rows(block):
    block = block.astype(F32)
    return [block[l : l + 1, 0:U] * 16.0 + block[l : l + 1, U : 2 * U] for l in range(LEVELS)]


def sep_rows(block):
    block = block.astype(F32)
    return [
        block[s : s + 1, 2 * U : 3 * U] * 16.0 + block[s : s + 1, 3 * U : 4 * U]
        for s in range(LEVELS - 1)
    ]


def push_values(factor, y, slots):
    return dot_t(y, factor[PANEL : PANEL + slots * U]).astype(BF)


def solve_back(factor, hots, y, above):
    back = y
    slots = len(above)
    if slots:
        taken = [dot(above[k], hots[k]).astype(BF) for k in range(slots)]
        taken = taken[0] if slots == 1 else jnp.concatenate(taken, axis=1)
        sub = dot(taken, factor[PANEL : PANEL + slots * U])
        back = (y.astype(F32) - sub).astype(BF)
    return dot(back, factor[0:PANEL]).astype(BF)


def pack_factor(place, inv, cpl, leaf_idx, sep_idx, out, up, codes_out, codes, leaf_v, sep_v, sems):
    loads = [
        pltpu.make_async_copy(leaf_idx.at[0], leaf_v, sems.at[0]),
        pltpu.make_async_copy(sep_idx.at[0], sep_v, sems.at[1]),
    ]
    copies = []
    for n, (dst, slots) in enumerate(((up, 3), (out, 4))):
        for i, (r, c, pr, pc) in enumerate(triangle_blocks()):
            copies.append(pltpu.make_async_copy(inv.at[r, c], dst.at[pr, pc], sems.at[2 + 6 * n + i]))
        copies.append(
            pltpu.make_async_copy(cpl.at[0 : slots * U], dst.at[CPL0 : packed_rows(slots)], sems.at[7 + 6 * n])
        )
    for copy in loads + copies:
        copy.start()
    codes[...] = jnp.zeros_like(codes)
    for ref, load, count, at in ((leaf_v, loads[0], LEVELS, 0), (sep_v, loads[1], LEVELS - 1, 2 * U)):
        load.wait()
        value = ref[...]
        codes[0:count, at : at + U] = (value >> 4).astype(F32)
        codes[0:count, at + U : at + 2 * U] = (value & 15).astype(F32)
    coded = codes[...].astype(BF)
    out[IDX] = coded
    up[IDX] = coded
    for q in range(4):
        codes_out[16 * q : 16 * (q + 1)] = coded[:, q * U : (q + 1) * U]
    for copy in copies:
        copy.wait()


def leaf_forward(
    place, inv, rhs, cpl, rsep, codes, yt_out, terms, rhs_out, one_out, inv_v, cpl_v, rhs_v, rsep_v, y, sems
):
    loads = [pltpu.make_async_copy(rhs, rhs_v, sems.at[0])]
    for i in range(4):
        rows = pl.ds(i * 256, 256)
        loads.append(pltpu.make_async_copy(inv.at[rows], inv_v.at[rows], sems.at[1 + i]))
    loads.append(pltpu.make_async_copy(cpl.at[0], cpl_v, sems.at[5]))
    loads.append(pltpu.make_async_copy(rsep, rsep_v, sems.at[6]))
    for load in loads:
        load.start()
    loads[0].wait()
    for i in range(4):
        loads[1 + i].wait()
        span = (i + 1) * 256
        y[i * 256 : span] = dot(inv_v[i * 256 : span, 0:span], rhs_v[0:span])
    yt_out[...] = y[...].T.astype(BF)
    loads[5].wait()
    one_out[0:NC] = dot_t(yt_out[...], cpl_v[0]).astype(BF)
    one_out[NC:] = codes[...]
    for l in range(1, LEVELS):
        terms[:, (l - 1) * U : l * U] = dot_t(yt_out[...], cpl_v[l]).astype(BF)
    loads[6].wait()
    rhs_out[...] = rsep_v[...].astype(F32).T.astype(BF)


def which(place):
    return place[0], place[1], place[2]


def pick_two(core, y, z):
    return (
        y == 1,
        ((y == 0) & (core == 0)) | ((y == 2) & (core == 1)),
        ((y == 0) & (core == 1)) | ((y == 2) & (core == 0)),
        y == 3,
    )


def pick_top(core, y, z):
    return (
        y == 3,
        ((y == 2) & (core == 0)) | ((y == 0) & (core == 1)),
        ((y == 2) & (core == 1)) | ((y == 0) & (core == 0)),
        y == 1,
    )


def pick_four(core, y, z):
    after_me = (z == 0) | (z == 4)
    first = core == 0
    return (after_me & first) | (~after_me & ~first), (after_me & ~first) | (~after_me & first)


def pick_five(core, y, z):
    inner = (z == 2) | (z == 4)
    first = core == 0
    low = (z == 2) | (z == 0)
    same = (low & first) | (~low & ~first)
    return inner & same, inner & ~same, ~inner & same, ~inner & ~same


def pick_one(core, y, z):
    even = (y == 0) | (y == 2)
    return even, ~even


def stage(slots, pick, split, count, place, *refs):
    if split:
        sources = [(refs[2 * i], refs[2 * i + 1], 0) for i in range(count)]
    else:
        sources = [(refs[i], refs[i], TRI) for i in range(count)]
    factor, hots, idx, sems = refs[(2 if split else 1) * count :]
    cases = pick(*which(place))

    def copies_of(triangle, rest, at):
        copies = [
            pltpu.make_async_copy(triangle.at[pr, pc], factor.at[r, c], sems.at[i])
            for i, (r, c, pr, pc) in enumerate(triangle_blocks())
        ]
        if slots:
            coupling = rest.at[at + 16 : at + 16 + slots * U]
            copies.append(pltpu.make_async_copy(coupling, factor.at[PANEL:], sems.at[5]))
            copies.append(pltpu.make_async_copy(rest.at[at : at + 16], idx, sems.at[6]))
        return copies

    for case, source in zip(cases, sources):

        @pl.when(case)
        def _(source=source):
            for copy in copies_of(*source):
                copy.start()

    for rows, cols in (
        (slice(0, 128), slice(128, 512)),
        (slice(128, 256), slice(256, 512)),
        (slice(256, 384), slice(384, 512)),
    ):
        factor[rows, cols] = jnp.zeros((rows.stop - rows.start, cols.stop - cols.start), BF)
    copies = copies_of(*sources[0])
    if slots:
        copies[-1].wait()
        taken = sep_rows(idx[...])
        for k in range(slots):
            hots[:, k * U : (k + 1) * U] = hot(taken[k])
        copies = copies[:-1]
    else:
        hots[...] = jnp.zeros_like(hots)
    for copy in copies:
        copy.wait()


def stage_and_pass(place, own, near, near_o, far, factor, hots, triangle, rest, idx, sems):
    sources = (own, near, near_o, far)

    def copies_of(source):
        return [
            pltpu.make_async_copy(source.at[0:TRI], triangle, sems.at[7]),
            pltpu.make_async_copy(source.at[TRI : packed_rows(1)], rest, sems.at[8]),
        ]

    for case, source in zip(pick_top(*which(place)), sources):

        @pl.when(case)
        def _(source=source):
            for copy in copies_of(source):
                copy.start()

    stage(2, pick_top, False, 4, place, *sources, factor, hots, idx, sems)
    for copy in copies_of(own):
        copy.wait()


ONE = 2 * U
ONE_HOTS = ONE + 4 * 3 * U


def stage_pair(place, one, other, hots):
    even = place[1] % 2 == 0
    mine, far = one[NC:], other[NC:]

    def rows(block, at, count):
        block = block.astype(F32)
        return [
            block[at + i : at + i + 1] * 16.0 + block[at + 16 + i : at + 17 + i] for i in range(count)
        ]

    left, right = jnp.where(even, mine, far), jnp.where(even, far, mine)
    a, b, up = rows(left, 0, LEVELS), rows(right, 0, LEVELS), rows(left, 32, LEVELS - 1)
    hots[:, 0:ONE] = hot(jnp.concatenate([a[0], b[0]], axis=1))
    for k in range(4):
        at = ONE + k * 3 * U
        hots[:, at : at + 3 * U] = hot(jnp.concatenate([a[k + 1], b[k + 1], up[k]], axis=1))


def half_of(place):
    y = place[1]
    return jnp.where((y == 1) | (y == 2), 1, 0)


def level_one(place, one, recv, terms, rhs, factor, hots, y_keep, y_send, keep, send, y_all):
    even = place[1] % 2 == 0
    total = dot_t(jnp.concatenate([one[0:NC], recv[0:NC]], axis=1), hots[:, 0:ONE])
    resid = (rhs[...].astype(F32) - total).astype(BF)
    y = dot_t(resid, factor[0:PANEL]).astype(BF)
    y_all[:, 0:PANEL] = y
    y_all[:, PANEL:] = jnp.where(even, push_values(factor, y, 4), rhs[...])
    side = half_of(place)
    mine = pl.ds(pl.multiple_of(side * 128, 128), 128)
    theirs = pl.ds(pl.multiple_of((1 - side) * 128, 128), 128)
    send[:, 0:PANEL] = terms[theirs]
    send[:, PANEL:] = y_all[theirs, PANEL:]
    keep[:, 0:PANEL] = terms[mine]
    keep[:, PANEL:] = y_all[mine, PANEL:]
    y_keep[...] = y_all[mine, 0:PANEL]
    y_send[...] = y_all[theirs, 0:PANEL]


def join_pair(place, keep, recv, hots, panel_keep, panel_send, panels):
    ring, even = place[1], place[1] % 2 == 0
    a, b = keep[...], recv[...]
    left, right = jnp.where(even, a, b), jnp.where(even, b, a)
    held = right[:, PANEL:].astype(F32)
    level = jnp.where(ring < 2, 2, place[3])
    for k in range(4):
        at = slice(k * U, (k + 1) * U)
        start = ONE + k * 3 * U
        parts = [left[:, at], right[:, at], left[:, PANEL + k * U : PANEL + (k + 1) * U]]
        total = dot_t(jnp.concatenate(parts, axis=1), hots[:, start : start + 3 * U])
        total = total - jnp.where(level == k + 2, held, 0.0)
        panels[:, k * PANEL : (k + 1) * PANEL] = total.astype(BF)
    side = ring // 2
    panel_keep[...] = panels[pl.ds(pl.multiple_of(side * 64, 64), 64)]
    panel_send[...] = panels[pl.ds(pl.multiple_of((1 - side) * 64, 64), 64)]


def level_up(level, mine, recv, factor, hots, y_out, panels):
    slots = LEVELS - level
    total = mine[...].astype(F32) + recv[...].astype(F32)
    y = dot_t((-total[:, 0:PANEL]).astype(BF), factor[0:PANEL]).astype(BF)
    y_out[...] = y
    values = push_values(factor, y, slots)
    for k in range(slots):
        at = slice((k + 1) * PANEL, (k + 2) * PANEL)
        term = dot_t(values[:, k * U : (k + 1) * U], hots[:, k * U : (k + 1) * U])
        panels[:, k * PANEL : (k + 1) * PANEL] = (total[:, at] + term).astype(BF)


def turn(mine, recv, f3, f4, f5, h3, h4, y3, y4, x_out):
    total = mine[...].astype(F32) + recv[...].astype(F32)
    y5 = dot_t((-total).astype(BF), f5[0:PANEL]).astype(BF)
    x5 = solve_back(f5, [], y5, [])
    x4 = solve_back(f4, [h4[...]], y4[...], [x5])
    x3 = solve_back(f3, [h3[:, 0:U], h3[:, U : 2 * U]], y3[...], [x4, x5])
    for k, x in enumerate((x3, x4, x5)):
        x_out[:, k * PANEL : (k + 1) * PANEL] = x


def level_two_back(place, mine, recv, f2, h2, y2, x_out):
    x = jnp.where(place[2] % 2 == 0, mine[...], recv[...])
    above = [x[:, k * PANEL : (k + 1) * PANEL] for k in range(3)]
    x_out[:, 0:PANEL] = solve_back(f2, [h2[:, k * U : (k + 1) * U] for k in range(3)], y2[...], above)
    x_out[:, PANEL:] = x


def level_one_back(
    place, mine, recv, y_mine, y_recv, factor, hots, rows_keep, rows_send, sep_keep, sep_send, x, sep_a, sep_b, sems
):
    side = place[1] // 2
    even = place[1] % 2 == 0
    x[pl.ds(pl.multiple_of(side * 64, 64), 64)] = mine[...]
    x[pl.ds(pl.multiple_of((1 - side) * 64, 64), 64)] = recv[...]
    above = [x[:, k * PANEL : (k + 1) * PANEL] for k in range(4)]
    ups = [hots[:, ONE + k * 3 * U + 2 * U : ONE + (k + 1) * 3 * U] for k in range(4)]
    x1 = solve_back(factor, ups, jnp.where(even, y_mine[...], y_recv[...]), above)
    level = jnp.where(place[1] < 2, 2, place[3])
    held = jnp.where(level == 0, jnp.zeros_like(x1), above[0])
    for k in (1, 2, 3):
        held = jnp.where(level == k + 2, above[k], held)
    sep_a[...] = jnp.where(even, x1, held)
    sep_b[...] = jnp.where(even, held, x1)
    stores = [
        pltpu.make_async_copy(sep_a, sep_keep, sems.at[0]),
        pltpu.make_async_copy(sep_b, sep_send, sems.at[1]),
    ]
    for store in stores:
        store.start()
    for l, value in enumerate([x1] + above):
        start = 0 if l == 0 else ONE + (l - 1) * 3 * U
        both = dot(value, hots[:, start : start + 2 * U]).astype(BF)
        left, right = both[:, 0:U], both[:, U : 2 * U]
        rows_keep[:, l * U : (l + 1) * U] = jnp.where(even, left, right)
        rows_send[:, l * U : (l + 1) * U] = jnp.where(even, right, left)
    for store in stores:
        store.wait()


def leaf_backward(place, keep, recv, inv, cpl, yt, chosen, x_leaf, picks_out, rows, sub, picks, sems):
    side = half_of(place)
    rows[pl.ds(pl.multiple_of(side * 128, 128), 128)] = keep[...]
    rows[pl.ds(pl.multiple_of((1 - side) * 128, 128), 128)] = recv[...]
    total = yt[...].astype(F32)
    for l in range(LEVELS):
        total = total - dot(rows[:, l * U : (l + 1) * U], cpl[l])
    sub[...] = total.astype(BF)
    for i in range(4):
        start = i * 256
        part = dot(sub[:, start:], inv[start:, start : start + 256])
        x_leaf[start : start + 256] = part.T.astype(BF)
    stores = []
    for i in range(2):
        part = slice(i * 256, (i + 1) * 256)
        picks[part] = dot(chosen[part], x_leaf[...]).astype(BF)
        stores.append(pltpu.make_async_copy(picks.at[part], picks_out.at[part], sems.at[i]))
        stores[-1].start()
    for store in stores:
        store.wait()


def sep_out(place, keep, recv, x_sep, keep_v, recv_v, xt, sems):
    loads = [
        pltpu.make_async_copy(keep, keep_v, sems.at[0]),
        pltpu.make_async_copy(recv, recv_v, sems.at[1]),
    ]
    for load in loads:
        load.start()
    for load in loads:
        load.wait()
    side = half_of(place)
    xt[pl.ds(pl.multiple_of(side * 128, 128), 128)] = keep_v[...].astype(F32)
    xt[pl.ds(pl.multiple_of((1 - side) * 128, 128), 128)] = recv_v[...].astype(F32)
    x_sep[...] = xt[...].T.astype(BF)


def stretch_sum(weight, got, out, weight_v, sems):
    load = pltpu.make_async_copy(weight, weight_v, sems.at[0])
    load.start()
    load.wait()
    out[...] = dot(weight_v[0], got[...]) + dot(weight_v[1], got[...])


def iota(rows, cols, axis):
    return lax.broadcasted_iota(jnp.int32, (rows, cols), axis)


def ones_where(mask):
    return jnp.where(mask, 1.0, 0.0)


def stay_plan(place, dofs, coef, chosen, weight_out, grid, turned, dof_t, coef_t, weight, sems):
    me = place[2] * RING + place[1]
    grid[...] = jnp.full((128, 128), -1, jnp.int32)
    for r in range(16):
        grid[8 * r : 8 * r + 6] = dofs[:, 128 * r : 128 * (r + 1)]
    dof = grid[...]
    match = ones_where((dof >> 10) == me)
    row, col = iota(128, 128, 0), iota(128, 128, 1)
    same = (row >> 3) == (col >> 3)
    earlier = ((row >> 6) == (col >> 6)) & (row < col)
    match_b = match.astype(BF)
    count = dot(ones_where(same).astype(BF), match_b).astype(BF)
    rank = dot(count, ones_where(earlier).astype(BF))
    rank = rank + dot(ones_where(same & (col < row)).astype(BF), match_b)
    high = ((dof >> 5) & 31).astype(F32) + 1.0
    low = (dof & 31).astype(F32)
    rank = jnp.where(match > 0.0, rank, -1.0)
    parts = []
    for value in (high, low):
        for s in range(SLOTS):
            parts.append(jnp.where(rank == float(s), value, 0.0).astype(BF))
    block = ones_where(iota(16, 128, 0) == (iota(16, 128, 1) >> 3)).astype(BF)
    flat = dot(block, jnp.concatenate(parts, axis=1)).astype(BF)
    width = SLOTS * 128
    lane, q = iota(width, 32, 0), iota(width, 32, 1)
    gather = ones_where(q == ((lane >> 6) & 1) * SLOTS + (lane >> 7)).astype(BF)
    table_high = dot(flat[:, 0:width], gather).astype(BF)
    table_low = dot(flat[:, width:], gather).astype(BF)
    spread = ones_where((iota(512, 16, 0) >> 5) == iota(512, 16, 1)).astype(BF)
    here = ones_where((iota(512, 32, 0) & 31) == iota(512, 32, 1))
    sel_high = jnp.sum(dot(spread, table_high) * here, axis=1, keepdims=True)
    sel_low = jnp.sum(dot(spread, table_low) * here, axis=1, keepdims=True)
    sel = (sel_high - 1.0) * 32.0 + sel_low
    for part in range(4):
        at = slice(part * 128, (part + 1) * 128)
        chosen[at] = ones_where(iota(128, LEAF, 1).astype(F32) == sel[at]).astype(BF)

    block_row = pl.multiple_of((me >> 1) * 8, 8)
    block_col = pl.multiple_of((me >> 1) * 128, 128)
    half = pl.ds(pl.multiple_of((me & 1) * 64, 64), 64)
    turned[...] = jnp.zeros_like(turned)
    turned[0:8] = grid[pl.ds(block_row, 8)].astype(F32)
    dof_t[...] = turned[...].T
    turned[0:6] = coef[:, pl.ds(block_col, 128)]
    coef_t[...] = turned[...].T
    my_dof, my_coef = dof_t[half], coef_t[half]
    lanes = iota(64, 32, 1)
    source = [my_dof[:, k : k + 1].astype(jnp.int32) >> 10 for k in range(6)]
    named = [ones_where(source[k] == lanes) for k in range(6)]
    every = named[0]
    for k in range(1, 6):
        every = every + named[k]
    lower = ones_where(iota(64, 64, 1) < iota(64, 64, 0)).astype(BF)
    running = dot(lower, every.astype(BF))
    total = jnp.zeros((64, 512), F32)
    slots = iota(64, 512, 1).astype(F32)
    for k in range(6):
        at = jnp.sum(named[k] * running, axis=1, keepdims=True)
        slot = source[k].astype(F32) * float(SLOTS) + at
        total = total + jnp.where(slots == slot, my_coef[:, k : k + 1], 0.0)
        running = running + named[k]
    first = total.astype(BF)
    weight[0] = first
    weight[1] = (total - first.astype(F32)).astype(BF)
    store = pltpu.make_async_copy(weight, weight_out, sems.at[0])
    store.start()
    store.wait()


def after(value, *others):
    return lax.optimization_barrier((value, *others))[0]


def on_device(
    rhs_leaf, rhs_sep, leaf_inv, leaf_cpl, leaf_idx, sep_inv, sep_cpl, sep_idx, stay_dofs, stay_coef
):
    rows_axis, cols_axis = "rows", "cols"
    columns, rows = lax.axis_size(cols_axis), lax.axis_size(rows_axis)
    me = lax.axis_index(rows_axis)
    core = lax.axis_index(cols_axis) % 2
    y, z = me % RING, me // RING
    top_level = jnp.where(z % 2 == 0, 3, jnp.where(z % 4 == 1, 4, jnp.where(z == 3, 5, 0)))
    place = jnp.stack([core, y, z, top_level]).astype(jnp.int32)

    def route(value, target):
        pairs = []
        for c in range(columns):
            for r in range(rows):
                to = target(c % 2, r % RING, r // RING)
                if to is not None:
                    pairs.append((c * rows + r, (c - c % 2 + to[0]) * rows + to[2] * RING + to[1]))
        return lax.ppermute(value, (cols_axis, rows_axis), pairs)

    def swap_core(value):
        return route(value, lambda c, y, z: (1 - c, y, z))

    def swap(value, flip):
        return route(value, lambda c, y, z: (c, y ^ flip, z))

    def to_odd(value):
        return route(value, lambda c, y, z: (c, y + 1, z) if y % 2 == 0 else None)

    own, own_up, codes = call(
        pack_factor,
        [pinned(packed_rows(4), PANEL), pinned(packed_rows(3), PANEL), pinned(4 * 16, U)],
        [place, sep_inv, sep_cpl.reshape(4 * U, PANEL), leaf_idx, sep_idx],
        [SMEM, HBM, HBM, HBM, HBM],
        [
            pltpu.VMEM((16, PANEL), F32),
            pltpu.VMEM((LEVELS, U), jnp.int32),
            pltpu.VMEM((LEVELS - 1, U), jnp.int32),
            dma(14),
        ],
    )
    with jax.named_scope("factors_to_neighbours"):
        near = route(own_up, lambda c, y, z: (c, y ^ (3 if c else 1), z) if y % 2 else None)
    yt, terms, rhs, one, inv_v, cpl_v = call(
        leaf_forward,
        [
            pinned(NC, LEAF),
            pinned(NC, PANEL),
            pinned(NC, PANEL),
            pinned(NC + 4 * 16, U),
            pinned(LEAF, LEAF),
            pinned(LEVELS, U, LEAF),
        ],
        [after(place, own), leaf_inv, rhs_leaf, leaf_cpl, rhs_sep, codes],
        [SMEM, HBM, HBM, HBM, HBM, VMEM],
        [pltpu.VMEM((LEAF, NC), BF), pltpu.VMEM((PANEL, NC), BF), pltpu.VMEM((LEAF, NC), F32), dma(7)],
    )
    with jax.named_scope("first_terms"):
        recv = swap(one, 1)

    def ready(slots, pick, sources, split=False):
        return call(
            functools.partial(stage, slots, pick, split, len(sources) // (2 if split else 1)),
            [pinned(factor_rows(slots), PANEL), pinned(PANEL, max(slots, 1) * U)],
            [place, *sources],
            [SMEM] + [ANY] * len(sources),
            [pltpu.VMEM((16, PANEL), BF), dma(7)],
        )

    def rise(level, panel, recv, factor, hots):
        slots = LEVELS - level
        return call(
            functools.partial(level_up, level),
            [pinned(64, PANEL), pinned(64, slots * PANEL)],
            [panel, recv, factor, hots],
            [VMEM] * 4,
        )

    f1, _ = ready(4, lambda core, y, z: (core >= 0,), [after(own, one)])
    (h1,) = call(
        stage_pair,
        [pinned(PANEL, ONE_HOTS)],
        [place, one, recv],
        [SMEM, VMEM, VMEM],
    )
    recv = after(recv, f1)
    y1, y1_send, keep, send = call(
        level_one,
        [pinned(128, PANEL), pinned(128, PANEL), pinned(128, 2 * PANEL), pinned(128, 2 * PANEL)],
        [place, one, recv, terms, rhs, f1, h1],
        [SMEM] + [VMEM] * 6,
        [pltpu.VMEM((NC, 2 * PANEL), BF)],
    )
    with jax.named_scope("terms_pair"):
        recv = swap(send, 1)
    chosen, weight = call(
        stay_plan,
        [pinned(32 * SLOTS, LEAF), stored(2, 64, 512)],
        [place, stay_dofs, after(stay_coef, send)],
        [SMEM, VMEM, VMEM],
        [
            pltpu.VMEM((128, 128), jnp.int32),
            pltpu.VMEM((128, 128), F32),
            pltpu.VMEM((128, 128), F32),
            pltpu.VMEM((128, 128), F32),
            pltpu.VMEM((2, 64, 512), BF),
            dma(1),
        ],
        [VMEM, HBM],
    )
    recv = after(recv, chosen)
    panel, send = call(
        join_pair,
        [pinned(64, 4 * PANEL), pinned(64, 4 * PANEL)],
        [place, keep, recv, h1],
        [SMEM] + [VMEM] * 3,
        [pltpu.VMEM((128, 4 * PANEL), BF)],
    )
    with jax.named_scope("panels_ring"):
        recv = swap(send, 3)
    near = after(near, keep)
    with jax.named_scope("near_to_core"):
        near_o = swap_core(near)
    with jax.named_scope("factors_across"):
        far = route(near, lambda c, y, z: (c, y ^ (1 if c else 3), z) if y % 2 == 0 else None)
    far = after(far, send)
    at = [own_up, near, near_o, far]
    f2, h2 = ready(3, pick_two, at)
    f3, h3, top, top_rest = call(
        stage_and_pass,
        [
            pinned(factor_rows(2), PANEL),
            pinned(PANEL, 2 * U),
            pinned(TRI, PANEL),
            pinned(16 + U, PANEL),
        ],
        [place, *at],
        [SMEM] + [ANY] * 4,
        [pltpu.VMEM((16, PANEL), BF), dma(9)],
    )

    def next_up(value):
        return route(value, lambda c, y, z: (c, y, (z + (1 if c else -1)) % DEPTH) if z % 2 else None)

    with jax.named_scope("factors_up"):
        up = next_up(top)
    with jax.named_scope("factors_up_rest"):
        rest = next_up(top_rest)
    recv = after(recv, f2, h2, f3, h3)
    y2, panel = rise(2, panel, recv, f2, h2)
    with jax.named_scope("panels_z1"):
        recv = route(panel, lambda c, y, z: (c, y, z - 1) if z % 2 else None)
    own_far, y1_far = after((own, y1_send), panel)
    with jax.named_scope("first_factor_to_odd"):
        own_far = to_odd(own_far)
    with jax.named_scope("first_solution_to_odd"):
        y1_far = to_odd(y1_far)
    y3, panel = rise(3, panel, recv, f3, h3)
    with jax.named_scope("panels_z2"):
        recv = route(panel, lambda c, y, z: (c, y, z ^ 2) if z % 2 == 0 else None)
    up, rest = after((up, rest), panel)
    with jax.named_scope("up_to_core"):
        up_o = swap_core(up)
    with jax.named_scope("rest_to_core"):
        rest_o = swap_core(rest)
    with jax.named_scope("factor_top"):
        last = route(
            up,
            lambda c, y, z: (c, y, 0) if (c, z) == (0, 2) else (c, y, 6) if (c, z) == (1, 4) else None,
        )
    f4, h4 = ready(1, pick_four, [up, rest, up_o, rest_o], True)
    recv = after(recv, f4, h4)
    y4, panel = rise(4, panel, recv, f4, h4)
    with jax.named_scope("panels_z3"):
        recv = route(panel, lambda c, y, z: (c, y, 6 - z) if z % 2 == 0 else None)
    last = after(last, panel)
    with jax.named_scope("last_to_core"):
        last_o = swap_core(last)
    f5, _ = ready(0, pick_five, [up, up_o, last, last_o])
    recv = after(recv, f5)
    (x,) = call(
        turn,
        [pinned(64, 3 * PANEL)],
        [panel, recv, f3, f4, f5, h3, h4, y3, y4],
        [VMEM] * 9,
    )
    with jax.named_scope("down_z1"):
        recv = route(x, lambda c, y, z: (c, y, z + 1) if z % 2 == 0 else None)
    (x,) = call(
        level_two_back,
        [pinned(64, 4 * PANEL)],
        [place, x, recv, f2, h2, y2],
        [SMEM] + [VMEM] * 5,
    )
    with jax.named_scope("down_ring"):
        recv = swap(x, 3)
    f1, _ = ready(4, pick_one, [own, after(own_far, x)])
    recv = after(recv, f1)
    rows_keep, rows_send, sep_keep, sep_send = call(
        level_one_back,
        [pinned(128, TERM), pinned(128, TERM), stored(128, PANEL), stored(128, PANEL)],
        [place, x, recv, y1, y1_far, f1, h1],
        [SMEM] + [VMEM] * 6,
        [
            pltpu.VMEM((128, 4 * PANEL), BF),
            pltpu.VMEM((128, PANEL), BF),
            pltpu.VMEM((128, PANEL), BF),
            dma(2),
        ],
        [VMEM, VMEM, HBM, HBM],
    )
    with jax.named_scope("rows_back"):
        recv = swap(rows_send, 1)
    with jax.named_scope("sep_back"):
        sep_recv = swap(sep_send, 1)
    x_leaf, picks = call(
        leaf_backward,
        [plain(LEAF, NC), stored(32 * SLOTS, NC)],
        [place, rows_keep, recv, inv_v, cpl_v, yt, chosen],
        [SMEM] + [VMEM] * 6,
        [
            pltpu.VMEM((NC, TERM), BF),
            pltpu.VMEM((NC, LEAF), BF),
            pltpu.VMEM((32 * SLOTS, NC), BF),
            dma(2),
        ],
        [VMEM, HBM],
    )
    got = lax.all_to_all(
        picks.reshape(32, SLOTS, NC), rows_axis, 0, 0, tiled=True
    ).reshape(32 * SLOTS, NC)
    (x_sep,) = call(
        sep_out,
        [plain(PANEL, NC)],
        [place, sep_keep, after(sep_recv, picks)],
        [SMEM, HBM, HBM],
        [pltpu.VMEM((128, PANEL), BF), pltpu.VMEM((128, PANEL), BF), pltpu.VMEM((NC, PANEL), F32), dma(2)],
    )
    (stretch,) = call(
        stretch_sum,
        [plain(64, NC, dtype=F32)],
        [weight, got],
        [HBM, VMEM],
        [pltpu.VMEM((2, 64, 512), BF), dma(1)],
    )
    return (x_leaf, x_sep, stretch)


def solution(mesh):
    return jax.shard_map(
        on_device,
        mesh=mesh,
        in_specs=(
            P("rows", "cols"),
            P("rows", "cols"),
            P("rows", None),
            P("rows", None, None, None),
            P("rows", None, None),
            P("rows", None),
            P("rows", None, None, None),
            P("rows", None, None),
            P(),
            P(),
        ),
        out_specs=(P("rows", "cols"), P("rows", "cols"), P("rows", "cols")),
        check_vma=False,
    )
```

time: 147 us -> 130 us (0.88)
  waiting for transfers between devices: 64 us -> 48.6 us
  local copies, waits for them, and re-layouts: 17.2 us -> 1.95 us
  Pallas kernels: 24.8 us -> 35.1 us
  starting transfers between devices: 37 us -> 42.2 us
  other arithmetic: 2.03 us -> 0.08 us
    ppermute x12 -> x0, waiting for transfers between devices: 48.9 us -> none  [the longest x5 24.4 us: swap(): return lax.ppermute(value, rows_axis, [(i, i ^ flip) for i in range(rows)])]
    ppermute x4 -> x21, waiting for transfers between devices: 9.17 us -> 45.5 us  [route(): return lax.ppermute(value, (cols_axis, rows_axis), pairs)]
    ppermute x4 -> x21, starting transfers between devices: 10.2 us -> 33.8 us  [route(): return lax.ppermute(value, (cols_axis, rows_axis), pairs)]
    ppermute x12 -> x0, starting transfers between devices: 19.9 us -> none  [the longest x5 6.11 us: swap(): return lax.ppermute(value, rows_axis, [(i, i ^ flip) for i in range(rows)])]
    unnamed x79 -> x9, local copies, waits for them, and re-layouts: 15.1 us -> 1.95 us
    pallas_call x17 -> x21, Pallas kernels: 24.8 us -> 35.1 us  [call(): pl.pallas_call(body, out_shape=outs, in_specs=specs, out_specs=out_specs...]
    all_to_all x1, waiting for transfers between devices: 5.84 us -> 3.06 us  [on_device(): lax.all_to_all(picks.reshape(32, SLOTS, NC), rows_axis, 0, 0, tiled=True)]
    reduce_sum x3 -> x0, other arithmetic: 1.61 us -> none  [the longest x1 0.83 us: stay_plan(): weight = jnp.sum(jnp.where(hit, coef[:, :, None], 0.0), axis=0)]
  transfers between devices with their start and end apart: 17 -> 22, of which waited for: 11 -> 12; matrix products, arithmetic and copies ran while one was open for 3% -> 0% of each run, Pallas kernels for 9% -> 20%
where the time goes in v3:
time: 130 us; the launch traced here: 129 us
  waiting for transfers between devices  48.6 us (37%)
  starting transfers between devices  42.2 us (32%)
  Pallas kernels  35.1 us (27%)
  local copies, waits for them, and re-layouts  1.95 us (2%)
    ppermute x21, waiting for transfers between devices, route(): return lax.ppermute(value, (cols_axis, rows_axis), pairs)  45.5 us
    pallas_call x21, Pallas kernels, call(): pl.pallas_call(body, out_shape=outs, in_specs=specs, out_specs=out_specs...  35.1 us
    ppermute x21, starting transfers between devices, route(): return lax.ppermute(value, (cols_axis, rows_axis), pairs)  33.8 us
    all_to_all x1, starting transfers between devices, on_device(): lax.all_to_all(picks.reshape(32, SLOTS, NC), rows_axis, 0, 0, tiled=True)  8.36 us
    all_to_all x1, waiting for transfers between devices, on_device(): lax.all_to_all(picks.reshape(32, SLOTS, NC), rows_axis, 0, 0, tiled=True)  3.06 us
  transfers between devices with their start and end apart: 22, of which 12 were waited for; matrix products, arithmetic and copies ran while one was open for 0% of the time, Pallas kernels for 20%

profile of v3, /device:TPU:2, one launch (start us, length us, event | category | flops | bytes accessed | tf_op | source)
XLA Modules:
  0.0 129.1 jit_solution(7967163615704491180)
XLA Ops:
  2.0 2.1 %shard_map.121 = (bf16[848,512]{1,0:T(8,128)(2,1)S(1)}, bf16[720,512]{1,0:T(8,128)(2,1)S(1)}, bf16[64,128]{1,0:T(8,128)(2,1)S(1)}) custom-call(s32[4]{0:T(128)S(1)} %pad_add_fusion.place, bf16[512,512]{1,0:T(8,128)(2,1)} %inv.2, bf16[512,512]{1,0:T(8,128)(2,1)} %bitcast.8, s32[1,5,128]{2,1,0:T(8,128)} %copy.13.leaf_idx, s32[1,4,128]{2,1,0:T(4,128)} %sep_idx.1), custom_call_target="tpu_custom_call" | custom-call | flops 100000000 | bytes 1000000 | tf_op jit(solution)/shard_map/pallas_call | solution.py:60
  4.2 1.3 %collective-permute-start.3 = (bf16[720,512]{1,0:T(8,128)(2,1)S(1)}, bf16[720,512]{1,0:T(8,128)(2,1)S(1)}, u32[]{:S(2)}, u32[]{:S(2)}) collective-permute-start(bf16[720,512]{1,0:T(8,128)(2,1)S(1)} %get-tuple-element.77.refs_0_.own), channel_id=1, source_target_pairs={{1,0},{3,2},{5,4},{7,6},{9,8},{11,10},{13,12},{15,14},{17,16},{19,... | collective-permute-start | bytes 2211848 | tf_op jit(solution)/shard_map/factors_to_neighbours/ppermute | solution.py:557
  5.5 4.3 %shard_map.122 = (bf16[256,1024]{1,0:T(8,128)(2,1)S(1)}, bf16[256,512]{1,0:T(8,128)(2,1)S(1)}, bf16[256,512]{1,0:T(8,128)(2,1)S(1)}, bf16[320,128]{1,0:T(8,128)(...) custom-call(s32[4]{0:T(128)S(1)} %pad_add_fusion.place, bf16[1024,1024]{1,0:T(8,128)(2,1)} %inv.3, ...), custom_call_target="tpu_custom_call" | custom-call | flops 100000000 | bytes 1000000 | tf_op jit(solution)/shard_map/pallas_call | solution.py:60
  9.8 2.8 %collective-permute-start = (bf16[320,128]{1,0:T(8,128)(2,1)S(1)}, bf16[320,128]{1,0:T(8,128)(2,1)S(1)}, u32[]{:S(2)}, u32[]{:S(2)}) collective-permute-start(bf16[320,128]{1,0:T(8,128)(2,1)S(1)} %get-tuple-element.64.one), channel_id=1, source_target_pairs={{0,1},{1,0},{2,3},{3,2},{4,5},{5,4},{6,7},{7,6},{8,9},{9,8},{10,11... | collective-permute-start | bytes 245768 | tf_op jit(solution)/shard_map/first_terms/ppermute | solution.py:557
  12.5 1.8 %shard_map.123 = (bf16[1024,512]{1,0:T(8,128)(2,1)S(1)}, bf16[512,512]{1,0:T(8,128)(2,1)}) custom-call(s32[4]{0:T(128)S(1)} %pad_add_fusion.place, bf16[848,512]{1,0:T(8,128)(2,1)S(1)} %get-tuple-element.102.refs_0_), custom_call_target="tpu_custom_call" | custom-call | flops 100000000 | bytes 1000000 | tf_op jit(solution)/shard_map/pallas_call | solution.py:60
  14.3 4.9 %collective-permute-done.other.recv = bf16[320,128]{1,0:T(8,128)(2,1)S(1)} collective-permute-done((bf16[320,128]{1,0:T(8,128)(2,1)S(1)}, bf16[320,128]{1,0:T(8,128)(2,1)S(1)}, u32[]{:S(2)}, u32[]{:S(2)}) %collective-permute-start) | collective-permute-done | bytes 81952 | tf_op jit(solution)/shard_map/first_terms/ppermute | solution.py:557
  21.5 3.2 %collective-permute-start.5 = (bf16[720,512]{1,0:T(8,128)(2,1)S(1)}, bf16[720,512]{1,0:T(8,128)(2,1)S(1)}, u32[]{:S(2)}, u32[]{:S(2)}) collective-permute-start(bf16[720,512]{1,0:T(8,128)(2,1)S(1)} %collective-permute-done.3.refs_1_.near), channel_id=1, source_target_pairs={{0,3},{2,1},{4,7},{6,5},{8,11},{10,9},{12,15},{14,13},{16,19},{18,... | collective-permute-start | bytes 2211848 | tf_op jit(solution)/shard_map/factors_across/ppermute | solution.py:557
  24.9 2.5 %shard_map.126 = (bf16[512,1024]{1,0:T(8,128)(2,1)S(1)}, bf16[2,64,512]{2,1,0:T(8,128)(2,1)}) custom-call(s32[4]{0:T(128)S(1)} %pad_add_fusion.place, s32[6,2048]{1,0:T(8,128)S(1)} %copy-done, f32[6,2048]{1,0:T(8,128)S(1)} %copy-done.1), custom_call_target="tpu_custom_call" | custom-call | flops 100000000 | bytes 1000000 | tf_op jit(solution)/shard_map/pallas_call | solution.py:60
  27.5 6.1 %collective-permute-done.1.recv = bf16[128,1024]{1,0:T(8,128)(2,1)S(1)} collective-permute-done((bf16[128,1024]{1,0:T(8,128)(2,1)S(1)}, bf16[128,1024]{1,0:T(8,128)(2,1)S(1)}, u32[]{:S(2)}, u32[]{:S(2)}) %collective-permute-start.1) | collective-permute-done | bytes 262176 | tf_op jit(solution)/shard_map/terms_pair/ppermute | solution.py:557
  35.3 1.3 %shard_map.129 = (bf16[768,512]{1,0:T(8,128)(2,1)S(1)}, bf16[512,256]{1,0:T(8,128)(2,1)S(1)}, bf16[320,512]{1,0:T(8,128)(2,1)S(1)}, bf16[144,512]{1,0:T(8,128)(2,1)S(1)}) custom-call(s32[4]{0:T(128)S(1)} %pad_add_fusion.place, bf16[720,512]{1,0:T(8,128)(2,1)S(1)} %get-tuple-element.77.refs_0_.own, bf16[720,512]{1,0:T(8,128)(2,1)S(1)} %collective-permute-done.3.refs_1_.near, ...), custom_call_target="tpu_custom_call" | custom-call | flops 100000000 | bytes 1000000 | tf_op jit(solution)/shard_map/pallas_call | solution.py:60
  39.1 5.5 %collective-permute-done.2.recv = bf16[64,2048]{1,0:T(8,128)(2,1)S(1)} collective-permute-done((bf16[64,2048]{1,0:T(8,128)(2,1)S(1)}, bf16[64,2048]{1,0:T(8,128)(2,1)S(1)}, u32[]{:S(2)}, u32[]{:S(2)}) %collective-permute-start.2) | collective-permute-done | bytes 262176 | tf_op jit(solution)/shard_map/panels_ring/ppermute | solution.py:557
  47.9 6.6 %collective-permute-done.6.recv = bf16[64,1536]{1,0:T(8,128)(2,1)S(1)} collective-permute-done((bf16[64,1536]{1,0:T(8,128)(2,1)S(1)}, bf16[64,1536]{1,0:T(8,128)(2,1)S(1)}, u32[]{:S(2)}, u32[]{:S(2)}) %collective-permute-start.6) | collective-permute-done | bytes 196640 | tf_op jit(solution)/shard_map/panels_z1/ppermute | solution.py:557
  56.1 1.7 %collective-permute-start.10 = (bf16[320,512]{1,0:T(8,128)(2,1)S(1)}, bf16[320,512]{1,0:T(8,128)(2,1)S(1)}, u32[]{:S(2)}, u32[]{:S(2)}) collective-permute-start(bf16[320,512]{1,0:T(8,128)(2,1)S(1)} %collective-permute-done.8.refs_0_), channel_id=1, source_target_pairs={{0,32},{1,33},{2,34},{3,35},{4,36},{5,37},{6,38},{7,39},{8,40},{9,... | collective-permute-start | bytes 983048 | tf_op jit(solution)/shard_map/up_to_core/ppermute | solution.py:557
  59.2 5.5 %collective-permute-start.7 = (bf16[64,1024]{1,0:T(8,128)(2,1)S(1)}, bf16[64,1024]{1,0:T(8,128)(2,1)S(1)}, u32[]{:S(2)}, u32[]{:S(2)}) collective-permute-start(bf16[64,1024]{1,0:T(8,128)(2,1)S(1)} %get-tuple-element.86.mine), channel_id=1, source_target_pairs={{0,8},{1,9},{2,10},{3,11},{8,0},{9,1},{10,2},{11,3},{16,24},{17,25... | collective-permute-start | bytes 393224 | tf_op jit(solution)/shard_map/panels_z2/ppermute | solution.py:557
  64.7 1.7 %collective-permute-start.17 = (bf16[848,512]{1,0:T(8,128)(2,1)S(1)}, bf16[848,512]{1,0:T(8,128)(2,1)S(1)}, u32[]{:S(2)}, u32[]{:S(2)}) collective-permute-start(bf16[848,512]{1,0:T(8,128)(2,1)S(1)} %get-tuple-element.102.refs_0_), channel_id=1, source_target_pairs={{0,1},{2,3},{4,5},{6,7},{8,9},{10,11},{12,13},{14,15},{16,17},{18,... | collective-permute-start | bytes 2605064 | tf_op jit(solution)/shard_map/first_factor_to_odd/ppermute | solution.py:557
  67.4 3.0 %collective-permute-done.7.recv = bf16[64,1024]{1,0:T(8,128)(2,1)S(1)} collective-permute-done((bf16[64,1024]{1,0:T(8,128)(2,1)S(1)}, bf16[64,1024]{1,0:T(8,128)(2,1)S(1)}, u32[]{:S(2)}, u32[]{:S(2)}) %collective-permute-start.7) | collective-permute-done | bytes 131104 | tf_op jit(solution)/shard_map/panels_z2/ppermute | solution.py:557
  71.2 5.8 %collective-permute-start.12 = (bf16[64,512]{1,0:T(8,128)(2,1)S(1)}, bf16[64,512]{1,0:T(8,128)(2,1)S(1)}, u32[]{:S(2)}, u32[]{:S(2)}) collective-permute-start(bf16[64,512]{1,0:T(8,128)(2,1)S(1)} %get-tuple-element.94.mine), channel_id=1, source_target_pairs={{0,24},{1,25},{2,26},{3,27},{8,16},{9,17},{10,18},{11,19},{16,8},{... | collective-permute-start | bytes 196616 | tf_op jit(solution)/shard_map/panels_z3/ppermute | solution.py:557
  77.0 1.5 %shard_map.134 = (bf16[512,512]{1,0:T(8,128)(2,1)S(1)}, bf16[512,128]{1,0:T(8,128)(2,1)}) custom-call(s32[4]{0:T(128)S(1)} %pad_add_fusion.place, bf16[320,512]{1,0:T(8,128)(2,1)S(1)} %collective-permute-done.8.refs_0_, bf16[320,512]{1,0:T(8,128)(2,1)S(1)} %collective-permute-done.10.refs_2_.refs_1_, bf16[320,512]{1,0:T(8,128)(2,1)S(1)} %collective-permute-done.13.refs_2_, ...), custom_call_target="tpu_custom_call" | custom-call | flops 100000000 | bytes 1000000 | tf_op jit(solution)/shard_map/pallas_call | solution.py:60
  80.9 1.5 %collective-permute-start.15 = (bf16[64,1536]{1,0:T(8,128)(2,1)S(1)}, bf16[64,1536]{1,0:T(8,128)(2,1)S(1)}, u32[]{:S(2)}, u32[]{:S(2)}) collective-permute-start(bf16[64,1536]{1,0:T(8,128)(2,1)S(1)} %shard_map.135.mine), channel_id=1, source_target_pairs={{0,4},{1,5},{2,6},{3,7},{8,12},{9,13},{10,14},{11,15},{16,20},{17,... | collective-permute-start | bytes 589832 | tf_op jit(solution)/shard_map/down_z1/ppermute | solution.py:557
  82.4 4.1 %collective-permute-done.15.recv = bf16[64,1536]{1,0:T(8,128)(2,1)S(1)} collective-permute-done((bf16[64,1536]{1,0:T(8,128)(2,1)S(1)}, bf16[64,1536]{1,0:T(8,128)(2,1)S(1)}, u32[]{:S(2)}, u32[]{:S(2)}) %collective-permute-start.15) | collective-permute-done | bytes 196640 | tf_op jit(solution)/shard_map/down_z1/ppermute | solution.py:557
  88.1 1.8 %collective-permute-start.18 = (bf16[128,512]{1,0:T(8,128)(2,1)S(1)}, bf16[128,512]{1,0:T(8,128)(2,1)S(1)}, u32[]{:S(2)}, u32[]{:S(2)}) collective-permute-start(bf16[128,512]{1,0:T(8,128)(2,1)S(1)} %get-tuple-element.107), channel_id=1, source_target_pairs={{0,1},{2,3},{4,5},{6,7},{8,9},{10,11},{12,13},{14,15},{16,17},{18,... | collective-permute-start | bytes 393224 | tf_op jit(solution)/shard_map/first_solution_to_odd/ppermute | solution.py:557
  89.9 1.8 %shard_map.137 = (bf16[1024,512]{1,0:T(8,128)(2,1)S(1)}, bf16[512,512]{1,0:T(8,128)(2,1)}) custom-call(s32[4]{0:T(128)S(1)} %pad_add_fusion.place, bf16[848,512]{1,0:T(8,128)(2,1)S(1)} %get-tuple-element.102.refs_0_, bf16[848,512]{1,0:T(8,128)(2,1)S(1)} %collective-permute-done.17.refs_1_), custom_call_target="tpu_custom_call" | custom-call | flops 100000000 | bytes 1000000 | tf_op jit(solution)/shard_map/pallas_call | solution.py:60
  91.7 4.5 %collective-permute-done.16.recv = bf16[64,2048]{1,0:T(8,128)(2,1)S(1)} collective-permute-done((bf16[64,2048]{1,0:T(8,128)(2,1)S(1)}, bf16[64,2048]{1,0:T(8,128)(2,1)S(1)}, u32[]{:S(2)}, u32[]{:S(2)}) %collective-permute-start.16) | collective-permute-done | bytes 262176 | tf_op jit(solution)/shard_map/down_ring/ppermute | solution.py:557
  96.2 2.0 %shard_map.138 = (bf16[128,640]{1,0:T(8,128)(2,1)S(1)}, bf16[128,640]{1,0:T(8,128)(2,1)S(1)}, bf16[128,512]{1,0:T(8,128)(2,1)}, bf16[128,512]{1,0:T(8,128)(2,1)}) custom-call(s32[4]{0:T(128)S(1)} %pad_add_fusion.place, bf16[64,2048]{1,0:T(8,128)(2,1)S(1)} %shard_map.136.mine, bf16[64,2048]{1,0:T(8,128)(2,1)S(1)} %collective-permute-done.16.recv, ...), custom_call_target="tpu_custom_call" | custom-call | flops 100000000 | bytes 1000000 | tf_op jit(solution)/shard_map/pallas_call | solution.py:60
  98.3 5.3 %collective-permute-done.19.recv = bf16[128,640]{1,0:T(8,128)(2,1)S(1)} collective-permute-done((bf16[128,640]{1,0:T(8,128)(2,1)S(1)}, bf16[128,640]{1,0:T(8,128)(2,1)S(1)}, u32[]{:S(2)}, u32[]{:S(2)}) %collective-permute-start.19) | collective-permute-done | bytes 163872 | tf_op jit(solution)/shard_map/rows_back/ppermute | solution.py:557
  103.6 3.8 %shard_map.139 = (bf16[1024,256]{1,0:T(8,128)(2,1)}, bf16[512,256]{1,0:T(8,128)(2,1)}) custom-call(s32[4]{0:T(128)S(1)} %pad_add_fusion.place, bf16[128,640]{1,0:T(8,128)(2,1)S(1)} %get-tuple-element.108.keep, bf16[128,640]{1,0:T(8,128)(2,1)S(1)} %collective-permute-done.19.recv, bf16[1024,1024]{1,0:T(8,128)(2,1)S(1)} %get-tuple-element.110.inv, ...), custom_call_target="tpu_custom_call" | custom-call | flops 100000000 | bytes 1000000 | tf_op jit(solution)/shard_map/pallas_call | solution.py:60
  107.3 8.4 %all-to-all-start = ((bf16[32,16,256]{2,1,0:T(8,128)(2,1)}), bf16[32,16,256]{2,1,0:T(8,128)(2,1)S(1)}, u32[]{:S(2)}, u32[]{:S(2)}) async-start(bf16[32,16,256]{2,1,0:T(8,128)(2,1)} %bitcast.9), calls=%async_computation | async-start | bytes 524288 | tf_op jit(solution)/shard_map/all_to_all | solution.py:767
  115.7 1.9 %collective-permute-start.20 = (bf16[128,512]{1,0:T(8,128)(2,1)S(1)}, bf16[128,512]{1,0:T(8,128)(2,1)S(1)}, u32[]{:S(2)}, u32[]{:S(2)}) collective-permute-start(bf16[128,512]{1,0:T(8,128)(2,1)S(1)} %copy-done.3), channel_id=1, source_target_pairs={{0,1},{1,0},{2,3},{3,2},{4,5},{5,4},{6,7},{7,6},{8,9},{9,8},{10,11... | collective-permute-start | bytes 393224 | tf_op jit(solution)/shard_map/sep_back/ppermute | solution.py:557
  117.6 3.4 %collective-permute-done.20.recv = bf16[128,512]{1,0:T(8,128)(2,1)S(1)} collective-permute-done((bf16[128,512]{1,0:T(8,128)(2,1)S(1)}, bf16[128,512]{1,0:T(8,128)(2,1)S(1)}, u32[]{:S(2)}, u32[]{:S(2)}) %collective-permute-start.20) | collective-permute-done | bytes 131104 | tf_op jit(solution)/shard_map/sep_back/ppermute | solution.py:557
  121.7 2.4 %shard_map.140 = bf16[512,256]{1,0:T(8,128)(2,1)} custom-call(s32[4]{0:T(128)S(1)} %pad_add_fusion.place, bf16[128,512]{1,0:T(8,128)(2,1)} %get-tuple-element.114.keep, bf16[128,512]{1,0:T(8,128)(2,1)} %copy-done.2), custom_call_target="tpu_custom_call" | custom-call | flops 100000000 | bytes 1000000 | tf_op jit(solution)/shard_map/pallas_call | solution.py:60
  124.1 3.1 %all-to-all-done = bf16[32,16,256]{2,1,0:T(8,128)(2,1)S(1)} async-done(((bf16[32,16,256]{2,1,0:T(8,128)(2,1)}), bf16[32,16,256]{2,1,0:T(8,128)(2,1)S(1)}, u32[]{:S(2)}, u32[]{:S(2)}) %all-to-all-start) | async-done | bytes 262176 | tf_op jit(solution)/shard_map/all_to_all | solution.py:767
  127.2 1.7 %shard_map.141 = f32[64,256]{1,0:T(8,128)} custom-call(bf16[2,64,512]{2,1,0:T(8,128)(2,1)} %get-tuple-element.118.weight, bf16[512,256]{1,0:T(8,128)(2,1)S(1)} %bitcast.7), custom_call_target="tpu_custom_call" | custom-call | flops 100000000 | bytes 1000000 | tf_op jit(solution)/shard_map/pallas_call | solution.py:60
  (43 shorter events, 20.6 us)
Async XLA Ops:
  4.2 17.3 %collective-permute-start.3 = (bf16[720,512]{1,0:T(8,128)(2,1)S(1)}, bf16[720,512]{1,0:T(8,128)(2,1)S(1)}, u32[]{:S(2)}, u32[]{:S(2)}) collective-permute-start(bf16[720,512]{1,0:T(8,128)(2,1)S(1)} %get-tuple-element.77.refs_0_.own), channel_id=1, source_target_pairs={{1,0},{3,2},{5,4},{7,6},{9,8},{11,10},{13,12},{15,14},{17,16},{19,... | collective-permute-start | bytes 2211848 | tf_op jit(solution)/shard_map/factors_to_neighbours/ppermute | solution.py:557
  9.8 9.5 %collective-permute-start = (bf16[320,128]{1,0:T(8,128)(2,1)S(1)}, bf16[320,128]{1,0:T(8,128)(2,1)S(1)}, u32[]{:S(2)}, u32[]{:S(2)}) collective-permute-start(bf16[320,128]{1,0:T(8,128)(2,1)S(1)} %get-tuple-element.64.one), channel_id=1, source_target_pairs={{0,1},{1,0},{2,3},{3,2},{4,5},{5,4},{6,7},{7,6},{8,9},{9,8},{10,11... | collective-permute-start | bytes 245768 | tf_op jit(solution)/shard_map/first_terms/ppermute | solution.py:557
  20.2 4.7 %copy-start = (s32[6,2048]{1,0:T(8,128)S(1)}, s32[6,2048]{1,0:T(8,128)}, u32[]{:S(2)}) copy-start(s32[6,2048]{1,0:T(8,128)} %dofs.1) | copy-start | bytes 147460
  20.2 4.7 %copy-start.1 = (f32[6,2048]{1,0:T(8,128)S(1)}, f32[6,2048]{1,0:T(8,128)}, u32[]{:S(2)}) copy-start(f32[6,2048]{1,0:T(8,128)} %coef) | copy-start | bytes 147460
  21.5 13.8 %collective-permute-start.5 = (bf16[720,512]{1,0:T(8,128)(2,1)S(1)}, bf16[720,512]{1,0:T(8,128)(2,1)S(1)}, u32[]{:S(2)}, u32[]{:S(2)}) collective-permute-start(bf16[720,512]{1,0:T(8,128)(2,1)S(1)} %collective-permute-done.3.refs_1_.near), channel_id=1, source_target_pairs={{0,3},{2,1},{4,7},{6,5},{8,11},{10,9},{12,15},{14,13},{16,19},{18,... | collective-permute-start | bytes 2211848 | tf_op jit(solution)/shard_map/factors_across/ppermute | solution.py:557
  24.7 10.6 %collective-permute-start.4 = (bf16[720,512]{1,0:T(8,128)(2,1)S(1)}, bf16[720,512]{1,0:T(8,128)(2,1)S(1)}, u32[]{:S(2)}, u32[]{:S(2)}) collective-permute-start(bf16[720,512]{1,0:T(8,128)(2,1)S(1)} %collective-permute-done.3.refs_1_.near), channel_id=1, source_target_pairs={{0,32},{1,33},{2,34},{3,35},{4,36},{5,37},{6,38},{7,39},{8,40},{9,... | collective-permute-start | bytes 2211848 | tf_op jit(solution)/shard_map/near_to_core/ppermute | solution.py:557
  24.8 8.7 %collective-permute-start.1 = (bf16[128,1024]{1,0:T(8,128)(2,1)S(1)}, bf16[128,1024]{1,0:T(8,128)(2,1)S(1)}, u32[]{:S(2)}, u32[]{:S(2)}) collective-permute-start(bf16[128,1024]{1,0:T(8,128)(2,1)S(1)} %get-tuple-element.71), channel_id=1, source_target_pairs={{0,1},{1,0},{2,3},{3,2},{4,5},{5,4},{6,7},{7,6},{8,9},{9,8},{10,11... | collective-permute-start | bytes 786440 | tf_op jit(solution)/shard_map/terms_pair/ppermute | solution.py:557
  34.8 9.8 %collective-permute-start.2 = (bf16[64,2048]{1,0:T(8,128)(2,1)S(1)}, bf16[64,2048]{1,0:T(8,128)(2,1)S(1)}, u32[]{:S(2)}, u32[]{:S(2)}) collective-permute-start(bf16[64,2048]{1,0:T(8,128)(2,1)S(1)} %get-tuple-element.76), channel_id=1, source_target_pairs={{0,3},{1,2},{2,1},{3,0},{4,7},{5,6},{6,5},{7,4},{8,11},{9,10},{10,... | collective-permute-start | bytes 786440 | tf_op jit(solution)/shard_map/panels_ring/ppermute | solution.py:557
  36.6 19.4 %collective-permute-start.8 = (bf16[320,512]{1,0:T(8,128)(2,1)S(1)}, bf16[320,512]{1,0:T(8,128)(2,1)S(1)}, u32[]{:S(2)}, u32[]{:S(2)}) collective-permute-start(bf16[320,512]{1,0:T(8,128)(2,1)S(1)} %get-tuple-element.87), channel_id=1, source_target_pairs={{4,0},{5,1},{6,2},{7,3},{12,8},{13,9},{14,10},{15,11},{20,16},{21,... | collective-permute-start | bytes 983048 | tf_op jit(solution)/shard_map/factors_up/ppermute | solution.py:557
  45.3 9.2 %collective-permute-start.6 = (bf16[64,1536]{1,0:T(8,128)(2,1)S(1)}, bf16[64,1536]{1,0:T(8,128)(2,1)S(1)}, u32[]{:S(2)}, u32[]{:S(2)}) collective-permute-start(bf16[64,1536]{1,0:T(8,128)(2,1)S(1)} %get-tuple-element.85.mine), channel_id=1, source_target_pairs={{4,0},{5,1},{6,2},{7,3},{12,8},{13,9},{14,10},{15,11},{20,16},{21,... | collective-permute-start | bytes 589832 | tf_op jit(solution)/shard_map/panels_z1/ppermute | solution.py:557
  46.6 9.5 %collective-permute-start.9 = (bf16[144,512]{1,0:T(8,128)(2,1)S(1)}, bf16[144,512]{1,0:T(8,128)(2,1)S(1)}, u32[]{:S(2)}, u32[]{:S(2)}) collective-permute-start(bf16[144,512]{1,0:T(8,128)(2,1)S(1)} %get-tuple-element.88), channel_id=1, source_target_pairs={{4,0},{5,1},{6,2},{7,3},{12,8},{13,9},{14,10},{15,11},{20,16},{21,... | collective-permute-start | bytes 442376 | tf_op jit(solution)/shard_map/factors_up_rest/ppermute | solution.py:557
  56.1 10.3 %collective-permute-start.10 = (bf16[320,512]{1,0:T(8,128)(2,1)S(1)}, bf16[320,512]{1,0:T(8,128)(2,1)S(1)}, u32[]{:S(2)}, u32[]{:S(2)}) collective-permute-start(bf16[320,512]{1,0:T(8,128)(2,1)S(1)} %collective-permute-done.8.refs_0_), channel_id=1, source_target_pairs={{0,32},{1,33},{2,34},{3,35},{4,36},{5,37},{6,38},{7,39},{8,40},{9,... | collective-permute-start | bytes 983048 | tf_op jit(solution)/shard_map/up_to_core/ppermute | solution.py:557
  57.8 13.3 %collective-permute-start.13 = (bf16[320,512]{1,0:T(8,128)(2,1)S(1)}, bf16[320,512]{1,0:T(8,128)(2,1)S(1)}, u32[]{:S(2)}, u32[]{:S(2)}) collective-permute-start(bf16[320,512]{1,0:T(8,128)(2,1)S(1)} %collective-permute-done.8.refs_0_), channel_id=1, source_target_pairs={{8,0},{9,1},{10,2},{11,3},{48,56},{49,57},{50,58},{51,59},{72,64},... | collective-permute-start | bytes 983048 | tf_op jit(solution)/shard_map/factor_top/ppermute | solution.py:557
  59.1 7.2 %collective-permute-start.11 = (bf16[144,512]{1,0:T(8,128)(2,1)S(1)}, bf16[144,512]{1,0:T(8,128)(2,1)S(1)}, u32[]{:S(2)}, u32[]{:S(2)}) collective-permute-start(bf16[144,512]{1,0:T(8,128)(2,1)S(1)} %collective-permute-done.9.refs_1_), channel_id=1, source_target_pairs={{0,32},{1,33},{2,34},{3,35},{4,36},{5,37},{6,38},{7,39},{8,40},{9,... | collective-permute-start | bytes 442376 | tf_op jit(solution)/shard_map/rest_to_core/ppermute | solution.py:557
  59.2 11.3 %collective-permute-start.7 = (bf16[64,1024]{1,0:T(8,128)(2,1)S(1)}, bf16[64,1024]{1,0:T(8,128)(2,1)S(1)}, u32[]{:S(2)}, u32[]{:S(2)}) collective-permute-start(bf16[64,1024]{1,0:T(8,128)(2,1)S(1)} %get-tuple-element.86.mine), channel_id=1, source_target_pairs={{0,8},{1,9},{2,10},{3,11},{8,0},{9,1},{10,2},{11,3},{16,24},{17,25... | collective-permute-start | bytes 393224 | tf_op jit(solution)/shard_map/panels_z2/ppermute | solution.py:557
  64.7 25.2 %collective-permute-start.17 = (bf16[848,512]{1,0:T(8,128)(2,1)S(1)}, bf16[848,512]{1,0:T(8,128)(2,1)S(1)}, u32[]{:S(2)}, u32[]{:S(2)}) collective-permute-start(bf16[848,512]{1,0:T(8,128)(2,1)S(1)} %get-tuple-element.102.refs_0_), channel_id=1, source_target_pairs={{0,1},{2,3},{4,5},{6,7},{8,9},{10,11},{12,13},{14,15},{16,17},{18,... | collective-permute-start | bytes 2605064 | tf_op jit(solution)/shard_map/first_factor_to_odd/ppermute | solution.py:557
  71.1 5.9 %collective-permute-start.14 = (bf16[320,512]{1,0:T(8,128)(2,1)S(1)}, bf16[320,512]{1,0:T(8,128)(2,1)S(1)}, u32[]{:S(2)}, u32[]{:S(2)}) collective-permute-start(bf16[320,512]{1,0:T(8,128)(2,1)S(1)} %collective-permute-done.13.refs_2_), channel_id=1, source_target_pairs={{0,32},{1,33},{2,34},{3,35},{4,36},{5,37},{6,38},{7,39},{8,40},{9,... | collective-permute-start | bytes 983048 | tf_op jit(solution)/shard_map/last_to_core/ppermute | solution.py:557
  71.2 8.5 %collective-permute-start.12 = (bf16[64,512]{1,0:T(8,128)(2,1)S(1)}, bf16[64,512]{1,0:T(8,128)(2,1)S(1)}, u32[]{:S(2)}, u32[]{:S(2)}) collective-permute-start(bf16[64,512]{1,0:T(8,128)(2,1)S(1)} %get-tuple-element.94.mine), channel_id=1, source_target_pairs={{0,24},{1,25},{2,26},{3,27},{8,16},{9,17},{10,18},{11,19},{16,8},{... | collective-permute-start | bytes 196616 | tf_op jit(solution)/shard_map/panels_z3/ppermute | solution.py:557
  80.9 5.6 %collective-permute-start.15 = (bf16[64,1536]{1,0:T(8,128)(2,1)S(1)}, bf16[64,1536]{1,0:T(8,128)(2,1)S(1)}, u32[]{:S(2)}, u32[]{:S(2)}) collective-permute-start(bf16[64,1536]{1,0:T(8,128)(2,1)S(1)} %shard_map.135.mine), channel_id=1, source_target_pairs={{0,4},{1,5},{2,6},{3,7},{8,12},{9,13},{10,14},{11,15},{16,20},{17,... | collective-permute-start | bytes 589832 | tf_op jit(solution)/shard_map/down_z1/ppermute | solution.py:557
  87.6 8.6 %collective-permute-start.16 = (bf16[64,2048]{1,0:T(8,128)(2,1)S(1)}, bf16[64,2048]{1,0:T(8,128)(2,1)S(1)}, u32[]{:S(2)}, u32[]{:S(2)}) collective-permute-start(bf16[64,2048]{1,0:T(8,128)(2,1)S(1)} %shard_map.136.mine), channel_id=1, source_target_pairs={{0,3},{1,2},{2,1},{3,0},{4,7},{5,6},{6,5},{7,4},{8,11},{9,10},{10,... | collective-permute-start | bytes 786440 | tf_op jit(solution)/shard_map/down_ring/ppermute | solution.py:557
  88.1 8.1 %collective-permute-start.18 = (bf16[128,512]{1,0:T(8,128)(2,1)S(1)}, bf16[128,512]{1,0:T(8,128)(2,1)S(1)}, u32[]{:S(2)}, u32[]{:S(2)}) collective-permute-start(bf16[128,512]{1,0:T(8,128)(2,1)S(1)} %get-tuple-element.107), channel_id=1, source_target_pairs={{0,1},{2,3},{4,5},{6,7},{8,9},{10,11},{12,13},{14,15},{16,17},{18,... | collective-permute-start | bytes 393224 | tf_op jit(solution)/shard_map/first_solution_to_odd/ppermute | solution.py:557
  98.2 5.4 %collective-permute-start.19 = (bf16[128,640]{1,0:T(8,128)(2,1)S(1)}, bf16[128,640]{1,0:T(8,128)(2,1)S(1)}, u32[]{:S(2)}, u32[]{:S(2)}) collective-permute-start(bf16[128,640]{1,0:T(8,128)(2,1)S(1)} %get-tuple-element.109), channel_id=1, source_target_pairs={{0,1},{1,0},{2,3},{3,2},{4,5},{5,4},{6,7},{7,6},{8,9},{9,8},{10,11... | collective-permute-start | bytes 491528 | tf_op jit(solution)/shard_map/rows_back/ppermute | solution.py:557
  103.6 12.1 %copy-start.3 = (bf16[128,512]{1,0:T(8,128)(2,1)S(1)}, bf16[128,512]{1,0:T(8,128)(2,1)}, u32[]{:S(2)}) copy-start(bf16[128,512]{1,0:T(8,128)(2,1)} %get-tuple-element.115) | copy-start | bytes 393220
  107.3 19.8 %all-to-all-start = ((bf16[32,16,256]{2,1,0:T(8,128)(2,1)}), bf16[32,16,256]{2,1,0:T(8,128)(2,1)S(1)}, u32[]{:S(2)}, u32[]{:S(2)}) async-start(bf16[32,16,256]{2,1,0:T(8,128)(2,1)} %bitcast.9), calls=%async_computation | async-start | bytes 524288 | tf_op jit(solution)/shard_map/all_to_all | solution.py:767
  115.7 5.3 %collective-permute-start.20 = (bf16[128,512]{1,0:T(8,128)(2,1)S(1)}, bf16[128,512]{1,0:T(8,128)(2,1)S(1)}, u32[]{:S(2)}, u32[]{:S(2)}) collective-permute-start(bf16[128,512]{1,0:T(8,128)(2,1)S(1)} %copy-done.3), channel_id=1, source_target_pairs={{0,1},{1,0},{2,3},{3,2},{4,5},{5,4},{6,7},{7,6},{8,9},{9,8},{10,11... | collective-permute-start | bytes 393224 | tf_op jit(solution)/shard_map/sep_back/ppermute | solution.py:557
  121.0 0.7 copy-start.2

commit v4 on v3

--- a/solution.py
+++ b/solution.py
@@ -52,7 +52,7 @@
 ANY = pl.BlockSpec(memory_space=pl.ANY)
 
 
-def call(body, outs, args, specs, scratch=(), out_specs=None, flops=10**8, moved=10**6):
+def call(body, outs, args, specs, scratch=(), out_specs=None, aliases=None, flops=10**8, moved=10**6):
     args = [
         in_vmem(arg) if spec is VMEM else in_hbm(arg) if spec is HBM else arg
         for arg, spec in zip(args, specs)
@@ -63,6 +63,7 @@
         in_specs=specs,
         out_specs=out_specs or [VMEM] * len(outs),
         scratch_shapes=list(scratch),
+        input_output_aliases=aliases or {},
         compiler_params=pltpu.CompilerParams(vmem_limit_bytes=VMEM_LIMIT),
         cost_estimate=pl.CostEstimate(flops=flops, bytes_accessed=moved, transcendentals=0),
     )(*args)
@@ -97,17 +98,9 @@
     return jnp.where(place == rows, 1.0, 0.0).astype(BF)
 
 
-def leaf_rows(block):
-    block = block.astype(F32)
-    return [block[l : l + 1, 0:U] * 16.0 + block[l : l + 1, U : 2 * U] for l in range(LEVELS)]
-
-
 def sep_rows(block):
     block = block.astype(F32)
-    return [
-        block[s : s + 1, 2 * U : 3 * U] * 16.0 + block[s : s + 1, 3 * U : 4 * U]
-        for s in range(LEVELS - 1)
-    ]
+    return [block[s : s + 1, 0:U] * 16.0 + block[s : s + 1, U : 2 * U] for s in range(LEVELS - 1)]
 
 
 def push_values(factor, y, slots):
@@ -125,59 +118,69 @@
     return dot(back, factor[0:PANEL]).astype(BF)
 
 
-def pack_factor(place, inv, cpl, leaf_idx, sep_idx, out, up, codes_out, codes, leaf_v, sep_v, sems):
+def pack_factor(place, inv, cpl, sep_idx, out, up, codes, sep_v, sems):
+    load = pltpu.make_async_copy(sep_idx.at[0], sep_v, sems.at[0])
+    copies = []
+    for n, (dst, slots) in enumerate(((up, 3), (out, 4))):
+        for i, (r, c, pr, pc) in enumerate(triangle_blocks()):
+            copies.append(pltpu.make_async_copy(inv.at[r, c], dst.at[pr, pc], sems.at[1 + 6 * n + i]))
+        copies.append(
+            pltpu.make_async_copy(cpl.at[0 : slots * U], dst.at[CPL0 : packed_rows(slots)], sems.at[6 + 6 * n])
+        )
+    load.start()
+    for copy in copies:
+        copy.start()
+    codes[...] = jnp.zeros_like(codes)
+    out[packed_rows(4) :] = jnp.zeros((128, PANEL), BF)
+    load.wait()
+    value = sep_v[...]
+    codes[0 : LEVELS - 1, 0:U] = (value >> 4).astype(F32)
+    codes[0 : LEVELS - 1, U : 2 * U] = (value & 15).astype(F32)
+    coded = codes[...].astype(BF)
+    out[IDX] = coded
+    up[IDX] = coded
+    for copy in copies:
+        copy.wait()
+
+
+def leaf_first(
+    place, inv, rhs, cpl, rsep, leaf_idx, sep_idx, yt, rhs_out, one, inv_v, cpl_v,
+    rhs_v, rsep_v, leaf_v, sep_v, codes, sems
+):
     loads = [
         pltpu.make_async_copy(leaf_idx.at[0], leaf_v, sems.at[0]),
         pltpu.make_async_copy(sep_idx.at[0], sep_v, sems.at[1]),
+        pltpu.make_async_copy(rhs, rhs_v, sems.at[2]),
     ]
-    copies = []
-    for n, (dst, slots) in enumerate(((up, 3), (out, 4))):
-        for i, (r, c, pr, pc) in enumerate(triangle_blocks()):
-            copies.append(pltpu.make_async_copy(inv.at[r, c], dst.at[pr, pc], sems.at[2 + 6 * n + i]))
-        copies.append(
-            pltpu.make_async_copy(cpl.at[0 : slots * U], dst.at[CPL0 : packed_rows(slots)], sems.at[7 + 6 * n])
-        )
-    for copy in loads + copies:
-        copy.start()
+    for i in range(4):
+        rows = pl.ds(i * 256, 256)
+        loads.append(pltpu.make_async_copy(inv.at[rows], inv_v.at[rows], sems.at[3 + i]))
+    loads.append(pltpu.make_async_copy(cpl.at[0], cpl_v, sems.at[7]))
+    loads.append(pltpu.make_async_copy(rsep, rsep_v, sems.at[8]))
+    for load in loads:
+        load.start()
     codes[...] = jnp.zeros_like(codes)
-    for ref, load, count, at in ((leaf_v, loads[0], LEVELS, 0), (sep_v, loads[1], LEVELS - 1, 2 * U)):
+    for ref, load, count, at in ((leaf_v, loads[0], LEVELS, 0), (sep_v, loads[1], LEVELS - 1, 32)):
         load.wait()
         value = ref[...]
-        codes[0:count, at : at + U] = (value >> 4).astype(F32)
-        codes[0:count, at + U : at + 2 * U] = (value & 15).astype(F32)
-    coded = codes[...].astype(BF)
-    out[IDX] = coded
-    up[IDX] = coded
-    for q in range(4):
-        codes_out[16 * q : 16 * (q + 1)] = coded[:, q * U : (q + 1) * U]
-    for copy in copies:
-        copy.wait()
-
-
-def leaf_forward(
-    place, inv, rhs, cpl, rsep, codes, yt_out, terms, rhs_out, one_out, inv_v, cpl_v, rhs_v, rsep_v, y, sems
-):
-    loads = [pltpu.make_async_copy(rhs, rhs_v, sems.at[0])]
+        codes[at : at + count] = (value >> 4).astype(F32)
+        codes[at + 16 : at + 16 + count] = (value & 15).astype(F32)
+    one[NC:] = codes[...].astype(BF)
+    loads[2].wait()
+    rhs_t = rhs_v[...].astype(F32).T.astype(BF)
     for i in range(4):
-        rows = pl.ds(i * 256, 256)
-        loads.append(pltpu.make_async_copy(inv.at[rows], inv_v.at[rows], sems.at[1 + i]))
-    loads.append(pltpu.make_async_copy(cpl.at[0], cpl_v, sems.at[5]))
-    loads.append(pltpu.make_async_copy(rsep, rsep_v, sems.at[6]))
-    for load in loads:
-        load.start()
-    loads[0].wait()
-    for i in range(4):
-        loads[1 + i].wait()
+        loads[3 + i].wait()
         span = (i + 1) * 256
-        y[i * 256 : span] = dot(inv_v[i * 256 : span, 0:span], rhs_v[0:span])
-    yt_out[...] = y[...].T.astype(BF)
-    loads[5].wait()
-    one_out[0:NC] = dot_t(yt_out[...], cpl_v[0]).astype(BF)
-    one_out[NC:] = codes[...]
+        yt[:, i * 256 : span] = dot_t(rhs_t[:, 0:span], inv_v[i * 256 : span, 0:span]).astype(BF)
+    loads[7].wait()
+    one[0:NC] = dot_t(yt[...], cpl_v[0]).astype(BF)
+    loads[8].wait()
+    rhs_out[...] = rsep_v[...].astype(F32).T.astype(BF)
+
+
+def leaf_second(yt, cpl_v, terms):
     for l in range(1, LEVELS):
-        terms[:, (l - 1) * U : l * U] = dot_t(yt_out[...], cpl_v[l]).astype(BF)
-    loads[6].wait()
-    rhs_out[...] = rsep_v[...].astype(F32).T.astype(BF)
+        terms[:, (l - 1) * U : l * U] = dot_t(yt[...], cpl_v[l]).astype(BF)
 
 
 def which(place):
@@ -288,10 +291,10 @@
 
 
 ONE = 2 * U
-ONE_HOTS = ONE + 4 * 3 * U
-
-
-def stage_pair(place, one, other, hots):
+PAIR_HOTS = 4 * 3 * U
+
+
+def pair_rows(place, one, other):
     even = place[1] % 2 == 0
     mine, far = one[NC:], other[NC:]
 
@@ -302,10 +305,13 @@
         ]
 
     left, right = jnp.where(even, mine, far), jnp.where(even, far, mine)
-    a, b, up = rows(left, 0, LEVELS), rows(right, 0, LEVELS), rows(left, 32, LEVELS - 1)
-    hots[:, 0:ONE] = hot(jnp.concatenate([a[0], b[0]], axis=1))
+    return rows(left, 0, LEVELS), rows(right, 0, LEVELS), rows(left, 32, LEVELS - 1)
+
+
+def stage_pair(place, one, other, hots):
+    a, b, up = pair_rows(place, one, other)
     for k in range(4):
-        at = ONE + k * 3 * U
+        at = k * 3 * U
         hots[:, at : at + 3 * U] = hot(jnp.concatenate([a[k + 1], b[k + 1], up[k]], axis=1))
 
 
@@ -314,9 +320,11 @@
     return jnp.where((y == 1) | (y == 2), 1, 0)
 
 
-def level_one(place, one, recv, terms, rhs, factor, hots, y_keep, y_send, keep, send, y_all):
+def level_one(place, one, recv, terms, rhs, factor, own, hots, y_keep, passed, keep, send, y_all):
     even = place[1] % 2 == 0
-    total = dot_t(jnp.concatenate([one[0:NC], recv[0:NC]], axis=1), hots[:, 0:ONE])
+    a, b, _ = pair_rows(place, one, recv)
+    hots[...] = hot(jnp.concatenate([a[0], b[0]], axis=1))
+    total = dot_t(jnp.concatenate([one[0:NC], recv[0:NC]], axis=1), hots[...])
     resid = (rhs[...].astype(F32) - total).astype(BF)
     y = dot_t(resid, factor[0:PANEL]).astype(BF)
     y_all[:, 0:PANEL] = y
@@ -329,7 +337,7 @@
     keep[:, 0:PANEL] = terms[mine]
     keep[:, PANEL:] = y_all[mine, PANEL:]
     y_keep[...] = y_all[mine, 0:PANEL]
-    y_send[...] = y_all[theirs, 0:PANEL]
+    passed[packed_rows(4) :] = y_all[theirs, 0:PANEL]
 
 
 def join_pair(place, keep, recv, hots, panel_keep, panel_send, panels):
@@ -340,7 +348,7 @@
     level = jnp.where(ring < 2, 2, place[3])
     for k in range(4):
         at = slice(k * U, (k + 1) * U)
-        start = ONE + k * 3 * U
+        start = k * 3 * U
         parts = [left[:, at], right[:, at], left[:, PANEL + k * U : PANEL + (k + 1) * U]]
         total = dot_t(jnp.concatenate(parts, axis=1), hots[:, start : start + 3 * U])
         total = total - jnp.where(level == k + 2, held, 0.0)
@@ -380,15 +388,15 @@
 
 
 def level_one_back(
-    place, mine, recv, y_mine, y_recv, factor, hots, rows_keep, rows_send, sep_keep, sep_send, x, sep_a, sep_b, sems
+    place, mine, recv, y_mine, passed, factor, first_hots, hots, rows_keep, rows_send, sep_keep, sep_send, x, sep_a, sep_b, sems
 ):
     side = place[1] // 2
     even = place[1] % 2 == 0
     x[pl.ds(pl.multiple_of(side * 64, 64), 64)] = mine[...]
     x[pl.ds(pl.multiple_of((1 - side) * 64, 64), 64)] = recv[...]
     above = [x[:, k * PANEL : (k + 1) * PANEL] for k in range(4)]
-    ups = [hots[:, ONE + k * 3 * U + 2 * U : ONE + (k + 1) * 3 * U] for k in range(4)]
-    x1 = solve_back(factor, ups, jnp.where(even, y_mine[...], y_recv[...]), above)
+    ups = [hots[:, k * 3 * U + 2 * U : (k + 1) * 3 * U] for k in range(4)]
+    x1 = solve_back(factor, ups, jnp.where(even, y_mine[...], passed[packed_rows(4) :]), above)
     level = jnp.where(place[1] < 2, 2, place[3])
     held = jnp.where(level == 0, jnp.zeros_like(x1), above[0])
     for k in (1, 2, 3):
@@ -402,8 +410,8 @@
     for store in stores:
         store.start()
     for l, value in enumerate([x1] + above):
-        start = 0 if l == 0 else ONE + (l - 1) * 3 * U
-        both = dot(value, hots[:, start : start + 2 * U]).astype(BF)
+        pair = first_hots[...] if l == 0 else hots[:, (l - 1) * 3 * U : (l - 1) * 3 * U + 2 * U]
+        both = dot(value, pair).astype(BF)
         left, right = both[:, 0:U], both[:, U : 2 * U]
         rows_keep[:, l * U : (l + 1) * U] = jnp.where(even, left, right)
         rows_send[:, l * U : (l + 1) * U] = jnp.where(even, right, left)
@@ -411,7 +419,7 @@
         store.wait()
 
 
-def leaf_backward(place, keep, recv, inv, cpl, yt, chosen, x_leaf, picks_out, rows, sub, picks, sems):
+def leaf_backward(place, keep, recv, inv, cpl, yt, chosen, xt_out, picks_out, rows, sub, xt, picks, sems):
     side = half_of(place)
     rows[pl.ds(pl.multiple_of(side * 128, 128), 128)] = keep[...]
     rows[pl.ds(pl.multiple_of((1 - side) * 128, 128), 128)] = recv[...]
@@ -421,31 +429,36 @@
     sub[...] = total.astype(BF)
     for i in range(4):
         start = i * 256
-        part = dot(sub[:, start:], inv[start:, start : start + 256])
-        x_leaf[start : start + 256] = part.T.astype(BF)
-    stores = []
+        xt[:, start : start + 256] = dot(sub[:, start:], inv[start:, start : start + 256]).astype(BF)
+    stores = [pltpu.make_async_copy(xt, xt_out, sems.at[2])]
+    stores[0].start()
     for i in range(2):
         part = slice(i * 256, (i + 1) * 256)
-        picks[part] = dot(chosen[part], x_leaf[...]).astype(BF)
+        picks[part] = dot_t(chosen[part], xt[...]).astype(BF)
         stores.append(pltpu.make_async_copy(picks.at[part], picks_out.at[part], sems.at[i]))
         stores[-1].start()
     for store in stores:
         store.wait()
 
 
-def sep_out(place, keep, recv, x_sep, keep_v, recv_v, xt, sems):
+def turn_back(place, keep, recv, xt, x_sep, x_leaf, keep_v, recv_v, xt_v, both, sems):
     loads = [
         pltpu.make_async_copy(keep, keep_v, sems.at[0]),
         pltpu.make_async_copy(recv, recv_v, sems.at[1]),
+        pltpu.make_async_copy(xt, xt_v, sems.at[2]),
     ]
     for load in loads:
         load.start()
-    for load in loads:
+    loads[2].wait()
+    for i in range(4):
+        part = slice(i * 256, (i + 1) * 256)
+        x_leaf[part] = xt_v[:, part].astype(F32).T.astype(BF)
+    for load in loads[:2]:
         load.wait()
     side = half_of(place)
-    xt[pl.ds(pl.multiple_of(side * 128, 128), 128)] = keep_v[...].astype(F32)
-    xt[pl.ds(pl.multiple_of((1 - side) * 128, 128), 128)] = recv_v[...].astype(F32)
-    x_sep[...] = xt[...].T.astype(BF)
+    both[pl.ds(pl.multiple_of(side * 128, 128), 128)] = keep_v[...].astype(F32)
+    both[pl.ds(pl.multiple_of((1 - side) * 128, 128), 128)] = recv_v[...].astype(F32)
+    x_sep[...] = both[...].T.astype(BF)
 
 
 def stretch_sum(weight, got, out, weight_v, sems):
@@ -565,36 +578,40 @@
     def to_odd(value):
         return route(value, lambda c, y, z: (c, y + 1, z) if y % 2 == 0 else None)
 
-    own, own_up, codes = call(
+    own, own_up = call(
         pack_factor,
-        [pinned(packed_rows(4), PANEL), pinned(packed_rows(3), PANEL), pinned(4 * 16, U)],
-        [place, sep_inv, sep_cpl.reshape(4 * U, PANEL), leaf_idx, sep_idx],
-        [SMEM, HBM, HBM, HBM, HBM],
-        [
-            pltpu.VMEM((16, PANEL), F32),
-            pltpu.VMEM((LEVELS, U), jnp.int32),
-            pltpu.VMEM((LEVELS - 1, U), jnp.int32),
-            dma(14),
-        ],
+        [pinned(packed_rows(4) + 128, PANEL), pinned(packed_rows(3), PANEL)],
+        [place, sep_inv, sep_cpl.reshape(4 * U, PANEL), sep_idx],
+        [SMEM, HBM, HBM, HBM],
+        [pltpu.VMEM((16, PANEL), F32), pltpu.VMEM((LEVELS - 1, U), jnp.int32), dma(13)],
     )
     with jax.named_scope("factors_to_neighbours"):
         near = route(own_up, lambda c, y, z: (c, y ^ (3 if c else 1), z) if y % 2 else None)
-    yt, terms, rhs, one, inv_v, cpl_v = call(
-        leaf_forward,
+    yt, rhs, one, inv_v, cpl_v = call(
+        leaf_first,
         [
             pinned(NC, LEAF),
-            pinned(NC, PANEL),
             pinned(NC, PANEL),
             pinned(NC + 4 * 16, U),
             pinned(LEAF, LEAF),
             pinned(LEVELS, U, LEAF),
         ],
-        [after(place, own), leaf_inv, rhs_leaf, leaf_cpl, rhs_sep, codes],
-        [SMEM, HBM, HBM, HBM, HBM, VMEM],
-        [pltpu.VMEM((LEAF, NC), BF), pltpu.VMEM((PANEL, NC), BF), pltpu.VMEM((LEAF, NC), F32), dma(7)],
+        [place, leaf_inv, rhs_leaf, leaf_cpl, rhs_sep, after(leaf_idx, own), sep_idx],
+        [SMEM] + [HBM] * 6,
+        [
+            pltpu.VMEM((LEAF, NC), BF),
+            pltpu.VMEM((PANEL, NC), BF),
+            pltpu.VMEM((LEVELS, U), jnp.int32),
+            pltpu.VMEM((LEVELS - 1, U), jnp.int32),
+            pltpu.VMEM((64, U), F32),
+            dma(9),
+        ],
     )
     with jax.named_scope("first_terms"):
         recv = swap(one, 1)
+    (terms,) = call(
+        leaf_second, [pinned(NC, PANEL)], [yt, cpl_v], [VMEM, VMEM]
+    )
 
     def ready(slots, pick, sources, split=False):
         return call(
@@ -615,19 +632,25 @@
         )
 
     f1, _ = ready(4, lambda core, y, z: (core >= 0,), [after(own, one)])
-    (h1,) = call(
-        stage_pair,
-        [pinned(PANEL, ONE_HOTS)],
-        [place, one, recv],
-        [SMEM, VMEM, VMEM],
-    )
-    recv = after(recv, f1)
-    y1, y1_send, keep, send = call(
+    near = after(near, recv, f1, terms)
+    with jax.named_scope("factors_across"):
+        far = route(near, lambda c, y, z: (c, y ^ (1 if c else 3), z) if y % 2 == 0 else None)
+    with jax.named_scope("near_to_core"):
+        near_o = swap_core(near)
+    first = after(recv, f1)
+    first_hots, y1, passed, keep, send = call(
         level_one,
-        [pinned(128, PANEL), pinned(128, PANEL), pinned(128, 2 * PANEL), pinned(128, 2 * PANEL)],
-        [place, one, recv, terms, rhs, f1, h1],
+        [
+            pinned(PANEL, ONE),
+            pinned(128, PANEL),
+            pinned(packed_rows(4) + 128, PANEL),
+            pinned(128, 2 * PANEL),
+            pinned(128, 2 * PANEL),
+        ],
+        [place, one, first, terms, rhs, f1, own],
         [SMEM] + [VMEM] * 6,
         [pltpu.VMEM((NC, 2 * PANEL), BF)],
+        aliases={6: 2},
     )
     with jax.named_scope("terms_pair"):
         recv = swap(send, 1)
@@ -646,7 +669,10 @@
         ],
         [VMEM, HBM],
     )
-    recv = after(recv, chosen)
+    (h1,) = call(
+        stage_pair, [pinned(PANEL, PAIR_HOTS)], [place, one, after(first, send)], [SMEM, VMEM, VMEM]
+    )
+    recv = after(recv, chosen, h1)
     panel, send = call(
         join_pair,
         [pinned(64, 4 * PANEL), pinned(64, 4 * PANEL)],
@@ -656,11 +682,6 @@
     )
     with jax.named_scope("panels_ring"):
         recv = swap(send, 3)
-    near = after(near, keep)
-    with jax.named_scope("near_to_core"):
-        near_o = swap_core(near)
-    with jax.named_scope("factors_across"):
-        far = route(near, lambda c, y, z: (c, y ^ (1 if c else 3), z) if y % 2 == 0 else None)
     far = after(far, send)
     at = [own_up, near, near_o, far]
     f2, h2 = ready(3, pick_two, at)
@@ -682,40 +703,36 @@
 
     with jax.named_scope("factors_up"):
         up = next_up(top)
+    with jax.named_scope("factor_top"):
+        last = route(
+            top,
+            lambda c, y, z: (0, y, 0) if (c, z) == (0, 3) else (1, y, 6) if (c, z) == (1, 3) else None,
+        )
     with jax.named_scope("factors_up_rest"):
         rest = next_up(top_rest)
+    with jax.named_scope("first_factor_to_odd"):
+        passed_far = to_odd(after(passed, f2))
     recv = after(recv, f2, h2, f3, h3)
     y2, panel = rise(2, panel, recv, f2, h2)
     with jax.named_scope("panels_z1"):
         recv = route(panel, lambda c, y, z: (c, y, z - 1) if z % 2 else None)
-    own_far, y1_far = after((own, y1_send), panel)
-    with jax.named_scope("first_factor_to_odd"):
-        own_far = to_odd(own_far)
-    with jax.named_scope("first_solution_to_odd"):
-        y1_far = to_odd(y1_far)
-    y3, panel = rise(3, panel, recv, f3, h3)
-    with jax.named_scope("panels_z2"):
-        recv = route(panel, lambda c, y, z: (c, y, z ^ 2) if z % 2 == 0 else None)
-    up, rest = after((up, rest), panel)
+    up, rest, last = after((up, rest, last), recv)
     with jax.named_scope("up_to_core"):
         up_o = swap_core(up)
     with jax.named_scope("rest_to_core"):
         rest_o = swap_core(rest)
-    with jax.named_scope("factor_top"):
-        last = route(
-            up,
-            lambda c, y, z: (c, y, 0) if (c, z) == (0, 2) else (c, y, 6) if (c, z) == (1, 4) else None,
-        )
+    with jax.named_scope("last_to_core"):
+        last_o = swap_core(last)
+    y3, panel = rise(3, panel, recv, f3, h3)
+    with jax.named_scope("panels_z2"):
+        recv = route(panel, lambda c, y, z: (c, y, z ^ 2) if z % 2 == 0 else None)
+    up, rest, last, up_o, rest_o, last_o = after((up, rest, last, up_o, rest_o, last_o), panel)
     f4, h4 = ready(1, pick_four, [up, rest, up_o, rest_o], True)
-    recv = after(recv, f4, h4)
+    f5, _ = ready(0, pick_five, [up, up_o, last, last_o])
+    recv = after(recv, f4, h4, f5)
     y4, panel = rise(4, panel, recv, f4, h4)
     with jax.named_scope("panels_z3"):
         recv = route(panel, lambda c, y, z: (c, y, 6 - z) if z % 2 == 0 else None)
-    last = after(last, panel)
-    with jax.named_scope("last_to_core"):
-        last_o = swap_core(last)
-    f5, _ = ready(0, pick_five, [up, up_o, last, last_o])
-    recv = after(recv, f5)
     (x,) = call(
         turn,
         [pinned(64, 3 * PANEL)],
@@ -732,13 +749,14 @@
     )
     with jax.named_scope("down_ring"):
         recv = swap(x, 3)
-    f1, _ = ready(4, pick_one, [own, after(own_far, x)])
+    passed_far = after(passed_far, x)
+    f1, _ = ready(4, pick_one, [passed, passed_far])
     recv = after(recv, f1)
     rows_keep, rows_send, sep_keep, sep_send = call(
         level_one_back,
         [pinned(128, TERM), pinned(128, TERM), stored(128, PANEL), stored(128, PANEL)],
-        [place, x, recv, y1, y1_far, f1, h1],
-        [SMEM] + [VMEM] * 6,
+        [place, x, recv, y1, passed_far, f1, first_hots, h1],
+        [SMEM] + [VMEM] * 7,
         [
             pltpu.VMEM((128, 4 * PANEL), BF),
             pltpu.VMEM((128, PANEL), BF),
@@ -750,29 +768,38 @@
     with jax.named_scope("rows_back"):
         recv = swap(rows_send, 1)
     with jax.named_scope("sep_back"):
-        sep_recv = swap(sep_send, 1)
-    x_leaf, picks = call(
+        sep_recv = swap(after(sep_send, recv), 1)
+    xt, picks = call(
         leaf_backward,
-        [plain(LEAF, NC), stored(32 * SLOTS, NC)],
+        [stored(NC, LEAF), stored(32 * SLOTS, NC)],
         [place, rows_keep, recv, inv_v, cpl_v, yt, chosen],
         [SMEM] + [VMEM] * 6,
         [
             pltpu.VMEM((NC, TERM), BF),
             pltpu.VMEM((NC, LEAF), BF),
+            pltpu.VMEM((NC, LEAF), BF),
             pltpu.VMEM((32 * SLOTS, NC), BF),
-            dma(2),
+            dma(3),
         ],
-        [VMEM, HBM],
-    )
+        [HBM, HBM],
+        moved=14 * 10**6,
+    )
+    sep_recv = after(sep_recv, picks)
     got = lax.all_to_all(
         picks.reshape(32, SLOTS, NC), rows_axis, 0, 0, tiled=True
     ).reshape(32 * SLOTS, NC)
-    (x_sep,) = call(
-        sep_out,
-        [plain(PANEL, NC)],
-        [place, sep_keep, after(sep_recv, picks)],
-        [SMEM, HBM, HBM],
-        [pltpu.VMEM((128, PANEL), BF), pltpu.VMEM((128, PANEL), BF), pltpu.VMEM((NC, PANEL), F32), dma(2)],
+    x_sep, x_leaf = call(
+        turn_back,
+        [plain(PANEL, NC), plain(LEAF, NC)],
+        [place, sep_keep, sep_recv, xt],
+        [SMEM, HBM, HBM, HBM],
+        [
+            pltpu.VMEM((128, PANEL), BF),
+            pltpu.VMEM((128, PANEL), BF),
+            pltpu.VMEM((NC, LEAF), BF),
+            pltpu.VMEM((NC, PANEL), F32),
+            dma(3),
+        ],
     )
     (stretch,) = call(
         stretch_sum,

time: 130 us -> 121 us (0.931)
  waiting for transfers between devices: 48.6 us -> 43.6 us
  starting transfers between devices: 42.2 us -> 39.3 us
    ppermute x21 -> x20, waiting for transfers between devices: 45.5 us -> 40.9 us  [route(): return lax.ppermute(value, (cols_axis, rows_axis), pairs)]
    ppermute x21 -> x20, starting transfers between devices: 33.8 us -> 31.7 us  [route(): return lax.ppermute(value, (cols_axis, rows_axis), pairs)]
    pallas_call x21 -> x22, Pallas kernels: 35.1 us -> 34.9 us  [call(): pl.pallas_call(body, out_shape=outs, in_specs=specs, out_specs=out_specs...]
  transfers between devices with their start and end apart: 22 -> 21, of which waited for: 12 -> 11; matrix products, arithmetic and copies ran while one was open for 0% -> 1% of each run, Pallas kernels for 20% -> 22%
where the time goes in v4:
time: 121 us
  waiting for transfers between devices  43.6 us (36%)
  starting transfers between devices  39.3 us (32%)
  Pallas kernels  34.9 us (29%)
  local copies, waits for them, and re-layouts  1.95 us (2%)
    ppermute x20, waiting for transfers between devices, route(): return lax.ppermute(value, (cols_axis, rows_axis), pairs)  40.9 us
    pallas_call x22, Pallas kernels, call(): pl.pallas_call(body, out_shape=outs, in_specs=specs, out_specs=out_specs...  34.9 us
    ppermute x20, starting transfers between devices, route(): return lax.ppermute(value, (cols_axis, rows_axis), pairs)  31.7 us
    all_to_all x1, starting transfers between devices, on_device(): lax.all_to_all(picks.reshape(32, SLOTS, NC), rows_axis, 0, 0, tiled=True)  7.5 us
    all_to_all x1, waiting for transfers between devices, on_device(): lax.all_to_all(picks.reshape(32, SLOTS, NC), rows_axis, 0, 0, tiled=True)  2.68 us
  transfers between devices with their start and end apart: 21, of which 11 were waited for; matrix products, arithmetic and copies ran while one was open for 1% of the time, Pallas kernels for 22%

profile of v4, /device:TPU:2, one launch (start us, length us, event | category | flops | bytes accessed | tf_op | source)
XLA Modules:
  0.0 120.9 jit_solution(12293615558692382652)
XLA Ops:
  0.8 2.1 %shard_map.121 = (bf16[976,512]{1,0:T(8,128)(2,1)S(1)}, bf16[720,512]{1,0:T(8,128)(2,1)S(1)}) custom-call(s32[4]{0:T(128)S(1)} %pad_add_fusion.place, bf16[512,512]{1,0:T(8,128)(2,1)} %inv.2, bf16[512,512]{1,0:T(8,128)(2,1)} %bitcast.8, s32[1,4,128]{2,1,0:T(4,128)} %sep_idx.3), custom_call_target="tpu_custom_call" | custom-call | flops 100000000 | bytes 1000000 | tf_op jit(solution)/shard_map/pallas_call | solution.py:60
  2.9 1.3 %collective-permute-start.3 = (bf16[720,512]{1,0:T(8,128)(2,1)S(1)}, bf16[720,512]{1,0:T(8,128)(2,1)S(1)}, u32[]{:S(2)}, u32[]{:S(2)}) collective-permute-start(bf16[720,512]{1,0:T(8,128)(2,1)S(1)} %get-tuple-element.85.refs_0_.own), channel_id=1, source_target_pairs={{1,0},{3,2},{5,4},{7,6},{9,8},{11,10},{13,12},{15,14},{17,16},{19,... | collective-permute-start | bytes 2211848 | tf_op jit(solution)/shard_map/factors_to_neighbours/ppermute | solution.py:570
  5.5 3.9 %shard_map.122 = (bf16[256,1024]{1,0:T(8,128)(2,1)S(1)}, bf16[256,512]{1,0:T(8,128)(2,1)S(1)}, bf16[320,128]{1,0:T(8,128)(2,1)S(1)}, bf16[1024,1024]{1,0:T(8,128)(2,1)S(1)}, bf16[5,128,1024]{2,1,0:T(8,128)(2,1)S(1)}) custom-call(s32[4]{0:T(128)S(1)} %pad_add_fusion.place, bf16[1024,1024]{1,0:T(8,128)(2,1)} %inv.3, bf16[1024,256]{1,0:T(8,128)(2,1)} %rhs.1, ...), custom_call_target="tpu_custom_call" | custom-call | flops 100000000 | bytes 1000000 | tf_op jit(solution)/shard_map/pallas_call | solution.py:60
  9.3 2.8 %collective-permute-start = (bf16[320,128]{1,0:T(8,128)(2,1)S(1)}, bf16[320,128]{1,0:T(8,128)(2,1)S(1)}, u32[]{:S(2)}, u32[]{:S(2)}) collective-permute-start(bf16[320,128]{1,0:T(8,128)(2,1)S(1)} %get-tuple-element.70.one), channel_id=1, source_target_pairs={{0,1},{1,0},{2,3},{3,2},{4,5},{5,4},{6,7},{7,6},{8,9},{9,8},{10,11... | collective-permute-start | bytes 245768 | tf_op jit(solution)/shard_map/first_terms/ppermute | solution.py:570
  12.1 1.8 %shard_map.123 = (bf16[1024,512]{1,0:T(8,128)(2,1)S(1)}, bf16[512,512]{1,0:T(8,128)(2,1)}) custom-call(s32[4]{0:T(128)S(1)} %pad_add_fusion.place, bf16[976,512]{1,0:T(8,128)(2,1)S(1)} %get-tuple-element.71.refs_0_.own), custom_call_target="tpu_custom_call" | custom-call | flops 100000000 | bytes 1000000 | tf_op jit(solution)/shard_map/pallas_call | solution.py:60
  14.6 3.4 %collective-permute-done.recv.other = bf16[320,128]{1,0:T(8,128)(2,1)S(1)} collective-permute-done((bf16[320,128]{1,0:T(8,128)(2,1)S(1)}, bf16[320,128]{1,0:T(8,128)(2,1)S(1)}, u32[]{:S(2)}, u32[]{:S(2)}) %collective-permute-start) | collective-permute-done | bytes 81952 | tf_op jit(solution)/shard_map/first_terms/ppermute | solution.py:570
  18.0 3.2 %collective-permute-start.5 = (bf16[720,512]{1,0:T(8,128)(2,1)S(1)}, bf16[720,512]{1,0:T(8,128)(2,1)S(1)}, u32[]{:S(2)}, u32[]{:S(2)}) collective-permute-start(bf16[720,512]{1,0:T(8,128)(2,1)S(1)} %collective-permute-done.3.refs_1_.near), channel_id=1, source_target_pairs={{0,3},{2,1},{4,7},{6,5},{8,11},{10,9},{12,15},{14,13},{16,19},{18,... | collective-permute-start | bytes 2211848 | tf_op jit(solution)/shard_map/factors_across/ppermute | solution.py:570
  23.6 2.5 %shard_map.126 = (bf16[512,1024]{1,0:T(8,128)(2,1)S(1)}, bf16[2,64,512]{2,1,0:T(8,128)(2,1)}) custom-call(s32[4]{0:T(128)S(1)} %pad_add_fusion.place, s32[6,2048]{1,0:T(8,128)S(1)} %copy-done, f32[6,2048]{1,0:T(8,128)S(1)} %copy-done.1), custom_call_target="tpu_custom_call" | custom-call | flops 100000000 | bytes 1000000 | tf_op jit(solution)/shard_map/pallas_call | solution.py:60
  26.1 5.3 %collective-permute-done.1.recv = bf16[128,1024]{1,0:T(8,128)(2,1)S(1)} collective-permute-done((bf16[128,1024]{1,0:T(8,128)(2,1)S(1)}, bf16[128,1024]{1,0:T(8,128)(2,1)S(1)}, u32[]{:S(2)}, u32[]{:S(2)}) %collective-permute-start.1) | collective-permute-done | bytes 262176 | tf_op jit(solution)/shard_map/terms_pair/ppermute | solution.py:570
  33.1 1.3 %shard_map.130 = (bf16[768,512]{1,0:T(8,128)(2,1)S(1)}, bf16[512,256]{1,0:T(8,128)(2,1)S(1)}, bf16[320,512]{1,0:T(8,128)(2,1)S(1)}, bf16[144,512]{1,0:T(8,128)(2,1)S(1)}) custom-call(s32[4]{0:T(128)S(1)} %pad_add_fusion.place, bf16[720,512]{1,0:T(8,128)(2,1)S(1)} %get-tuple-element.85.refs_0_.own, bf16[720,512]{1,0:T(8,128)(2,1)S(1)} %collective-permute-done.3.refs_1_.near, ...), custom_call_target="tpu_custom_call" | custom-call | flops 100000000 | bytes 1000000 | tf_op jit(solution)/shard_map/pallas_call | solution.py:60
  38.2 4.7 %collective-permute-done.2.recv = bf16[64,2048]{1,0:T(8,128)(2,1)S(1)} collective-permute-done((bf16[64,2048]{1,0:T(8,128)(2,1)S(1)}, bf16[64,2048]{1,0:T(8,128)(2,1)S(1)}, u32[]{:S(2)}, u32[]{:S(2)}) %collective-permute-start.2) | collective-permute-done | bytes 262176 | tf_op jit(solution)/shard_map/panels_ring/ppermute | solution.py:570
  46.2 1.4 %collective-permute-start.17 = (bf16[976,512]{1,0:T(8,128)(2,1)S(1)}, bf16[976,512]{1,0:T(8,128)(2,1)S(1)}, u32[]{:S(2)}, u32[]{:S(2)}) collective-permute-start(bf16[976,512]{1,0:T(8,128)(2,1)S(1)} %get-tuple-element.115.refs_0_), channel_id=1, source_target_pairs={{0,1},{2,3},{4,5},{6,7},{8,9},{10,11},{12,13},{14,15},{16,17},{18,... | collective-permute-start | bytes 2998280 | tf_op jit(solution)/shard_map/first_factor_to_odd/ppermute | solution.py:570
  47.5 6.7 %collective-permute-done.9.refs_1_ = bf16[144,512]{1,0:T(8,128)(2,1)S(1)} collective-permute-done((bf16[144,512]{1,0:T(8,128)(2,1)S(1)}, bf16[144,512]{1,0:T(8,128)(2,1)S(1)}, u32[]{:S(2)}, u32[]{:S(2)}) %collective-permute-start.9) | collective-permute-done | bytes 147488 | tf_op jit(solution)/shard_map/factors_up_rest/ppermute | solution.py:570
  54.2 1.6 %collective-permute-start.11 = (bf16[320,512]{1,0:T(8,128)(2,1)S(1)}, bf16[320,512]{1,0:T(8,128)(2,1)S(1)}, u32[]{:S(2)}, u32[]{:S(2)}) collective-permute-start(bf16[320,512]{1,0:T(8,128)(2,1)S(1)} %collective-permute-done.8.refs_0_), channel_id=1, source_target_pairs={{0,32},{1,33},{2,34},{3,35},{4,36},{5,37},{6,38},{7,39},{8,40},{9,... | collective-permute-start | bytes 983048 | tf_op jit(solution)/shard_map/up_to_core/ppermute | solution.py:570
  57.0 4.4 %collective-permute-start.7 = (bf16[64,1024]{1,0:T(8,128)(2,1)S(1)}, bf16[64,1024]{1,0:T(8,128)(2,1)S(1)}, u32[]{:S(2)}, u32[]{:S(2)}) collective-permute-start(bf16[64,1024]{1,0:T(8,128)(2,1)S(1)} %get-tuple-element.94.mine), channel_id=1, source_target_pairs={{0,8},{1,9},{2,10},{3,11},{8,0},{9,1},{10,2},{11,3},{16,24},{17,25... | collective-permute-start | bytes 393224 | tf_op jit(solution)/shard_map/panels_z2/ppermute | solution.py:570
  62.6 1.5 %shard_map.134 = (bf16[512,512]{1,0:T(8,128)(2,1)S(1)}, bf16[512,128]{1,0:T(8,128)(2,1)}) custom-call(s32[4]{0:T(128)S(1)} %pad_add_fusion.place, bf16[320,512]{1,0:T(8,128)(2,1)S(1)} %collective-permute-done.8.refs_0_, bf16[320,512]{1,0:T(8,128)(2,1)S(1)} %collective-permute-done.11.refs_2_.refs_1_, bf16[320,512]{1,0:T(8,128)(2,1)S(1)} %collective-permute-done.10.refs_2_, ...), custom_call_target="tpu_custom_call" | custom-call | flops 100000000 | bytes 1000000 | tf_op jit(solution)/shard_map/pallas_call | solution.py:60
  64.1 1.4 %collective-permute-done.7.recv = bf16[64,1024]{1,0:T(8,128)(2,1)S(1)} collective-permute-done((bf16[64,1024]{1,0:T(8,128)(2,1)S(1)}, bf16[64,1024]{1,0:T(8,128)(2,1)S(1)}, u32[]{:S(2)}, u32[]{:S(2)}) %collective-permute-start.7) | collective-permute-done | bytes 131104 | tf_op jit(solution)/shard_map/panels_z2/ppermute | solution.py:570
  66.1 6.7 %collective-permute-start.14 = (bf16[64,512]{1,0:T(8,128)(2,1)S(1)}, bf16[64,512]{1,0:T(8,128)(2,1)S(1)}, u32[]{:S(2)}, u32[]{:S(2)}) collective-permute-start(bf16[64,512]{1,0:T(8,128)(2,1)S(1)} %get-tuple-element.110.mine), channel_id=1, source_target_pairs={{0,24},{1,25},{2,26},{3,27},{8,16},{9,17},{10,18},{11,19},{16,8},{... | collective-permute-start | bytes 196616 | tf_op jit(solution)/shard_map/panels_z3/ppermute | solution.py:570
  72.8 2.2 %collective-permute-done.14.recv = bf16[64,512]{1,0:T(8,128)(2,1)S(1)} collective-permute-done((bf16[64,512]{1,0:T(8,128)(2,1)S(1)}, bf16[64,512]{1,0:T(8,128)(2,1)S(1)}, u32[]{:S(2)}, u32[]{:S(2)}) %collective-permute-start.14) | collective-permute-done | bytes 65568 | tf_op jit(solution)/shard_map/panels_z3/ppermute | solution.py:570
  76.3 1.5 %collective-permute-start.15 = (bf16[64,1536]{1,0:T(8,128)(2,1)S(1)}, bf16[64,1536]{1,0:T(8,128)(2,1)S(1)}, u32[]{:S(2)}, u32[]{:S(2)}) collective-permute-start(bf16[64,1536]{1,0:T(8,128)(2,1)S(1)} %shard_map.136.mine), channel_id=1, source_target_pairs={{0,4},{1,5},{2,6},{3,7},{8,12},{9,13},{10,14},{11,15},{16,20},{17,... | collective-permute-start | bytes 589832 | tf_op jit(solution)/shard_map/down_z1/ppermute | solution.py:570
  77.8 3.2 %collective-permute-done.15.recv = bf16[64,1536]{1,0:T(8,128)(2,1)S(1)} collective-permute-done((bf16[64,1536]{1,0:T(8,128)(2,1)S(1)}, bf16[64,1536]{1,0:T(8,128)(2,1)S(1)}, u32[]{:S(2)}, u32[]{:S(2)}) %collective-permute-start.15) | collective-permute-done | bytes 196640 | tf_op jit(solution)/shard_map/down_z1/ppermute | solution.py:570
  82.6 1.8 %shard_map.138 = (bf16[1024,512]{1,0:T(8,128)(2,1)S(1)}, bf16[512,512]{1,0:T(8,128)(2,1)}) custom-call(s32[4]{0:T(128)S(1)} %pad_add_fusion.place, bf16[976,512]{1,0:T(8,128)(2,1)S(1)} %get-tuple-element.115.refs_0_, bf16[976,512]{1,0:T(8,128)(2,1)S(1)} %collective-permute-done.17.refs_1_.passed), custom_call_target="tpu_custom_call" | custom-call | flops 100000000 | bytes 1000000 | tf_op jit(solution)/shard_map/pallas_call | solution.py:60
  84.4 5.3 %collective-permute-done.16.recv = bf16[64,2048]{1,0:T(8,128)(2,1)S(1)} collective-permute-done((bf16[64,2048]{1,0:T(8,128)(2,1)S(1)}, bf16[64,2048]{1,0:T(8,128)(2,1)S(1)}, u32[]{:S(2)}, u32[]{:S(2)}) %collective-permute-start.16) | collective-permute-done | bytes 262176 | tf_op jit(solution)/shard_map/down_ring/ppermute | solution.py:570
  89.7 2.0 %shard_map.139 = (bf16[128,640]{1,0:T(8,128)(2,1)S(1)}, bf16[128,640]{1,0:T(8,128)(2,1)S(1)}, bf16[128,512]{1,0:T(8,128)(2,1)}, bf16[128,512]{1,0:T(8,128)(2,1)}) custom-call(s32[4]{0:T(128)S(1)} %pad_add_fusion.place, bf16[64,2048]{1,0:T(8,128)(2,1)S(1)} %shard_map.137.mine, bf16[64,2048]{1,0:T(8,128)(2,1)S(1)} %collective-permute-done.16.recv, ...), custom_call_target="tpu_custom_call" | custom-call | flops 100000000 | bytes 1000000 | tf_op jit(solution)/shard_map/pallas_call | solution.py:60
  91.8 5.3 %collective-permute-done.18.recv = bf16[128,640]{1,0:T(8,128)(2,1)S(1)} collective-permute-done((bf16[128,640]{1,0:T(8,128)(2,1)S(1)}, bf16[128,640]{1,0:T(8,128)(2,1)S(1)}, u32[]{:S(2)}, u32[]{:S(2)}) %collective-permute-start.18) | collective-permute-done | bytes 163872 | tf_op jit(solution)/shard_map/rows_back/ppermute | solution.py:570
  97.1 2.9 %shard_map.140 = (bf16[256,1024]{1,0:T(8,128)(2,1)}, bf16[512,256]{1,0:T(8,128)(2,1)}) custom-call(s32[4]{0:T(128)S(1)} %pad_add_fusion.place, bf16[128,640]{1,0:T(8,128)(2,1)S(1)} %get-tuple-element.125.keep, bf16[128,640]{1,0:T(8,128)(2,1)S(1)} %collective-permute-done.18.recv, bf16[1024,1024]{1,0:T(8,128)(2,1)S(1)} %get-tuple-element.126.inv, ...), custom_call_target="tpu_custom_call" | custom-call | flops 100000000 | bytes 14000000 | tf_op jit(solution)/shard_map/pallas_call | solution.py:60
  100.0 7.5 %all-to-all-start = ((bf16[32,16,256]{2,1,0:T(8,128)(2,1)}), bf16[32,16,256]{2,1,0:T(8,128)(2,1)S(1)}, u32[]{:S(2)}, u32[]{:S(2)}) async-start(bf16[32,16,256]{2,1,0:T(8,128)(2,1)} %bitcast.9), calls=%async_computation | async-start | bytes 524288 | tf_op jit(solution)/shard_map/all_to_all | solution.py:788
  107.5 1.9 %collective-permute-start.19 = (bf16[128,512]{1,0:T(8,128)(2,1)S(1)}, bf16[128,512]{1,0:T(8,128)(2,1)S(1)}, u32[]{:S(2)}, u32[]{:S(2)}) collective-permute-start(bf16[128,512]{1,0:T(8,128)(2,1)S(1)} %copy-done.3), channel_id=1, source_target_pairs={{0,1},{1,0},{2,3},{3,2},{4,5},{5,4},{6,7},{7,6},{8,9},{9,8},{10,11... | collective-permute-start | bytes 393224 | tf_op jit(solution)/shard_map/sep_back/ppermute | solution.py:570
  109.4 3.5 %collective-permute-done.19.recv = bf16[128,512]{1,0:T(8,128)(2,1)S(1)} collective-permute-done((bf16[128,512]{1,0:T(8,128)(2,1)S(1)}, bf16[128,512]{1,0:T(8,128)(2,1)S(1)}, u32[]{:S(2)}, u32[]{:S(2)}) %collective-permute-start.19) | collective-permute-done | bytes 131104 | tf_op jit(solution)/shard_map/sep_back/ppermute | solution.py:570
  113.5 2.8 %shard_map.141 = (bf16[512,256]{1,0:T(8,128)(2,1)}, bf16[1024,256]{1,0:T(8,128)(2,1)}) custom-call(s32[4]{0:T(128)S(1)} %pad_add_fusion.place, bf16[128,512]{1,0:T(8,128)(2,1)} %get-tuple-element.121.keep, bf16[128,512]{1,0:T(8,128)(2,1)} %copy-done.2, bf16[256,1024]{1,0:T(8,128)(2,1)} %get-tuple-element.129.xt), custom_call_target="tpu_custom_call" | custom-call | flops 100000000 | bytes 1000000 | tf_op jit(solution)/shard_map/pallas_call | solution.py:60
  116.3 2.7 %all-to-all-done = bf16[32,16,256]{2,1,0:T(8,128)(2,1)S(1)} async-done(((bf16[32,16,256]{2,1,0:T(8,128)(2,1)}), bf16[32,16,256]{2,1,0:T(8,128)(2,1)S(1)}, u32[]{:S(2)}, u32[]{:S(2)}) %all-to-all-start) | async-done | bytes 262176 | tf_op jit(solution)/shard_map/all_to_all | solution.py:788
  119.0 1.7 %shard_map.142 = f32[64,256]{1,0:T(8,128)} custom-call(bf16[2,64,512]{2,1,0:T(8,128)(2,1)} %get-tuple-element.132.weight, bf16[512,256]{1,0:T(8,128)(2,1)S(1)} %bitcast.7), custom_call_target="tpu_custom_call" | custom-call | flops 100000000 | bytes 1000000 | tf_op jit(solution)/shard_map/pallas_call | solution.py:60
  (42 shorter events, 19.6 us)
Async XLA Ops:
  2.9 15.1 %collective-permute-start.3 = (bf16[720,512]{1,0:T(8,128)(2,1)S(1)}, bf16[720,512]{1,0:T(8,128)(2,1)S(1)}, u32[]{:S(2)}, u32[]{:S(2)}) collective-permute-start(bf16[720,512]{1,0:T(8,128)(2,1)S(1)} %get-tuple-element.85.refs_0_.own), channel_id=1, source_target_pairs={{1,0},{3,2},{5,4},{7,6},{9,8},{11,10},{13,12},{15,14},{17,16},{19,... | collective-permute-start | bytes 2211848 | tf_op jit(solution)/shard_map/factors_to_neighbours/ppermute | solution.py:570
  9.3 8.7 %collective-permute-start = (bf16[320,128]{1,0:T(8,128)(2,1)S(1)}, bf16[320,128]{1,0:T(8,128)(2,1)S(1)}, u32[]{:S(2)}, u32[]{:S(2)}) collective-permute-start(bf16[320,128]{1,0:T(8,128)(2,1)S(1)} %get-tuple-element.70.one), channel_id=1, source_target_pairs={{0,1},{1,0},{2,3},{3,2},{4,5},{5,4},{6,7},{7,6},{8,9},{9,8},{10,11... | collective-permute-start | bytes 245768 | tf_op jit(solution)/shard_map/first_terms/ppermute | solution.py:570
  18.0 15.1 %collective-permute-start.5 = (bf16[720,512]{1,0:T(8,128)(2,1)S(1)}, bf16[720,512]{1,0:T(8,128)(2,1)S(1)}, u32[]{:S(2)}, u32[]{:S(2)}) collective-permute-start(bf16[720,512]{1,0:T(8,128)(2,1)S(1)} %collective-permute-done.3.refs_1_.near), channel_id=1, source_target_pairs={{0,3},{2,1},{4,7},{6,5},{8,11},{10,9},{12,15},{14,13},{16,19},{18,... | collective-permute-start | bytes 2211848 | tf_op jit(solution)/shard_map/factors_across/ppermute | solution.py:570
  21.2 11.9 %collective-permute-start.4 = (bf16[720,512]{1,0:T(8,128)(2,1)S(1)}, bf16[720,512]{1,0:T(8,128)(2,1)S(1)}, u32[]{:S(2)}, u32[]{:S(2)}) collective-permute-start(bf16[720,512]{1,0:T(8,128)(2,1)S(1)} %collective-permute-done.3.refs_1_.near), channel_id=1, source_target_pairs={{0,32},{1,33},{2,34},{3,35},{4,36},{5,37},{6,38},{7,39},{8,40},{9,... | collective-permute-start | bytes 2211848 | tf_op jit(solution)/shard_map/near_to_core/ppermute | solution.py:570
  21.3 2.3 %copy-start = (s32[6,2048]{1,0:T(8,128)S(1)}, s32[6,2048]{1,0:T(8,128)}, u32[]{:S(2)}) copy-start(s32[6,2048]{1,0:T(8,128)} %dofs.1) | copy-start | bytes 147460
  21.3 2.3 %copy-start.1 = (f32[6,2048]{1,0:T(8,128)S(1)}, f32[6,2048]{1,0:T(8,128)}, u32[]{:S(2)}) copy-start(f32[6,2048]{1,0:T(8,128)} %coef) | copy-start | bytes 147460
  22.6 8.8 %collective-permute-start.1 = (bf16[128,1024]{1,0:T(8,128)(2,1)S(1)}, bf16[128,1024]{1,0:T(8,128)(2,1)S(1)}, u32[]{:S(2)}, u32[]{:S(2)}) collective-permute-start(bf16[128,1024]{1,0:T(8,128)(2,1)S(1)} %get-tuple-element.78), channel_id=1, source_target_pairs={{0,1},{1,0},{2,3},{3,2},{4,5},{5,4},{6,7},{7,6},{8,9},{9,8},{10,11... | collective-permute-start | bytes 786440 | tf_op jit(solution)/shard_map/terms_pair/ppermute | solution.py:570
  32.6 10.2 %collective-permute-start.2 = (bf16[64,2048]{1,0:T(8,128)(2,1)S(1)}, bf16[64,2048]{1,0:T(8,128)(2,1)S(1)}, u32[]{:S(2)}, u32[]{:S(2)}) collective-permute-start(bf16[64,2048]{1,0:T(8,128)(2,1)S(1)} %get-tuple-element.84), channel_id=1, source_target_pairs={{0,3},{1,2},{2,1},{3,0},{4,7},{5,6},{6,5},{7,4},{8,11},{9,10},{10,... | collective-permute-start | bytes 786440 | tf_op jit(solution)/shard_map/panels_ring/ppermute | solution.py:570
  34.4 19.8 %collective-permute-start.10 = (bf16[320,512]{1,0:T(8,128)(2,1)S(1)}, bf16[320,512]{1,0:T(8,128)(2,1)S(1)}, u32[]{:S(2)}, u32[]{:S(2)}) collective-permute-start(bf16[320,512]{1,0:T(8,128)(2,1)S(1)} %get-tuple-element.95), channel_id=1, source_target_pairs={{12,0},{13,1},{14,2},{15,3},{44,56},{45,57},{46,58},{47,59},{76,64... | collective-permute-start | bytes 983048 | tf_op jit(solution)/shard_map/factor_top/ppermute | solution.py:570
  35.7 18.5 %collective-permute-start.8 = (bf16[320,512]{1,0:T(8,128)(2,1)S(1)}, bf16[320,512]{1,0:T(8,128)(2,1)S(1)}, u32[]{:S(2)}, u32[]{:S(2)}) collective-permute-start(bf16[320,512]{1,0:T(8,128)(2,1)S(1)} %get-tuple-element.95), channel_id=1, source_target_pairs={{4,0},{5,1},{6,2},{7,3},{12,8},{13,9},{14,10},{15,11},{20,16},{21,... | collective-permute-start | bytes 983048 | tf_op jit(solution)/shard_map/factors_up/ppermute | solution.py:570
  43.6 10.6 %collective-permute-start.6 = (bf16[64,1536]{1,0:T(8,128)(2,1)S(1)}, bf16[64,1536]{1,0:T(8,128)(2,1)S(1)}, u32[]{:S(2)}, u32[]{:S(2)}) collective-permute-start(bf16[64,1536]{1,0:T(8,128)(2,1)S(1)} %get-tuple-element.93.mine), channel_id=1, source_target_pairs={{4,0},{5,1},{6,2},{7,3},{12,8},{13,9},{14,10},{15,11},{20,16},{21,... | collective-permute-start | bytes 589832 | tf_op jit(solution)/shard_map/panels_z1/ppermute | solution.py:570
  44.9 9.3 %collective-permute-start.9 = (bf16[144,512]{1,0:T(8,128)(2,1)S(1)}, bf16[144,512]{1,0:T(8,128)(2,1)S(1)}, u32[]{:S(2)}, u32[]{:S(2)}) collective-permute-start(bf16[144,512]{1,0:T(8,128)(2,1)S(1)} %get-tuple-element.96), channel_id=1, source_target_pairs={{4,0},{5,1},{6,2},{7,3},{12,8},{13,9},{14,10},{15,11},{20,16},{21,... | collective-permute-start | bytes 442376 | tf_op jit(solution)/shard_map/factors_up_rest/ppermute | solution.py:570
  46.2 36.4 %collective-permute-start.17 = (bf16[976,512]{1,0:T(8,128)(2,1)S(1)}, bf16[976,512]{1,0:T(8,128)(2,1)S(1)}, u32[]{:S(2)}, u32[]{:S(2)}) collective-permute-start(bf16[976,512]{1,0:T(8,128)(2,1)S(1)} %get-tuple-element.115.refs_0_), channel_id=1, source_target_pairs={{0,1},{2,3},{4,5},{6,7},{8,9},{10,11},{12,13},{14,15},{16,17},{18,... | collective-permute-start | bytes 2998280 | tf_op jit(solution)/shard_map/first_factor_to_odd/ppermute | solution.py:570
  54.2 7.2 %collective-permute-start.11 = (bf16[320,512]{1,0:T(8,128)(2,1)S(1)}, bf16[320,512]{1,0:T(8,128)(2,1)S(1)}, u32[]{:S(2)}, u32[]{:S(2)}) collective-permute-start(bf16[320,512]{1,0:T(8,128)(2,1)S(1)} %collective-permute-done.8.refs_0_), channel_id=1, source_target_pairs={{0,32},{1,33},{2,34},{3,35},{4,36},{5,37},{6,38},{7,39},{8,40},{9,... | collective-permute-start | bytes 983048 | tf_op jit(solution)/shard_map/up_to_core/ppermute | solution.py:570
  55.8 5.6 %collective-permute-start.13 = (bf16[320,512]{1,0:T(8,128)(2,1)S(1)}, bf16[320,512]{1,0:T(8,128)(2,1)S(1)}, u32[]{:S(2)}, u32[]{:S(2)}) collective-permute-start(bf16[320,512]{1,0:T(8,128)(2,1)S(1)} %collective-permute-done.10.refs_2_), channel_id=1, source_target_pairs={{0,32},{1,33},{2,34},{3,35},{4,36},{5,37},{6,38},{7,39},{8,40},{9,... | collective-permute-start | bytes 983048 | tf_op jit(solution)/shard_map/last_to_core/ppermute | solution.py:570
  55.9 5.5 %collective-permute-start.12 = (bf16[144,512]{1,0:T(8,128)(2,1)S(1)}, bf16[144,512]{1,0:T(8,128)(2,1)S(1)}, u32[]{:S(2)}, u32[]{:S(2)}) collective-permute-start(bf16[144,512]{1,0:T(8,128)(2,1)S(1)} %collective-permute-done.9.refs_1_), channel_id=1, source_target_pairs={{0,32},{1,33},{2,34},{3,35},{4,36},{5,37},{6,38},{7,39},{8,40},{9,... | collective-permute-start | bytes 442376 | tf_op jit(solution)/shard_map/rest_to_core/ppermute | solution.py:570
  57.0 8.5 %collective-permute-start.7 = (bf16[64,1024]{1,0:T(8,128)(2,1)S(1)}, bf16[64,1024]{1,0:T(8,128)(2,1)S(1)}, u32[]{:S(2)}, u32[]{:S(2)}) collective-permute-start(bf16[64,1024]{1,0:T(8,128)(2,1)S(1)} %get-tuple-element.94.mine), channel_id=1, source_target_pairs={{0,8},{1,9},{2,10},{3,11},{8,0},{9,1},{10,2},{11,3},{16,24},{17,25... | collective-permute-start | bytes 393224 | tf_op jit(solution)/shard_map/panels_z2/ppermute | solution.py:570
  66.1 9.0 %collective-permute-start.14 = (bf16[64,512]{1,0:T(8,128)(2,1)S(1)}, bf16[64,512]{1,0:T(8,128)(2,1)S(1)}, u32[]{:S(2)}, u32[]{:S(2)}) collective-permute-start(bf16[64,512]{1,0:T(8,128)(2,1)S(1)} %get-tuple-element.110.mine), channel_id=1, source_target_pairs={{0,24},{1,25},{2,26},{3,27},{8,16},{9,17},{10,18},{11,19},{16,8},{... | collective-permute-start | bytes 196616 | tf_op jit(solution)/shard_map/panels_z3/ppermute | solution.py:570
  76.3 4.7 %collective-permute-start.15 = (bf16[64,1536]{1,0:T(8,128)(2,1)S(1)}, bf16[64,1536]{1,0:T(8,128)(2,1)S(1)}, u32[]{:S(2)}, u32[]{:S(2)}) collective-permute-start(bf16[64,1536]{1,0:T(8,128)(2,1)S(1)} %shard_map.136.mine), channel_id=1, source_target_pairs={{0,4},{1,5},{2,6},{3,7},{8,12},{9,13},{10,14},{11,15},{16,20},{17,... | collective-permute-start | bytes 589832 | tf_op jit(solution)/shard_map/down_z1/ppermute | solution.py:570
  82.0 7.7 %collective-permute-start.16 = (bf16[64,2048]{1,0:T(8,128)(2,1)S(1)}, bf16[64,2048]{1,0:T(8,128)(2,1)S(1)}, u32[]{:S(2)}, u32[]{:S(2)}) collective-permute-start(bf16[64,2048]{1,0:T(8,128)(2,1)S(1)} %shard_map.137.mine), channel_id=1, source_target_pairs={{0,3},{1,2},{2,1},{3,0},{4,7},{5,6},{6,5},{7,4},{8,11},{9,10},{10,... | collective-permute-start | bytes 786440 | tf_op jit(solution)/shard_map/down_ring/ppermute | solution.py:570
  91.7 5.4 %collective-permute-start.18 = (bf16[128,640]{1,0:T(8,128)(2,1)S(1)}, bf16[128,640]{1,0:T(8,128)(2,1)S(1)}, u32[]{:S(2)}, u32[]{:S(2)}) collective-permute-start(bf16[128,640]{1,0:T(8,128)(2,1)S(1)} %get-tuple-element.123), channel_id=1, source_target_pairs={{0,1},{1,0},{2,3},{3,2},{4,5},{5,4},{6,7},{7,6},{8,9},{9,8},{10,11... | collective-permute-start | bytes 491528 | tf_op jit(solution)/shard_map/rows_back/ppermute | solution.py:570
  97.1 10.4 %copy-start.3 = (bf16[128,512]{1,0:T(8,128)(2,1)S(1)}, bf16[128,512]{1,0:T(8,128)(2,1)}, u32[]{:S(2)}) copy-start(bf16[128,512]{1,0:T(8,128)(2,1)} %get-tuple-element.124) | copy-start | bytes 393220
  100.0 19.1 %all-to-all-start = ((bf16[32,16,256]{2,1,0:T(8,128)(2,1)}), bf16[32,16,256]{2,1,0:T(8,128)(2,1)S(1)}, u32[]{:S(2)}, u32[]{:S(2)}) async-start(bf16[32,16,256]{2,1,0:T(8,128)(2,1)} %bitcast.9), calls=%async_computation | async-start | bytes 524288 | tf_op jit(solution)/shard_map/all_to_all | solution.py:788
  107.5 5.4 %collective-permute-start.19 = (bf16[128,512]{1,0:T(8,128)(2,1)S(1)}, bf16[128,512]{1,0:T(8,128)(2,1)S(1)}, u32[]{:S(2)}, u32[]{:S(2)}) collective-permute-start(bf16[128,512]{1,0:T(8,128)(2,1)S(1)} %copy-done.3), channel_id=1, source_target_pairs={{0,1},{1,0},{2,3},{3,2},{4,5},{5,4},{6,7},{7,6},{8,9},{9,8},{10,11... | collective-permute-start | bytes 393224 | tf_op jit(solution)/shard_map/sep_back/ppermute | solution.py:570
  112.8 0.7 copy-start.2

commit v5 on v4

--- a/solution.py
+++ b/solution.py
@@ -118,29 +118,53 @@
     return dot(back, factor[0:PANEL]).astype(BF)
 
 
-def pack_factor(place, inv, cpl, sep_idx, out, up, codes, sep_v, sems):
+def pack_factor(place, inv, cpl, sep_idx, up, codes, sep_v, sems):
     load = pltpu.make_async_copy(sep_idx.at[0], sep_v, sems.at[0])
-    copies = []
-    for n, (dst, slots) in enumerate(((up, 3), (out, 4))):
-        for i, (r, c, pr, pc) in enumerate(triangle_blocks()):
-            copies.append(pltpu.make_async_copy(inv.at[r, c], dst.at[pr, pc], sems.at[1 + 6 * n + i]))
-        copies.append(
-            pltpu.make_async_copy(cpl.at[0 : slots * U], dst.at[CPL0 : packed_rows(slots)], sems.at[6 + 6 * n])
-        )
+    copies = [
+        pltpu.make_async_copy(inv.at[r, c], up.at[pr, pc], sems.at[1 + i])
+        for i, (r, c, pr, pc) in enumerate(triangle_blocks())
+    ]
+    copies.append(pltpu.make_async_copy(cpl.at[0 : 3 * U], up.at[CPL0 : packed_rows(3)], sems.at[6]))
     load.start()
     for copy in copies:
         copy.start()
     codes[...] = jnp.zeros_like(codes)
-    out[packed_rows(4) :] = jnp.zeros((128, PANEL), BF)
     load.wait()
     value = sep_v[...]
     codes[0 : LEVELS - 1, 0:U] = (value >> 4).astype(F32)
     codes[0 : LEVELS - 1, U : 2 * U] = (value & 15).astype(F32)
-    coded = codes[...].astype(BF)
-    out[IDX] = coded
-    up[IDX] = coded
+    up[IDX] = codes[...].astype(BF)
     for copy in copies:
         copy.wait()
+
+
+def load_first(inv, cpl, out, sems):
+    copies = [
+        pltpu.make_async_copy(inv, out.at[0:PANEL], sems.at[0]),
+        pltpu.make_async_copy(cpl, out.at[PANEL : 2 * PANEL], sems.at[1]),
+    ]
+    for copy in copies:
+        copy.start()
+    out[2 * PANEL :] = jnp.zeros((128, PANEL), BF)
+    for copy in copies:
+        copy.wait()
+
+
+def pick_first(place, own, far, factor, sems):
+    even = place[1] % 2 == 0
+    copies = [
+        pltpu.make_async_copy(source, factor, sems.at[0]) for source in (own, far)
+    ]
+
+    @pl.when(even)
+    def _():
+        copies[0].start()
+
+    @pl.when(jnp.logical_not(even))
+    def _():
+        copies[1].start()
+
+    copies[0].wait()
 
 
 def leaf_first(
@@ -148,7 +172,7 @@
     rhs_v, rsep_v, leaf_v, sep_v, codes, sems
 ):
     loads = [
-        pltpu.make_async_copy(leaf_idx.at[0], leaf_v, sems.at[0]),
+        pltpu.make_async_copy(leaf_idx, leaf_v, sems.at[0]),
         pltpu.make_async_copy(sep_idx.at[0], sep_v, sems.at[1]),
         pltpu.make_async_copy(rhs, rhs_v, sems.at[2]),
     ]
@@ -160,11 +184,15 @@
     for load in loads:
         load.start()
     codes[...] = jnp.zeros_like(codes)
-    for ref, load, count, at in ((leaf_v, loads[0], LEVELS, 0), (sep_v, loads[1], LEVELS - 1, 32)):
-        load.wait()
-        value = ref[...]
-        codes[at : at + count] = (value >> 4).astype(F32)
-        codes[at + 16 : at + 16 + count] = (value & 15).astype(F32)
+    loads[0].wait()
+    for l in range(LEVELS):
+        value = leaf_v[l]
+        codes[l : l + 1] = (value >> 4).astype(F32)
+        codes[16 + l : 17 + l] = (value & 15).astype(F32)
+    loads[1].wait()
+    value = sep_v[...]
+    codes[32 : 32 + LEVELS - 1] = (value >> 4).astype(F32)
+    codes[48 : 48 + LEVELS - 1] = (value & 15).astype(F32)
     one[NC:] = codes[...].astype(BF)
     loads[2].wait()
     rhs_t = rhs_v[...].astype(F32).T.astype(BF)
@@ -320,7 +348,7 @@
     return jnp.where((y == 1) | (y == 2), 1, 0)
 
 
-def level_one(place, one, recv, terms, rhs, factor, own, hots, y_keep, passed, keep, send, y_all):
+def level_one(place, one, recv, terms, rhs, factor, hots, y_keep, passed, keep, send, y_all):
     even = place[1] % 2 == 0
     a, b, _ = pair_rows(place, one, recv)
     hots[...] = hot(jnp.concatenate([a[0], b[0]], axis=1))
@@ -337,7 +365,7 @@
     keep[:, 0:PANEL] = terms[mine]
     keep[:, PANEL:] = y_all[mine, PANEL:]
     y_keep[...] = y_all[mine, 0:PANEL]
-    passed[packed_rows(4) :] = y_all[theirs, 0:PANEL]
+    passed[2 * PANEL :] = y_all[theirs, 0:PANEL]
 
 
 def join_pair(place, keep, recv, hots, panel_keep, panel_send, panels):
@@ -387,16 +415,25 @@
     x_out[:, PANEL:] = x
 
 
-def level_one_back(
-    place, mine, recv, y_mine, passed, factor, first_hots, hots, rows_keep, rows_send, sep_keep, sep_send, x, sep_a, sep_b, sems
-):
+def level_one_back(place, mine, recv, y_mine, factor, first_hots, hots, x1_out, x, rows_send):
     side = place[1] // 2
     even = place[1] % 2 == 0
     x[pl.ds(pl.multiple_of(side * 64, 64), 64)] = mine[...]
     x[pl.ds(pl.multiple_of((1 - side) * 64, 64), 64)] = recv[...]
     above = [x[:, k * PANEL : (k + 1) * PANEL] for k in range(4)]
     ups = [hots[:, k * 3 * U + 2 * U : (k + 1) * 3 * U] for k in range(4)]
-    x1 = solve_back(factor, ups, jnp.where(even, y_mine[...], passed[packed_rows(4) :]), above)
+    x1 = solve_back(factor, ups, jnp.where(even, y_mine[...], factor[2 * PANEL :]), above)
+    x1_out[...] = x1
+    for l, value in enumerate([x1] + above):
+        pair = first_hots[...] if l == 0 else hots[:, (l - 1) * 3 * U : (l - 1) * 3 * U + 2 * U]
+        pair = jnp.where(even, pair[:, U:], pair[:, 0:U])
+        rows_send[:, l * U : (l + 1) * U] = dot(value, pair).astype(BF)
+
+
+def level_one_rest(place, x1_ref, x, first_hots, hots, rows_keep, sep_keep, sep_send, sep_a, sep_b, sems):
+    even = place[1] % 2 == 0
+    x1 = x1_ref[...]
+    above = [x[:, k * PANEL : (k + 1) * PANEL] for k in range(4)]
     level = jnp.where(place[1] < 2, 2, place[3])
     held = jnp.where(level == 0, jnp.zeros_like(x1), above[0])
     for k in (1, 2, 3):
@@ -411,32 +448,45 @@
         store.start()
     for l, value in enumerate([x1] + above):
         pair = first_hots[...] if l == 0 else hots[:, (l - 1) * 3 * U : (l - 1) * 3 * U + 2 * U]
-        both = dot(value, pair).astype(BF)
-        left, right = both[:, 0:U], both[:, U : 2 * U]
-        rows_keep[:, l * U : (l + 1) * U] = jnp.where(even, left, right)
-        rows_send[:, l * U : (l + 1) * U] = jnp.where(even, right, left)
+        pair = jnp.where(even, pair[:, 0:U], pair[:, U:])
+        rows_keep[:, l * U : (l + 1) * U] = dot(value, pair).astype(BF)
     for store in stores:
         store.wait()
 
 
-def leaf_backward(place, keep, recv, inv, cpl, yt, chosen, xt_out, picks_out, rows, sub, xt, picks, sems):
-    side = half_of(place)
-    rows[pl.ds(pl.multiple_of(side * 128, 128), 128)] = keep[...]
-    rows[pl.ds(pl.multiple_of((1 - side) * 128, 128), 128)] = recv[...]
-    total = yt[...].astype(F32)
+def leaf_half(rows, inv, cpl, yt, chosen):
+    total = yt.astype(F32)
     for l in range(LEVELS):
         total = total - dot(rows[:, l * U : (l + 1) * U], cpl[l])
-    sub[...] = total.astype(BF)
+    back = total.astype(BF)
+    parts = []
     for i in range(4):
         start = i * 256
-        xt[:, start : start + 256] = dot(sub[:, start:], inv[start:, start : start + 256]).astype(BF)
-    stores = [pltpu.make_async_copy(xt, xt_out, sems.at[2])]
+        parts.append(dot(back[:, start:], inv[start:, start : start + 256]).astype(BF))
+    xt = jnp.concatenate(parts, axis=1)
+    return xt, dot_t(chosen[...], xt).astype(BF)
+
+
+def leaf_mine(place, keep, inv, cpl, yt, chosen, xt_out, picks_out):
+    side = half_of(place)
+    xt, picks = leaf_half(keep, inv, cpl, yt[pl.ds(pl.multiple_of(side * 128, 128), 128)], chosen)
+    xt_out[...] = xt
+    picks_out[...] = picks
+
+
+def leaf_other(place, recv, inv, cpl, yt, chosen, xt_mine, picks_mine, xt_out, picks_out, xt, picks, sems):
+    side = half_of(place)
+    mine = pl.ds(pl.multiple_of(side * 128, 128), 128)
+    other = pl.ds(pl.multiple_of((1 - side) * 128, 128), 128)
+    picks[:, mine] = picks_mine[...]
+    xt[mine] = xt_mine[...]
+    far, far_picks = leaf_half(recv, inv, cpl, yt[other], chosen)
+    picks[:, other] = far_picks
+    stores = [pltpu.make_async_copy(picks, picks_out, sems.at[0])]
     stores[0].start()
-    for i in range(2):
-        part = slice(i * 256, (i + 1) * 256)
-        picks[part] = dot_t(chosen[part], xt[...]).astype(BF)
-        stores.append(pltpu.make_async_copy(picks.at[part], picks_out.at[part], sems.at[i]))
-        stores[-1].start()
+    xt[other] = far
+    stores.append(pltpu.make_async_copy(xt, xt_out, sems.at[1]))
+    stores[1].start()
     for store in stores:
         store.wait()
 
@@ -578,12 +628,13 @@
     def to_odd(value):
         return route(value, lambda c, y, z: (c, y + 1, z) if y % 2 == 0 else None)
 
-    own, own_up = call(
+    sep_rows_flat = sep_cpl.reshape(4 * U, PANEL)
+    (own_up,) = call(
         pack_factor,
-        [pinned(packed_rows(4) + 128, PANEL), pinned(packed_rows(3), PANEL)],
-        [place, sep_inv, sep_cpl.reshape(4 * U, PANEL), sep_idx],
+        [pinned(packed_rows(3), PANEL)],
+        [place, sep_inv, sep_rows_flat, sep_idx],
         [SMEM, HBM, HBM, HBM],
-        [pltpu.VMEM((16, PANEL), F32), pltpu.VMEM((LEVELS - 1, U), jnp.int32), dma(13)],
+        [pltpu.VMEM((16, PANEL), F32), pltpu.VMEM((LEVELS - 1, U), jnp.int32), dma(7)],
     )
     with jax.named_scope("factors_to_neighbours"):
         near = route(own_up, lambda c, y, z: (c, y ^ (3 if c else 1), z) if y % 2 else None)
@@ -596,12 +647,12 @@
             pinned(LEAF, LEAF),
             pinned(LEVELS, U, LEAF),
         ],
-        [place, leaf_inv, rhs_leaf, leaf_cpl, rhs_sep, after(leaf_idx, own), sep_idx],
+        [after(place, own_up), leaf_inv, rhs_leaf, leaf_cpl, rhs_sep, leaf_idx.transpose(1, 0, 2), sep_idx],
         [SMEM] + [HBM] * 6,
         [
             pltpu.VMEM((LEAF, NC), BF),
             pltpu.VMEM((PANEL, NC), BF),
-            pltpu.VMEM((LEVELS, U), jnp.int32),
+            pltpu.VMEM((LEVELS, 1, U), jnp.int32),
             pltpu.VMEM((LEVELS - 1, U), jnp.int32),
             pltpu.VMEM((64, U), F32),
             dma(9),
@@ -631,29 +682,36 @@
             [VMEM] * 4,
         )
 
-    f1, _ = ready(4, lambda core, y, z: (core >= 0,), [after(own, one)])
+    (f1,) = call(
+        load_first,
+        [pinned(2 * PANEL + 128, PANEL)],
+        [after(sep_inv, one), sep_rows_flat],
+        [HBM, HBM],
+        [dma(2)],
+    )
     near = after(near, recv, f1, terms)
     with jax.named_scope("factors_across"):
         far = route(near, lambda c, y, z: (c, y ^ (1 if c else 3), z) if y % 2 == 0 else None)
-    with jax.named_scope("near_to_core"):
-        near_o = swap_core(near)
     first = after(recv, f1)
     first_hots, y1, passed, keep, send = call(
         level_one,
         [
             pinned(PANEL, ONE),
             pinned(128, PANEL),
-            pinned(packed_rows(4) + 128, PANEL),
+            pinned(2 * PANEL + 128, PANEL),
             pinned(128, 2 * PANEL),
             pinned(128, 2 * PANEL),
         ],
-        [place, one, first, terms, rhs, f1, own],
-        [SMEM] + [VMEM] * 6,
+        [place, one, first, terms, rhs, f1],
+        [SMEM] + [VMEM] * 5,
         [pltpu.VMEM((NC, 2 * PANEL), BF)],
-        aliases={6: 2},
+        aliases={5: 2},
     )
     with jax.named_scope("terms_pair"):
         recv = swap(send, 1)
+    near = after(near, send)
+    with jax.named_scope("near_to_core"):
+        near_o = swap_core(near)
     chosen, weight = call(
         stay_plan,
         [pinned(32 * SLOTS, LEAF), stored(2, 64, 512)],
@@ -698,18 +756,18 @@
         [pltpu.VMEM((16, PANEL), BF), dma(9)],
     )
 
-    def next_up(value):
-        return route(value, lambda c, y, z: (c, y, (z + (1 if c else -1)) % DEPTH) if z % 2 else None)
+    def next_up(value, senders):
+        return route(value, lambda c, y, z: (c, y, z + (1 if c else -1)) if z in senders else None)
 
     with jax.named_scope("factors_up"):
-        up = next_up(top)
+        up = next_up(top, (1, 3, 5))
     with jax.named_scope("factor_top"):
         last = route(
             top,
             lambda c, y, z: (0, y, 0) if (c, z) == (0, 3) else (1, y, 6) if (c, z) == (1, 3) else None,
         )
     with jax.named_scope("factors_up_rest"):
-        rest = next_up(top_rest)
+        rest = next_up(top_rest, (1, 5))
     with jax.named_scope("first_factor_to_odd"):
         passed_far = to_odd(after(passed, f2))
     recv = after(recv, f2, h2, f3, h3)
@@ -750,41 +808,49 @@
     with jax.named_scope("down_ring"):
         recv = swap(x, 3)
     passed_far = after(passed_far, x)
-    f1, _ = ready(4, pick_one, [passed, passed_far])
+    (f1,) = call(
+        pick_first,
+        [pinned(2 * PANEL + 128, PANEL)],
+        [place, passed, passed_far],
+        [SMEM, ANY, ANY],
+        [dma(1)],
+    )
     recv = after(recv, f1)
-    rows_keep, rows_send, sep_keep, sep_send = call(
+    x1, x, rows_send = call(
         level_one_back,
-        [pinned(128, TERM), pinned(128, TERM), stored(128, PANEL), stored(128, PANEL)],
-        [place, x, recv, y1, passed_far, f1, first_hots, h1],
-        [SMEM] + [VMEM] * 7,
-        [
-            pltpu.VMEM((128, 4 * PANEL), BF),
-            pltpu.VMEM((128, PANEL), BF),
-            pltpu.VMEM((128, PANEL), BF),
-            dma(2),
-        ],
-        [VMEM, VMEM, HBM, HBM],
+        [pinned(128, PANEL), pinned(128, 4 * PANEL), pinned(128, TERM)],
+        [place, x, recv, y1, f1, first_hots, h1],
+        [SMEM] + [VMEM] * 6,
     )
     with jax.named_scope("rows_back"):
         recv = swap(rows_send, 1)
+    rows_keep, sep_keep, sep_send = call(
+        level_one_rest,
+        [pinned(128, TERM), stored(128, PANEL), stored(128, PANEL)],
+        [place, x1, x, first_hots, h1],
+        [SMEM] + [VMEM] * 4,
+        [pltpu.VMEM((128, PANEL), BF), pltpu.VMEM((128, PANEL), BF), dma(2)],
+        [VMEM, HBM, HBM],
+    )
+    xt_mine, picks_mine = call(
+        leaf_mine,
+        [pinned(128, LEAF), pinned(32 * SLOTS, 128)],
+        [place, rows_keep, inv_v, cpl_v, yt, chosen],
+        [SMEM] + [VMEM] * 5,
+    )
+    recv = after(recv, xt_mine)
     with jax.named_scope("sep_back"):
-        sep_recv = swap(after(sep_send, recv), 1)
+        sep_recv = swap(sep_send, 1)
     xt, picks = call(
-        leaf_backward,
+        leaf_other,
         [stored(NC, LEAF), stored(32 * SLOTS, NC)],
-        [place, rows_keep, recv, inv_v, cpl_v, yt, chosen],
-        [SMEM] + [VMEM] * 6,
-        [
-            pltpu.VMEM((NC, TERM), BF),
-            pltpu.VMEM((NC, LEAF), BF),
-            pltpu.VMEM((NC, LEAF), BF),
-            pltpu.VMEM((32 * SLOTS, NC), BF),
-            dma(3),
-        ],
+        [place, recv, inv_v, cpl_v, yt, chosen, xt_mine, picks_mine],
+        [SMEM] + [VMEM] * 7,
+        [pltpu.VMEM((NC, LEAF), BF), pltpu.VMEM((32 * SLOTS, NC), BF), dma(2)],
         [HBM, HBM],
         moved=14 * 10**6,
     )
-    sep_recv = after(sep_recv, picks)
+    picks, sep_recv = lax.optimization_barrier((picks, sep_recv))
     got = lax.all_to_all(
         picks.reshape(32, SLOTS, NC), rows_axis, 0, 0, tiled=True
     ).reshape(32 * SLOTS, NC)

time: 121 us -> 120 us (level)
  starting transfers between devices: 39.3 us -> 41.7 us
  waiting for transfers between devices: 43.6 us -> 41.2 us
  local copies, waits for them, and re-layouts: 1.95 us -> 0.02 us
    ppermute x20, waiting for transfers between devices: 40.9 us -> 32.5 us  [route(): return lax.ppermute(value, (cols_axis, rows_axis), pairs)]
    all_to_all x1, waiting for transfers between devices: 2.68 us -> 8.69 us  [on_device(): lax.all_to_all(picks.reshape(32, SLOTS, NC), rows_axis, 0, 0, tiled=True)]
    all_to_all x1, starting transfers between devices: 7.5 us -> 9.05 us  [on_device(): lax.all_to_all(picks.reshape(32, SLOTS, NC), rows_axis, 0, 0, tiled=True)]
    optimization_barrier x1 -> x0, local copies, waits for them, and re-layouts: 1.28 us -> none  [after(): return lax.optimization_barrier((value, *others))[0]]
    pallas_call x22 -> x24, Pallas kernels: 34.9 us -> 35.4 us  [call(): pl.pallas_call(body, out_shape=outs, in_specs=specs, out_specs=out_specs...]
  transfers between devices with their start and end apart: 21 -> 21, of which waited for: 11 -> 9; matrix products, arithmetic and copies ran while one was open for 1% -> 0% of each run, Pallas kernels for 22% -> 25%
where the time goes in v5:
time: 120 us; the launch traced here: 119 us
  starting transfers between devices  41.7 us (35%)
  waiting for transfers between devices  41.2 us (34%)
  Pallas kernels  35.4 us (30%)
  between operations  1.23 us (1%)
    pallas_call x24, Pallas kernels, call(): pl.pallas_call(body, out_shape=outs, in_specs=specs, out_specs=out_specs...  35.4 us
    ppermute x20, starting transfers between devices, route(): return lax.ppermute(value, (cols_axis, rows_axis), pairs)  32.6 us
    ppermute x20, waiting for transfers between devices, route(): return lax.ppermute(value, (cols_axis, rows_axis), pairs)  32.5 us
    all_to_all x1, starting transfers between devices, on_device(): lax.all_to_all(picks.reshape(32, SLOTS, NC), rows_axis, 0, 0, tiled=True)  9.05 us
    all_to_all x1, waiting for transfers between devices, on_device(): lax.all_to_all(picks.reshape(32, SLOTS, NC), rows_axis, 0, 0, tiled=True)  8.69 us
  transfers between devices with their start and end apart: 21, of which 9 were waited for; matrix products, arithmetic and copies ran while one was open for 0% of the time, Pallas kernels for 25%

profile of v5, /device:TPU:2, one launch (start us, length us, event | category | flops | bytes accessed | tf_op | source)
XLA Modules:
  0.0 119.5 jit_solution(8933376961407944190)
XLA Ops:
  0.8 1.8 %shard_map.121.refs_0_.own = bf16[720,512]{1,0:T(8,128)(2,1)S(1)} custom-call(s32[4]{0:T(128)S(1)} %pad_add_fusion.place, bf16[512,512]{1,0:T(8,128)(2,1)} %inv.4, bf16[512,512]{1,0:T(8,128)(2,1)} %bitcast.9, s32[1,4,128]{2,1,0:T(4,128)} %sep_idx.3), custom_call_target="tpu_custom_call" | custom-call | flops 100000000 | bytes 1000000 | tf_op jit(solution)/shard_map/pallas_call | solution.py:60
  3.9 3.9 %shard_map.122 = (bf16[256,1024]{1,0:T(8,128)(2,1)S(1)}, bf16[256,512]{1,0:T(8,128)(2,1)S(1)}, bf16[320,128]{1,0:T(8,128)(2,1)S(1)}, bf16[1024,1024]{1,0:T(8,128)(2,1)S(1)}, bf16[5,128,1024]{2,1,0:T(8,128)(2,1)S(1)}) custom-call(s32[4]{0:T(128)S(1)} %pad_add_fusion.place, bf16[1024,1024]{1,0:T(8,128)(2,1)} %inv.3, bf16[1024,256]{1,0:T(8,128)(2,1)} %rhs.1, ...), custom_call_target="tpu_custom_call" | custom-call | flops 100000000 | bytes 1000000 | tf_op jit(solution)/shard_map/pallas_call | solution.py:60
  7.7 2.8 %collective-permute-start = (bf16[320,128]{1,0:T(8,128)(2,1)S(1)}, bf16[320,128]{1,0:T(8,128)(2,1)S(1)}, u32[]{:S(2)}, u32[]{:S(2)}) collective-permute-start(bf16[320,128]{1,0:T(8,128)(2,1)S(1)} %get-tuple-element.71.one), channel_id=1, source_target_pairs={{0,1},{1,0},{2,3},{3,2},{4,5},{5,4},{6,7},{7,6},{8,9},{9,8},{10,11... | collective-permute-start | bytes 245768 | tf_op jit(solution)/shard_map/first_terms/ppermute | solution.py:620
  12.5 5.2 %collective-permute-done.recv.other = bf16[320,128]{1,0:T(8,128)(2,1)S(1)} collective-permute-done((bf16[320,128]{1,0:T(8,128)(2,1)S(1)}, bf16[320,128]{1,0:T(8,128)(2,1)S(1)}, u32[]{:S(2)}, u32[]{:S(2)}) %collective-permute-start) | collective-permute-done | bytes 81952 | tf_op jit(solution)/shard_map/first_terms/ppermute | solution.py:620
  17.7 3.2 %collective-permute-start.5 = (bf16[720,512]{1,0:T(8,128)(2,1)S(1)}, bf16[720,512]{1,0:T(8,128)(2,1)S(1)}, u32[]{:S(2)}, u32[]{:S(2)}) collective-permute-start(bf16[720,512]{1,0:T(8,128)(2,1)S(1)} %collective-permute-done.3.refs_1_.near), channel_id=1, source_target_pairs={{0,3},{2,1},{4,7},{6,5},{8,11},{10,9},{12,15},{14,13},{16,19},{18,... | collective-permute-start | bytes 2211848 | tf_op jit(solution)/shard_map/factors_across/ppermute | solution.py:620
  23.3 2.5 %shard_map.126 = (bf16[512,1024]{1,0:T(8,128)(2,1)S(1)}, bf16[2,64,512]{2,1,0:T(8,128)(2,1)}) custom-call(s32[4]{0:T(128)S(1)} %pad_add_fusion.place, s32[6,2048]{1,0:T(8,128)S(1)} %copy-done, f32[6,2048]{1,0:T(8,128)S(1)} %copy-done.1), custom_call_target="tpu_custom_call" | custom-call | flops 100000000 | bytes 1000000 | tf_op jit(solution)/shard_map/pallas_call | solution.py:60
  25.8 5.2 %collective-permute-done.1.recv = bf16[128,1024]{1,0:T(8,128)(2,1)S(1)} collective-permute-done((bf16[128,1024]{1,0:T(8,128)(2,1)S(1)}, bf16[128,1024]{1,0:T(8,128)(2,1)S(1)}, u32[]{:S(2)}, u32[]{:S(2)}) %collective-permute-start.1) | collective-permute-done | bytes 262176 | tf_op jit(solution)/shard_map/terms_pair/ppermute | solution.py:620
  32.8 1.3 %shard_map.130 = (bf16[768,512]{1,0:T(8,128)(2,1)S(1)}, bf16[512,256]{1,0:T(8,128)(2,1)S(1)}, bf16[320,512]{1,0:T(8,128)(2,1)S(1)}, bf16[144,512]{1,0:T(8,128)(2,1)S(1)}) custom-call(s32[4]{0:T(128)S(1)} %pad_add_fusion.place, bf16[720,512]{1,0:T(8,128)(2,1)S(1)} %shard_map.121.refs_0_.own, bf16[720,512]{1,0:T(8,128)(2,1)S(1)} %collective-permute-done.3.refs_1_.near, ...), custom_call_target="tpu_custom_call" | custom-call | flops 100000000 | bytes 1000000 | tf_op jit(solution)/shard_map/pallas_call | solution.py:60
  34.1 1.3 %collective-permute-start.10 = (bf16[320,512]{1,0:T(8,128)(2,1)S(1)}, bf16[320,512]{1,0:T(8,128)(2,1)S(1)}, u32[]{:S(2)}, u32[]{:S(2)}) collective-permute-start(bf16[320,512]{1,0:T(8,128)(2,1)S(1)} %get-tuple-element.95), channel_id=1, source_target_pairs={{12,0},{13,1},{14,2},{15,3},{44,56},{45,57},{46,58},{47,59},{76,64... | collective-permute-start | bytes 983048 | tf_op jit(solution)/shard_map/factor_top/ppermute | solution.py:620
  35.4 1.3 %collective-permute-start.8 = (bf16[320,512]{1,0:T(8,128)(2,1)S(1)}, bf16[320,512]{1,0:T(8,128)(2,1)S(1)}, u32[]{:S(2)}, u32[]{:S(2)}) collective-permute-start(bf16[320,512]{1,0:T(8,128)(2,1)S(1)} %get-tuple-element.95), channel_id=1, source_target_pairs={{4,0},{5,1},{6,2},{7,3},{12,8},{13,9},{14,10},{15,11},{20,16},{21,... | collective-permute-start | bytes 983048 | tf_op jit(solution)/shard_map/factors_up/ppermute | solution.py:620
  37.9 2.8 %collective-permute-start.17 = (bf16[1152,512]{1,0:T(8,128)(2,1)S(1)}, bf16[1152,512]{1,0:T(8,128)(2,1)S(1)}, u32[]{:S(2)}, u32[]{:S(2)}) collective-permute-start(bf16[1152,512]{1,0:T(8,128)(2,1)S(1)} %get-tuple-element.115.own), channel_id=1, source_target_pairs={{0,1},{2,3},{4,5},{6,7},{8,9},{10,11},{12,13},{14,15},{16,17},{18,... | collective-permute-start | bytes 3538952 | tf_op jit(solution)/shard_map/first_factor_to_odd/ppermute | solution.py:620
  42.6 1.3 %collective-permute-start.6 = (bf16[64,1536]{1,0:T(8,128)(2,1)S(1)}, bf16[64,1536]{1,0:T(8,128)(2,1)S(1)}, u32[]{:S(2)}, u32[]{:S(2)}) collective-permute-start(bf16[64,1536]{1,0:T(8,128)(2,1)S(1)} %get-tuple-element.93.mine), channel_id=1, source_target_pairs={{4,0},{5,1},{6,2},{7,3},{12,8},{13,9},{14,10},{15,11},{20,16},{21,... | collective-permute-start | bytes 589832 | tf_op jit(solution)/shard_map/panels_z1/ppermute | solution.py:620
  43.9 1.3 %collective-permute-start.9 = (bf16[144,512]{1,0:T(8,128)(2,1)S(1)}, bf16[144,512]{1,0:T(8,128)(2,1)S(1)}, u32[]{:S(2)}, u32[]{:S(2)}) collective-permute-start(bf16[144,512]{1,0:T(8,128)(2,1)S(1)} %get-tuple-element.96), channel_id=1, source_target_pairs={{4,0},{5,1},{6,2},{7,3},{20,16},{21,17},{22,18},{23,19},{36,40},{3... | collective-permute-start | bytes 442376 | tf_op jit(solution)/shard_map/factors_up_rest/ppermute | solution.py:620
  45.2 8.6 %collective-permute-done.9.refs_1_ = bf16[144,512]{1,0:T(8,128)(2,1)S(1)} collective-permute-done((bf16[144,512]{1,0:T(8,128)(2,1)S(1)}, bf16[144,512]{1,0:T(8,128)(2,1)S(1)}, u32[]{:S(2)}, u32[]{:S(2)}) %collective-permute-start.9) | collective-permute-done | bytes 147488 | tf_op jit(solution)/shard_map/factors_up_rest/ppermute | solution.py:620
  55.2 3.9 %collective-permute-start.7 = (bf16[64,1024]{1,0:T(8,128)(2,1)S(1)}, bf16[64,1024]{1,0:T(8,128)(2,1)S(1)}, u32[]{:S(2)}, u32[]{:S(2)}) collective-permute-start(bf16[64,1024]{1,0:T(8,128)(2,1)S(1)} %get-tuple-element.94.mine), channel_id=1, source_target_pairs={{0,8},{1,9},{2,10},{3,11},{8,0},{9,1},{10,2},{11,3},{16,24},{17,25... | collective-permute-start | bytes 393224 | tf_op jit(solution)/shard_map/panels_z2/ppermute | solution.py:620
  60.2 1.5 %shard_map.134 = (bf16[512,512]{1,0:T(8,128)(2,1)S(1)}, bf16[512,128]{1,0:T(8,128)(2,1)}) custom-call(s32[4]{0:T(128)S(1)} %pad_add_fusion.place, bf16[320,512]{1,0:T(8,128)(2,1)S(1)} %collective-permute-done.8.refs_0_, bf16[320,512]{1,0:T(8,128)(2,1)S(1)} %collective-permute-done.11.refs_2_.refs_1_, bf16[320,512]{1,0:T(8,128)(2,1)S(1)} %collective-permute-done.10.refs_2_, ...), custom_call_target="tpu_custom_call" | custom-call | flops 100000000 | bytes 1000000 | tf_op jit(solution)/shard_map/pallas_call | solution.py:60
  61.7 2.1 %collective-permute-done.7.recv = bf16[64,1024]{1,0:T(8,128)(2,1)S(1)} collective-permute-done((bf16[64,1024]{1,0:T(8,128)(2,1)S(1)}, bf16[64,1024]{1,0:T(8,128)(2,1)S(1)}, u32[]{:S(2)}, u32[]{:S(2)}) %collective-permute-start.7) | collective-permute-done | bytes 131104 | tf_op jit(solution)/shard_map/panels_z2/ppermute | solution.py:620
  64.4 5.8 %collective-permute-start.14 = (bf16[64,512]{1,0:T(8,128)(2,1)S(1)}, bf16[64,512]{1,0:T(8,128)(2,1)S(1)}, u32[]{:S(2)}, u32[]{:S(2)}) collective-permute-start(bf16[64,512]{1,0:T(8,128)(2,1)S(1)} %get-tuple-element.110.mine), channel_id=1, source_target_pairs={{0,24},{1,25},{2,26},{3,27},{8,16},{9,17},{10,18},{11,19},{16,8},{... | collective-permute-start | bytes 196616 | tf_op jit(solution)/shard_map/panels_z3/ppermute | solution.py:620
  70.3 2.4 %collective-permute-done.14.recv = bf16[64,512]{1,0:T(8,128)(2,1)S(1)} collective-permute-done((bf16[64,512]{1,0:T(8,128)(2,1)S(1)}, bf16[64,512]{1,0:T(8,128)(2,1)S(1)}, u32[]{:S(2)}, u32[]{:S(2)}) %collective-permute-start.14) | collective-permute-done | bytes 65568 | tf_op jit(solution)/shard_map/panels_z3/ppermute | solution.py:620
  74.0 1.3 %collective-permute-start.15 = (bf16[64,1536]{1,0:T(8,128)(2,1)S(1)}, bf16[64,1536]{1,0:T(8,128)(2,1)S(1)}, u32[]{:S(2)}, u32[]{:S(2)}) collective-permute-start(bf16[64,1536]{1,0:T(8,128)(2,1)S(1)} %shard_map.136.mine), channel_id=1, source_target_pairs={{0,4},{1,5},{2,6},{3,7},{8,12},{9,13},{10,14},{11,15},{16,20},{17,... | collective-permute-start | bytes 589832 | tf_op jit(solution)/shard_map/down_z1/ppermute | solution.py:620
  75.3 3.3 %collective-permute-done.15.recv = bf16[64,1536]{1,0:T(8,128)(2,1)S(1)} collective-permute-done((bf16[64,1536]{1,0:T(8,128)(2,1)S(1)}, bf16[64,1536]{1,0:T(8,128)(2,1)S(1)}, u32[]{:S(2)}, u32[]{:S(2)}) %collective-permute-start.15) | collective-permute-done | bytes 196640 | tf_op jit(solution)/shard_map/down_z1/ppermute | solution.py:620
  79.6 2.8 %collective-permute-start.16 = (bf16[64,2048]{1,0:T(8,128)(2,1)S(1)}, bf16[64,2048]{1,0:T(8,128)(2,1)S(1)}, u32[]{:S(2)}, u32[]{:S(2)}) collective-permute-start(bf16[64,2048]{1,0:T(8,128)(2,1)S(1)} %shard_map.137.mine), channel_id=1, source_target_pairs={{0,3},{1,2},{2,1},{3,0},{4,7},{5,6},{6,5},{7,4},{8,11},{9,10},{10,... | collective-permute-start | bytes 786440 | tf_op jit(solution)/shard_map/down_ring/ppermute | solution.py:620
  83.2 4.3 %collective-permute-done.16.recv = bf16[64,2048]{1,0:T(8,128)(2,1)S(1)} collective-permute-done((bf16[64,2048]{1,0:T(8,128)(2,1)S(1)}, bf16[64,2048]{1,0:T(8,128)(2,1)S(1)}, u32[]{:S(2)}, u32[]{:S(2)}) %collective-permute-start.16) | collective-permute-done | bytes 262176 | tf_op jit(solution)/shard_map/down_ring/ppermute | solution.py:620
  87.5 1.5 %shard_map.139 = (bf16[128,512]{1,0:T(8,128)(2,1)S(1)}, bf16[128,2048]{1,0:T(8,128)(2,1)S(1)}, bf16[128,640]{1,0:T(8,128)(2,1)S(1)}) custom-call(s32[4]{0:T(128)S(1)} %pad_add_fusion.place, bf16[64,2048]{1,0:T(8,128)(2,1)S(1)} %shard_map.137.mine, bf16[64,2048]{1,0:T(8,128)(2,1)S(1)} %collective-permute-done.16.recv, ...), custom_call_target="tpu_custom_call" | custom-call | flops 100000000 | bytes 1000000 | tf_op jit(solution)/shard_map/pallas_call | solution.py:60
  89.0 1.5 %shard_map.140 = (bf16[128,640]{1,0:T(8,128)(2,1)S(1)}, bf16[128,512]{1,0:T(8,128)(2,1)}, bf16[128,512]{1,0:T(8,128)(2,1)}) custom-call(s32[4]{0:T(128)S(1)} %pad_add_fusion.place, bf16[128,512]{1,0:T(8,128)(2,1)S(1)} %get-tuple-element.120.x1_ref, bf16[128,2048]{1,0:T(8,128)(2,1)S(1)} %get-tuple-element.121.x, ...), custom_call_target="tpu_custom_call" | custom-call | flops 100000000 | bytes 1000000 | tf_op jit(solution)/shard_map/pallas_call | solution.py:60
  90.5 2.1 %collective-permute-start.19 = (bf16[128,512]{1,0:T(8,128)(2,1)}, bf16[128,512]{1,0:T(8,128)(2,1)S(1)}, u32[]{:S(2)}, u32[]{:S(2)}) collective-permute-start(bf16[128,512]{1,0:T(8,128)(2,1)} %get-tuple-element.130), channel_id=1, source_target_pairs={{0,1},{1,0},{2,3},{3,2},{4,5},{5,4},{6,7},{7,6},{8,9},{9,8},{10,11... | collective-permute-start | bytes 393224 | tf_op jit(solution)/shard_map/sep_back/ppermute | solution.py:620
  92.6 1.7 %shard_map.141 = (bf16[128,1024]{1,0:T(8,128)(2,1)S(1)}, bf16[512,128]{1,0:T(8,128)(2,1)S(1)}) custom-call(s32[4]{0:T(128)S(1)} %pad_add_fusion.place, bf16[128,640]{1,0:T(8,128)(2,1)S(1)} %get-tuple-element.124.keep, bf16[1024,1024]{1,0:T(8,128)(2,1)S(1)} %get-tuple-element.125.inv, bf16[5,128,1024]{2,1,0:T(8,128)(2,1)S(1)} %get-tuple-element.75.cpl_v.cpl, ...), custom_call_target="tpu_custom_call" | custom-call | flops 100000000 | bytes 1000000 | tf_op jit(solution)/shard_map/pallas_call | solution.py:60
  94.4 2.6 %shard_map.142 = (bf16[256,1024]{1,0:T(8,128)(2,1)}, bf16[512,256]{1,0:T(8,128)(2,1)}) custom-call(s32[4]{0:T(128)S(1)} %pad_add_fusion.place, bf16[128,640]{1,0:T(8,128)(2,1)S(1)} %collective-permute-done.18.recv, bf16[1024,1024]{1,0:T(8,128)(2,1)S(1)} %get-tuple-element.125.inv, bf16[5,128,1024]{2,1,0:T(8,128)(2,1)S(1)} %get-tuple-element.75.cpl_v.cpl, ...), custom_call_target="tpu_custom_call" | custom-call | flops 100000000 | bytes 14000000 | tf_op jit(solution)/shard_map/pallas_call | solution.py:60
  97.0 9.1 %all-to-all-start = ((bf16[32,16,256]{2,1,0:T(8,128)(2,1)}), bf16[32,16,256]{2,1,0:T(8,128)(2,1)S(1)}, u32[]{:S(2)}, u32[]{:S(2)}) async-start(bf16[32,16,256]{2,1,0:T(8,128)(2,1)} %bitcast.11), calls=%async_computation | async-start | bytes 524288 | tf_op jit(solution)/shard_map/all_to_all | solution.py:854
  106.0 2.8 %shard_map.143 = (bf16[512,256]{1,0:T(8,128)(2,1)}, bf16[1024,256]{1,0:T(8,128)(2,1)}) custom-call(s32[4]{0:T(128)S(1)} %pad_add_fusion.place, bf16[128,512]{1,0:T(8,128)(2,1)} %get-tuple-element.122.keep, bf16[128,512]{1,0:T(8,128)(2,1)} %copy-done.2, bf16[256,1024]{1,0:T(8,128)(2,1)} %get-tuple-element.132.xt), custom_call_target="tpu_custom_call" | custom-call | flops 100000000 | bytes 1000000 | tf_op jit(solution)/shard_map/pallas_call | solution.py:60
  108.9 8.7 %all-to-all-done = bf16[32,16,256]{2,1,0:T(8,128)(2,1)S(1)} async-done(((bf16[32,16,256]{2,1,0:T(8,128)(2,1)}), bf16[32,16,256]{2,1,0:T(8,128)(2,1)S(1)}, u32[]{:S(2)}, u32[]{:S(2)}) %all-to-all-start) | async-done | bytes 262176 | tf_op jit(solution)/shard_map/all_to_all | solution.py:854
  117.6 1.7 %shard_map.144 = f32[64,256]{1,0:T(8,128)} custom-call(bf16[2,64,512]{2,1,0:T(8,128)(2,1)} %get-tuple-element.135.weight, bf16[512,256]{1,0:T(8,128)(2,1)S(1)} %bitcast.8), custom_call_target="tpu_custom_call" | custom-call | flops 100000000 | bytes 1000000 | tf_op jit(solution)/shard_map/pallas_call | solution.py:60
  (41 shorter events, 16.8 us)
Async XLA Ops:
  2.6 15.1 %collective-permute-start.3 = (bf16[720,512]{1,0:T(8,128)(2,1)S(1)}, bf16[720,512]{1,0:T(8,128)(2,1)S(1)}, u32[]{:S(2)}, u32[]{:S(2)}) collective-permute-start(bf16[720,512]{1,0:T(8,128)(2,1)S(1)} %shard_map.121.refs_0_.own), channel_id=1, source_target_pairs={{1,0},{3,2},{5,4},{7,6},{9,8},{11,10},{13,12},{15,14},{17,16},{19,... | collective-permute-start | bytes 2211848 | tf_op jit(solution)/shard_map/factors_to_neighbours/ppermute | solution.py:620
  7.7 9.9 %collective-permute-start = (bf16[320,128]{1,0:T(8,128)(2,1)S(1)}, bf16[320,128]{1,0:T(8,128)(2,1)S(1)}, u32[]{:S(2)}, u32[]{:S(2)}) collective-permute-start(bf16[320,128]{1,0:T(8,128)(2,1)S(1)} %get-tuple-element.71.one), channel_id=1, source_target_pairs={{0,1},{1,0},{2,3},{3,2},{4,5},{5,4},{6,7},{7,6},{8,9},{9,8},{10,11... | collective-permute-start | bytes 245768 | tf_op jit(solution)/shard_map/first_terms/ppermute | solution.py:620
  17.7 15.1 %collective-permute-start.5 = (bf16[720,512]{1,0:T(8,128)(2,1)S(1)}, bf16[720,512]{1,0:T(8,128)(2,1)S(1)}, u32[]{:S(2)}, u32[]{:S(2)}) collective-permute-start(bf16[720,512]{1,0:T(8,128)(2,1)S(1)} %collective-permute-done.3.refs_1_.near), channel_id=1, source_target_pairs={{0,3},{2,1},{4,7},{6,5},{8,11},{10,9},{12,15},{14,13},{16,19},{18,... | collective-permute-start | bytes 2211848 | tf_op jit(solution)/shard_map/factors_across/ppermute | solution.py:620
  22.2 1.1 copy-start
  22.2 1.1 copy-start.1
  22.2 10.6 %collective-permute-start.4 = (bf16[720,512]{1,0:T(8,128)(2,1)S(1)}, bf16[720,512]{1,0:T(8,128)(2,1)S(1)}, u32[]{:S(2)}, u32[]{:S(2)}) collective-permute-start(bf16[720,512]{1,0:T(8,128)(2,1)S(1)} %collective-permute-done.3.refs_1_.near), channel_id=1, source_target_pairs={{0,32},{1,33},{2,34},{3,35},{4,36},{5,37},{6,38},{7,39},{8,40},{9,... | collective-permute-start | bytes 2211848 | tf_op jit(solution)/shard_map/near_to_core/ppermute | solution.py:620
  22.3 8.7 %collective-permute-start.1 = (bf16[128,1024]{1,0:T(8,128)(2,1)S(1)}, bf16[128,1024]{1,0:T(8,128)(2,1)S(1)}, u32[]{:S(2)}, u32[]{:S(2)}) collective-permute-start(bf16[128,1024]{1,0:T(8,128)(2,1)S(1)} %get-tuple-element.78), channel_id=1, source_target_pairs={{0,1},{1,0},{2,3},{3,2},{4,5},{5,4},{6,7},{7,6},{8,9},{9,8},{10,11... | collective-permute-start | bytes 786440 | tf_op jit(solution)/shard_map/terms_pair/ppermute | solution.py:620
  32.2 9.7 %collective-permute-start.2 = (bf16[64,2048]{1,0:T(8,128)(2,1)S(1)}, bf16[64,2048]{1,0:T(8,128)(2,1)S(1)}, u32[]{:S(2)}, u32[]{:S(2)}) collective-permute-start(bf16[64,2048]{1,0:T(8,128)(2,1)S(1)} %get-tuple-element.84), channel_id=1, source_target_pairs={{0,3},{1,2},{2,1},{3,0},{4,7},{5,6},{6,5},{7,4},{8,11},{9,10},{10,... | collective-permute-start | bytes 786440 | tf_op jit(solution)/shard_map/panels_ring/ppermute | solution.py:620
  34.1 19.7 %collective-permute-start.10 = (bf16[320,512]{1,0:T(8,128)(2,1)S(1)}, bf16[320,512]{1,0:T(8,128)(2,1)S(1)}, u32[]{:S(2)}, u32[]{:S(2)}) collective-permute-start(bf16[320,512]{1,0:T(8,128)(2,1)S(1)} %get-tuple-element.95), channel_id=1, source_target_pairs={{12,0},{13,1},{14,2},{15,3},{44,56},{45,57},{46,58},{47,59},{76,64... | collective-permute-start | bytes 983048 | tf_op jit(solution)/shard_map/factor_top/ppermute | solution.py:620
  35.4 18.4 %collective-permute-start.8 = (bf16[320,512]{1,0:T(8,128)(2,1)S(1)}, bf16[320,512]{1,0:T(8,128)(2,1)S(1)}, u32[]{:S(2)}, u32[]{:S(2)}) collective-permute-start(bf16[320,512]{1,0:T(8,128)(2,1)S(1)} %get-tuple-element.95), channel_id=1, source_target_pairs={{4,0},{5,1},{6,2},{7,3},{12,8},{13,9},{14,10},{15,11},{20,16},{21,... | collective-permute-start | bytes 983048 | tf_op jit(solution)/shard_map/factors_up/ppermute | solution.py:620
  37.9 44.5 %collective-permute-start.17 = (bf16[1152,512]{1,0:T(8,128)(2,1)S(1)}, bf16[1152,512]{1,0:T(8,128)(2,1)S(1)}, u32[]{:S(2)}, u32[]{:S(2)}) collective-permute-start(bf16[1152,512]{1,0:T(8,128)(2,1)S(1)} %get-tuple-element.115.own), channel_id=1, source_target_pairs={{0,1},{2,3},{4,5},{6,7},{8,9},{10,11},{12,13},{14,15},{16,17},{18,... | collective-permute-start | bytes 3538952 | tf_op jit(solution)/shard_map/first_factor_to_odd/ppermute | solution.py:620
  42.6 11.2 %collective-permute-start.6 = (bf16[64,1536]{1,0:T(8,128)(2,1)S(1)}, bf16[64,1536]{1,0:T(8,128)(2,1)S(1)}, u32[]{:S(2)}, u32[]{:S(2)}) collective-permute-start(bf16[64,1536]{1,0:T(8,128)(2,1)S(1)} %get-tuple-element.93.mine), channel_id=1, source_target_pairs={{4,0},{5,1},{6,2},{7,3},{12,8},{13,9},{14,10},{15,11},{20,16},{21,... | collective-permute-start | bytes 589832 | tf_op jit(solution)/shard_map/panels_z1/ppermute | solution.py:620
  43.9 9.9 %collective-permute-start.9 = (bf16[144,512]{1,0:T(8,128)(2,1)S(1)}, bf16[144,512]{1,0:T(8,128)(2,1)S(1)}, u32[]{:S(2)}, u32[]{:S(2)}) collective-permute-start(bf16[144,512]{1,0:T(8,128)(2,1)S(1)} %get-tuple-element.96), channel_id=1, source_target_pairs={{4,0},{5,1},{6,2},{7,3},{20,16},{21,17},{22,18},{23,19},{36,40},{3... | collective-permute-start | bytes 442376 | tf_op jit(solution)/shard_map/factors_up_rest/ppermute | solution.py:620
  53.8 5.3 %collective-permute-start.11 = (bf16[320,512]{1,0:T(8,128)(2,1)S(1)}, bf16[320,512]{1,0:T(8,128)(2,1)S(1)}, u32[]{:S(2)}, u32[]{:S(2)}) collective-permute-start(bf16[320,512]{1,0:T(8,128)(2,1)S(1)} %collective-permute-done.8.refs_0_), channel_id=1, source_target_pairs={{0,32},{1,33},{2,34},{3,35},{4,36},{5,37},{6,38},{7,39},{8,40},{9,... | collective-permute-start | bytes 983048 | tf_op jit(solution)/shard_map/up_to_core/ppermute | solution.py:620
  53.9 5.2 %collective-permute-start.13 = (bf16[320,512]{1,0:T(8,128)(2,1)S(1)}, bf16[320,512]{1,0:T(8,128)(2,1)S(1)}, u32[]{:S(2)}, u32[]{:S(2)}) collective-permute-start(bf16[320,512]{1,0:T(8,128)(2,1)S(1)} %collective-permute-done.10.refs_2_), channel_id=1, source_target_pairs={{0,32},{1,33},{2,34},{3,35},{4,36},{5,37},{6,38},{7,39},{8,40},{9,... | collective-permute-start | bytes 983048 | tf_op jit(solution)/shard_map/last_to_core/ppermute | solution.py:620
  54.4 4.7 %collective-permute-start.12 = (bf16[144,512]{1,0:T(8,128)(2,1)S(1)}, bf16[144,512]{1,0:T(8,128)(2,1)S(1)}, u32[]{:S(2)}, u32[]{:S(2)}) collective-permute-start(bf16[144,512]{1,0:T(8,128)(2,1)S(1)} %collective-permute-done.9.refs_1_), channel_id=1, source_target_pairs={{0,32},{1,33},{2,34},{3,35},{4,36},{5,37},{6,38},{7,39},{8,40},{9,... | collective-permute-start | bytes 442376 | tf_op jit(solution)/shard_map/rest_to_core/ppermute | solution.py:620
  55.2 8.6 %collective-permute-start.7 = (bf16[64,1024]{1,0:T(8,128)(2,1)S(1)}, bf16[64,1024]{1,0:T(8,128)(2,1)S(1)}, u32[]{:S(2)}, u32[]{:S(2)}) collective-permute-start(bf16[64,1024]{1,0:T(8,128)(2,1)S(1)} %get-tuple-element.94.mine), channel_id=1, source_target_pairs={{0,8},{1,9},{2,10},{3,11},{8,0},{9,1},{10,2},{11,3},{16,24},{17,25... | collective-permute-start | bytes 393224 | tf_op jit(solution)/shard_map/panels_z2/ppermute | solution.py:620
  64.4 8.3 %collective-permute-start.14 = (bf16[64,512]{1,0:T(8,128)(2,1)S(1)}, bf16[64,512]{1,0:T(8,128)(2,1)S(1)}, u32[]{:S(2)}, u32[]{:S(2)}) collective-permute-start(bf16[64,512]{1,0:T(8,128)(2,1)S(1)} %get-tuple-element.110.mine), channel_id=1, source_target_pairs={{0,24},{1,25},{2,26},{3,27},{8,16},{9,17},{10,18},{11,19},{16,8},{... | collective-permute-start | bytes 196616 | tf_op jit(solution)/shard_map/panels_z3/ppermute | solution.py:620
  74.0 4.6 %collective-permute-start.15 = (bf16[64,1536]{1,0:T(8,128)(2,1)S(1)}, bf16[64,1536]{1,0:T(8,128)(2,1)S(1)}, u32[]{:S(2)}, u32[]{:S(2)}) collective-permute-start(bf16[64,1536]{1,0:T(8,128)(2,1)S(1)} %shard_map.136.mine), channel_id=1, source_target_pairs={{0,4},{1,5},{2,6},{3,7},{8,12},{9,13},{10,14},{11,15},{16,20},{17,... | collective-permute-start | bytes 589832 | tf_op jit(solution)/shard_map/down_z1/ppermute | solution.py:620
  79.6 7.8 %collective-permute-start.16 = (bf16[64,2048]{1,0:T(8,128)(2,1)S(1)}, bf16[64,2048]{1,0:T(8,128)(2,1)S(1)}, u32[]{:S(2)}, u32[]{:S(2)}) collective-permute-start(bf16[64,2048]{1,0:T(8,128)(2,1)S(1)} %shard_map.137.mine), channel_id=1, source_target_pairs={{0,3},{1,2},{2,1},{3,0},{4,7},{5,6},{6,5},{7,4},{8,11},{9,10},{10,... | collective-permute-start | bytes 786440 | tf_op jit(solution)/shard_map/down_ring/ppermute | solution.py:620
  88.9 5.4 %collective-permute-start.18 = (bf16[128,640]{1,0:T(8,128)(2,1)S(1)}, bf16[128,640]{1,0:T(8,128)(2,1)S(1)}, u32[]{:S(2)}, u32[]{:S(2)}) collective-permute-start(bf16[128,640]{1,0:T(8,128)(2,1)S(1)} %get-tuple-element.123), channel_id=1, source_target_pairs={{0,1},{1,0},{2,3},{3,2},{4,5},{5,4},{6,7},{7,6},{8,9},{9,8},{10,11... | collective-permute-start | bytes 491528 | tf_op jit(solution)/shard_map/rows_back/ppermute | solution.py:620
  90.5 6.4 %collective-permute-start.19 = (bf16[128,512]{1,0:T(8,128)(2,1)}, bf16[128,512]{1,0:T(8,128)(2,1)S(1)}, u32[]{:S(2)}, u32[]{:S(2)}) collective-permute-start(bf16[128,512]{1,0:T(8,128)(2,1)} %get-tuple-element.130), channel_id=1, source_target_pairs={{0,1},{1,0},{2,3},{3,2},{4,5},{5,4},{6,7},{7,6},{8,9},{9,8},{10,11... | collective-permute-start | bytes 393224 | tf_op jit(solution)/shard_map/sep_back/ppermute | solution.py:620
  97.0 9.1 %copy-start.2 = (bf16[128,512]{1,0:T(8,128)(2,1)}, bf16[128,512]{1,0:T(8,128)(2,1)S(1)}, u32[]{:S(2)}) copy-start(bf16[128,512]{1,0:T(8,128)(2,1)S(1)} %collective-permute-done.19.recv) | copy-start | bytes 393220
  97.0 20.6 %all-to-all-start = ((bf16[32,16,256]{2,1,0:T(8,128)(2,1)}), bf16[32,16,256]{2,1,0:T(8,128)(2,1)S(1)}, u32[]{:S(2)}, u32[]{:S(2)}) async-start(bf16[32,16,256]{2,1,0:T(8,128)(2,1)} %bitcast.11), calls=%async_computation | async-start | bytes 524288 | tf_op jit(solution)/shard_map/all_to_all | solution.py:854

commit v6 on v5

--- a/solution.py
+++ b/solution.py
@@ -17,6 +17,7 @@
 
 TRI = 320
 IDX = slice(TRI, TRI + 16)
+CUT, WINDOW = 352, 368
 CPL0 = TRI + 16
 
 
@@ -118,7 +119,7 @@
     return dot(back, factor[0:PANEL]).astype(BF)
 
 
-def pack_factor(place, inv, cpl, sep_idx, up, codes, sep_v, sems):
+def pack_factor(place, inv, cpl, sep_idx, up, window, codes, sep_v, sems):
     load = pltpu.make_async_copy(sep_idx.at[0], sep_v, sems.at[0])
     copies = [
         pltpu.make_async_copy(inv.at[r, c], up.at[pr, pc], sems.at[1 + i])
@@ -136,6 +137,7 @@
     up[IDX] = codes[...].astype(BF)
     for copy in copies:
         copy.wait()
+    window[...] = up[pl.ds(pl.multiple_of(place[0] * CUT, 16), WINDOW)]
 
 
 def load_first(inv, cpl, out, sems):
@@ -216,21 +218,11 @@
 
 
 def pick_two(core, y, z):
-    return (
-        y == 1,
-        ((y == 0) & (core == 0)) | ((y == 2) & (core == 1)),
-        ((y == 0) & (core == 1)) | ((y == 2) & (core == 0)),
-        y == 3,
-    )
+    return y == 1, y == 0, y == 2, y == 3
 
 
 def pick_top(core, y, z):
-    return (
-        y == 3,
-        ((y == 2) & (core == 0)) | ((y == 0) & (core == 1)),
-        ((y == 2) & (core == 1)) | ((y == 0) & (core == 0)),
-        y == 1,
-    )
+    return y == 3, y == 2, y == 0, y == 1
 
 
 def pick_four(core, y, z):
@@ -252,39 +244,56 @@
     return even, ~even
 
 
-def stage(slots, pick, split, count, place, *refs):
-    if split:
-        sources = [(refs[2 * i], refs[2 * i + 1], 0) for i in range(count)]
-    else:
-        sources = [(refs[i], refs[i], TRI) for i in range(count)]
-    factor, hots, idx, sems = refs[(2 if split else 1) * count :]
-    cases = pick(*which(place))
-
-    def copies_of(triangle, rest, at):
+def window_sources(core, refs):
+    own = refs[0]
+    sources = [[(None, own, own, 0)]]
+    for i in range(1, len(refs), 2):
+        mine, other = refs[i], refs[i + 1]
+        sources.append([(core == 0, mine, other, CUT), (core != 0, other, mine, CUT)])
+    return sources
+
+
+def start_one(cases, sources, copies_of):
+    for case, versions in zip(cases, sources):
+        for on_core, low, high, at in versions:
+
+            @pl.when(case if on_core is None else case & on_core)
+            def _(low=low, high=high, at=at):
+                for copy in copies_of(low, high, at):
+                    copy.start()
+
+    return copies_of(*sources[0][0][1:])
+
+
+def factor_copies(slots, factor, idx, sems):
+    def copies_of(low, high, at):
         copies = [
-            pltpu.make_async_copy(triangle.at[pr, pc], factor.at[r, c], sems.at[i])
+            pltpu.make_async_copy(low.at[pr, pc], factor.at[r, c], sems.at[i])
             for i, (r, c, pr, pc) in enumerate(triangle_blocks())
         ]
         if slots:
-            coupling = rest.at[at + 16 : at + 16 + slots * U]
-            copies.append(pltpu.make_async_copy(coupling, factor.at[PANEL:], sems.at[5]))
-            copies.append(pltpu.make_async_copy(rest.at[at : at + 16], idx, sems.at[6]))
+            split = CUT - CPL0
+            copies.append(
+                pltpu.make_async_copy(low.at[CPL0:CUT], factor.at[PANEL : PANEL + split], sems.at[5])
+            )
+            copies.append(
+                pltpu.make_async_copy(
+                    high.at[CUT - at : packed_rows(slots) - at], factor.at[PANEL + split :], sems.at[6]
+                )
+            )
+            copies.append(pltpu.make_async_copy(low.at[IDX], idx, sems.at[7]))
         return copies
 
-    for case, source in zip(cases, sources):
-
-        @pl.when(case)
-        def _(source=source):
-            for copy in copies_of(*source):
-                copy.start()
-
+    return copies_of
+
+
+def finish_factor(slots, factor, hots, idx, copies):
     for rows, cols in (
         (slice(0, 128), slice(128, 512)),
         (slice(128, 256), slice(256, 512)),
         (slice(256, 384), slice(384, 512)),
     ):
         factor[rows, cols] = jnp.zeros((rows.stop - rows.start, cols.stop - cols.start), BF)
-    copies = copies_of(*sources[0])
     if slots:
         copies[-1].wait()
         taken = sep_rows(idx[...])
@@ -297,24 +306,36 @@
         copy.wait()
 
 
-def stage_and_pass(place, own, near, near_o, far, factor, hots, triangle, rest, idx, sems):
-    sources = (own, near, near_o, far)
-
-    def copies_of(source):
+def stage(slots, pick, count, place, *refs):
+    factor, hots, idx, sems = refs[count:]
+    sources = [[(None, ref, ref, 0)] for ref in refs[:count]]
+    copies = start_one(pick(*which(place)), sources, factor_copies(slots, factor, idx, sems))
+    finish_factor(slots, factor, hots, idx, copies)
+
+
+def stage_two(place, *refs):
+    factor, hots, idx, sems = refs[7:]
+    sources = window_sources(place[0], refs[:7])
+    copies = start_one(pick_two(*which(place)), sources, factor_copies(3, factor, idx, sems))
+    finish_factor(3, factor, hots, idx, copies)
+
+
+def stage_and_pass(place, *refs):
+    factor, hots, top, triangle, idx, sems = refs[7:]
+    sources = window_sources(place[0], refs[:7])
+    cases = pick_top(*which(place))
+
+    def pass_copies(low, high, at):
         return [
-            pltpu.make_async_copy(source.at[0:TRI], triangle, sems.at[7]),
-            pltpu.make_async_copy(source.at[TRI : packed_rows(1)], rest, sems.at[8]),
+            pltpu.make_async_copy(low.at[0:CUT], top.at[0:CUT], sems.at[8]),
+            pltpu.make_async_copy(high.at[CUT - at : packed_rows(1) - at], top.at[CUT:], sems.at[9]),
+            pltpu.make_async_copy(low.at[0:TRI], triangle, sems.at[10]),
         ]
 
-    for case, source in zip(pick_top(*which(place)), sources):
-
-        @pl.when(case)
-        def _(source=source):
-            for copy in copies_of(source):
-                copy.start()
-
-    stage(2, pick_top, False, 4, place, *sources, factor, hots, idx, sems)
-    for copy in copies_of(own):
+    passed = start_one(cases, sources, pass_copies)
+    copies = start_one(cases, sources, factor_copies(2, factor, idx, sems))
+    finish_factor(2, factor, hots, idx, copies)
+    for copy in passed:
         copy.wait()
 
 
@@ -629,15 +650,17 @@
         return route(value, lambda c, y, z: (c, y + 1, z) if y % 2 == 0 else None)
 
     sep_rows_flat = sep_cpl.reshape(4 * U, PANEL)
-    (own_up,) = call(
+    own_up, window = call(
         pack_factor,
-        [pinned(packed_rows(3), PANEL)],
+        [pinned(packed_rows(3), PANEL), pinned(WINDOW, PANEL)],
         [place, sep_inv, sep_rows_flat, sep_idx],
         [SMEM, HBM, HBM, HBM],
         [pltpu.VMEM((16, PANEL), F32), pltpu.VMEM((LEVELS - 1, U), jnp.int32), dma(7)],
     )
-    with jax.named_scope("factors_to_neighbours"):
-        near = route(own_up, lambda c, y, z: (c, y ^ (3 if c else 1), z) if y % 2 else None)
+    with jax.named_scope("factors_to_pair"):
+        pair = route(window, lambda c, y, z: (c, y ^ 1, z) if y % 2 else None)
+    with jax.named_scope("factors_to_other"):
+        beside = route(window, lambda c, y, z: (c, y ^ 3, z) if y % 2 else None)
     yt, rhs, one, inv_v, cpl_v = call(
         leaf_first,
         [
@@ -664,13 +687,13 @@
         leaf_second, [pinned(NC, PANEL)], [yt, cpl_v], [VMEM, VMEM]
     )
 
-    def ready(slots, pick, sources, split=False):
+    def ready(slots, pick, sources):
         return call(
-            functools.partial(stage, slots, pick, split, len(sources) // (2 if split else 1)),
+            functools.partial(stage, slots, pick, len(sources)),
             [pinned(factor_rows(slots), PANEL), pinned(PANEL, max(slots, 1) * U)],
             [place, *sources],
             [SMEM] + [ANY] * len(sources),
-            [pltpu.VMEM((16, PANEL), BF), dma(7)],
+            [pltpu.VMEM((16, PANEL), BF), dma(8)],
         )
 
     def rise(level, panel, recv, factor, hots):
@@ -689,9 +712,9 @@
         [HBM, HBM],
         [dma(2)],
     )
-    near = after(near, recv, f1, terms)
+    pair = after(pair, recv, f1, terms)
     with jax.named_scope("factors_across"):
-        far = route(near, lambda c, y, z: (c, y ^ (1 if c else 3), z) if y % 2 == 0 else None)
+        far = route(pair, lambda c, y, z: (c, y ^ 3, z) if y % 2 == 0 else None)
     first = after(recv, f1)
     first_hots, y1, passed, keep, send = call(
         level_one,
@@ -709,9 +732,11 @@
     )
     with jax.named_scope("terms_pair"):
         recv = swap(send, 1)
-    near = after(near, send)
-    with jax.named_scope("near_to_core"):
-        near_o = swap_core(near)
+    pair, beside = after((pair, beside), send)
+    with jax.named_scope("pair_to_core"):
+        pair_o = swap_core(pair)
+    with jax.named_scope("beside_to_core"):
+        beside_o = swap_core(beside)
     chosen, weight = call(
         stay_plan,
         [pinned(32 * SLOTS, LEAF), stored(2, 64, 512)],
@@ -741,19 +766,27 @@
     with jax.named_scope("panels_ring"):
         recv = swap(send, 3)
     far = after(far, send)
-    at = [own_up, near, near_o, far]
-    f2, h2 = ready(3, pick_two, at)
-    f3, h3, top, top_rest = call(
+    with jax.named_scope("far_to_core"):
+        far_o = swap_core(far)
+    at = [own_up, pair, pair_o, beside, beside_o, far, far_o]
+    f2, h2 = call(
+        stage_two,
+        [pinned(factor_rows(3), PANEL), pinned(PANEL, 3 * U)],
+        [place, *at],
+        [SMEM] + [ANY] * 7,
+        [pltpu.VMEM((16, PANEL), BF), dma(8)],
+    )
+    f3, h3, top, triangle = call(
         stage_and_pass,
         [
             pinned(factor_rows(2), PANEL),
             pinned(PANEL, 2 * U),
+            pinned(packed_rows(1), PANEL),
             pinned(TRI, PANEL),
-            pinned(16 + U, PANEL),
         ],
         [place, *at],
-        [SMEM] + [ANY] * 4,
-        [pltpu.VMEM((16, PANEL), BF), dma(9)],
+        [SMEM] + [ANY] * 7,
+        [pltpu.VMEM((16, PANEL), BF), dma(11)],
     )
 
     def next_up(value, senders):
@@ -763,29 +796,24 @@
         up = next_up(top, (1, 3, 5))
     with jax.named_scope("factor_top"):
         last = route(
-            top,
+            triangle,
             lambda c, y, z: (0, y, 0) if (c, z) == (0, 3) else (1, y, 6) if (c, z) == (1, 3) else None,
         )
-    with jax.named_scope("factors_up_rest"):
-        rest = next_up(top_rest, (1, 5))
     with jax.named_scope("first_factor_to_odd"):
         passed_far = to_odd(after(passed, f2))
     recv = after(recv, f2, h2, f3, h3)
     y2, panel = rise(2, panel, recv, f2, h2)
     with jax.named_scope("panels_z1"):
         recv = route(panel, lambda c, y, z: (c, y, z - 1) if z % 2 else None)
-    up, rest, last = after((up, rest, last), recv)
-    with jax.named_scope("up_to_core"):
-        up_o = swap_core(up)
-    with jax.named_scope("rest_to_core"):
-        rest_o = swap_core(rest)
-    with jax.named_scope("last_to_core"):
-        last_o = swap_core(last)
     y3, panel = rise(3, panel, recv, f3, h3)
     with jax.named_scope("panels_z2"):
         recv = route(panel, lambda c, y, z: (c, y, z ^ 2) if z % 2 == 0 else None)
-    up, rest, last, up_o, rest_o, last_o = after((up, rest, last, up_o, rest_o, last_o), panel)
-    f4, h4 = ready(1, pick_four, [up, rest, up_o, rest_o], True)
+    up, last = after((up, last), panel)
+    with jax.named_scope("up_to_core"):
+        up_o = swap_core(up)
+    with jax.named_scope("last_to_core"):
+        last_o = swap_core(last)
+    f4, h4 = ready(1, pick_four, [up, up_o])
     f5, _ = ready(0, pick_five, [up, up_o, last, last_o])
     recv = after(recv, f4, h4, f5)
     y4, panel = rise(4, panel, recv, f4, h4)

time: 120 us -> 116 us (0.967)
  starting transfers between devices: 41.7 us -> 37.8 us
    ppermute x20 -> x21, starting transfers between devices: 32.6 us -> 30.4 us  [route(): return lax.ppermute(value, (cols_axis, rows_axis), pairs)]
    all_to_all x1, starting transfers between devices: 9.05 us -> 7.42 us  [on_device(): lax.all_to_all(picks.reshape(32, SLOTS, NC), rows_axis, 0, 0, tiled=True)]
    ppermute x20 -> x21, waiting for transfers between devices: 32.5 us -> 31.4 us  [route(): return lax.ppermute(value, (cols_axis, rows_axis), pairs)]
  transfers between devices with their start and end apart: 21 -> 22, of which waited for: 9 -> 11; matrix products, arithmetic and copies ran while one was open for 0% -> 0% of each run, Pallas kernels for 25% -> 27%
where the time goes in v6:
time: 116 us; the launch traced here: 115 us
  waiting for transfers between devices  40.1 us (35%)
  starting transfers between devices  37.8 us (33%)
  Pallas kernels  36.1 us (31%)
  between operations  1.24 us (1%)
    pallas_call x24, Pallas kernels, call(): pl.pallas_call(body, out_shape=outs, in_specs=specs, out_specs=out_specs...  36.1 us
    ppermute x21, waiting for transfers between devices, route(): return lax.ppermute(value, (cols_axis, rows_axis), pairs)  31.4 us
    ppermute x21, starting transfers between devices, route(): return lax.ppermute(value, (cols_axis, rows_axis), pairs)  30.4 us
    all_to_all x1, waiting for transfers between devices, on_device(): lax.all_to_all(picks.reshape(32, SLOTS, NC), rows_axis, 0, 0, tiled=True)  8.69 us
    all_to_all x1, starting transfers between devices, on_device(): lax.all_to_all(picks.reshape(32, SLOTS, NC), rows_axis, 0, 0, tiled=True)  7.42 us
  transfers between devices with their start and end apart: 22, of which 11 were waited for; matrix products, arithmetic and copies ran while one was open for 0% of the time, Pallas kernels for 27%

profile of v6, /device:TPU:2, one launch (start us, length us, event | category | flops | bytes accessed | tf_op | source)
XLA Modules:
  0.0 115.4 jit_solution(1967281085090608275)
XLA Ops:
  0.8 1.8 %shard_map.121 = (bf16[720,512]{1,0:T(8,128)(2,1)S(1)}, bf16[368,512]{1,0:T(8,128)(2,1)S(1)}) custom-call(s32[4]{0:T(128)S(1)} %pad_add_fusion.place, bf16[512,512]{1,0:T(8,128)(2,1)} %inv.4, bf16[512,512]{1,0:T(8,128)(2,1)} %bitcast.9, s32[1,4,128]{2,1,0:T(4,128)} %sep_idx.3), custom_call_target="tpu_custom_call" | custom-call | flops 100000000 | bytes 1000000 | tf_op jit(solution)/shard_map/pallas_call | solution.py:61
  2.6 1.3 %collective-permute-start.3 = (bf16[368,512]{1,0:T(8,128)(2,1)S(1)}, bf16[368,512]{1,0:T(8,128)(2,1)S(1)}, u32[]{:S(2)}, u32[]{:S(2)}) collective-permute-start(bf16[368,512]{1,0:T(8,128)(2,1)S(1)} %get-tuple-element.82), channel_id=1, source_target_pairs={{1,0},{3,2},{5,4},{7,6},{9,8},{11,10},{13,12},{15,14},{17,16},{19,... | collective-permute-start | bytes 1130504 | tf_op jit(solution)/shard_map/factors_to_pair/ppermute | solution.py:641
  3.9 3.9 %shard_map.122 = (bf16[256,1024]{1,0:T(8,128)(2,1)S(1)}, bf16[256,512]{1,0:T(8,128)(2,1)S(1)}, bf16[320,128]{1,0:T(8,128)(2,1)S(1)}, bf16[1024,1024]{1,0:T(8,128)(2,1)S(1)}, bf16[5,128,1024]{2,1,0:T(8,128)(2,1)S(1)}) custom-call(s32[4]{0:T(128)S(1)} %pad_add_fusion.place, bf16[1024,1024]{1,0:T(8,128)(2,1)} %inv.3, bf16[1024,256]{1,0:T(8,128)(2,1)} %rhs.1, ...), custom_call_target="tpu_custom_call" | custom-call | flops 100000000 | bytes 1000000 | tf_op jit(solution)/shard_map/pallas_call | solution.py:61
  7.8 2.7 %collective-permute-start = (bf16[320,128]{1,0:T(8,128)(2,1)S(1)}, bf16[320,128]{1,0:T(8,128)(2,1)S(1)}, u32[]{:S(2)}, u32[]{:S(2)}) collective-permute-start(bf16[320,128]{1,0:T(8,128)(2,1)S(1)} %get-tuple-element.68.one), channel_id=1, source_target_pairs={{0,1},{1,0},{2,3},{3,2},{4,5},{5,4},{6,7},{7,6},{8,9},{9,8},{10,11... | collective-permute-start | bytes 245768 | tf_op jit(solution)/shard_map/first_terms/ppermute | solution.py:641
  13.7 3.0 %collective-permute-done.recv.other = bf16[320,128]{1,0:T(8,128)(2,1)S(1)} collective-permute-done((bf16[320,128]{1,0:T(8,128)(2,1)S(1)}, bf16[320,128]{1,0:T(8,128)(2,1)S(1)}, u32[]{:S(2)}, u32[]{:S(2)}) %collective-permute-start) | collective-permute-done | bytes 81952 | tf_op jit(solution)/shard_map/first_terms/ppermute | solution.py:641
  16.7 3.2 %collective-permute-start.7 = (bf16[368,512]{1,0:T(8,128)(2,1)S(1)}, bf16[368,512]{1,0:T(8,128)(2,1)S(1)}, u32[]{:S(2)}, u32[]{:S(2)}) collective-permute-start(bf16[368,512]{1,0:T(8,128)(2,1)S(1)} %collective-permute-done.3.refs_1_), channel_id=1, source_target_pairs={{0,3},{2,1},{4,7},{6,5},{8,11},{10,9},{12,15},{14,13},{16,19},{18,... | collective-permute-start | bytes 1130504 | tf_op jit(solution)/shard_map/factors_across/ppermute | solution.py:641
  19.9 1.3 %shard_map.125 = (bf16[512,256]{1,0:T(8,128)(2,1)S(1)}, bf16[128,512]{1,0:T(8,128)(2,1)S(1)}, bf16[1152,512]{1,0:T(8,128)(2,1)S(1)}, bf16[128,1024]{1,0:T(8,128)(2,1)S(1)}, bf16[128,1024]{1,0:T(8,128)(2,1)S(1)}) custom-call(s32[4]{0:T(128)S(1)} %pad_add_fusion.place, bf16[320,128]{1,0:T(8,128)(2,1)S(1)} %get-tuple-element.68.one, ...), custom_call_target="tpu_custom_call", output_to_operand_aliasing={{2}: (5, {})} | custom-call | flops 100000000 | bytes 1000000 | tf_op jit(solution)/shard_map/pallas_call | solution.py:61
  21.4 2.2 %collective-permute-done.4.refs_3_ = bf16[368,512]{1,0:T(8,128)(2,1)S(1)} collective-permute-done((bf16[368,512]{1,0:T(8,128)(2,1)S(1)}, bf16[368,512]{1,0:T(8,128)(2,1)S(1)}, u32[]{:S(2)}, u32[]{:S(2)}) %collective-permute-start.4) | collective-permute-done | bytes 376864 | tf_op jit(solution)/shard_map/factors_to_other/ppermute | solution.py:641
  24.9 2.5 %shard_map.126 = (bf16[512,1024]{1,0:T(8,128)(2,1)S(1)}, bf16[2,64,512]{2,1,0:T(8,128)(2,1)}) custom-call(s32[4]{0:T(128)S(1)} %pad_add_fusion.place, s32[6,2048]{1,0:T(8,128)S(1)} %copy-done, f32[6,2048]{1,0:T(8,128)S(1)} %copy-done.1), custom_call_target="tpu_custom_call" | custom-call | flops 100000000 | bytes 1000000 | tf_op jit(solution)/shard_map/pallas_call | solution.py:61
  31.3 1.8 %shard_map.130 = (bf16[768,512]{1,0:T(8,128)(2,1)S(1)}, bf16[512,256]{1,0:T(8,128)(2,1)S(1)}, bf16[464,512]{1,0:T(8,128)(2,1)S(1)}, bf16[320,512]{1,0:T(8,128)(2,1)S(1)}) custom-call(s32[4]{0:T(128)S(1)} %pad_add_fusion.place, bf16[720,512]{1,0:T(8,128)(2,1)S(1)} %get-tuple-element.66.refs_0_, bf16[368,512]{1,0:T(8,128)(2,1)S(1)} %collective-permute-done.3.refs_1_, ...), custom_call_target="tpu_custom_call" | custom-call | flops 100000000 | bytes 1000000 | tf_op jit(solution)/shard_map/pallas_call | solution.py:61
  33.0 1.3 %collective-permute-start.11 = (bf16[464,512]{1,0:T(8,128)(2,1)S(1)}, bf16[464,512]{1,0:T(8,128)(2,1)S(1)}, u32[]{:S(2)}, u32[]{:S(2)}) collective-permute-start(bf16[464,512]{1,0:T(8,128)(2,1)S(1)} %get-tuple-element.94), channel_id=1, source_target_pairs={{4,0},{5,1},{6,2},{7,3},{12,8},{13,9},{14,10},{15,11},{20,16},{21,... | collective-permute-start | bytes 1425416 | tf_op jit(solution)/shard_map/factors_up/ppermute | solution.py:641
  36.8 2.7 %collective-permute-done.2.recv = bf16[64,2048]{1,0:T(8,128)(2,1)S(1)} collective-permute-done((bf16[64,2048]{1,0:T(8,128)(2,1)S(1)}, bf16[64,2048]{1,0:T(8,128)(2,1)S(1)}, u32[]{:S(2)}, u32[]{:S(2)}) %collective-permute-start.2) | collective-permute-done | bytes 262176 | tf_op jit(solution)/shard_map/panels_ring/ppermute | solution.py:641
  40.2 1.3 %collective-permute-start.9 = (bf16[64,1536]{1,0:T(8,128)(2,1)S(1)}, bf16[64,1536]{1,0:T(8,128)(2,1)S(1)}, u32[]{:S(2)}, u32[]{:S(2)}) collective-permute-start(bf16[64,1536]{1,0:T(8,128)(2,1)S(1)} %get-tuple-element.92.mine), channel_id=1, source_target_pairs={{4,0},{5,1},{6,2},{7,3},{12,8},{13,9},{14,10},{15,11},{20,16},{21,... | collective-permute-start | bytes 589832 | tf_op jit(solution)/shard_map/panels_z1/ppermute | solution.py:641
  41.5 1.4 %collective-permute-start.18 = (bf16[1152,512]{1,0:T(8,128)(2,1)S(1)}, bf16[1152,512]{1,0:T(8,128)(2,1)S(1)}, u32[]{:S(2)}, u32[]{:S(2)}) collective-permute-start(bf16[1152,512]{1,0:T(8,128)(2,1)S(1)} %get-tuple-element.107.own), channel_id=1, source_target_pairs={{0,1},{2,3},{4,5},{6,7},{8,9},{10,11},{12,13},{14,15},{16,17},{18,... | collective-permute-start | bytes 3538952 | tf_op jit(solution)/shard_map/first_factor_to_odd/ppermute | solution.py:641
  42.9 9.2 %collective-permute-done.9.recv = bf16[64,1536]{1,0:T(8,128)(2,1)S(1)} collective-permute-done((bf16[64,1536]{1,0:T(8,128)(2,1)S(1)}, bf16[64,1536]{1,0:T(8,128)(2,1)S(1)}, u32[]{:S(2)}, u32[]{:S(2)}) %collective-permute-start.9) | collective-permute-done | bytes 196640 | tf_op jit(solution)/shard_map/panels_z1/ppermute | solution.py:641
  53.4 4.4 %collective-permute-start.10 = (bf16[64,1024]{1,0:T(8,128)(2,1)S(1)}, bf16[64,1024]{1,0:T(8,128)(2,1)S(1)}, u32[]{:S(2)}, u32[]{:S(2)}) collective-permute-start(bf16[64,1024]{1,0:T(8,128)(2,1)S(1)} %get-tuple-element.93.mine), channel_id=1, source_target_pairs={{0,8},{1,9},{2,10},{3,11},{8,0},{9,1},{10,2},{11,3},{16,24},{17,25... | collective-permute-start | bytes 393224 | tf_op jit(solution)/shard_map/panels_z2/ppermute | solution.py:641
  58.9 1.7 %shard_map.134 = (bf16[512,512]{1,0:T(8,128)(2,1)S(1)}, bf16[512,128]{1,0:T(8,128)(2,1)}) custom-call(s32[4]{0:T(128)S(1)} %pad_add_fusion.place, bf16[464,512]{1,0:T(8,128)(2,1)S(1)} %collective-permute-done.11.refs_0_, bf16[464,512]{1,0:T(8,128)(2,1)S(1)} %collective-permute-done.13.refs_1_, bf16[320,512]{1,0:T(8,128)(2,1)S(1)} %collective-permute-done.12.refs_2_, ...), custom_call_target="tpu_custom_call" | custom-call | flops 100000000 | bytes 1000000 | tf_op jit(solution)/shard_map/pallas_call | solution.py:61
  62.3 4.7 %collective-permute-start.15 = (bf16[64,512]{1,0:T(8,128)(2,1)S(1)}, bf16[64,512]{1,0:T(8,128)(2,1)S(1)}, u32[]{:S(2)}, u32[]{:S(2)}) collective-permute-start(bf16[64,512]{1,0:T(8,128)(2,1)S(1)} %get-tuple-element.102.mine), channel_id=1, source_target_pairs={{0,24},{1,25},{2,26},{3,27},{8,16},{9,17},{10,18},{11,19},{16,8},{... | collective-permute-start | bytes 196616 | tf_op jit(solution)/shard_map/panels_z3/ppermute | solution.py:641
  67.0 3.6 %collective-permute-done.15.recv = bf16[64,512]{1,0:T(8,128)(2,1)S(1)} collective-permute-done((bf16[64,512]{1,0:T(8,128)(2,1)S(1)}, bf16[64,512]{1,0:T(8,128)(2,1)S(1)}, u32[]{:S(2)}, u32[]{:S(2)}) %collective-permute-start.15) | collective-permute-done | bytes 65568 | tf_op jit(solution)/shard_map/panels_z3/ppermute | solution.py:641
  71.8 1.3 %collective-permute-start.16 = (bf16[64,1536]{1,0:T(8,128)(2,1)S(1)}, bf16[64,1536]{1,0:T(8,128)(2,1)S(1)}, u32[]{:S(2)}, u32[]{:S(2)}) collective-permute-start(bf16[64,1536]{1,0:T(8,128)(2,1)S(1)} %shard_map.136.mine), channel_id=1, source_target_pairs={{0,4},{1,5},{2,6},{3,7},{8,12},{9,13},{10,14},{11,15},{16,20},{17,... | collective-permute-start | bytes 589832 | tf_op jit(solution)/shard_map/down_z1/ppermute | solution.py:641
  73.1 3.2 %collective-permute-done.16.recv = bf16[64,1536]{1,0:T(8,128)(2,1)S(1)} collective-permute-done((bf16[64,1536]{1,0:T(8,128)(2,1)S(1)}, bf16[64,1536]{1,0:T(8,128)(2,1)S(1)}, u32[]{:S(2)}, u32[]{:S(2)}) %collective-permute-start.16) | collective-permute-done | bytes 196640 | tf_op jit(solution)/shard_map/down_z1/ppermute | solution.py:641
  77.3 1.6 %collective-permute-start.17 = (bf16[64,2048]{1,0:T(8,128)(2,1)S(1)}, bf16[64,2048]{1,0:T(8,128)(2,1)S(1)}, u32[]{:S(2)}, u32[]{:S(2)}) collective-permute-start(bf16[64,2048]{1,0:T(8,128)(2,1)S(1)} %shard_map.137.mine), channel_id=1, source_target_pairs={{0,3},{1,2},{2,1},{3,0},{4,7},{5,6},{6,5},{7,4},{8,11},{9,10},{10,... | collective-permute-start | bytes 786440 | tf_op jit(solution)/shard_map/down_ring/ppermute | solution.py:641
  79.7 5.2 %collective-permute-done.17.recv = bf16[64,2048]{1,0:T(8,128)(2,1)S(1)} collective-permute-done((bf16[64,2048]{1,0:T(8,128)(2,1)S(1)}, bf16[64,2048]{1,0:T(8,128)(2,1)S(1)}, u32[]{:S(2)}, u32[]{:S(2)}) %collective-permute-start.17) | collective-permute-done | bytes 262176 | tf_op jit(solution)/shard_map/down_ring/ppermute | solution.py:641
  85.0 1.5 %shard_map.139 = (bf16[128,512]{1,0:T(8,128)(2,1)S(1)}, bf16[128,2048]{1,0:T(8,128)(2,1)S(1)}, bf16[128,640]{1,0:T(8,128)(2,1)S(1)}) custom-call(s32[4]{0:T(128)S(1)} %pad_add_fusion.place, bf16[64,2048]{1,0:T(8,128)(2,1)S(1)} %shard_map.137.mine, bf16[64,2048]{1,0:T(8,128)(2,1)S(1)} %collective-permute-done.17.recv, ...), custom_call_target="tpu_custom_call" | custom-call | flops 100000000 | bytes 1000000 | tf_op jit(solution)/shard_map/pallas_call | solution.py:61
  86.5 1.5 %shard_map.140 = (bf16[128,640]{1,0:T(8,128)(2,1)S(1)}, bf16[128,512]{1,0:T(8,128)(2,1)}, bf16[128,512]{1,0:T(8,128)(2,1)}) custom-call(s32[4]{0:T(128)S(1)} %pad_add_fusion.place, bf16[128,512]{1,0:T(8,128)(2,1)S(1)} %get-tuple-element.112.x1_ref, bf16[128,2048]{1,0:T(8,128)(2,1)S(1)} %get-tuple-element.113.x, ...), custom_call_target="tpu_custom_call" | custom-call | flops 100000000 | bytes 1000000 | tf_op jit(solution)/shard_map/pallas_call | solution.py:61
  88.0 2.1 %collective-permute-start.20 = (bf16[128,512]{1,0:T(8,128)(2,1)}, bf16[128,512]{1,0:T(8,128)(2,1)S(1)}, u32[]{:S(2)}, u32[]{:S(2)}) collective-permute-start(bf16[128,512]{1,0:T(8,128)(2,1)} %get-tuple-element.122), channel_id=1, source_target_pairs={{0,1},{1,0},{2,3},{3,2},{4,5},{5,4},{6,7},{7,6},{8,9},{9,8},{10,11... | collective-permute-start | bytes 393224 | tf_op jit(solution)/shard_map/sep_back/ppermute | solution.py:641
  90.1 1.7 %shard_map.141 = (bf16[128,1024]{1,0:T(8,128)(2,1)S(1)}, bf16[512,128]{1,0:T(8,128)(2,1)S(1)}) custom-call(s32[4]{0:T(128)S(1)} %pad_add_fusion.place, bf16[128,640]{1,0:T(8,128)(2,1)S(1)} %get-tuple-element.116.keep, bf16[1024,1024]{1,0:T(8,128)(2,1)S(1)} %get-tuple-element.117.inv, bf16[5,128,1024]{2,1,0:T(8,128)(2,1)S(1)} %get-tuple-element.72.cpl_v.cpl, ...), custom_call_target="tpu_custom_call" | custom-call | flops 100000000 | bytes 1000000 | tf_op jit(solution)/shard_map/pallas_call | solution.py:61
  91.8 2.6 %shard_map.142 = (bf16[256,1024]{1,0:T(8,128)(2,1)}, bf16[512,256]{1,0:T(8,128)(2,1)}) custom-call(s32[4]{0:T(128)S(1)} %pad_add_fusion.place, bf16[128,640]{1,0:T(8,128)(2,1)S(1)} %collective-permute-done.19.recv, bf16[1024,1024]{1,0:T(8,128)(2,1)S(1)} %get-tuple-element.117.inv, bf16[5,128,1024]{2,1,0:T(8,128)(2,1)S(1)} %get-tuple-element.72.cpl_v.cpl, ...), custom_call_target="tpu_custom_call" | custom-call | flops 100000000 | bytes 14000000 | tf_op jit(solution)/shard_map/pallas_call | solution.py:61
  94.5 7.4 %all-to-all-start = ((bf16[32,16,256]{2,1,0:T(8,128)(2,1)}), bf16[32,16,256]{2,1,0:T(8,128)(2,1)S(1)}, u32[]{:S(2)}, u32[]{:S(2)}) async-start(bf16[32,16,256]{2,1,0:T(8,128)(2,1)} %bitcast.11), calls=%async_computation | async-start | bytes 524288 | tf_op jit(solution)/shard_map/all_to_all | solution.py:882
  101.9 2.8 %shard_map.143 = (bf16[512,256]{1,0:T(8,128)(2,1)}, bf16[1024,256]{1,0:T(8,128)(2,1)}) custom-call(s32[4]{0:T(128)S(1)} %pad_add_fusion.place, bf16[128,512]{1,0:T(8,128)(2,1)} %get-tuple-element.114.keep, bf16[128,512]{1,0:T(8,128)(2,1)} %copy-done.2, bf16[256,1024]{1,0:T(8,128)(2,1)} %get-tuple-element.124.xt), custom_call_target="tpu_custom_call" | custom-call | flops 100000000 | bytes 1000000 | tf_op jit(solution)/shard_map/pallas_call | solution.py:61
  104.8 8.7 %all-to-all-done = bf16[32,16,256]{2,1,0:T(8,128)(2,1)S(1)} async-done(((bf16[32,16,256]{2,1,0:T(8,128)(2,1)}), bf16[32,16,256]{2,1,0:T(8,128)(2,1)S(1)}, u32[]{:S(2)}, u32[]{:S(2)}) %all-to-all-start) | async-done | bytes 262176 | tf_op jit(solution)/shard_map/all_to_all | solution.py:882
  113.5 1.7 %shard_map.144 = f32[64,256]{1,0:T(8,128)} custom-call(bf16[2,64,512]{2,1,0:T(8,128)(2,1)} %get-tuple-element.127.weight, bf16[512,256]{1,0:T(8,128)(2,1)S(1)} %bitcast.8), custom_call_target="tpu_custom_call" | custom-call | flops 100000000 | bytes 1000000 | tf_op jit(solution)/shard_map/pallas_call | solution.py:61
  (43 shorter events, 18.9 us)
Async XLA Ops:
  2.6 14.2 %collective-permute-start.3 = (bf16[368,512]{1,0:T(8,128)(2,1)S(1)}, bf16[368,512]{1,0:T(8,128)(2,1)S(1)}, u32[]{:S(2)}, u32[]{:S(2)}) collective-permute-start(bf16[368,512]{1,0:T(8,128)(2,1)S(1)} %get-tuple-element.82), channel_id=1, source_target_pairs={{1,0},{3,2},{5,4},{7,6},{9,8},{11,10},{13,12},{15,14},{17,16},{19,... | collective-permute-start | bytes 1130504 | tf_op jit(solution)/shard_map/factors_to_pair/ppermute | solution.py:641
  7.8 9.0 %collective-permute-start = (bf16[320,128]{1,0:T(8,128)(2,1)S(1)}, bf16[320,128]{1,0:T(8,128)(2,1)S(1)}, u32[]{:S(2)}, u32[]{:S(2)}) collective-permute-start(bf16[320,128]{1,0:T(8,128)(2,1)S(1)} %get-tuple-element.68.one), channel_id=1, source_target_pairs={{0,1},{1,0},{2,3},{3,2},{4,5},{5,4},{6,7},{7,6},{8,9},{9,8},{10,11... | collective-permute-start | bytes 245768 | tf_op jit(solution)/shard_map/first_terms/ppermute | solution.py:641
  10.5 13.0 %collective-permute-start.4 = (bf16[368,512]{1,0:T(8,128)(2,1)S(1)}, bf16[368,512]{1,0:T(8,128)(2,1)S(1)}, u32[]{:S(2)}, u32[]{:S(2)}) collective-permute-start(bf16[368,512]{1,0:T(8,128)(2,1)S(1)} %get-tuple-element.82), channel_id=1, source_target_pairs={{1,2},{3,0},{5,6},{7,4},{9,10},{11,8},{13,14},{15,12},{17,18},{19,... | collective-permute-start | bytes 1130504 | tf_op jit(solution)/shard_map/factors_to_other/ppermute | solution.py:641
  16.7 12.7 %collective-permute-start.7 = (bf16[368,512]{1,0:T(8,128)(2,1)S(1)}, bf16[368,512]{1,0:T(8,128)(2,1)S(1)}, u32[]{:S(2)}, u32[]{:S(2)}) collective-permute-start(bf16[368,512]{1,0:T(8,128)(2,1)S(1)} %collective-permute-done.3.refs_1_), channel_id=1, source_target_pairs={{0,3},{2,1},{4,7},{6,5},{8,11},{10,9},{12,15},{14,13},{16,19},{18,... | collective-permute-start | bytes 1130504 | tf_op jit(solution)/shard_map/factors_across/ppermute | solution.py:641
  21.2 3.7 %copy-start = (s32[6,2048]{1,0:T(8,128)S(1)}, s32[6,2048]{1,0:T(8,128)}, u32[]{:S(2)}) copy-start(s32[6,2048]{1,0:T(8,128)} %dofs.1) | copy-start | bytes 147460
  21.3 3.7 %copy-start.1 = (f32[6,2048]{1,0:T(8,128)S(1)}, f32[6,2048]{1,0:T(8,128)}, u32[]{:S(2)}) copy-start(f32[6,2048]{1,0:T(8,128)} %coef) | copy-start | bytes 147460
  21.3 7.0 %collective-permute-start.1 = (bf16[128,1024]{1,0:T(8,128)(2,1)S(1)}, bf16[128,1024]{1,0:T(8,128)(2,1)S(1)}, u32[]{:S(2)}, u32[]{:S(2)}) collective-permute-start(bf16[128,1024]{1,0:T(8,128)(2,1)S(1)} %get-tuple-element.75), channel_id=1, source_target_pairs={{0,1},{1,0},{2,3},{3,2},{4,5},{5,4},{6,7},{7,6},{8,9},{9,8},{10,11... | collective-permute-start | bytes 786440 | tf_op jit(solution)/shard_map/terms_pair/ppermute | solution.py:641
  23.6 7.2 %collective-permute-start.5 = (bf16[368,512]{1,0:T(8,128)(2,1)S(1)}, bf16[368,512]{1,0:T(8,128)(2,1)S(1)}, u32[]{:S(2)}, u32[]{:S(2)}) collective-permute-start(bf16[368,512]{1,0:T(8,128)(2,1)S(1)} %collective-permute-done.3.refs_1_), channel_id=1, source_target_pairs={{0,32},{1,33},{2,34},{3,35},{4,36},{5,37},{6,38},{7,39},{8,40},{9,... | collective-permute-start | bytes 1130504 | tf_op jit(solution)/shard_map/pair_to_core/ppermute | solution.py:641
  23.6 7.2 %collective-permute-start.6 = (bf16[368,512]{1,0:T(8,128)(2,1)S(1)}, bf16[368,512]{1,0:T(8,128)(2,1)S(1)}, u32[]{:S(2)}, u32[]{:S(2)}) collective-permute-start(bf16[368,512]{1,0:T(8,128)(2,1)S(1)} %collective-permute-done.4.refs_3_), channel_id=1, source_target_pairs={{0,32},{1,33},{2,34},{3,35},{4,36},{5,37},{6,38},{7,39},{8,40},{9,... | collective-permute-start | bytes 1130504 | tf_op jit(solution)/shard_map/beside_to_core/ppermute | solution.py:641
  29.5 1.8 %collective-permute-start.8 = (bf16[368,512]{1,0:T(8,128)(2,1)S(1)}, bf16[368,512]{1,0:T(8,128)(2,1)S(1)}, u32[]{:S(2)}, u32[]{:S(2)}) collective-permute-start(bf16[368,512]{1,0:T(8,128)(2,1)S(1)} %collective-permute-done.7.refs_5_), channel_id=1, source_target_pairs={{0,32},{1,33},{2,34},{3,35},{4,36},{5,37},{6,38},{7,39},{8,40},{9,... | collective-permute-start | bytes 1130504 | tf_op jit(solution)/shard_map/far_to_core/ppermute | solution.py:641
  29.6 9.9 %collective-permute-start.2 = (bf16[64,2048]{1,0:T(8,128)(2,1)S(1)}, bf16[64,2048]{1,0:T(8,128)(2,1)S(1)}, u32[]{:S(2)}, u32[]{:S(2)}) collective-permute-start(bf16[64,2048]{1,0:T(8,128)(2,1)S(1)} %get-tuple-element.81), channel_id=1, source_target_pairs={{0,3},{1,2},{2,1},{3,0},{4,7},{5,6},{6,5},{7,4},{8,11},{9,10},{10,... | collective-permute-start | bytes 786440 | tf_op jit(solution)/shard_map/panels_ring/ppermute | solution.py:641
  33.0 19.8 %collective-permute-start.11 = (bf16[464,512]{1,0:T(8,128)(2,1)S(1)}, bf16[464,512]{1,0:T(8,128)(2,1)S(1)}, u32[]{:S(2)}, u32[]{:S(2)}) collective-permute-start(bf16[464,512]{1,0:T(8,128)(2,1)S(1)} %get-tuple-element.94), channel_id=1, source_target_pairs={{4,0},{5,1},{6,2},{7,3},{12,8},{13,9},{14,10},{15,11},{20,16},{21,... | collective-permute-start | bytes 1425416 | tf_op jit(solution)/shard_map/factors_up/ppermute | solution.py:641
  34.3 18.4 %collective-permute-start.12 = (bf16[320,512]{1,0:T(8,128)(2,1)S(1)}, bf16[320,512]{1,0:T(8,128)(2,1)S(1)}, u32[]{:S(2)}, u32[]{:S(2)}) collective-permute-start(bf16[320,512]{1,0:T(8,128)(2,1)S(1)} %get-tuple-element.95), channel_id=1, source_target_pairs={{12,0},{13,1},{14,2},{15,3},{44,56},{45,57},{46,58},{47,59},{76,64... | collective-permute-start | bytes 983048 | tf_op jit(solution)/shard_map/factor_top/ppermute | solution.py:641
  40.2 11.9 %collective-permute-start.9 = (bf16[64,1536]{1,0:T(8,128)(2,1)S(1)}, bf16[64,1536]{1,0:T(8,128)(2,1)S(1)}, u32[]{:S(2)}, u32[]{:S(2)}) collective-permute-start(bf16[64,1536]{1,0:T(8,128)(2,1)S(1)} %get-tuple-element.92.mine), channel_id=1, source_target_pairs={{4,0},{5,1},{6,2},{7,3},{12,8},{13,9},{14,10},{15,11},{20,16},{21,... | collective-permute-start | bytes 589832 | tf_op jit(solution)/shard_map/panels_z1/ppermute | solution.py:641
  41.5 37.4 %collective-permute-start.18 = (bf16[1152,512]{1,0:T(8,128)(2,1)S(1)}, bf16[1152,512]{1,0:T(8,128)(2,1)S(1)}, u32[]{:S(2)}, u32[]{:S(2)}) collective-permute-start(bf16[1152,512]{1,0:T(8,128)(2,1)S(1)} %get-tuple-element.107.own), channel_id=1, source_target_pairs={{0,1},{2,3},{4,5},{6,7},{8,9},{10,11},{12,13},{14,15},{16,17},{18,... | collective-permute-start | bytes 3538952 | tf_op jit(solution)/shard_map/first_factor_to_odd/ppermute | solution.py:641
  52.8 5.0 %collective-permute-start.13 = (bf16[464,512]{1,0:T(8,128)(2,1)S(1)}, bf16[464,512]{1,0:T(8,128)(2,1)S(1)}, u32[]{:S(2)}, u32[]{:S(2)}) collective-permute-start(bf16[464,512]{1,0:T(8,128)(2,1)S(1)} %collective-permute-done.11.refs_0_), channel_id=1, source_target_pairs={{0,32},{1,33},{2,34},{3,35},{4,36},{5,37},{6,38},{7,39},{8,40},{9,... | collective-permute-start | bytes 1425416 | tf_op jit(solution)/shard_map/up_to_core/ppermute | solution.py:641
  52.9 6.0 %collective-permute-start.14 = (bf16[320,512]{1,0:T(8,128)(2,1)S(1)}, bf16[320,512]{1,0:T(8,128)(2,1)S(1)}, u32[]{:S(2)}, u32[]{:S(2)}) collective-permute-start(bf16[320,512]{1,0:T(8,128)(2,1)S(1)} %collective-permute-done.12.refs_2_), channel_id=1, source_target_pairs={{0,32},{1,33},{2,34},{3,35},{4,36},{5,37},{6,38},{7,39},{8,40},{9,... | collective-permute-start | bytes 983048 | tf_op jit(solution)/shard_map/last_to_core/ppermute | solution.py:641
  53.4 8.3 %collective-permute-start.10 = (bf16[64,1024]{1,0:T(8,128)(2,1)S(1)}, bf16[64,1024]{1,0:T(8,128)(2,1)S(1)}, u32[]{:S(2)}, u32[]{:S(2)}) collective-permute-start(bf16[64,1024]{1,0:T(8,128)(2,1)S(1)} %get-tuple-element.93.mine), channel_id=1, source_target_pairs={{0,8},{1,9},{2,10},{3,11},{8,0},{9,1},{10,2},{11,3},{16,24},{17,25... | collective-permute-start | bytes 393224 | tf_op jit(solution)/shard_map/panels_z2/ppermute | solution.py:641
  62.3 8.3 %collective-permute-start.15 = (bf16[64,512]{1,0:T(8,128)(2,1)S(1)}, bf16[64,512]{1,0:T(8,128)(2,1)S(1)}, u32[]{:S(2)}, u32[]{:S(2)}) collective-permute-start(bf16[64,512]{1,0:T(8,128)(2,1)S(1)} %get-tuple-element.102.mine), channel_id=1, source_target_pairs={{0,24},{1,25},{2,26},{3,27},{8,16},{9,17},{10,18},{11,19},{16,8},{... | collective-permute-start | bytes 196616 | tf_op jit(solution)/shard_map/panels_z3/ppermute | solution.py:641
  71.8 4.5 %collective-permute-start.16 = (bf16[64,1536]{1,0:T(8,128)(2,1)S(1)}, bf16[64,1536]{1,0:T(8,128)(2,1)S(1)}, u32[]{:S(2)}, u32[]{:S(2)}) collective-permute-start(bf16[64,1536]{1,0:T(8,128)(2,1)S(1)} %shard_map.136.mine), channel_id=1, source_target_pairs={{0,4},{1,5},{2,6},{3,7},{8,12},{9,13},{10,14},{11,15},{16,20},{17,... | collective-permute-start | bytes 589832 | tf_op jit(solution)/shard_map/down_z1/ppermute | solution.py:641
  77.3 7.7 %collective-permute-start.17 = (bf16[64,2048]{1,0:T(8,128)(2,1)S(1)}, bf16[64,2048]{1,0:T(8,128)(2,1)S(1)}, u32[]{:S(2)}, u32[]{:S(2)}) collective-permute-start(bf16[64,2048]{1,0:T(8,128)(2,1)S(1)} %shard_map.137.mine), channel_id=1, source_target_pairs={{0,3},{1,2},{2,1},{3,0},{4,7},{5,6},{6,5},{7,4},{8,11},{9,10},{10,... | collective-permute-start | bytes 786440 | tf_op jit(solution)/shard_map/down_ring/ppermute | solution.py:641
  86.4 5.4 %collective-permute-start.19 = (bf16[128,640]{1,0:T(8,128)(2,1)S(1)}, bf16[128,640]{1,0:T(8,128)(2,1)S(1)}, u32[]{:S(2)}, u32[]{:S(2)}) collective-permute-start(bf16[128,640]{1,0:T(8,128)(2,1)S(1)} %get-tuple-element.115), channel_id=1, source_target_pairs={{0,1},{1,0},{2,3},{3,2},{4,5},{5,4},{6,7},{7,6},{8,9},{9,8},{10,11... | collective-permute-start | bytes 491528 | tf_op jit(solution)/shard_map/rows_back/ppermute | solution.py:641
  88.0 6.5 %collective-permute-start.20 = (bf16[128,512]{1,0:T(8,128)(2,1)}, bf16[128,512]{1,0:T(8,128)(2,1)S(1)}, u32[]{:S(2)}, u32[]{:S(2)}) collective-permute-start(bf16[128,512]{1,0:T(8,128)(2,1)} %get-tuple-element.122), channel_id=1, source_target_pairs={{0,1},{1,0},{2,3},{3,2},{4,5},{5,4},{6,7},{7,6},{8,9},{9,8},{10,11... | collective-permute-start | bytes 393224 | tf_op jit(solution)/shard_map/sep_back/ppermute | solution.py:641
  94.5 7.4 %copy-start.2 = (bf16[128,512]{1,0:T(8,128)(2,1)}, bf16[128,512]{1,0:T(8,128)(2,1)S(1)}, u32[]{:S(2)}) copy-start(bf16[128,512]{1,0:T(8,128)(2,1)S(1)} %collective-permute-done.20.recv) | copy-start | bytes 393220
  94.5 19.0 %all-to-all-start = ((bf16[32,16,256]{2,1,0:T(8,128)(2,1)}), bf16[32,16,256]{2,1,0:T(8,128)(2,1)S(1)}, u32[]{:S(2)}, u32[]{:S(2)}) async-start(bf16[32,16,256]{2,1,0:T(8,128)(2,1)} %bitcast.11), calls=%async_computation | async-start | bytes 524288 | tf_op jit(solution)/shard_map/all_to_all | solution.py:882

commit v7 on v6

--- a/solution.py
+++ b/solution.py
@@ -209,8 +209,7 @@
 
 
 def leaf_second(yt, cpl_v, terms):
-    for l in range(1, LEVELS):
-        terms[:, (l - 1) * U : l * U] = dot_t(yt[...], cpl_v[l]).astype(BF)
+    terms[...] = dot_t(yt[...], cpl_v[1:].reshape(PANEL, LEAF)).astype(BF)
 
 
 def which(place):
@@ -236,7 +235,7 @@
     first = core == 0
     low = (z == 2) | (z == 0)
     same = (low & first) | (~low & ~first)
-    return inner & same, inner & ~same, ~inner & same, ~inner & ~same
+    return inner & same, inner & ~same, ~inner & ~same, ~inner & same
 
 
 def pick_one(core, y, z):
@@ -475,56 +474,58 @@
         store.wait()
 
 
-def leaf_half(rows, inv, cpl, yt, chosen):
-    total = yt.astype(F32)
-    for l in range(LEVELS):
-        total = total - dot(rows[:, l * U : (l + 1) * U], cpl[l])
-    back = total.astype(BF)
+def leaf_half(rows, inv, cpl, yt):
+    back = (yt.astype(F32) - dot(rows[...], cpl[...].reshape(TERM, LEAF))).astype(BF)
     parts = []
     for i in range(4):
         start = i * 256
         parts.append(dot(back[:, start:], inv[start:, start : start + 256]).astype(BF))
-    xt = jnp.concatenate(parts, axis=1)
-    return xt, dot_t(chosen[...], xt).astype(BF)
+    return jnp.concatenate(parts, axis=1)
 
 
 def leaf_mine(place, keep, inv, cpl, yt, chosen, xt_out, picks_out):
     side = half_of(place)
-    xt, picks = leaf_half(keep, inv, cpl, yt[pl.ds(pl.multiple_of(side * 128, 128), 128)], chosen)
+    xt = leaf_half(keep, inv, cpl, yt[pl.ds(pl.multiple_of(side * 128, 128), 128)])
     xt_out[...] = xt
-    picks_out[...] = picks
+    picks_out[...] = dot_t(chosen[...], xt).astype(BF)
 
 
 def leaf_other(place, recv, inv, cpl, yt, chosen, xt_mine, picks_mine, xt_out, picks_out, xt, picks, sems):
     side = half_of(place)
     mine = pl.ds(pl.multiple_of(side * 128, 128), 128)
     other = pl.ds(pl.multiple_of((1 - side) * 128, 128), 128)
+    xt[mine] = xt_mine[...]
     picks[:, mine] = picks_mine[...]
-    xt[mine] = xt_mine[...]
-    far, far_picks = leaf_half(recv, inv, cpl, yt[other], chosen)
-    picks[:, other] = far_picks
-    stores = [pltpu.make_async_copy(picks, picks_out, sems.at[0])]
+    far = leaf_half(recv, inv, cpl, yt[other])
+    xt[other] = far
+    stores = [pltpu.make_async_copy(xt, xt_out, sems.at[0])]
     stores[0].start()
-    xt[other] = far
-    stores.append(pltpu.make_async_copy(xt, xt_out, sems.at[1]))
-    stores[1].start()
+    for i in range(2):
+        part = slice(i * 16 * SLOTS, (i + 1) * 16 * SLOTS)
+        picks[part, other] = dot_t(chosen[part], far).astype(BF)
+        stores.append(pltpu.make_async_copy(picks.at[part], picks_out.at[part], sems.at[1 + i]))
+        stores[-1].start()
     for store in stores:
         store.wait()
 
 
-def turn_back(place, keep, recv, xt, x_sep, x_leaf, keep_v, recv_v, xt_v, both, sems):
+def turn_leaf(xt, x_leaf, xt_v, sems):
+    load = pltpu.make_async_copy(xt, xt_v, sems.at[0])
+    load.start()
+    load.wait()
+    for i in range(4):
+        part = slice(i * 256, (i + 1) * 256)
+        x_leaf[part] = xt_v[:, part].astype(F32).T.astype(BF)
+
+
+def turn_sep(place, keep, recv, x_sep, keep_v, recv_v, both, sems):
     loads = [
         pltpu.make_async_copy(keep, keep_v, sems.at[0]),
         pltpu.make_async_copy(recv, recv_v, sems.at[1]),
-        pltpu.make_async_copy(xt, xt_v, sems.at[2]),
     ]
     for load in loads:
         load.start()
-    loads[2].wait()
-    for i in range(4):
-        part = slice(i * 256, (i + 1) * 256)
-        x_leaf[part] = xt_v[:, part].astype(F32).T.astype(BF)
-    for load in loads[:2]:
+    for load in loads:
         load.wait()
     side = half_of(place)
     both[pl.ds(pl.multiple_of(side * 128, 128), 128)] = keep_v[...].astype(F32)
@@ -797,7 +798,7 @@
     with jax.named_scope("factor_top"):
         last = route(
             triangle,
-            lambda c, y, z: (0, y, 0) if (c, z) == (0, 3) else (1, y, 6) if (c, z) == (1, 3) else None,
+            lambda c, y, z: (c, y, 0 if c else 6) if z == 3 else None,
         )
     with jax.named_scope("first_factor_to_odd"):
         passed_far = to_odd(after(passed, f2))
@@ -867,32 +868,33 @@
         [SMEM] + [VMEM] * 5,
     )
     recv = after(recv, xt_mine)
-    with jax.named_scope("sep_back"):
-        sep_recv = swap(sep_send, 1)
     xt, picks = call(
         leaf_other,
         [stored(NC, LEAF), stored(32 * SLOTS, NC)],
         [place, recv, inv_v, cpl_v, yt, chosen, xt_mine, picks_mine],
         [SMEM] + [VMEM] * 7,
-        [pltpu.VMEM((NC, LEAF), BF), pltpu.VMEM((32 * SLOTS, NC), BF), dma(2)],
+        [pltpu.VMEM((NC, LEAF), BF), pltpu.VMEM((32 * SLOTS, NC), BF), dma(3)],
         [HBM, HBM],
         moved=14 * 10**6,
     )
-    picks, sep_recv = lax.optimization_barrier((picks, sep_recv))
+    with jax.named_scope("sep_back"):
+        sep_recv = swap(after(sep_send, picks), 1)
     got = lax.all_to_all(
         picks.reshape(32, SLOTS, NC), rows_axis, 0, 0, tiled=True
     ).reshape(32 * SLOTS, NC)
-    x_sep, x_leaf = call(
-        turn_back,
-        [plain(PANEL, NC), plain(LEAF, NC)],
-        [place, sep_keep, sep_recv, xt],
-        [SMEM, HBM, HBM, HBM],
+    (x_leaf,) = call(
+        turn_leaf, [plain(LEAF, NC)], [xt], [HBM], [pltpu.VMEM((NC, LEAF), BF), dma(1)]
+    )
+    (x_sep,) = call(
+        turn_sep,
+        [plain(PANEL, NC)],
+        [place, sep_keep, sep_recv],
+        [SMEM, HBM, HBM],
         [
             pltpu.VMEM((128, PANEL), BF),
             pltpu.VMEM((128, PANEL), BF),
-            pltpu.VMEM((NC, LEAF), BF),
             pltpu.VMEM((NC, PANEL), F32),
-            dma(3),
+            dma(2),
         ],
     )
     (stretch,) = call(

time: 116 us -> 115 us (level)
  starting transfers between devices: 37.8 us -> 36.2 us
    all_to_all x1, waiting for transfers between devices: 8.69 us -> 3.08 us  [on_device(): lax.all_to_all(picks.reshape(32, SLOTS, NC), rows_axis, 0, 0, tiled=True)]
    ppermute x21, waiting for transfers between devices: 31.4 us -> 36.5 us  [route(): return lax.ppermute(value, (cols_axis, rows_axis), pairs)]
    ppermute x21, starting transfers between devices: 30.4 us -> 29 us  [route(): return lax.ppermute(value, (cols_axis, rows_axis), pairs)]
    pallas_call x24 -> x25, Pallas kernels: 36.1 us -> 37 us  [call(): pl.pallas_call(body, out_shape=outs, in_specs=specs, out_specs=out_specs...]
  transfers between devices with their start and end apart: 22 -> 22, of which waited for: 11 -> 13; matrix products, arithmetic and copies ran while one was open for 0% -> 0% of each run, Pallas kernels for 27% -> 26%
where the time goes in v7:
time: 115 us
  waiting for transfers between devices  39.6 us (34%)
  Pallas kernels  37 us (32%)
  starting transfers between devices  36.2 us (31%)
  between operations  1.23 us (1%)
    pallas_call x25, Pallas kernels, call(): pl.pallas_call(body, out_shape=outs, in_specs=specs, out_specs=out_specs...  37 us
    ppermute x21, waiting for transfers between devices, route(): return lax.ppermute(value, (cols_axis, rows_axis), pairs)  36.5 us
    ppermute x21, starting transfers between devices, route(): return lax.ppermute(value, (cols_axis, rows_axis), pairs)  29 us
    all_to_all x1, starting transfers between devices, on_device(): lax.all_to_all(picks.reshape(32, SLOTS, NC), rows_axis, 0, 0, tiled=True)  7.22 us
    all_to_all x1, waiting for transfers between devices, on_device(): lax.all_to_all(picks.reshape(32, SLOTS, NC), rows_axis, 0, 0, tiled=True)  3.08 us
  transfers between devices with their start and end apart: 22, of which 13 were waited for; matrix products, arithmetic and copies ran while one was open for 0% of the time, Pallas kernels for 26%

profile of v7, /device:TPU:2, one launch (start us, length us, event | category | flops | bytes accessed | tf_op | source)
XLA Modules:
  0.0 114.8 jit_solution(9994027927679135901)
XLA Ops:
  0.8 1.8 %shard_map.121 = (bf16[720,512]{1,0:T(8,128)(2,1)S(1)}, bf16[368,512]{1,0:T(8,128)(2,1)S(1)}) custom-call(s32[4]{0:T(128)S(1)} %pad_add_fusion.place, bf16[512,512]{1,0:T(8,128)(2,1)} %inv.4, bf16[512,512]{1,0:T(8,128)(2,1)} %bitcast.9, s32[1,4,128]{2,1,0:T(4,128)} %sep_idx.3), custom_call_target="tpu_custom_call" | custom-call | flops 100000000 | bytes 1000000 | tf_op jit(solution)/shard_map/pallas_call | solution.py:61
  3.9 3.9 %shard_map.122 = (bf16[256,1024]{1,0:T(8,128)(2,1)S(1)}, bf16[256,512]{1,0:T(8,128)(2,1)S(1)}, bf16[320,128]{1,0:T(8,128)(2,1)S(1)}, bf16[1024,1024]{1,0:T(8,128)(2,1)S(1)}, bf16[5,128,1024]{2,1,0:T(8,128)(2,1)S(1)}) custom-call(s32[4]{0:T(128)S(1)} %pad_add_fusion.place, bf16[1024,1024]{1,0:T(8,128)(2,1)} %inv.3, bf16[1024,256]{1,0:T(8,128)(2,1)} %rhs.1, ...), custom_call_target="tpu_custom_call" | custom-call | flops 100000000 | bytes 1000000 | tf_op jit(solution)/shard_map/pallas_call | solution.py:61
  7.8 2.7 %collective-permute-start = (bf16[320,128]{1,0:T(8,128)(2,1)S(1)}, bf16[320,128]{1,0:T(8,128)(2,1)S(1)}, u32[]{:S(2)}, u32[]{:S(2)}) collective-permute-start(bf16[320,128]{1,0:T(8,128)(2,1)S(1)} %get-tuple-element.65.one), channel_id=1, source_target_pairs={{0,1},{1,0},{2,3},{3,2},{4,5},{5,4},{6,7},{7,6},{8,9},{9,8},{10,11... | collective-permute-start | bytes 245768 | tf_op jit(solution)/shard_map/first_terms/ppermute | solution.py:642
  13.5 3.2 %collective-permute-done.recv.other = bf16[320,128]{1,0:T(8,128)(2,1)S(1)} collective-permute-done((bf16[320,128]{1,0:T(8,128)(2,1)S(1)}, bf16[320,128]{1,0:T(8,128)(2,1)S(1)}, u32[]{:S(2)}, u32[]{:S(2)}) %collective-permute-start) | collective-permute-done | bytes 81952 | tf_op jit(solution)/shard_map/first_terms/ppermute | solution.py:642
  16.7 3.2 %collective-permute-start.7 = (bf16[368,512]{1,0:T(8,128)(2,1)S(1)}, bf16[368,512]{1,0:T(8,128)(2,1)S(1)}, u32[]{:S(2)}, u32[]{:S(2)}) collective-permute-start(bf16[368,512]{1,0:T(8,128)(2,1)S(1)} %collective-permute-done.3.refs_1_), channel_id=1, source_target_pairs={{0,3},{2,1},{4,7},{6,5},{8,11},{10,9},{12,15},{14,13},{16,19},{18,... | collective-permute-start | bytes 1130504 | tf_op jit(solution)/shard_map/factors_across/ppermute | solution.py:642
  21.4 2.2 %collective-permute-done.4.refs_3_ = bf16[368,512]{1,0:T(8,128)(2,1)S(1)} collective-permute-done((bf16[368,512]{1,0:T(8,128)(2,1)S(1)}, bf16[368,512]{1,0:T(8,128)(2,1)S(1)}, u32[]{:S(2)}, u32[]{:S(2)}) %collective-permute-start.4) | collective-permute-done | bytes 376864 | tf_op jit(solution)/shard_map/factors_to_other/ppermute | solution.py:642
  24.9 2.5 %shard_map.126 = (bf16[512,1024]{1,0:T(8,128)(2,1)S(1)}, bf16[2,64,512]{2,1,0:T(8,128)(2,1)}) custom-call(s32[4]{0:T(128)S(1)} %pad_add_fusion.place, s32[6,2048]{1,0:T(8,128)S(1)} %copy-done, f32[6,2048]{1,0:T(8,128)S(1)} %copy-done.1), custom_call_target="tpu_custom_call" | custom-call | flops 100000000 | bytes 1000000 | tf_op jit(solution)/shard_map/pallas_call | solution.py:61
  31.3 1.8 %shard_map.130 = (bf16[768,512]{1,0:T(8,128)(2,1)S(1)}, bf16[512,256]{1,0:T(8,128)(2,1)S(1)}, bf16[464,512]{1,0:T(8,128)(2,1)S(1)}, bf16[320,512]{1,0:T(8,128)(2,1)S(1)}) custom-call(s32[4]{0:T(128)S(1)} %pad_add_fusion.place, bf16[720,512]{1,0:T(8,128)(2,1)S(1)} %get-tuple-element.63.refs_0_, bf16[368,512]{1,0:T(8,128)(2,1)S(1)} %collective-permute-done.3.refs_1_, ...), custom_call_target="tpu_custom_call" | custom-call | flops 100000000 | bytes 1000000 | tf_op jit(solution)/shard_map/pallas_call | solution.py:61
  36.2 3.3 %collective-permute-done.2.recv = bf16[64,2048]{1,0:T(8,128)(2,1)S(1)} collective-permute-done((bf16[64,2048]{1,0:T(8,128)(2,1)S(1)}, bf16[64,2048]{1,0:T(8,128)(2,1)S(1)}, u32[]{:S(2)}, u32[]{:S(2)}) %collective-permute-start.2) | collective-permute-done | bytes 262176 | tf_op jit(solution)/shard_map/panels_ring/ppermute | solution.py:642
  41.5 1.4 %collective-permute-start.18 = (bf16[1152,512]{1,0:T(8,128)(2,1)S(1)}, bf16[1152,512]{1,0:T(8,128)(2,1)S(1)}, u32[]{:S(2)}, u32[]{:S(2)}) collective-permute-start(bf16[1152,512]{1,0:T(8,128)(2,1)S(1)} %get-tuple-element.104.own), channel_id=1, source_target_pairs={{0,1},{2,3},{4,5},{6,7},{8,9},{10,11},{12,13},{14,15},{16,17},{18,... | collective-permute-start | bytes 3538952 | tf_op jit(solution)/shard_map/first_factor_to_odd/ppermute | solution.py:642
  42.9 9.2 %collective-permute-done.9.recv = bf16[64,1536]{1,0:T(8,128)(2,1)S(1)} collective-permute-done((bf16[64,1536]{1,0:T(8,128)(2,1)S(1)}, bf16[64,1536]{1,0:T(8,128)(2,1)S(1)}, u32[]{:S(2)}, u32[]{:S(2)}) %collective-permute-start.9) | collective-permute-done | bytes 196640 | tf_op jit(solution)/shard_map/panels_z1/ppermute | solution.py:642
  53.4 3.8 %collective-permute-start.10 = (bf16[64,1024]{1,0:T(8,128)(2,1)S(1)}, bf16[64,1024]{1,0:T(8,128)(2,1)S(1)}, u32[]{:S(2)}, u32[]{:S(2)}) collective-permute-start(bf16[64,1024]{1,0:T(8,128)(2,1)S(1)} %get-tuple-element.90.mine), channel_id=1, source_target_pairs={{0,8},{1,9},{2,10},{3,11},{8,0},{9,1},{10,2},{11,3},{16,24},{17,25... | collective-permute-start | bytes 393224 | tf_op jit(solution)/shard_map/panels_z2/ppermute | solution.py:642
  58.3 1.7 %shard_map.134 = (bf16[512,512]{1,0:T(8,128)(2,1)S(1)}, bf16[512,128]{1,0:T(8,128)(2,1)}) custom-call(s32[4]{0:T(128)S(1)} %pad_add_fusion.place, bf16[464,512]{1,0:T(8,128)(2,1)S(1)} %collective-permute-done.11.refs_0_, bf16[464,512]{1,0:T(8,128)(2,1)S(1)} %collective-permute-done.13.refs_1_, bf16[320,512]{1,0:T(8,128)(2,1)S(1)} %collective-permute-done.12.refs_2_, ...), custom_call_target="tpu_custom_call" | custom-call | flops 100000000 | bytes 1000000 | tf_op jit(solution)/shard_map/pallas_call | solution.py:61
  60.0 1.6 %collective-permute-done.10.recv = bf16[64,1024]{1,0:T(8,128)(2,1)S(1)} collective-permute-done((bf16[64,1024]{1,0:T(8,128)(2,1)S(1)}, bf16[64,1024]{1,0:T(8,128)(2,1)S(1)}, u32[]{:S(2)}, u32[]{:S(2)}) %collective-permute-start.10) | collective-permute-done | bytes 131104 | tf_op jit(solution)/shard_map/panels_z2/ppermute | solution.py:642
  62.3 4.7 %collective-permute-start.15 = (bf16[64,512]{1,0:T(8,128)(2,1)S(1)}, bf16[64,512]{1,0:T(8,128)(2,1)S(1)}, u32[]{:S(2)}, u32[]{:S(2)}) collective-permute-start(bf16[64,512]{1,0:T(8,128)(2,1)S(1)} %get-tuple-element.99.mine), channel_id=1, source_target_pairs={{0,24},{1,25},{2,26},{3,27},{8,16},{9,17},{10,18},{11,19},{16,8},{... | collective-permute-start | bytes 196616 | tf_op jit(solution)/shard_map/panels_z3/ppermute | solution.py:642
  67.0 3.6 %collective-permute-done.15.recv = bf16[64,512]{1,0:T(8,128)(2,1)S(1)} collective-permute-done((bf16[64,512]{1,0:T(8,128)(2,1)S(1)}, bf16[64,512]{1,0:T(8,128)(2,1)S(1)}, u32[]{:S(2)}, u32[]{:S(2)}) %collective-permute-start.15) | collective-permute-done | bytes 65568 | tf_op jit(solution)/shard_map/panels_z3/ppermute | solution.py:642
  71.8 1.3 %collective-permute-start.16 = (bf16[64,1536]{1,0:T(8,128)(2,1)S(1)}, bf16[64,1536]{1,0:T(8,128)(2,1)S(1)}, u32[]{:S(2)}, u32[]{:S(2)}) collective-permute-start(bf16[64,1536]{1,0:T(8,128)(2,1)S(1)} %shard_map.136.mine), channel_id=1, source_target_pairs={{0,4},{1,5},{2,6},{3,7},{8,12},{9,13},{10,14},{11,15},{16,20},{17,... | collective-permute-start | bytes 589832 | tf_op jit(solution)/shard_map/down_z1/ppermute | solution.py:642
  73.1 3.2 %collective-permute-done.16.recv = bf16[64,1536]{1,0:T(8,128)(2,1)S(1)} collective-permute-done((bf16[64,1536]{1,0:T(8,128)(2,1)S(1)}, bf16[64,1536]{1,0:T(8,128)(2,1)S(1)}, u32[]{:S(2)}, u32[]{:S(2)}) %collective-permute-start.16) | collective-permute-done | bytes 196640 | tf_op jit(solution)/shard_map/down_z1/ppermute | solution.py:642
  77.3 1.6 %collective-permute-start.17 = (bf16[64,2048]{1,0:T(8,128)(2,1)S(1)}, bf16[64,2048]{1,0:T(8,128)(2,1)S(1)}, u32[]{:S(2)}, u32[]{:S(2)}) collective-permute-start(bf16[64,2048]{1,0:T(8,128)(2,1)S(1)} %shard_map.137.mine), channel_id=1, source_target_pairs={{0,3},{1,2},{2,1},{3,0},{4,7},{5,6},{6,5},{7,4},{8,11},{9,10},{10,... | collective-permute-start | bytes 786440 | tf_op jit(solution)/shard_map/down_ring/ppermute | solution.py:642
  79.7 5.2 %collective-permute-done.17.recv = bf16[64,2048]{1,0:T(8,128)(2,1)S(1)} collective-permute-done((bf16[64,2048]{1,0:T(8,128)(2,1)S(1)}, bf16[64,2048]{1,0:T(8,128)(2,1)S(1)}, u32[]{:S(2)}, u32[]{:S(2)}) %collective-permute-start.17) | collective-permute-done | bytes 262176 | tf_op jit(solution)/shard_map/down_ring/ppermute | solution.py:642
  85.0 1.5 %shard_map.139 = (bf16[128,512]{1,0:T(8,128)(2,1)S(1)}, bf16[128,2048]{1,0:T(8,128)(2,1)S(1)}, bf16[128,640]{1,0:T(8,128)(2,1)S(1)}) custom-call(s32[4]{0:T(128)S(1)} %pad_add_fusion.place, bf16[64,2048]{1,0:T(8,128)(2,1)S(1)} %shard_map.137.mine, bf16[64,2048]{1,0:T(8,128)(2,1)S(1)} %collective-permute-done.17.recv, ...), custom_call_target="tpu_custom_call" | custom-call | flops 100000000 | bytes 1000000 | tf_op jit(solution)/shard_map/pallas_call | solution.py:61
  86.5 1.5 %shard_map.140 = (bf16[128,640]{1,0:T(8,128)(2,1)S(1)}, bf16[128,512]{1,0:T(8,128)(2,1)}, bf16[128,512]{1,0:T(8,128)(2,1)}) custom-call(s32[4]{0:T(128)S(1)} %pad_add_fusion.place, bf16[128,512]{1,0:T(8,128)(2,1)S(1)} %get-tuple-element.110.x1_ref, bf16[128,2048]{1,0:T(8,128)(2,1)S(1)} %get-tuple-element.111.x, ...), custom_call_target="tpu_custom_call" | custom-call | flops 100000000 | bytes 1000000 | tf_op jit(solution)/shard_map/pallas_call | solution.py:61
  88.0 1.6 %shard_map.141 = (bf16[128,1024]{1,0:T(8,128)(2,1)S(1)}, bf16[512,128]{1,0:T(8,128)(2,1)S(1)}) custom-call(s32[4]{0:T(128)S(1)} %pad_add_fusion.place, bf16[128,640]{1,0:T(8,128)(2,1)S(1)} %get-tuple-element.112.keep, bf16[1024,1024]{1,0:T(8,128)(2,1)S(1)} %get-tuple-element.113.inv, bf16[5,128,1024]{2,1,0:T(8,128)(2,1)S(1)} %get-tuple-element.69.cpl_v.cpl, ...), custom_call_target="tpu_custom_call" | custom-call | flops 100000000 | bytes 1000000 | tf_op jit(solution)/shard_map/pallas_call | solution.py:61
  89.6 2.3 %collective-permute-done.19.recv = bf16[128,640]{1,0:T(8,128)(2,1)S(1)} collective-permute-done((bf16[128,640]{1,0:T(8,128)(2,1)S(1)}, bf16[128,640]{1,0:T(8,128)(2,1)S(1)}, u32[]{:S(2)}, u32[]{:S(2)}) %collective-permute-start.19) | collective-permute-done | bytes 163872 | tf_op jit(solution)/shard_map/rows_back/ppermute | solution.py:642
  91.8 2.2 %shard_map.142 = (bf16[256,1024]{1,0:T(8,128)(2,1)}, bf16[512,256]{1,0:T(8,128)(2,1)}) custom-call(s32[4]{0:T(128)S(1)} %pad_add_fusion.place, bf16[128,640]{1,0:T(8,128)(2,1)S(1)} %collective-permute-done.19.recv, bf16[1024,1024]{1,0:T(8,128)(2,1)S(1)} %get-tuple-element.113.inv, bf16[5,128,1024]{2,1,0:T(8,128)(2,1)S(1)} %get-tuple-element.69.cpl_v.cpl, ...), custom_call_target="tpu_custom_call" | custom-call | flops 100000000 | bytes 14000000 | tf_op jit(solution)/shard_map/pallas_call | solution.py:61
  94.1 7.2 %all-to-all-start = ((bf16[32,16,256]{2,1,0:T(8,128)(2,1)}), bf16[32,16,256]{2,1,0:T(8,128)(2,1)S(1)}, u32[]{:S(2)}, u32[]{:S(2)}) async-start(bf16[32,16,256]{2,1,0:T(8,128)(2,1)} %bitcast.11), calls=%async_computation | async-start | bytes 524288 | tf_op jit(solution)/shard_map/all_to_all | solution.py:882
  101.3 1.9 %collective-permute-start.20 = (bf16[128,512]{1,0:T(8,128)(2,1)S(1)}, bf16[128,512]{1,0:T(8,128)(2,1)S(1)}, u32[]{:S(2)}, u32[]{:S(2)}) collective-permute-start(bf16[128,512]{1,0:T(8,128)(2,1)S(1)} %copy-done.3), channel_id=1, source_target_pairs={{0,1},{1,0},{2,3},{3,2},{4,5},{5,4},{6,7},{7,6},{8,9},{9,8},{10,11... | collective-permute-start | bytes 393224 | tf_op jit(solution)/shard_map/sep_back/ppermute | solution.py:642
  103.2 2.0 %shard_map.143 = bf16[1024,256]{1,0:T(8,128)(2,1)} custom-call(bf16[256,1024]{1,0:T(8,128)(2,1)} %get-tuple-element.117.xt), custom_call_target="tpu_custom_call" | custom-call | flops 100000000 | bytes 1000000 | tf_op jit(solution)/shard_map/pallas_call | solution.py:61
  105.3 1.5 %collective-permute-done.20.recv = bf16[128,512]{1,0:T(8,128)(2,1)S(1)} collective-permute-done((bf16[128,512]{1,0:T(8,128)(2,1)S(1)}, bf16[128,512]{1,0:T(8,128)(2,1)S(1)}, u32[]{:S(2)}, u32[]{:S(2)}) %collective-permute-start.20) | collective-permute-done | bytes 131104 | tf_op jit(solution)/shard_map/sep_back/ppermute | solution.py:642
  107.4 2.4 %shard_map.144 = bf16[512,256]{1,0:T(8,128)(2,1)} custom-call(s32[4]{0:T(128)S(1)} %pad_add_fusion.place, bf16[128,512]{1,0:T(8,128)(2,1)} %get-tuple-element.118.keep, bf16[128,512]{1,0:T(8,128)(2,1)} %copy-done.2), custom_call_target="tpu_custom_call" | custom-call | flops 100000000 | bytes 1000000 | tf_op jit(solution)/shard_map/pallas_call | solution.py:61
  109.8 3.1 %all-to-all-done = bf16[32,16,256]{2,1,0:T(8,128)(2,1)S(1)} async-done(((bf16[32,16,256]{2,1,0:T(8,128)(2,1)}), bf16[32,16,256]{2,1,0:T(8,128)(2,1)S(1)}, u32[]{:S(2)}, u32[]{:S(2)}) %all-to-all-start) | async-done | bytes 262176 | tf_op jit(solution)/shard_map/all_to_all | solution.py:882
  112.9 1.7 %shard_map.145 = f32[64,256]{1,0:T(8,128)} custom-call(bf16[2,64,512]{2,1,0:T(8,128)(2,1)} %get-tuple-element.122.weight, bf16[512,256]{1,0:T(8,128)(2,1)S(1)} %bitcast.8), custom_call_target="tpu_custom_call" | custom-call | flops 100000000 | bytes 1000000 | tf_op jit(solution)/shard_map/pallas_call | solution.py:61
  (46 shorter events, 22.8 us)
Async XLA Ops:
  2.6 14.2 %collective-permute-start.3 = (bf16[368,512]{1,0:T(8,128)(2,1)S(1)}, bf16[368,512]{1,0:T(8,128)(2,1)S(1)}, u32[]{:S(2)}, u32[]{:S(2)}) collective-permute-start(bf16[368,512]{1,0:T(8,128)(2,1)S(1)} %get-tuple-element.79), channel_id=1, source_target_pairs={{1,0},{3,2},{5,4},{7,6},{9,8},{11,10},{13,12},{15,14},{17,16},{19,... | collective-permute-start | bytes 1130504 | tf_op jit(solution)/shard_map/factors_to_pair/ppermute | solution.py:642
  7.8 9.0 %collective-permute-start = (bf16[320,128]{1,0:T(8,128)(2,1)S(1)}, bf16[320,128]{1,0:T(8,128)(2,1)S(1)}, u32[]{:S(2)}, u32[]{:S(2)}) collective-permute-start(bf16[320,128]{1,0:T(8,128)(2,1)S(1)} %get-tuple-element.65.one), channel_id=1, source_target_pairs={{0,1},{1,0},{2,3},{3,2},{4,5},{5,4},{6,7},{7,6},{8,9},{9,8},{10,11... | collective-permute-start | bytes 245768 | tf_op jit(solution)/shard_map/first_terms/ppermute | solution.py:642
  10.5 13.0 %collective-permute-start.4 = (bf16[368,512]{1,0:T(8,128)(2,1)S(1)}, bf16[368,512]{1,0:T(8,128)(2,1)S(1)}, u32[]{:S(2)}, u32[]{:S(2)}) collective-permute-start(bf16[368,512]{1,0:T(8,128)(2,1)S(1)} %get-tuple-element.79), channel_id=1, source_target_pairs={{1,2},{3,0},{5,6},{7,4},{9,10},{11,8},{13,14},{15,12},{17,18},{19,... | collective-permute-start | bytes 1130504 | tf_op jit(solution)/shard_map/factors_to_other/ppermute | solution.py:642
  16.7 12.7 %collective-permute-start.7 = (bf16[368,512]{1,0:T(8,128)(2,1)S(1)}, bf16[368,512]{1,0:T(8,128)(2,1)S(1)}, u32[]{:S(2)}, u32[]{:S(2)}) collective-permute-start(bf16[368,512]{1,0:T(8,128)(2,1)S(1)} %collective-permute-done.3.refs_1_), channel_id=1, source_target_pairs={{0,3},{2,1},{4,7},{6,5},{8,11},{10,9},{12,15},{14,13},{16,19},{18,... | collective-permute-start | bytes 1130504 | tf_op jit(solution)/shard_map/factors_across/ppermute | solution.py:642
  21.2 3.7 %copy-start = (s32[6,2048]{1,0:T(8,128)S(1)}, s32[6,2048]{1,0:T(8,128)}, u32[]{:S(2)}) copy-start(s32[6,2048]{1,0:T(8,128)} %dofs.1) | copy-start | bytes 147460
  21.3 3.7 %copy-start.1 = (f32[6,2048]{1,0:T(8,128)S(1)}, f32[6,2048]{1,0:T(8,128)}, u32[]{:S(2)}) copy-start(f32[6,2048]{1,0:T(8,128)} %coef) | copy-start | bytes 147460
  21.3 7.0 %collective-permute-start.1 = (bf16[128,1024]{1,0:T(8,128)(2,1)S(1)}, bf16[128,1024]{1,0:T(8,128)(2,1)S(1)}, u32[]{:S(2)}, u32[]{:S(2)}) collective-permute-start(bf16[128,1024]{1,0:T(8,128)(2,1)S(1)} %get-tuple-element.72), channel_id=1, source_target_pairs={{0,1},{1,0},{2,3},{3,2},{4,5},{5,4},{6,7},{7,6},{8,9},{9,8},{10,11... | collective-permute-start | bytes 786440 | tf_op jit(solution)/shard_map/terms_pair/ppermute | solution.py:642
  23.6 7.2 %collective-permute-start.5 = (bf16[368,512]{1,0:T(8,128)(2,1)S(1)}, bf16[368,512]{1,0:T(8,128)(2,1)S(1)}, u32[]{:S(2)}, u32[]{:S(2)}) collective-permute-start(bf16[368,512]{1,0:T(8,128)(2,1)S(1)} %collective-permute-done.3.refs_1_), channel_id=1, source_target_pairs={{0,32},{1,33},{2,34},{3,35},{4,36},{5,37},{6,38},{7,39},{8,40},{9,... | collective-permute-start | bytes 1130504 | tf_op jit(solution)/shard_map/pair_to_core/ppermute | solution.py:642
  23.6 7.2 %collective-permute-start.6 = (bf16[368,512]{1,0:T(8,128)(2,1)S(1)}, bf16[368,512]{1,0:T(8,128)(2,1)S(1)}, u32[]{:S(2)}, u32[]{:S(2)}) collective-permute-start(bf16[368,512]{1,0:T(8,128)(2,1)S(1)} %collective-permute-done.4.refs_3_), channel_id=1, source_target_pairs={{0,32},{1,33},{2,34},{3,35},{4,36},{5,37},{6,38},{7,39},{8,40},{9,... | collective-permute-start | bytes 1130504 | tf_op jit(solution)/shard_map/beside_to_core/ppermute | solution.py:642
  29.5 1.8 %collective-permute-start.8 = (bf16[368,512]{1,0:T(8,128)(2,1)S(1)}, bf16[368,512]{1,0:T(8,128)(2,1)S(1)}, u32[]{:S(2)}, u32[]{:S(2)}) collective-permute-start(bf16[368,512]{1,0:T(8,128)(2,1)S(1)} %collective-permute-done.7.refs_5_), channel_id=1, source_target_pairs={{0,32},{1,33},{2,34},{3,35},{4,36},{5,37},{6,38},{7,39},{8,40},{9,... | collective-permute-start | bytes 1130504 | tf_op jit(solution)/shard_map/far_to_core/ppermute | solution.py:642
  29.6 9.9 %collective-permute-start.2 = (bf16[64,2048]{1,0:T(8,128)(2,1)S(1)}, bf16[64,2048]{1,0:T(8,128)(2,1)S(1)}, u32[]{:S(2)}, u32[]{:S(2)}) collective-permute-start(bf16[64,2048]{1,0:T(8,128)(2,1)S(1)} %get-tuple-element.78), channel_id=1, source_target_pairs={{0,3},{1,2},{2,1},{3,0},{4,7},{5,6},{6,5},{7,4},{8,11},{9,10},{10,... | collective-permute-start | bytes 786440 | tf_op jit(solution)/shard_map/panels_ring/ppermute | solution.py:642
  33.0 19.8 %collective-permute-start.11 = (bf16[464,512]{1,0:T(8,128)(2,1)S(1)}, bf16[464,512]{1,0:T(8,128)(2,1)S(1)}, u32[]{:S(2)}, u32[]{:S(2)}) collective-permute-start(bf16[464,512]{1,0:T(8,128)(2,1)S(1)} %get-tuple-element.91), channel_id=1, source_target_pairs={{4,0},{5,1},{6,2},{7,3},{12,8},{13,9},{14,10},{15,11},{20,16},{21,... | collective-permute-start | bytes 1425416 | tf_op jit(solution)/shard_map/factors_up/ppermute | solution.py:642
  34.3 18.4 %collective-permute-start.12 = (bf16[320,512]{1,0:T(8,128)(2,1)S(1)}, bf16[320,512]{1,0:T(8,128)(2,1)S(1)}, u32[]{:S(2)}, u32[]{:S(2)}) collective-permute-start(bf16[320,512]{1,0:T(8,128)(2,1)S(1)} %get-tuple-element.92), channel_id=1, source_target_pairs={{12,24},{13,25},{14,26},{15,27},{44,32},{45,33},{46,34},{47,35},{7... | collective-permute-start | bytes 983048 | tf_op jit(solution)/shard_map/factor_top/ppermute | solution.py:642
  40.2 11.9 %collective-permute-start.9 = (bf16[64,1536]{1,0:T(8,128)(2,1)S(1)}, bf16[64,1536]{1,0:T(8,128)(2,1)S(1)}, u32[]{:S(2)}, u32[]{:S(2)}) collective-permute-start(bf16[64,1536]{1,0:T(8,128)(2,1)S(1)} %get-tuple-element.89.mine), channel_id=1, source_target_pairs={{4,0},{5,1},{6,2},{7,3},{12,8},{13,9},{14,10},{15,11},{20,16},{21,... | collective-permute-start | bytes 589832 | tf_op jit(solution)/shard_map/panels_z1/ppermute | solution.py:642
  41.5 37.4 %collective-permute-start.18 = (bf16[1152,512]{1,0:T(8,128)(2,1)S(1)}, bf16[1152,512]{1,0:T(8,128)(2,1)S(1)}, u32[]{:S(2)}, u32[]{:S(2)}) collective-permute-start(bf16[1152,512]{1,0:T(8,128)(2,1)S(1)} %get-tuple-element.104.own), channel_id=1, source_target_pairs={{0,1},{2,3},{4,5},{6,7},{8,9},{10,11},{12,13},{14,15},{16,17},{18,... | collective-permute-start | bytes 3538952 | tf_op jit(solution)/shard_map/first_factor_to_odd/ppermute | solution.py:642
  52.8 4.4 %collective-permute-start.13 = (bf16[464,512]{1,0:T(8,128)(2,1)S(1)}, bf16[464,512]{1,0:T(8,128)(2,1)S(1)}, u32[]{:S(2)}, u32[]{:S(2)}) collective-permute-start(bf16[464,512]{1,0:T(8,128)(2,1)S(1)} %collective-permute-done.11.refs_0_), channel_id=1, source_target_pairs={{0,32},{1,33},{2,34},{3,35},{4,36},{5,37},{6,38},{7,39},{8,40},{9,... | collective-permute-start | bytes 1425416 | tf_op jit(solution)/shard_map/up_to_core/ppermute | solution.py:642
  52.9 5.4 %collective-permute-start.14 = (bf16[320,512]{1,0:T(8,128)(2,1)S(1)}, bf16[320,512]{1,0:T(8,128)(2,1)S(1)}, u32[]{:S(2)}, u32[]{:S(2)}) collective-permute-start(bf16[320,512]{1,0:T(8,128)(2,1)S(1)} %collective-permute-done.12.refs_2_), channel_id=1, source_target_pairs={{0,32},{1,33},{2,34},{3,35},{4,36},{5,37},{6,38},{7,39},{8,40},{9,... | collective-permute-start | bytes 983048 | tf_op jit(solution)/shard_map/last_to_core/ppermute | solution.py:642
  53.4 8.3 %collective-permute-start.10 = (bf16[64,1024]{1,0:T(8,128)(2,1)S(1)}, bf16[64,1024]{1,0:T(8,128)(2,1)S(1)}, u32[]{:S(2)}, u32[]{:S(2)}) collective-permute-start(bf16[64,1024]{1,0:T(8,128)(2,1)S(1)} %get-tuple-element.90.mine), channel_id=1, source_target_pairs={{0,8},{1,9},{2,10},{3,11},{8,0},{9,1},{10,2},{11,3},{16,24},{17,25... | collective-permute-start | bytes 393224 | tf_op jit(solution)/shard_map/panels_z2/ppermute | solution.py:642
  62.3 8.3 %collective-permute-start.15 = (bf16[64,512]{1,0:T(8,128)(2,1)S(1)}, bf16[64,512]{1,0:T(8,128)(2,1)S(1)}, u32[]{:S(2)}, u32[]{:S(2)}) collective-permute-start(bf16[64,512]{1,0:T(8,128)(2,1)S(1)} %get-tuple-element.99.mine), channel_id=1, source_target_pairs={{0,24},{1,25},{2,26},{3,27},{8,16},{9,17},{10,18},{11,19},{16,8},{... | collective-permute-start | bytes 196616 | tf_op jit(solution)/shard_map/panels_z3/ppermute | solution.py:642
  71.8 4.5 %collective-permute-start.16 = (bf16[64,1536]{1,0:T(8,128)(2,1)S(1)}, bf16[64,1536]{1,0:T(8,128)(2,1)S(1)}, u32[]{:S(2)}, u32[]{:S(2)}) collective-permute-start(bf16[64,1536]{1,0:T(8,128)(2,1)S(1)} %shard_map.136.mine), channel_id=1, source_target_pairs={{0,4},{1,5},{2,6},{3,7},{8,12},{9,13},{10,14},{11,15},{16,20},{17,... | collective-permute-start | bytes 589832 | tf_op jit(solution)/shard_map/down_z1/ppermute | solution.py:642
  77.3 7.7 %collective-permute-start.17 = (bf16[64,2048]{1,0:T(8,128)(2,1)S(1)}, bf16[64,2048]{1,0:T(8,128)(2,1)S(1)}, u32[]{:S(2)}, u32[]{:S(2)}) collective-permute-start(bf16[64,2048]{1,0:T(8,128)(2,1)S(1)} %shard_map.137.mine), channel_id=1, source_target_pairs={{0,3},{1,2},{2,1},{3,0},{4,7},{5,6},{6,5},{7,4},{8,11},{9,10},{10,... | collective-permute-start | bytes 786440 | tf_op jit(solution)/shard_map/down_ring/ppermute | solution.py:642
  86.4 5.4 %collective-permute-start.19 = (bf16[128,640]{1,0:T(8,128)(2,1)S(1)}, bf16[128,640]{1,0:T(8,128)(2,1)S(1)}, u32[]{:S(2)}, u32[]{:S(2)}) collective-permute-start(bf16[128,640]{1,0:T(8,128)(2,1)S(1)} %get-tuple-element.109), channel_id=1, source_target_pairs={{0,1},{1,0},{2,3},{3,2},{4,5},{5,4},{6,7},{7,6},{8,9},{9,8},{10,11... | collective-permute-start | bytes 491528 | tf_op jit(solution)/shard_map/rows_back/ppermute | solution.py:642
  91.8 9.5 %copy-start.3 = (bf16[128,512]{1,0:T(8,128)(2,1)S(1)}, bf16[128,512]{1,0:T(8,128)(2,1)}, u32[]{:S(2)}) copy-start(bf16[128,512]{1,0:T(8,128)(2,1)} %get-tuple-element.121) | copy-start | bytes 393220
  94.1 18.8 %all-to-all-start = ((bf16[32,16,256]{2,1,0:T(8,128)(2,1)}), bf16[32,16,256]{2,1,0:T(8,128)(2,1)S(1)}, u32[]{:S(2)}, u32[]{:S(2)}) async-start(bf16[32,16,256]{2,1,0:T(8,128)(2,1)} %bitcast.11), calls=%async_computation | async-start | bytes 524288 | tf_op jit(solution)/shard_map/all_to_all | solution.py:882
  101.3 5.4 %collective-permute-start.20 = (bf16[128,512]{1,0:T(8,128)(2,1)S(1)}, bf16[128,512]{1,0:T(8,128)(2,1)S(1)}, u32[]{:S(2)}, u32[]{:S(2)}) collective-permute-start(bf16[128,512]{1,0:T(8,128)(2,1)S(1)} %copy-done.3), channel_id=1, source_target_pairs={{0,1},{1,0},{2,3},{3,2},{4,5},{5,4},{6,7},{7,6},{8,9},{9,8},{10,11... | collective-permute-start | bytes 393224 | tf_op jit(solution)/shard_map/sep_back/ppermute | solution.py:642
  106.7 0.6 copy-start.2

commit v8 on v7

--- a/solution.py
+++ b/solution.py
@@ -808,7 +808,7 @@
         recv = route(panel, lambda c, y, z: (c, y, z - 1) if z % 2 else None)
     y3, panel = rise(3, panel, recv, f3, h3)
     with jax.named_scope("panels_z2"):
-        recv = route(panel, lambda c, y, z: (c, y, z ^ 2) if z % 2 == 0 else None)
+        recv = route(panel, lambda c, y, z: (c, y, z ^ 2))
     up, last = after((up, last), panel)
     with jax.named_scope("up_to_core"):
         up_o = swap_core(up)
@@ -819,7 +819,7 @@
     recv = after(recv, f4, h4, f5)
     y4, panel = rise(4, panel, recv, f4, h4)
     with jax.named_scope("panels_z3"):
-        recv = route(panel, lambda c, y, z: (c, y, 6 - z) if z % 2 == 0 else None)
+        recv = route(panel, lambda c, y, z: (c, y, 8 - z if z % 2 else 6 - z))
     (x,) = call(
         turn,
         [pinned(64, 3 * PANEL)],
@@ -827,7 +827,7 @@
         [VMEM] * 9,
     )
     with jax.named_scope("down_z1"):
-        recv = route(x, lambda c, y, z: (c, y, z + 1) if z % 2 == 0 else None)
+        recv = route(x, lambda c, y, z: (c, y, z ^ 1))
     (x,) = call(
         level_two_back,
         [pinned(64, 4 * PANEL)],

time: 115 us -> 113 us (0.983)
  starting transfers between devices: 36.2 us -> 28.5 us
  waiting for transfers between devices: 39.6 us -> 45.8 us
    ppermute x21, starting transfers between devices: 29 us -> 22.4 us  [route(): return lax.ppermute(value, (cols_axis, rows_axis), pairs)]
    ppermute x21, waiting for transfers between devices: 36.5 us -> 42.8 us  [route(): return lax.ppermute(value, (cols_axis, rows_axis), pairs)]
    all_to_all x1, starting transfers between devices: 7.22 us -> 6.06 us  [on_device(): lax.all_to_all(picks.reshape(32, SLOTS, NC), rows_axis, 0, 0, tiled=True)]
where the time goes in v8:
time: 113 us
  waiting for transfers between devices  45.8 us (41%)
  Pallas kernels  36.8 us (33%)
  starting transfers between devices  28.5 us (25%)
  between operations  1.21 us (1%)
    ppermute x21, waiting for transfers between devices, route(): return lax.ppermute(value, (cols_axis, rows_axis), pairs)  42.8 us
    pallas_call x25, Pallas kernels, call(): pl.pallas_call(body, out_shape=outs, in_specs=specs, out_specs=out_specs...  36.8 us
    ppermute x21, starting transfers between devices, route(): return lax.ppermute(value, (cols_axis, rows_axis), pairs)  22.4 us
    all_to_all x1, starting transfers between devices, on_device(): lax.all_to_all(picks.reshape(32, SLOTS, NC), rows_axis, 0, 0, tiled=True)  6.06 us
    all_to_all x1, waiting for transfers between devices, on_device(): lax.all_to_all(picks.reshape(32, SLOTS, NC), rows_axis, 0, 0, tiled=True)  3.08 us
  transfers between devices with their start and end apart: 22, of which 13 were waited for; matrix products, arithmetic and copies ran while one was open for 0% of the time, Pallas kernels for 26%

profile of v8, /device:TPU:2, one launch (start us, length us, event | category | flops | bytes accessed | tf_op | source)
XLA Modules:
  0.0 113.0 jit_solution(4832181372800172885)
XLA Ops:
  0.8 1.8 %shard_map.121 = (bf16[720,512]{1,0:T(8,128)(2,1)S(1)}, bf16[368,512]{1,0:T(8,128)(2,1)S(1)}) custom-call(s32[4]{0:T(128)S(1)} %pad_add_fusion.place, bf16[512,512]{1,0:T(8,128)(2,1)} %inv.4, bf16[512,512]{1,0:T(8,128)(2,1)} %bitcast.9, s32[1,4,128]{2,1,0:T(4,128)} %sep_idx.3), custom_call_target="tpu_custom_call" | custom-call | flops 100000000 | bytes 1000000 | tf_op jit(solution)/shard_map/pallas_call | solution.py:61
  3.9 3.9 %shard_map.122 = (bf16[256,1024]{1,0:T(8,128)(2,1)S(1)}, bf16[256,512]{1,0:T(8,128)(2,1)S(1)}, bf16[320,128]{1,0:T(8,128)(2,1)S(1)}, bf16[1024,1024]{1,0:T(8,128)(2,1)S(1)}, bf16[5,128,1024]{2,1,0:T(8,128)(2,1)S(1)}) custom-call(s32[4]{0:T(128)S(1)} %pad_add_fusion.place, bf16[1024,1024]{1,0:T(8,128)(2,1)} %inv.3, bf16[1024,256]{1,0:T(8,128)(2,1)} %rhs.1, ...), custom_call_target="tpu_custom_call" | custom-call | flops 100000000 | bytes 1000000 | tf_op jit(solution)/shard_map/pallas_call | solution.py:61
  7.8 2.7 %collective-permute-start = (bf16[320,128]{1,0:T(8,128)(2,1)S(1)}, bf16[320,128]{1,0:T(8,128)(2,1)S(1)}, u32[]{:S(2)}, u32[]{:S(2)}) collective-permute-start(bf16[320,128]{1,0:T(8,128)(2,1)S(1)} %get-tuple-element.65.one), channel_id=1, source_target_pairs={{0,1},{1,0},{2,3},{3,2},{4,5},{5,4},{6,7},{7,6},{8,9},{9,8},{10,11... | collective-permute-start | bytes 245768 | tf_op jit(solution)/shard_map/first_terms/ppermute | solution.py:642
  13.5 3.2 %collective-permute-done.recv.other = bf16[320,128]{1,0:T(8,128)(2,1)S(1)} collective-permute-done((bf16[320,128]{1,0:T(8,128)(2,1)S(1)}, bf16[320,128]{1,0:T(8,128)(2,1)S(1)}, u32[]{:S(2)}, u32[]{:S(2)}) %collective-permute-start) | collective-permute-done | bytes 81952 | tf_op jit(solution)/shard_map/first_terms/ppermute | solution.py:642
  16.7 3.2 %collective-permute-start.7 = (bf16[368,512]{1,0:T(8,128)(2,1)S(1)}, bf16[368,512]{1,0:T(8,128)(2,1)S(1)}, u32[]{:S(2)}, u32[]{:S(2)}) collective-permute-start(bf16[368,512]{1,0:T(8,128)(2,1)S(1)} %collective-permute-done.3.refs_1_), channel_id=1, source_target_pairs={{0,3},{2,1},{4,7},{6,5},{8,11},{10,9},{12,15},{14,13},{16,19},{18,... | collective-permute-start | bytes 1130504 | tf_op jit(solution)/shard_map/factors_across/ppermute | solution.py:642
  19.9 1.3 %shard_map.125 = (bf16[512,256]{1,0:T(8,128)(2,1)S(1)}, bf16[128,512]{1,0:T(8,128)(2,1)S(1)}, bf16[1152,512]{1,0:T(8,128)(2,1)S(1)}, bf16[128,1024]{1,0:T(8,128)(2,1)S(1)}, bf16[128,1024]{1,0:T(8,128)(2,1)S(1)}) custom-call(s32[4]{0:T(128)S(1)} %pad_add_fusion.place, bf16[320,128]{1,0:T(8,128)(2,1)S(1)} %get-tuple-element.65.one, ...), custom_call_target="tpu_custom_call", output_to_operand_aliasing={{2}: (5, {})} | custom-call | flops 100000000 | bytes 1000000 | tf_op jit(solution)/shard_map/pallas_call | solution.py:61
  21.4 2.2 %collective-permute-done.4.refs_3_ = bf16[368,512]{1,0:T(8,128)(2,1)S(1)} collective-permute-done((bf16[368,512]{1,0:T(8,128)(2,1)S(1)}, bf16[368,512]{1,0:T(8,128)(2,1)S(1)}, u32[]{:S(2)}, u32[]{:S(2)}) %collective-permute-start.4) | collective-permute-done | bytes 376864 | tf_op jit(solution)/shard_map/factors_to_other/ppermute | solution.py:642
  24.9 2.5 %shard_map.126 = (bf16[512,1024]{1,0:T(8,128)(2,1)S(1)}, bf16[2,64,512]{2,1,0:T(8,128)(2,1)}) custom-call(s32[4]{0:T(128)S(1)} %pad_add_fusion.place, s32[6,2048]{1,0:T(8,128)S(1)} %copy-done, f32[6,2048]{1,0:T(8,128)S(1)} %copy-done.1), custom_call_target="tpu_custom_call" | custom-call | flops 100000000 | bytes 1000000 | tf_op jit(solution)/shard_map/pallas_call | solution.py:61
  31.3 1.8 %shard_map.130 = (bf16[768,512]{1,0:T(8,128)(2,1)S(1)}, bf16[512,256]{1,0:T(8,128)(2,1)S(1)}, bf16[464,512]{1,0:T(8,128)(2,1)S(1)}, bf16[320,512]{1,0:T(8,128)(2,1)S(1)}) custom-call(s32[4]{0:T(128)S(1)} %pad_add_fusion.place, bf16[720,512]{1,0:T(8,128)(2,1)S(1)} %get-tuple-element.63.refs_0_, bf16[368,512]{1,0:T(8,128)(2,1)S(1)} %collective-permute-done.3.refs_1_, ...), custom_call_target="tpu_custom_call" | custom-call | flops 100000000 | bytes 1000000 | tf_op jit(solution)/shard_map/pallas_call | solution.py:61
  33.0 1.3 %collective-permute-start.11 = (bf16[464,512]{1,0:T(8,128)(2,1)S(1)}, bf16[464,512]{1,0:T(8,128)(2,1)S(1)}, u32[]{:S(2)}, u32[]{:S(2)}) collective-permute-start(bf16[464,512]{1,0:T(8,128)(2,1)S(1)} %get-tuple-element.91), channel_id=1, source_target_pairs={{4,0},{5,1},{6,2},{7,3},{12,8},{13,9},{14,10},{15,11},{20,16},{21,... | collective-permute-start | bytes 1425416 | tf_op jit(solution)/shard_map/factors_up/ppermute | solution.py:642
  36.2 3.3 %collective-permute-done.2.recv = bf16[64,2048]{1,0:T(8,128)(2,1)S(1)} collective-permute-done((bf16[64,2048]{1,0:T(8,128)(2,1)S(1)}, bf16[64,2048]{1,0:T(8,128)(2,1)S(1)}, u32[]{:S(2)}, u32[]{:S(2)}) %collective-permute-start.2) | collective-permute-done | bytes 262176 | tf_op jit(solution)/shard_map/panels_ring/ppermute | solution.py:642
  41.5 1.4 %collective-permute-start.18 = (bf16[1152,512]{1,0:T(8,128)(2,1)S(1)}, bf16[1152,512]{1,0:T(8,128)(2,1)S(1)}, u32[]{:S(2)}, u32[]{:S(2)}) collective-permute-start(bf16[1152,512]{1,0:T(8,128)(2,1)S(1)} %get-tuple-element.104.own), channel_id=1, source_target_pairs={{0,1},{2,3},{4,5},{6,7},{8,9},{10,11},{12,13},{14,15},{16,17},{18,... | collective-permute-start | bytes 3538952 | tf_op jit(solution)/shard_map/first_factor_to_odd/ppermute | solution.py:642
  42.9 9.2 %collective-permute-done.9.recv = bf16[64,1536]{1,0:T(8,128)(2,1)S(1)} collective-permute-done((bf16[64,1536]{1,0:T(8,128)(2,1)S(1)}, bf16[64,1536]{1,0:T(8,128)(2,1)S(1)}, u32[]{:S(2)}, u32[]{:S(2)}) %collective-permute-start.9) | collective-permute-done | bytes 196640 | tf_op jit(solution)/shard_map/panels_z1/ppermute | solution.py:642
  53.4 1.9 %collective-permute-start.10 = (bf16[64,1024]{1,0:T(8,128)(2,1)S(1)}, bf16[64,1024]{1,0:T(8,128)(2,1)S(1)}, u32[]{:S(2)}, u32[]{:S(2)}) collective-permute-start(bf16[64,1024]{1,0:T(8,128)(2,1)S(1)} %get-tuple-element.90.mine), channel_id=1, source_target_pairs={{0,8},{1,9},{2,10},{3,11},{4,12},{5,13},{6,14},{7,15},{8,0},{9,1},... | collective-permute-start | bytes 393224 | tf_op jit(solution)/shard_map/panels_z2/ppermute | solution.py:642
  56.4 1.5 %shard_map.134 = (bf16[512,512]{1,0:T(8,128)(2,1)S(1)}, bf16[512,128]{1,0:T(8,128)(2,1)}) custom-call(s32[4]{0:T(128)S(1)} %pad_add_fusion.place, bf16[464,512]{1,0:T(8,128)(2,1)S(1)} %collective-permute-done.11.refs_0_, bf16[464,512]{1,0:T(8,128)(2,1)S(1)} %collective-permute-done.13.refs_1_, bf16[320,512]{1,0:T(8,128)(2,1)S(1)} %collective-permute-done.12.refs_2_, ...), custom_call_target="tpu_custom_call" | custom-call | flops 100000000 | bytes 1000000 | tf_op jit(solution)/shard_map/pallas_call | solution.py:61
  57.9 3.6 %collective-permute-done.10.recv = bf16[64,1024]{1,0:T(8,128)(2,1)S(1)} collective-permute-done((bf16[64,1024]{1,0:T(8,128)(2,1)S(1)}, bf16[64,1024]{1,0:T(8,128)(2,1)S(1)}, u32[]{:S(2)}, u32[]{:S(2)}) %collective-permute-start.10) | collective-permute-done | bytes 131104 | tf_op jit(solution)/shard_map/panels_z2/ppermute | solution.py:642
  63.3 5.3 %collective-permute-done.15.recv = bf16[64,512]{1,0:T(8,128)(2,1)S(1)} collective-permute-done((bf16[64,512]{1,0:T(8,128)(2,1)S(1)}, bf16[64,512]{1,0:T(8,128)(2,1)S(1)}, u32[]{:S(2)}, u32[]{:S(2)}) %collective-permute-start.15) | collective-permute-done | bytes 65568 | tf_op jit(solution)/shard_map/panels_z3/ppermute | solution.py:642
  70.0 5.7 %collective-permute-done.16.recv = bf16[64,1536]{1,0:T(8,128)(2,1)S(1)} collective-permute-done((bf16[64,1536]{1,0:T(8,128)(2,1)S(1)}, bf16[64,1536]{1,0:T(8,128)(2,1)S(1)}, u32[]{:S(2)}, u32[]{:S(2)}) %collective-permute-start.16) | collective-permute-done | bytes 196640 | tf_op jit(solution)/shard_map/down_z1/ppermute | solution.py:642
  76.7 1.6 %collective-permute-start.17 = (bf16[64,2048]{1,0:T(8,128)(2,1)S(1)}, bf16[64,2048]{1,0:T(8,128)(2,1)S(1)}, u32[]{:S(2)}, u32[]{:S(2)}) collective-permute-start(bf16[64,2048]{1,0:T(8,128)(2,1)S(1)} %shard_map.137.mine), channel_id=1, source_target_pairs={{0,3},{1,2},{2,1},{3,0},{4,7},{5,6},{6,5},{7,4},{8,11},{9,10},{10,... | collective-permute-start | bytes 786440 | tf_op jit(solution)/shard_map/down_ring/ppermute | solution.py:642
  79.2 5.2 %collective-permute-done.17.recv = bf16[64,2048]{1,0:T(8,128)(2,1)S(1)} collective-permute-done((bf16[64,2048]{1,0:T(8,128)(2,1)S(1)}, bf16[64,2048]{1,0:T(8,128)(2,1)S(1)}, u32[]{:S(2)}, u32[]{:S(2)}) %collective-permute-start.17) | collective-permute-done | bytes 262176 | tf_op jit(solution)/shard_map/down_ring/ppermute | solution.py:642
  84.4 1.5 %shard_map.139 = (bf16[128,512]{1,0:T(8,128)(2,1)S(1)}, bf16[128,2048]{1,0:T(8,128)(2,1)S(1)}, bf16[128,640]{1,0:T(8,128)(2,1)S(1)}) custom-call(s32[4]{0:T(128)S(1)} %pad_add_fusion.place, bf16[64,2048]{1,0:T(8,128)(2,1)S(1)} %shard_map.137.mine, bf16[64,2048]{1,0:T(8,128)(2,1)S(1)} %collective-permute-done.17.recv, ...), custom_call_target="tpu_custom_call" | custom-call | flops 100000000 | bytes 1000000 | tf_op jit(solution)/shard_map/pallas_call | solution.py:61
  85.9 1.5 %shard_map.140 = (bf16[128,640]{1,0:T(8,128)(2,1)S(1)}, bf16[128,512]{1,0:T(8,128)(2,1)}, bf16[128,512]{1,0:T(8,128)(2,1)}) custom-call(s32[4]{0:T(128)S(1)} %pad_add_fusion.place, bf16[128,512]{1,0:T(8,128)(2,1)S(1)} %get-tuple-element.110.x1_ref, bf16[128,2048]{1,0:T(8,128)(2,1)S(1)} %get-tuple-element.111.x, ...), custom_call_target="tpu_custom_call" | custom-call | flops 100000000 | bytes 1000000 | tf_op jit(solution)/shard_map/pallas_call | solution.py:61
  87.4 1.5 %shard_map.141 = (bf16[128,1024]{1,0:T(8,128)(2,1)S(1)}, bf16[512,128]{1,0:T(8,128)(2,1)S(1)}) custom-call(s32[4]{0:T(128)S(1)} %pad_add_fusion.place, bf16[128,640]{1,0:T(8,128)(2,1)S(1)} %get-tuple-element.112.keep, bf16[1024,1024]{1,0:T(8,128)(2,1)S(1)} %get-tuple-element.113.inv, bf16[5,128,1024]{2,1,0:T(8,128)(2,1)S(1)} %get-tuple-element.69.cpl_v.cpl, ...), custom_call_target="tpu_custom_call" | custom-call | flops 100000000 | bytes 1000000 | tf_op jit(solution)/shard_map/pallas_call | solution.py:61
  89.0 2.3 %collective-permute-done.19.recv = bf16[128,640]{1,0:T(8,128)(2,1)S(1)} collective-permute-done((bf16[128,640]{1,0:T(8,128)(2,1)S(1)}, bf16[128,640]{1,0:T(8,128)(2,1)S(1)}, u32[]{:S(2)}, u32[]{:S(2)}) %collective-permute-start.19) | collective-permute-done | bytes 163872 | tf_op jit(solution)/shard_map/rows_back/ppermute | solution.py:642
  91.2 2.2 %shard_map.142 = (bf16[256,1024]{1,0:T(8,128)(2,1)}, bf16[512,256]{1,0:T(8,128)(2,1)}) custom-call(s32[4]{0:T(128)S(1)} %pad_add_fusion.place, bf16[128,640]{1,0:T(8,128)(2,1)S(1)} %collective-permute-done.19.recv, bf16[1024,1024]{1,0:T(8,128)(2,1)S(1)} %get-tuple-element.113.inv, bf16[5,128,1024]{2,1,0:T(8,128)(2,1)S(1)} %get-tuple-element.69.cpl_v.cpl, ...), custom_call_target="tpu_custom_call" | custom-call | flops 100000000 | bytes 14000000 | tf_op jit(solution)/shard_map/pallas_call | solution.py:61
  93.5 6.1 %all-to-all-start = ((bf16[32,16,256]{2,1,0:T(8,128)(2,1)}), bf16[32,16,256]{2,1,0:T(8,128)(2,1)S(1)}, u32[]{:S(2)}, u32[]{:S(2)}) async-start(bf16[32,16,256]{2,1,0:T(8,128)(2,1)} %bitcast.11), calls=%async_computation | async-start | bytes 524288 | tf_op jit(solution)/shard_map/all_to_all | solution.py:882
  99.6 1.9 %collective-permute-start.20 = (bf16[128,512]{1,0:T(8,128)(2,1)S(1)}, bf16[128,512]{1,0:T(8,128)(2,1)S(1)}, u32[]{:S(2)}, u32[]{:S(2)}) collective-permute-start(bf16[128,512]{1,0:T(8,128)(2,1)S(1)} %copy-done.3), channel_id=1, source_target_pairs={{0,1},{1,0},{2,3},{3,2},{4,5},{5,4},{6,7},{7,6},{8,9},{9,8},{10,11... | collective-permute-start | bytes 393224 | tf_op jit(solution)/shard_map/sep_back/ppermute | solution.py:642
  101.4 2.0 %shard_map.143 = bf16[1024,256]{1,0:T(8,128)(2,1)} custom-call(bf16[256,1024]{1,0:T(8,128)(2,1)} %get-tuple-element.117.xt), custom_call_target="tpu_custom_call" | custom-call | flops 100000000 | bytes 1000000 | tf_op jit(solution)/shard_map/pallas_call | solution.py:61
  103.5 1.5 %collective-permute-done.20.recv = bf16[128,512]{1,0:T(8,128)(2,1)S(1)} collective-permute-done((bf16[128,512]{1,0:T(8,128)(2,1)S(1)}, bf16[128,512]{1,0:T(8,128)(2,1)S(1)}, u32[]{:S(2)}, u32[]{:S(2)}) %collective-permute-start.20) | collective-permute-done | bytes 131104 | tf_op jit(solution)/shard_map/sep_back/ppermute | solution.py:642
  105.6 2.4 %shard_map.144 = bf16[512,256]{1,0:T(8,128)(2,1)} custom-call(s32[4]{0:T(128)S(1)} %pad_add_fusion.place, bf16[128,512]{1,0:T(8,128)(2,1)} %get-tuple-element.118.keep, bf16[128,512]{1,0:T(8,128)(2,1)} %copy-done.2), custom_call_target="tpu_custom_call" | custom-call | flops 100000000 | bytes 1000000 | tf_op jit(solution)/shard_map/pallas_call | solution.py:61
  108.0 3.1 %all-to-all-done = bf16[32,16,256]{2,1,0:T(8,128)(2,1)S(1)} async-done(((bf16[32,16,256]{2,1,0:T(8,128)(2,1)}), bf16[32,16,256]{2,1,0:T(8,128)(2,1)S(1)}, u32[]{:S(2)}, u32[]{:S(2)}) %all-to-all-start) | async-done | bytes 262176 | tf_op jit(solution)/shard_map/all_to_all | solution.py:882
  111.1 1.7 %shard_map.145 = f32[64,256]{1,0:T(8,128)} custom-call(bf16[2,64,512]{2,1,0:T(8,128)(2,1)} %get-tuple-element.122.weight, bf16[512,256]{1,0:T(8,128)(2,1)S(1)} %bitcast.8), custom_call_target="tpu_custom_call" | custom-call | flops 100000000 | bytes 1000000 | tf_op jit(solution)/shard_map/pallas_call | solution.py:61
  (46 shorter events, 21.5 us)
Async XLA Ops:
  2.6 14.2 %collective-permute-start.3 = (bf16[368,512]{1,0:T(8,128)(2,1)S(1)}, bf16[368,512]{1,0:T(8,128)(2,1)S(1)}, u32[]{:S(2)}, u32[]{:S(2)}) collective-permute-start(bf16[368,512]{1,0:T(8,128)(2,1)S(1)} %get-tuple-element.79), channel_id=1, source_target_pairs={{1,0},{3,2},{5,4},{7,6},{9,8},{11,10},{13,12},{15,14},{17,16},{19,... | collective-permute-start | bytes 1130504 | tf_op jit(solution)/shard_map/factors_to_pair/ppermute | solution.py:642
  7.8 9.0 %collective-permute-start = (bf16[320,128]{1,0:T(8,128)(2,1)S(1)}, bf16[320,128]{1,0:T(8,128)(2,1)S(1)}, u32[]{:S(2)}, u32[]{:S(2)}) collective-permute-start(bf16[320,128]{1,0:T(8,128)(2,1)S(1)} %get-tuple-element.65.one), channel_id=1, source_target_pairs={{0,1},{1,0},{2,3},{3,2},{4,5},{5,4},{6,7},{7,6},{8,9},{9,8},{10,11... | collective-permute-start | bytes 245768 | tf_op jit(solution)/shard_map/first_terms/ppermute | solution.py:642
  10.5 13.0 %collective-permute-start.4 = (bf16[368,512]{1,0:T(8,128)(2,1)S(1)}, bf16[368,512]{1,0:T(8,128)(2,1)S(1)}, u32[]{:S(2)}, u32[]{:S(2)}) collective-permute-start(bf16[368,512]{1,0:T(8,128)(2,1)S(1)} %get-tuple-element.79), channel_id=1, source_target_pairs={{1,2},{3,0},{5,6},{7,4},{9,10},{11,8},{13,14},{15,12},{17,18},{19,... | collective-permute-start | bytes 1130504 | tf_op jit(solution)/shard_map/factors_to_other/ppermute | solution.py:642
  16.7 12.7 %collective-permute-start.7 = (bf16[368,512]{1,0:T(8,128)(2,1)S(1)}, bf16[368,512]{1,0:T(8,128)(2,1)S(1)}, u32[]{:S(2)}, u32[]{:S(2)}) collective-permute-start(bf16[368,512]{1,0:T(8,128)(2,1)S(1)} %collective-permute-done.3.refs_1_), channel_id=1, source_target_pairs={{0,3},{2,1},{4,7},{6,5},{8,11},{10,9},{12,15},{14,13},{16,19},{18,... | collective-permute-start | bytes 1130504 | tf_op jit(solution)/shard_map/factors_across/ppermute | solution.py:642
  21.2 3.7 %copy-start = (s32[6,2048]{1,0:T(8,128)S(1)}, s32[6,2048]{1,0:T(8,128)}, u32[]{:S(2)}) copy-start(s32[6,2048]{1,0:T(8,128)} %dofs.1) | copy-start | bytes 147460
  21.3 3.7 %copy-start.1 = (f32[6,2048]{1,0:T(8,128)S(1)}, f32[6,2048]{1,0:T(8,128)}, u32[]{:S(2)}) copy-start(f32[6,2048]{1,0:T(8,128)} %coef) | copy-start | bytes 147460
  21.3 7.0 %collective-permute-start.1 = (bf16[128,1024]{1,0:T(8,128)(2,1)S(1)}, bf16[128,1024]{1,0:T(8,128)(2,1)S(1)}, u32[]{:S(2)}, u32[]{:S(2)}) collective-permute-start(bf16[128,1024]{1,0:T(8,128)(2,1)S(1)} %get-tuple-element.72), channel_id=1, source_target_pairs={{0,1},{1,0},{2,3},{3,2},{4,5},{5,4},{6,7},{7,6},{8,9},{9,8},{10,11... | collective-permute-start | bytes 786440 | tf_op jit(solution)/shard_map/terms_pair/ppermute | solution.py:642
  23.6 7.2 %collective-permute-start.5 = (bf16[368,512]{1,0:T(8,128)(2,1)S(1)}, bf16[368,512]{1,0:T(8,128)(2,1)S(1)}, u32[]{:S(2)}, u32[]{:S(2)}) collective-permute-start(bf16[368,512]{1,0:T(8,128)(2,1)S(1)} %collective-permute-done.3.refs_1_), channel_id=1, source_target_pairs={{0,32},{1,33},{2,34},{3,35},{4,36},{5,37},{6,38},{7,39},{8,40},{9,... | collective-permute-start | bytes 1130504 | tf_op jit(solution)/shard_map/pair_to_core/ppermute | solution.py:642
  23.6 7.2 %collective-permute-start.6 = (bf16[368,512]{1,0:T(8,128)(2,1)S(1)}, bf16[368,512]{1,0:T(8,128)(2,1)S(1)}, u32[]{:S(2)}, u32[]{:S(2)}) collective-permute-start(bf16[368,512]{1,0:T(8,128)(2,1)S(1)} %collective-permute-done.4.refs_3_), channel_id=1, source_target_pairs={{0,32},{1,33},{2,34},{3,35},{4,36},{5,37},{6,38},{7,39},{8,40},{9,... | collective-permute-start | bytes 1130504 | tf_op jit(solution)/shard_map/beside_to_core/ppermute | solution.py:642
  29.5 1.8 %collective-permute-start.8 = (bf16[368,512]{1,0:T(8,128)(2,1)S(1)}, bf16[368,512]{1,0:T(8,128)(2,1)S(1)}, u32[]{:S(2)}, u32[]{:S(2)}) collective-permute-start(bf16[368,512]{1,0:T(8,128)(2,1)S(1)} %collective-permute-done.7.refs_5_), channel_id=1, source_target_pairs={{0,32},{1,33},{2,34},{3,35},{4,36},{5,37},{6,38},{7,39},{8,40},{9,... | collective-permute-start | bytes 1130504 | tf_op jit(solution)/shard_map/far_to_core/ppermute | solution.py:642
  29.6 9.9 %collective-permute-start.2 = (bf16[64,2048]{1,0:T(8,128)(2,1)S(1)}, bf16[64,2048]{1,0:T(8,128)(2,1)S(1)}, u32[]{:S(2)}, u32[]{:S(2)}) collective-permute-start(bf16[64,2048]{1,0:T(8,128)(2,1)S(1)} %get-tuple-element.78), channel_id=1, source_target_pairs={{0,3},{1,2},{2,1},{3,0},{4,7},{5,6},{6,5},{7,4},{8,11},{9,10},{10,... | collective-permute-start | bytes 786440 | tf_op jit(solution)/shard_map/panels_ring/ppermute | solution.py:642
  33.0 19.8 %collective-permute-start.11 = (bf16[464,512]{1,0:T(8,128)(2,1)S(1)}, bf16[464,512]{1,0:T(8,128)(2,1)S(1)}, u32[]{:S(2)}, u32[]{:S(2)}) collective-permute-start(bf16[464,512]{1,0:T(8,128)(2,1)S(1)} %get-tuple-element.91), channel_id=1, source_target_pairs={{4,0},{5,1},{6,2},{7,3},{12,8},{13,9},{14,10},{15,11},{20,16},{21,... | collective-permute-start | bytes 1425416 | tf_op jit(solution)/shard_map/factors_up/ppermute | solution.py:642
  34.3 18.4 %collective-permute-start.12 = (bf16[320,512]{1,0:T(8,128)(2,1)S(1)}, bf16[320,512]{1,0:T(8,128)(2,1)S(1)}, u32[]{:S(2)}, u32[]{:S(2)}) collective-permute-start(bf16[320,512]{1,0:T(8,128)(2,1)S(1)} %get-tuple-element.92), channel_id=1, source_target_pairs={{12,24},{13,25},{14,26},{15,27},{44,32},{45,33},{46,34},{47,35},{7... | collective-permute-start | bytes 983048 | tf_op jit(solution)/shard_map/factor_top/ppermute | solution.py:642
  40.2 11.9 %collective-permute-start.9 = (bf16[64,1536]{1,0:T(8,128)(2,1)S(1)}, bf16[64,1536]{1,0:T(8,128)(2,1)S(1)}, u32[]{:S(2)}, u32[]{:S(2)}) collective-permute-start(bf16[64,1536]{1,0:T(8,128)(2,1)S(1)} %get-tuple-element.89.mine), channel_id=1, source_target_pairs={{4,0},{5,1},{6,2},{7,3},{12,8},{13,9},{14,10},{15,11},{20,16},{21,... | collective-permute-start | bytes 589832 | tf_op jit(solution)/shard_map/panels_z1/ppermute | solution.py:642
  41.5 36.8 %collective-permute-start.18 = (bf16[1152,512]{1,0:T(8,128)(2,1)S(1)}, bf16[1152,512]{1,0:T(8,128)(2,1)S(1)}, u32[]{:S(2)}, u32[]{:S(2)}) collective-permute-start(bf16[1152,512]{1,0:T(8,128)(2,1)S(1)} %get-tuple-element.104.own), channel_id=1, source_target_pairs={{0,1},{2,3},{4,5},{6,7},{8,9},{10,11},{12,13},{14,15},{16,17},{18,... | collective-permute-start | bytes 3538952 | tf_op jit(solution)/shard_map/first_factor_to_odd/ppermute | solution.py:642
  52.8 2.5 %collective-permute-start.13 = (bf16[464,512]{1,0:T(8,128)(2,1)S(1)}, bf16[464,512]{1,0:T(8,128)(2,1)S(1)}, u32[]{:S(2)}, u32[]{:S(2)}) collective-permute-start(bf16[464,512]{1,0:T(8,128)(2,1)S(1)} %collective-permute-done.11.refs_0_), channel_id=1, source_target_pairs={{0,32},{1,33},{2,34},{3,35},{4,36},{5,37},{6,38},{7,39},{8,40},{9,... | collective-permute-start | bytes 1425416 | tf_op jit(solution)/shard_map/up_to_core/ppermute | solution.py:642
  52.9 3.5 %collective-permute-start.14 = (bf16[320,512]{1,0:T(8,128)(2,1)S(1)}, bf16[320,512]{1,0:T(8,128)(2,1)S(1)}, u32[]{:S(2)}, u32[]{:S(2)}) collective-permute-start(bf16[320,512]{1,0:T(8,128)(2,1)S(1)} %collective-permute-done.12.refs_2_), channel_id=1, source_target_pairs={{0,32},{1,33},{2,34},{3,35},{4,36},{5,37},{6,38},{7,39},{8,40},{9,... | collective-permute-start | bytes 983048 | tf_op jit(solution)/shard_map/last_to_core/ppermute | solution.py:642
  53.4 8.2 %collective-permute-start.10 = (bf16[64,1024]{1,0:T(8,128)(2,1)S(1)}, bf16[64,1024]{1,0:T(8,128)(2,1)S(1)}, u32[]{:S(2)}, u32[]{:S(2)}) collective-permute-start(bf16[64,1024]{1,0:T(8,128)(2,1)S(1)} %get-tuple-element.90.mine), channel_id=1, source_target_pairs={{0,8},{1,9},{2,10},{3,11},{4,12},{5,13},{6,14},{7,15},{8,0},{9,1},... | collective-permute-start | bytes 393224 | tf_op jit(solution)/shard_map/panels_z2/ppermute | solution.py:642
  62.2 6.5 %collective-permute-start.15 = (bf16[64,512]{1,0:T(8,128)(2,1)S(1)}, bf16[64,512]{1,0:T(8,128)(2,1)S(1)}, u32[]{:S(2)}, u32[]{:S(2)}) collective-permute-start(bf16[64,512]{1,0:T(8,128)(2,1)S(1)} %get-tuple-element.99.mine), channel_id=1, source_target_pairs={{0,24},{1,25},{2,26},{3,27},{4,28},{5,29},{6,30},{7,31},{8,16},{9,... | collective-permute-start | bytes 196616 | tf_op jit(solution)/shard_map/panels_z3/ppermute | solution.py:642
  69.9 5.8 %collective-permute-start.16 = (bf16[64,1536]{1,0:T(8,128)(2,1)S(1)}, bf16[64,1536]{1,0:T(8,128)(2,1)S(1)}, u32[]{:S(2)}, u32[]{:S(2)}) collective-permute-start(bf16[64,1536]{1,0:T(8,128)(2,1)S(1)} %shard_map.136.mine), channel_id=1, source_target_pairs={{0,4},{1,5},{2,6},{3,7},{4,0},{5,1},{6,2},{7,3},{8,12},{9,13},{10,... | collective-permute-start | bytes 589832 | tf_op jit(solution)/shard_map/down_z1/ppermute | solution.py:642
  76.7 7.7 %collective-permute-start.17 = (bf16[64,2048]{1,0:T(8,128)(2,1)S(1)}, bf16[64,2048]{1,0:T(8,128)(2,1)S(1)}, u32[]{:S(2)}, u32[]{:S(2)}) collective-permute-start(bf16[64,2048]{1,0:T(8,128)(2,1)S(1)} %shard_map.137.mine), channel_id=1, source_target_pairs={{0,3},{1,2},{2,1},{3,0},{4,7},{5,6},{6,5},{7,4},{8,11},{9,10},{10,... | collective-permute-start | bytes 786440 | tf_op jit(solution)/shard_map/down_ring/ppermute | solution.py:642
  85.8 5.4 %collective-permute-start.19 = (bf16[128,640]{1,0:T(8,128)(2,1)S(1)}, bf16[128,640]{1,0:T(8,128)(2,1)S(1)}, u32[]{:S(2)}, u32[]{:S(2)}) collective-permute-start(bf16[128,640]{1,0:T(8,128)(2,1)S(1)} %get-tuple-element.109), channel_id=1, source_target_pairs={{0,1},{1,0},{2,3},{3,2},{4,5},{5,4},{6,7},{7,6},{8,9},{9,8},{10,11... | collective-permute-start | bytes 491528 | tf_op jit(solution)/shard_map/rows_back/ppermute | solution.py:642
  91.2 8.3 %copy-start.3 = (bf16[128,512]{1,0:T(8,128)(2,1)S(1)}, bf16[128,512]{1,0:T(8,128)(2,1)}, u32[]{:S(2)}) copy-start(bf16[128,512]{1,0:T(8,128)(2,1)} %get-tuple-element.121) | copy-start | bytes 393220
  93.5 17.6 %all-to-all-start = ((bf16[32,16,256]{2,1,0:T(8,128)(2,1)}), bf16[32,16,256]{2,1,0:T(8,128)(2,1)S(1)}, u32[]{:S(2)}, u32[]{:S(2)}) async-start(bf16[32,16,256]{2,1,0:T(8,128)(2,1)} %bitcast.11), calls=%async_computation | async-start | bytes 524288 | tf_op jit(solution)/shard_map/all_to_all | solution.py:882
  99.6 5.4 %collective-permute-start.20 = (bf16[128,512]{1,0:T(8,128)(2,1)S(1)}, bf16[128,512]{1,0:T(8,128)(2,1)S(1)}, u32[]{:S(2)}, u32[]{:S(2)}) collective-permute-start(bf16[128,512]{1,0:T(8,128)(2,1)S(1)} %copy-done.3), channel_id=1, source_target_pairs={{0,1},{1,0},{2,3},{3,2},{4,5},{5,4},{6,7},{7,6},{8,9},{9,8},{10,11... | collective-permute-start | bytes 393224 | tf_op jit(solution)/shard_map/sep_back/ppermute | solution.py:642
  105.0 0.6 copy-start.2

commit v9 on v8

--- a/solution.py
+++ b/solution.py
@@ -790,11 +790,11 @@
         [pltpu.VMEM((16, PANEL), BF), dma(11)],
     )
 
-    def next_up(value, senders):
-        return route(value, lambda c, y, z: (c, y, z + (1 if c else -1)) if z in senders else None)
+    def next_up(value):
+        return route(value, lambda c, y, z: (c, y, (z + (1 if c == z % 2 else -1)) % DEPTH))
 
     with jax.named_scope("factors_up"):
-        up = next_up(top, (1, 3, 5))
+        up = next_up(top)
     with jax.named_scope("factor_top"):
         last = route(
             triangle,

time: 113 us -> 113 us (level)
  starting transfers between devices: 28.5 us -> 26.4 us
  waiting for transfers between devices: 45.8 us -> 47.9 us
    ppermute x21, waiting for transfers between devices: 42.8 us -> 44.9 us  [route(): return lax.ppermute(value, (cols_axis, rows_axis), pairs)]
    ppermute x21, starting transfers between devices: 22.4 us -> 21.2 us  [route(): return lax.ppermute(value, (cols_axis, rows_axis), pairs)]
  transfers between devices with their start and end apart: 22 -> 22, of which waited for: 13 -> 14; matrix products, arithmetic and copies ran while one was open for 0% -> 0% of each run, Pallas kernels for 26% -> 26%
where the time goes in v9:
time: 113 us
  waiting for transfers between devices  47.9 us (42%)
  Pallas kernels  36.8 us (33%)
  starting transfers between devices  26.4 us (23%)
  between operations  1.19 us (1%)
    ppermute x21, waiting for transfers between devices, route(): return lax.ppermute(value, (cols_axis, rows_axis), pairs)  44.9 us
    pallas_call x25, Pallas kernels, call(): pl.pallas_call(body, out_shape=outs, in_specs=specs, out_specs=out_specs...  36.8 us
    ppermute x21, starting transfers between devices, route(): return lax.ppermute(value, (cols_axis, rows_axis), pairs)  21.2 us
    all_to_all x1, starting transfers between devices, on_device(): lax.all_to_all(picks.reshape(32, SLOTS, NC), rows_axis, 0, 0, tiled=True)  5.22 us
    all_to_all x1, waiting for transfers between devices, on_device(): lax.all_to_all(picks.reshape(32, SLOTS, NC), rows_axis, 0, 0, tiled=True)  3.08 us
  transfers between devices with their start and end apart: 22, of which 14 were waited for; matrix products, arithmetic and copies ran while one was open for 0% of the time, Pallas kernels for 26%

profile of v9, /device:TPU:2, one launch (start us, length us, event | category | flops | bytes accessed | tf_op | source)
XLA Modules:
  0.0 113.0 jit_solution(14116829899700264558)
XLA Ops:
  0.8 1.8 %shard_map.121 = (bf16[720,512]{1,0:T(8,128)(2,1)S(1)}, bf16[368,512]{1,0:T(8,128)(2,1)S(1)}) custom-call(s32[4]{0:T(128)S(1)} %pad_add_fusion.place, bf16[512,512]{1,0:T(8,128)(2,1)} %inv.4, bf16[512,512]{1,0:T(8,128)(2,1)} %bitcast.9, s32[1,4,128]{2,1,0:T(4,128)} %sep_idx.3), custom_call_target="tpu_custom_call" | custom-call | flops 100000000 | bytes 1000000 | tf_op jit(solution)/shard_map/pallas_call | solution.py:61
  2.6 1.3 %collective-permute-start.3 = (bf16[368,512]{1,0:T(8,128)(2,1)S(1)}, bf16[368,512]{1,0:T(8,128)(2,1)S(1)}, u32[]{:S(2)}, u32[]{:S(2)}) collective-permute-start(bf16[368,512]{1,0:T(8,128)(2,1)S(1)} %get-tuple-element.79), channel_id=1, source_target_pairs={{1,0},{3,2},{5,4},{7,6},{9,8},{11,10},{13,12},{15,14},{17,16},{19,... | collective-permute-start | bytes 1130504 | tf_op jit(solution)/shard_map/factors_to_pair/ppermute | solution.py:642
  3.9 3.9 %shard_map.122 = (bf16[256,1024]{1,0:T(8,128)(2,1)S(1)}, bf16[256,512]{1,0:T(8,128)(2,1)S(1)}, bf16[320,128]{1,0:T(8,128)(2,1)S(1)}, bf16[1024,1024]{1,0:T(8,128)(2,1)S(1)}, bf16[5,128,1024]{2,1,0:T(8,128)(2,1)S(1)}) custom-call(s32[4]{0:T(128)S(1)} %pad_add_fusion.place, bf16[1024,1024]{1,0:T(8,128)(2,1)} %inv.3, bf16[1024,256]{1,0:T(8,128)(2,1)} %rhs.1, ...), custom_call_target="tpu_custom_call" | custom-call | flops 100000000 | bytes 1000000 | tf_op jit(solution)/shard_map/pallas_call | solution.py:61
  7.8 2.7 %collective-permute-start = (bf16[320,128]{1,0:T(8,128)(2,1)S(1)}, bf16[320,128]{1,0:T(8,128)(2,1)S(1)}, u32[]{:S(2)}, u32[]{:S(2)}) collective-permute-start(bf16[320,128]{1,0:T(8,128)(2,1)S(1)} %get-tuple-element.65.one), channel_id=1, source_target_pairs={{0,1},{1,0},{2,3},{3,2},{4,5},{5,4},{6,7},{7,6},{8,9},{9,8},{10,11... | collective-permute-start | bytes 245768 | tf_op jit(solution)/shard_map/first_terms/ppermute | solution.py:642
  13.5 3.2 %collective-permute-done.recv.other = bf16[320,128]{1,0:T(8,128)(2,1)S(1)} collective-permute-done((bf16[320,128]{1,0:T(8,128)(2,1)S(1)}, bf16[320,128]{1,0:T(8,128)(2,1)S(1)}, u32[]{:S(2)}, u32[]{:S(2)}) %collective-permute-start) | collective-permute-done | bytes 81952 | tf_op jit(solution)/shard_map/first_terms/ppermute | solution.py:642
  16.7 3.2 %collective-permute-start.7 = (bf16[368,512]{1,0:T(8,128)(2,1)S(1)}, bf16[368,512]{1,0:T(8,128)(2,1)S(1)}, u32[]{:S(2)}, u32[]{:S(2)}) collective-permute-start(bf16[368,512]{1,0:T(8,128)(2,1)S(1)} %collective-permute-done.3.refs_1_), channel_id=1, source_target_pairs={{0,3},{2,1},{4,7},{6,5},{8,11},{10,9},{12,15},{14,13},{16,19},{18,... | collective-permute-start | bytes 1130504 | tf_op jit(solution)/shard_map/factors_across/ppermute | solution.py:642
  19.9 1.3 %shard_map.125 = (bf16[512,256]{1,0:T(8,128)(2,1)S(1)}, bf16[128,512]{1,0:T(8,128)(2,1)S(1)}, bf16[1152,512]{1,0:T(8,128)(2,1)S(1)}, bf16[128,1024]{1,0:T(8,128)(2,1)S(1)}, bf16[128,1024]{1,0:T(8,128)(2,1)S(1)}) custom-call(s32[4]{0:T(128)S(1)} %pad_add_fusion.place, bf16[320,128]{1,0:T(8,128)(2,1)S(1)} %get-tuple-element.65.one, ...), custom_call_target="tpu_custom_call", output_to_operand_aliasing={{2}: (5, {})} | custom-call | flops 100000000 | bytes 1000000 | tf_op jit(solution)/shard_map/pallas_call | solution.py:61
  21.4 2.2 %collective-permute-done.4.refs_3_ = bf16[368,512]{1,0:T(8,128)(2,1)S(1)} collective-permute-done((bf16[368,512]{1,0:T(8,128)(2,1)S(1)}, bf16[368,512]{1,0:T(8,128)(2,1)S(1)}, u32[]{:S(2)}, u32[]{:S(2)}) %collective-permute-start.4) | collective-permute-done | bytes 376864 | tf_op jit(solution)/shard_map/factors_to_other/ppermute | solution.py:642
  24.9 2.5 %shard_map.126 = (bf16[512,1024]{1,0:T(8,128)(2,1)S(1)}, bf16[2,64,512]{2,1,0:T(8,128)(2,1)}) custom-call(s32[4]{0:T(128)S(1)} %pad_add_fusion.place, s32[6,2048]{1,0:T(8,128)S(1)} %copy-done, f32[6,2048]{1,0:T(8,128)S(1)} %copy-done.1), custom_call_target="tpu_custom_call" | custom-call | flops 100000000 | bytes 1000000 | tf_op jit(solution)/shard_map/pallas_call | solution.py:61
  31.3 1.8 %shard_map.130 = (bf16[768,512]{1,0:T(8,128)(2,1)S(1)}, bf16[512,256]{1,0:T(8,128)(2,1)S(1)}, bf16[464,512]{1,0:T(8,128)(2,1)S(1)}, bf16[320,512]{1,0:T(8,128)(2,1)S(1)}) custom-call(s32[4]{0:T(128)S(1)} %pad_add_fusion.place, bf16[720,512]{1,0:T(8,128)(2,1)S(1)} %get-tuple-element.63.refs_0_, bf16[368,512]{1,0:T(8,128)(2,1)S(1)} %collective-permute-done.3.refs_1_, ...), custom_call_target="tpu_custom_call" | custom-call | flops 100000000 | bytes 1000000 | tf_op jit(solution)/shard_map/pallas_call | solution.py:61
  33.0 2.0 %collective-permute-start.11 = (bf16[464,512]{1,0:T(8,128)(2,1)S(1)}, bf16[464,512]{1,0:T(8,128)(2,1)S(1)}, u32[]{:S(2)}, u32[]{:S(2)}) collective-permute-start(bf16[464,512]{1,0:T(8,128)(2,1)S(1)} %get-tuple-element.91), channel_id=1, source_target_pairs={{0,4},{1,5},{2,6},{3,7},{4,0},{5,1},{6,2},{7,3},{8,12},{9,13},{10,... | collective-permute-start | bytes 1425416 | tf_op jit(solution)/shard_map/factors_up/ppermute | solution.py:642
  36.9 2.6 %collective-permute-done.2.recv = bf16[64,2048]{1,0:T(8,128)(2,1)S(1)} collective-permute-done((bf16[64,2048]{1,0:T(8,128)(2,1)S(1)}, bf16[64,2048]{1,0:T(8,128)(2,1)S(1)}, u32[]{:S(2)}, u32[]{:S(2)}) %collective-permute-start.2) | collective-permute-done | bytes 262176 | tf_op jit(solution)/shard_map/panels_ring/ppermute | solution.py:642
  41.5 1.4 %collective-permute-start.18 = (bf16[1152,512]{1,0:T(8,128)(2,1)S(1)}, bf16[1152,512]{1,0:T(8,128)(2,1)S(1)}, u32[]{:S(2)}, u32[]{:S(2)}) collective-permute-start(bf16[1152,512]{1,0:T(8,128)(2,1)S(1)} %get-tuple-element.104.own), channel_id=1, source_target_pairs={{0,1},{2,3},{4,5},{6,7},{8,9},{10,11},{12,13},{14,15},{16,17},{18,... | collective-permute-start | bytes 3538952 | tf_op jit(solution)/shard_map/first_factor_to_odd/ppermute | solution.py:642
  42.9 9.8 %collective-permute-done.9.recv = bf16[64,1536]{1,0:T(8,128)(2,1)S(1)} collective-permute-done((bf16[64,1536]{1,0:T(8,128)(2,1)S(1)}, bf16[64,1536]{1,0:T(8,128)(2,1)S(1)}, u32[]{:S(2)}, u32[]{:S(2)}) %collective-permute-start.9) | collective-permute-done | bytes 196640 | tf_op jit(solution)/shard_map/panels_z1/ppermute | solution.py:642
  56.5 1.5 %shard_map.134 = (bf16[512,512]{1,0:T(8,128)(2,1)S(1)}, bf16[512,128]{1,0:T(8,128)(2,1)}) custom-call(s32[4]{0:T(128)S(1)} %pad_add_fusion.place, bf16[464,512]{1,0:T(8,128)(2,1)S(1)} %collective-permute-done.11.refs_0_, bf16[464,512]{1,0:T(8,128)(2,1)S(1)} %collective-permute-done.13.refs_1_, bf16[320,512]{1,0:T(8,128)(2,1)S(1)} %collective-permute-done.12.refs_2_, ...), custom_call_target="tpu_custom_call" | custom-call | flops 100000000 | bytes 1000000 | tf_op jit(solution)/shard_map/pallas_call | solution.py:61
  58.0 4.4 %collective-permute-done.10.recv = bf16[64,1024]{1,0:T(8,128)(2,1)S(1)} collective-permute-done((bf16[64,1024]{1,0:T(8,128)(2,1)S(1)}, bf16[64,1024]{1,0:T(8,128)(2,1)S(1)}, u32[]{:S(2)}, u32[]{:S(2)}) %collective-permute-start.10) | collective-permute-done | bytes 131104 | tf_op jit(solution)/shard_map/panels_z2/ppermute | solution.py:642
  63.3 6.1 %collective-permute-done.15.recv = bf16[64,512]{1,0:T(8,128)(2,1)S(1)} collective-permute-done((bf16[64,512]{1,0:T(8,128)(2,1)S(1)}, bf16[64,512]{1,0:T(8,128)(2,1)S(1)}, u32[]{:S(2)}, u32[]{:S(2)}) %collective-permute-start.15) | collective-permute-done | bytes 65568 | tf_op jit(solution)/shard_map/panels_z3/ppermute | solution.py:642
  70.8 5.7 %collective-permute-done.16.recv = bf16[64,1536]{1,0:T(8,128)(2,1)S(1)} collective-permute-done((bf16[64,1536]{1,0:T(8,128)(2,1)S(1)}, bf16[64,1536]{1,0:T(8,128)(2,1)S(1)}, u32[]{:S(2)}, u32[]{:S(2)}) %collective-permute-start.16) | collective-permute-done | bytes 196640 | tf_op jit(solution)/shard_map/down_z1/ppermute | solution.py:642
  77.5 1.8 %collective-permute-start.17 = (bf16[64,2048]{1,0:T(8,128)(2,1)S(1)}, bf16[64,2048]{1,0:T(8,128)(2,1)S(1)}, u32[]{:S(2)}, u32[]{:S(2)}) collective-permute-start(bf16[64,2048]{1,0:T(8,128)(2,1)S(1)} %shard_map.137.mine), channel_id=1, source_target_pairs={{0,3},{1,2},{2,1},{3,0},{4,7},{5,6},{6,5},{7,4},{8,11},{9,10},{10,... | collective-permute-start | bytes 786440 | tf_op jit(solution)/shard_map/down_ring/ppermute | solution.py:642
  80.1 5.1 %collective-permute-done.17.recv = bf16[64,2048]{1,0:T(8,128)(2,1)S(1)} collective-permute-done((bf16[64,2048]{1,0:T(8,128)(2,1)S(1)}, bf16[64,2048]{1,0:T(8,128)(2,1)S(1)}, u32[]{:S(2)}, u32[]{:S(2)}) %collective-permute-start.17) | collective-permute-done | bytes 262176 | tf_op jit(solution)/shard_map/down_ring/ppermute | solution.py:642
  85.2 1.5 %shard_map.139 = (bf16[128,512]{1,0:T(8,128)(2,1)S(1)}, bf16[128,2048]{1,0:T(8,128)(2,1)S(1)}, bf16[128,640]{1,0:T(8,128)(2,1)S(1)}) custom-call(s32[4]{0:T(128)S(1)} %pad_add_fusion.place, bf16[64,2048]{1,0:T(8,128)(2,1)S(1)} %shard_map.137.mine, bf16[64,2048]{1,0:T(8,128)(2,1)S(1)} %collective-permute-done.17.recv, ...), custom_call_target="tpu_custom_call" | custom-call | flops 100000000 | bytes 1000000 | tf_op jit(solution)/shard_map/pallas_call | solution.py:61
  86.8 1.5 %shard_map.140 = (bf16[128,640]{1,0:T(8,128)(2,1)S(1)}, bf16[128,512]{1,0:T(8,128)(2,1)}, bf16[128,512]{1,0:T(8,128)(2,1)}) custom-call(s32[4]{0:T(128)S(1)} %pad_add_fusion.place, bf16[128,512]{1,0:T(8,128)(2,1)S(1)} %get-tuple-element.110.x1_ref, bf16[128,2048]{1,0:T(8,128)(2,1)S(1)} %get-tuple-element.111.x, ...), custom_call_target="tpu_custom_call" | custom-call | flops 100000000 | bytes 1000000 | tf_op jit(solution)/shard_map/pallas_call | solution.py:61
  88.3 1.5 %shard_map.141 = (bf16[128,1024]{1,0:T(8,128)(2,1)S(1)}, bf16[512,128]{1,0:T(8,128)(2,1)S(1)}) custom-call(s32[4]{0:T(128)S(1)} %pad_add_fusion.place, bf16[128,640]{1,0:T(8,128)(2,1)S(1)} %get-tuple-element.112.keep, bf16[1024,1024]{1,0:T(8,128)(2,1)S(1)} %get-tuple-element.113.inv, bf16[5,128,1024]{2,1,0:T(8,128)(2,1)S(1)} %get-tuple-element.69.cpl_v.cpl, ...), custom_call_target="tpu_custom_call" | custom-call | flops 100000000 | bytes 1000000 | tf_op jit(solution)/shard_map/pallas_call | solution.py:61
  89.8 2.3 %collective-permute-done.19.recv = bf16[128,640]{1,0:T(8,128)(2,1)S(1)} collective-permute-done((bf16[128,640]{1,0:T(8,128)(2,1)S(1)}, bf16[128,640]{1,0:T(8,128)(2,1)S(1)}, u32[]{:S(2)}, u32[]{:S(2)}) %collective-permute-start.19) | collective-permute-done | bytes 163872 | tf_op jit(solution)/shard_map/rows_back/ppermute | solution.py:642
  92.1 2.2 %shard_map.142 = (bf16[256,1024]{1,0:T(8,128)(2,1)}, bf16[512,256]{1,0:T(8,128)(2,1)}) custom-call(s32[4]{0:T(128)S(1)} %pad_add_fusion.place, bf16[128,640]{1,0:T(8,128)(2,1)S(1)} %collective-permute-done.19.recv, bf16[1024,1024]{1,0:T(8,128)(2,1)S(1)} %get-tuple-element.113.inv, bf16[5,128,1024]{2,1,0:T(8,128)(2,1)S(1)} %get-tuple-element.69.cpl_v.cpl, ...), custom_call_target="tpu_custom_call" | custom-call | flops 100000000 | bytes 14000000 | tf_op jit(solution)/shard_map/pallas_call | solution.py:61
  94.3 5.2 %all-to-all-start = ((bf16[32,16,256]{2,1,0:T(8,128)(2,1)}), bf16[32,16,256]{2,1,0:T(8,128)(2,1)S(1)}, u32[]{:S(2)}, u32[]{:S(2)}) async-start(bf16[32,16,256]{2,1,0:T(8,128)(2,1)} %bitcast.11), calls=%async_computation | async-start | bytes 524288 | tf_op jit(solution)/shard_map/all_to_all | solution.py:882
  99.6 1.9 %collective-permute-start.20 = (bf16[128,512]{1,0:T(8,128)(2,1)S(1)}, bf16[128,512]{1,0:T(8,128)(2,1)S(1)}, u32[]{:S(2)}, u32[]{:S(2)}) collective-permute-start(bf16[128,512]{1,0:T(8,128)(2,1)S(1)} %copy-done.3), channel_id=1, source_target_pairs={{0,1},{1,0},{2,3},{3,2},{4,5},{5,4},{6,7},{7,6},{8,9},{9,8},{10,11... | collective-permute-start | bytes 393224 | tf_op jit(solution)/shard_map/sep_back/ppermute | solution.py:642
  101.4 2.0 %shard_map.143 = bf16[1024,256]{1,0:T(8,128)(2,1)} custom-call(bf16[256,1024]{1,0:T(8,128)(2,1)} %get-tuple-element.117.xt), custom_call_target="tpu_custom_call" | custom-call | flops 100000000 | bytes 1000000 | tf_op jit(solution)/shard_map/pallas_call | solution.py:61
  103.5 1.5 %collective-permute-done.20.recv = bf16[128,512]{1,0:T(8,128)(2,1)S(1)} collective-permute-done((bf16[128,512]{1,0:T(8,128)(2,1)S(1)}, bf16[128,512]{1,0:T(8,128)(2,1)S(1)}, u32[]{:S(2)}, u32[]{:S(2)}) %collective-permute-start.20) | collective-permute-done | bytes 131104 | tf_op jit(solution)/shard_map/sep_back/ppermute | solution.py:642
  105.6 2.4 %shard_map.144 = bf16[512,256]{1,0:T(8,128)(2,1)} custom-call(s32[4]{0:T(128)S(1)} %pad_add_fusion.place, bf16[128,512]{1,0:T(8,128)(2,1)} %get-tuple-element.118.keep, bf16[128,512]{1,0:T(8,128)(2,1)} %copy-done.2), custom_call_target="tpu_custom_call" | custom-call | flops 100000000 | bytes 1000000 | tf_op jit(solution)/shard_map/pallas_call | solution.py:61
  108.0 3.1 %all-to-all-done = bf16[32,16,256]{2,1,0:T(8,128)(2,1)S(1)} async-done(((bf16[32,16,256]{2,1,0:T(8,128)(2,1)}), bf16[32,16,256]{2,1,0:T(8,128)(2,1)S(1)}, u32[]{:S(2)}, u32[]{:S(2)}) %all-to-all-start) | async-done | bytes 262176 | tf_op jit(solution)/shard_map/all_to_all | solution.py:882
  111.1 1.7 %shard_map.145 = f32[64,256]{1,0:T(8,128)} custom-call(bf16[2,64,512]{2,1,0:T(8,128)(2,1)} %get-tuple-element.122.weight, bf16[512,256]{1,0:T(8,128)(2,1)S(1)} %bitcast.8), custom_call_target="tpu_custom_call" | custom-call | flops 100000000 | bytes 1000000 | tf_op jit(solution)/shard_map/pallas_call | solution.py:61
  (46 shorter events, 20.7 us)
Async XLA Ops:
  2.6 14.2 %collective-permute-start.3 = (bf16[368,512]{1,0:T(8,128)(2,1)S(1)}, bf16[368,512]{1,0:T(8,128)(2,1)S(1)}, u32[]{:S(2)}, u32[]{:S(2)}) collective-permute-start(bf16[368,512]{1,0:T(8,128)(2,1)S(1)} %get-tuple-element.79), channel_id=1, source_target_pairs={{1,0},{3,2},{5,4},{7,6},{9,8},{11,10},{13,12},{15,14},{17,16},{19,... | collective-permute-start | bytes 1130504 | tf_op jit(solution)/shard_map/factors_to_pair/ppermute | solution.py:642
  7.8 9.0 %collective-permute-start = (bf16[320,128]{1,0:T(8,128)(2,1)S(1)}, bf16[320,128]{1,0:T(8,128)(2,1)S(1)}, u32[]{:S(2)}, u32[]{:S(2)}) collective-permute-start(bf16[320,128]{1,0:T(8,128)(2,1)S(1)} %get-tuple-element.65.one), channel_id=1, source_target_pairs={{0,1},{1,0},{2,3},{3,2},{4,5},{5,4},{6,7},{7,6},{8,9},{9,8},{10,11... | collective-permute-start | bytes 245768 | tf_op jit(solution)/shard_map/first_terms/ppermute | solution.py:642
  10.5 13.0 %collective-permute-start.4 = (bf16[368,512]{1,0:T(8,128)(2,1)S(1)}, bf16[368,512]{1,0:T(8,128)(2,1)S(1)}, u32[]{:S(2)}, u32[]{:S(2)}) collective-permute-start(bf16[368,512]{1,0:T(8,128)(2,1)S(1)} %get-tuple-element.79), channel_id=1, source_target_pairs={{1,2},{3,0},{5,6},{7,4},{9,10},{11,8},{13,14},{15,12},{17,18},{19,... | collective-permute-start | bytes 1130504 | tf_op jit(solution)/shard_map/factors_to_other/ppermute | solution.py:642
  16.7 12.7 %collective-permute-start.7 = (bf16[368,512]{1,0:T(8,128)(2,1)S(1)}, bf16[368,512]{1,0:T(8,128)(2,1)S(1)}, u32[]{:S(2)}, u32[]{:S(2)}) collective-permute-start(bf16[368,512]{1,0:T(8,128)(2,1)S(1)} %collective-permute-done.3.refs_1_), channel_id=1, source_target_pairs={{0,3},{2,1},{4,7},{6,5},{8,11},{10,9},{12,15},{14,13},{16,19},{18,... | collective-permute-start | bytes 1130504 | tf_op jit(solution)/shard_map/factors_across/ppermute | solution.py:642
  21.2 3.7 %copy-start = (s32[6,2048]{1,0:T(8,128)S(1)}, s32[6,2048]{1,0:T(8,128)}, u32[]{:S(2)}) copy-start(s32[6,2048]{1,0:T(8,128)} %dofs.1) | copy-start | bytes 147460
  21.3 3.7 %copy-start.1 = (f32[6,2048]{1,0:T(8,128)S(1)}, f32[6,2048]{1,0:T(8,128)}, u32[]{:S(2)}) copy-start(f32[6,2048]{1,0:T(8,128)} %coef) | copy-start | bytes 147460
  21.3 7.0 %collective-permute-start.1 = (bf16[128,1024]{1,0:T(8,128)(2,1)S(1)}, bf16[128,1024]{1,0:T(8,128)(2,1)S(1)}, u32[]{:S(2)}, u32[]{:S(2)}) collective-permute-start(bf16[128,1024]{1,0:T(8,128)(2,1)S(1)} %get-tuple-element.72), channel_id=1, source_target_pairs={{0,1},{1,0},{2,3},{3,2},{4,5},{5,4},{6,7},{7,6},{8,9},{9,8},{10,11... | collective-permute-start | bytes 786440 | tf_op jit(solution)/shard_map/terms_pair/ppermute | solution.py:642
  23.6 7.2 %collective-permute-start.5 = (bf16[368,512]{1,0:T(8,128)(2,1)S(1)}, bf16[368,512]{1,0:T(8,128)(2,1)S(1)}, u32[]{:S(2)}, u32[]{:S(2)}) collective-permute-start(bf16[368,512]{1,0:T(8,128)(2,1)S(1)} %collective-permute-done.3.refs_1_), channel_id=1, source_target_pairs={{0,32},{1,33},{2,34},{3,35},{4,36},{5,37},{6,38},{7,39},{8,40},{9,... | collective-permute-start | bytes 1130504 | tf_op jit(solution)/shard_map/pair_to_core/ppermute | solution.py:642
  23.6 7.2 %collective-permute-start.6 = (bf16[368,512]{1,0:T(8,128)(2,1)S(1)}, bf16[368,512]{1,0:T(8,128)(2,1)S(1)}, u32[]{:S(2)}, u32[]{:S(2)}) collective-permute-start(bf16[368,512]{1,0:T(8,128)(2,1)S(1)} %collective-permute-done.4.refs_3_), channel_id=1, source_target_pairs={{0,32},{1,33},{2,34},{3,35},{4,36},{5,37},{6,38},{7,39},{8,40},{9,... | collective-permute-start | bytes 1130504 | tf_op jit(solution)/shard_map/beside_to_core/ppermute | solution.py:642
  29.5 1.8 %collective-permute-start.8 = (bf16[368,512]{1,0:T(8,128)(2,1)S(1)}, bf16[368,512]{1,0:T(8,128)(2,1)S(1)}, u32[]{:S(2)}, u32[]{:S(2)}) collective-permute-start(bf16[368,512]{1,0:T(8,128)(2,1)S(1)} %collective-permute-done.7.refs_5_), channel_id=1, source_target_pairs={{0,32},{1,33},{2,34},{3,35},{4,36},{5,37},{6,38},{7,39},{8,40},{9,... | collective-permute-start | bytes 1130504 | tf_op jit(solution)/shard_map/far_to_core/ppermute | solution.py:642
  29.6 9.9 %collective-permute-start.2 = (bf16[64,2048]{1,0:T(8,128)(2,1)S(1)}, bf16[64,2048]{1,0:T(8,128)(2,1)S(1)}, u32[]{:S(2)}, u32[]{:S(2)}) collective-permute-start(bf16[64,2048]{1,0:T(8,128)(2,1)S(1)} %get-tuple-element.78), channel_id=1, source_target_pairs={{0,3},{1,2},{2,1},{3,0},{4,7},{5,6},{6,5},{7,4},{8,11},{9,10},{10,... | collective-permute-start | bytes 786440 | tf_op jit(solution)/shard_map/panels_ring/ppermute | solution.py:642
  33.0 20.4 %collective-permute-start.11 = (bf16[464,512]{1,0:T(8,128)(2,1)S(1)}, bf16[464,512]{1,0:T(8,128)(2,1)S(1)}, u32[]{:S(2)}, u32[]{:S(2)}) collective-permute-start(bf16[464,512]{1,0:T(8,128)(2,1)S(1)} %get-tuple-element.91), channel_id=1, source_target_pairs={{0,4},{1,5},{2,6},{3,7},{4,0},{5,1},{6,2},{7,3},{8,12},{9,13},{10,... | collective-permute-start | bytes 1425416 | tf_op jit(solution)/shard_map/factors_up/ppermute | solution.py:642
  35.0 18.4 %collective-permute-start.12 = (bf16[320,512]{1,0:T(8,128)(2,1)S(1)}, bf16[320,512]{1,0:T(8,128)(2,1)S(1)}, u32[]{:S(2)}, u32[]{:S(2)}) collective-permute-start(bf16[320,512]{1,0:T(8,128)(2,1)S(1)} %get-tuple-element.92), channel_id=1, source_target_pairs={{12,24},{13,25},{14,26},{15,27},{44,32},{45,33},{46,34},{47,35},{7... | collective-permute-start | bytes 983048 | tf_op jit(solution)/shard_map/factor_top/ppermute | solution.py:642
  40.2 12.5 %collective-permute-start.9 = (bf16[64,1536]{1,0:T(8,128)(2,1)S(1)}, bf16[64,1536]{1,0:T(8,128)(2,1)S(1)}, u32[]{:S(2)}, u32[]{:S(2)}) collective-permute-start(bf16[64,1536]{1,0:T(8,128)(2,1)S(1)} %get-tuple-element.89.mine), channel_id=1, source_target_pairs={{4,0},{5,1},{6,2},{7,3},{12,8},{13,9},{14,10},{15,11},{20,16},{21,... | collective-permute-start | bytes 589832 | tf_op jit(solution)/shard_map/panels_z1/ppermute | solution.py:642
  41.5 37.8 %collective-permute-start.18 = (bf16[1152,512]{1,0:T(8,128)(2,1)S(1)}, bf16[1152,512]{1,0:T(8,128)(2,1)S(1)}, u32[]{:S(2)}, u32[]{:S(2)}) collective-permute-start(bf16[1152,512]{1,0:T(8,128)(2,1)S(1)} %get-tuple-element.104.own), channel_id=1, source_target_pairs={{0,1},{2,3},{4,5},{6,7},{8,9},{10,11},{12,13},{14,15},{16,17},{18,... | collective-permute-start | bytes 3538952 | tf_op jit(solution)/shard_map/first_factor_to_odd/ppermute | solution.py:642
  53.4 1.9 %collective-permute-start.13 = (bf16[464,512]{1,0:T(8,128)(2,1)S(1)}, bf16[464,512]{1,0:T(8,128)(2,1)S(1)}, u32[]{:S(2)}, u32[]{:S(2)}) collective-permute-start(bf16[464,512]{1,0:T(8,128)(2,1)S(1)} %collective-permute-done.11.refs_0_), channel_id=1, source_target_pairs={{0,32},{1,33},{2,34},{3,35},{4,36},{5,37},{6,38},{7,39},{8,40},{9,... | collective-permute-start | bytes 1425416 | tf_op jit(solution)/shard_map/up_to_core/ppermute | solution.py:642
  53.6 2.8 %collective-permute-start.14 = (bf16[320,512]{1,0:T(8,128)(2,1)S(1)}, bf16[320,512]{1,0:T(8,128)(2,1)S(1)}, u32[]{:S(2)}, u32[]{:S(2)}) collective-permute-start(bf16[320,512]{1,0:T(8,128)(2,1)S(1)} %collective-permute-done.12.refs_2_), channel_id=1, source_target_pairs={{0,32},{1,33},{2,34},{3,35},{4,36},{5,37},{6,38},{7,39},{8,40},{9,... | collective-permute-start | bytes 983048 | tf_op jit(solution)/shard_map/last_to_core/ppermute | solution.py:642
  54.0 8.4 %collective-permute-start.10 = (bf16[64,1024]{1,0:T(8,128)(2,1)S(1)}, bf16[64,1024]{1,0:T(8,128)(2,1)S(1)}, u32[]{:S(2)}, u32[]{:S(2)}) collective-permute-start(bf16[64,1024]{1,0:T(8,128)(2,1)S(1)} %get-tuple-element.90.mine), channel_id=1, source_target_pairs={{0,8},{1,9},{2,10},{3,11},{4,12},{5,13},{6,14},{7,15},{8,0},{9,1},... | collective-permute-start | bytes 393224 | tf_op jit(solution)/shard_map/panels_z2/ppermute | solution.py:642
  63.0 6.5 %collective-permute-start.15 = (bf16[64,512]{1,0:T(8,128)(2,1)S(1)}, bf16[64,512]{1,0:T(8,128)(2,1)S(1)}, u32[]{:S(2)}, u32[]{:S(2)}) collective-permute-start(bf16[64,512]{1,0:T(8,128)(2,1)S(1)} %get-tuple-element.99.mine), channel_id=1, source_target_pairs={{0,24},{1,25},{2,26},{3,27},{4,28},{5,29},{6,30},{7,31},{8,16},{9,... | collective-permute-start | bytes 196616 | tf_op jit(solution)/shard_map/panels_z3/ppermute | solution.py:642
  70.7 5.8 %collective-permute-start.16 = (bf16[64,1536]{1,0:T(8,128)(2,1)S(1)}, bf16[64,1536]{1,0:T(8,128)(2,1)S(1)}, u32[]{:S(2)}, u32[]{:S(2)}) collective-permute-start(bf16[64,1536]{1,0:T(8,128)(2,1)S(1)} %shard_map.136.mine), channel_id=1, source_target_pairs={{0,4},{1,5},{2,6},{3,7},{4,0},{5,1},{6,2},{7,3},{8,12},{9,13},{10,... | collective-permute-start | bytes 589832 | tf_op jit(solution)/shard_map/down_z1/ppermute | solution.py:642
  77.5 7.7 %collective-permute-start.17 = (bf16[64,2048]{1,0:T(8,128)(2,1)S(1)}, bf16[64,2048]{1,0:T(8,128)(2,1)S(1)}, u32[]{:S(2)}, u32[]{:S(2)}) collective-permute-start(bf16[64,2048]{1,0:T(8,128)(2,1)S(1)} %shard_map.137.mine), channel_id=1, source_target_pairs={{0,3},{1,2},{2,1},{3,0},{4,7},{5,6},{6,5},{7,4},{8,11},{9,10},{10,... | collective-permute-start | bytes 786440 | tf_op jit(solution)/shard_map/down_ring/ppermute | solution.py:642
  86.7 5.4 %collective-permute-start.19 = (bf16[128,640]{1,0:T(8,128)(2,1)S(1)}, bf16[128,640]{1,0:T(8,128)(2,1)S(1)}, u32[]{:S(2)}, u32[]{:S(2)}) collective-permute-start(bf16[128,640]{1,0:T(8,128)(2,1)S(1)} %get-tuple-element.109), channel_id=1, source_target_pairs={{0,1},{1,0},{2,3},{3,2},{4,5},{5,4},{6,7},{7,6},{8,9},{9,8},{10,11... | collective-permute-start | bytes 491528 | tf_op jit(solution)/shard_map/rows_back/ppermute | solution.py:642
  92.1 7.5 %copy-start.3 = (bf16[128,512]{1,0:T(8,128)(2,1)S(1)}, bf16[128,512]{1,0:T(8,128)(2,1)}, u32[]{:S(2)}) copy-start(bf16[128,512]{1,0:T(8,128)(2,1)} %get-tuple-element.121) | copy-start | bytes 393220
  94.3 16.8 %all-to-all-start = ((bf16[32,16,256]{2,1,0:T(8,128)(2,1)}), bf16[32,16,256]{2,1,0:T(8,128)(2,1)S(1)}, u32[]{:S(2)}, u32[]{:S(2)}) async-start(bf16[32,16,256]{2,1,0:T(8,128)(2,1)} %bitcast.11), calls=%async_computation | async-start | bytes 524288 | tf_op jit(solution)/shard_map/all_to_all | solution.py:882
  99.6 5.4 %collective-permute-start.20 = (bf16[128,512]{1,0:T(8,128)(2,1)S(1)}, bf16[128,512]{1,0:T(8,128)(2,1)S(1)}, u32[]{:S(2)}, u32[]{:S(2)}) collective-permute-start(bf16[128,512]{1,0:T(8,128)(2,1)S(1)} %copy-done.3), channel_id=1, source_target_pairs={{0,1},{1,0},{2,3},{3,2},{4,5},{5,4},{6,7},{7,6},{8,9},{9,8},{10,11... | collective-permute-start | bytes 393224 | tf_op jit(solution)/shard_map/sep_back/ppermute | solution.py:642
  105.0 0.6 copy-start.2
